TPU v7x, 128 devices: a whole 4x4x4 slice. The times are simulated.
128 devices in a mesh: prow: 8 (over z, core), pcol: 16 (over x, y).
Axes of the slice: x: 4, y: 4, z: 4, core: 2. Of those that a mesh axis runs over, the one named last changes fastest.
Arguments:
- rhs: float32 [4, 8, 16, 128, 256], P(None, 'prow', 'pcol'), may hold values from -6 to 6
- dinv: float32 [4, 8, 16, 128, 128], P(None, 'prow', 'pcol'), as said below
- blocks: float32 [8, 16, 6, 32, 128, 128], P('prow', 'pcol'), may hold values from -0.046875 to 0.046875
- targets: int32 [8, 16, 6, 32], P('prow', 'pcol'), may hold values from -1 to 7, as said below
- sources: int32 [8, 16, 6, 32], P('prow', 'pcol'), may hold values from 0 to 15
Outputs:
- forward: float32 [4, 8, 16, 128, 256], P(None, 'prow', 'pcol')
- solution: float32 [4, 8, 16, 128, 256], P(None, 'prow', 'pcol')
Inputs may be any that keep to these rules, and one draw needn't show every extreme that they name: `dinv`: each diagonal-block inverse is lower triangular with diagonal entries between 0.5 and 1.5. `targets`: in each device's 32 slots of a level pair the live slots (not -1) come first; for every level pair some device has all 32 slots live.
All inputs are finite; a program needn't handle non-finite values.
Results may differ from a plain program's by a relative error of at most 0.0003.
Values sent between devices are 32-bit elements; how exact they have to be, the bound alone decides.
No kernel may reach another device: no remote copies, remote signals or barrier semaphores. Data moves between devices by JAX's collectives and lax.ppermute only.
A program may use at most 128 MiB of HBM per device.

v0:
```python
import jax
import jax.numpy as jnp
from jax import lax
from jax.sharding import PartitionSpec as P

W = 128
R = 256
LEV = 4


def pair_index(high, low):
    return high * (high - 1) // 2 + low


def body(rhs, dinv, blocks, targets, sources):
    best = lax.Precision.HIGHEST
    n_rows = lax.axis_size("prow")
    n_cols = lax.axis_size("pcol")
    right = rhs[:, 0, 0]
    inverse = dinv[:, 0, 0]
    panels = blocks[0, 0]
    aims = targets[0, 0]
    anchor = sources[0, 0]
    row_ids = jnp.arange(n_rows, dtype=jnp.int32)[:, None]
    col_ids = jnp.arange(n_cols, dtype=jnp.int32)[:, None]
    pools = []
    solved = []
    for level in range(LEV):
        if level > 0:
            partial_value = jnp.zeros((n_rows, W, R), jnp.float32)
            for lower in range(level):
                index = pair_index(level, lower)
                chosen = pools[lower][anchor[index]]
                product = jnp.einsum("bij,bjk->bik", panels[index], chosen, precision=best)
                hits = (aims[index][None, :] == row_ids).astype(jnp.float32)
                partial_value = partial_value + jnp.einsum(
                    "tb,bik->tik", hits, product, precision=best
                )
            update = lax.psum_scatter(partial_value, "prow", scatter_dimension=0, tiled=True)[0]
            current = jnp.dot(
                inverse[level],
                right[level] - update,
                precision=best,
                preferred_element_type=jnp.float32,
            )
        else:
            current = jnp.dot(
                inverse[0], right[0], precision=best, preferred_element_type=jnp.float32
            )
        solved.append(current)
        if level + 1 < LEV:
            pools.append(lax.all_gather(current[None], "pcol", axis=0, tiled=True))
    result = [None] * LEV
    columns = {}
    for level in reversed(range(LEV)):
        if level < LEV - 1:
            partial_value = jnp.zeros((n_cols, W, R), jnp.float32)
            for higher in range(level + 1, LEV):
                index = pair_index(higher, level)
                live = aims[index] >= 0
                chosen = columns[higher][jnp.maximum(aims[index], 0)]
                product = jnp.einsum("bji,bjk->bik", panels[index], chosen, precision=best)
                hits = ((anchor[index][None, :] == col_ids) & live[None, :]).astype(jnp.float32)
                partial_value = partial_value + jnp.einsum(
                    "sb,bik->sik", hits, product, precision=best
                )
            update = lax.psum_scatter(partial_value, "pcol", scatter_dimension=0, tiled=True)[0]
            current = jnp.dot(
                inverse[level].T,
                solved[level] - update,
                precision=best,
                preferred_element_type=jnp.float32,
            )
        else:
            current = jnp.dot(
                inverse[level].T, solved[level], precision=best, preferred_element_type=jnp.float32
            )
        result[level] = current
        if level > 0:
            columns[level] = lax.all_gather(current[None], "prow", axis=0, tiled=True)
    forward = jnp.stack(solved)[:, None, None]
    solution = jnp.stack(result)[:, None, None]
    return (forward, solution)


def solution(mesh):
    placed = (
        P(None, "prow", "pcol", None, None),
        P(None, "prow", "pcol", None, None),
        P("prow", "pcol", None, None, None, None),
        P("prow", "pcol", None, None),
        P("prow", "pcol", None, None),
    )
    return jax.shard_map(
        body,
        mesh=mesh,
        in_specs=placed,
        out_specs=(P(None, "prow", "pcol", None, None), P(None, "prow", "pcol", None, None)),
        check_vma=False,
    )
```

profile of v0, /device:TPU:0, one launch (start us, length us, event | category | flops | bytes accessed | tf_op | source)
XLA Modules:
  0.0 735.8 jit_solution(5242462495088841324)
XLA Ops:
  11.2 46.8 %all-gather.13.cloned.1.call-done = f32[2048,256]{1,0:T(8,128)} async-done(((f32[128,256]{1,0:T(8,128)}), f32[2048,256]{1,0:T(8,128)}) %all-gather.13.cloned.1.call-update) | async-done | bytes 2097168 | tf_op jit(solution)/shard_map/all_gather | solution.py:52
  58.0 4.4 gather_fusion
  62.4 10.6 %convolution_bitcast_fusion.11 = f32[32,128,256]{1,2,0:T(8,128)} fusion(f32[32,128,256]{2,1,0:T(8,128)} %gather_fusion, f32[1,1,6,32,128,128]{5,4,3,2,1,0:T(8,128)} %param.7), kind=kOutput, calls=%fused_computation.23 | convolution fusion | flops 1610612736 | bytes 10485760 | tf_op jit(solution)/shard_map/bij,bjk->bik/dot_general | solution.py:34
  73.0 5.5 copy.77
  78.5 3.8 fusion.84
  83.7 31.6 %reduce-scatter.13.cloned.1.call-done = f32[1,128,256]{2,1,0:T(8,128)} async-done(((f32[8,128,256]{2,1,0:T(8,128)}), f32[1,128,256]{2,1,0:T(8,128)}) %reduce-scatter.13.cloned.1.call-update) | async-done | bytes 131088 | tf_op jit(solution)/shard_map/reduce_scatter | solution.py:39
  115.3 1.9 fusion.30
  117.5 2.8 gather_fusion.1
  120.3 10.6 %convolution_bitcast_fusion.10 = f32[32,128,256]{1,2,0:T(8,128)} fusion(f32[32,128,256]{2,1,0:T(8,128)} %gather_fusion.1, f32[1,1,6,32,128,128]{5,4,3,2,1,0:T(8,128)} %param.7), kind=kOutput, calls=%fused_computation.22 | convolution fusion | flops 1610612736 | bytes 10485760 | tf_op jit(solution)/shard_map/bij,bjk->bik/dot_general | solution.py:34
  130.9 5.5 copy.81
  136.4 3.6 fusion.87
  140.0 21.5 %all-gather.15.cloned.1.call-done = f32[2048,256]{1,0:T(8,128)} async-done(((f32[128,256]{1,0:T(8,128)}), f32[2048,256]{1,0:T(8,128)}) %all-gather.15.cloned.1.call-update) | async-done | bytes 2097168 | tf_op jit(solution)/shard_map/all_gather | solution.py:52
  161.5 4.4 gather_fusion.2
  165.9 10.6 %convolution_bitcast_fusion.9 = f32[32,128,256]{1,2,0:T(8,128)} fusion(f32[32,128,256]{2,1,0:T(8,128)} %gather_fusion.2, f32[1,1,6,32,128,128]{5,4,3,2,1,0:T(8,128)} %param.7), kind=kOutput, calls=%fused_computation.21 | convolution fusion | flops 1610612736 | bytes 10485760 | tf_op jit(solution)/shard_map/bij,bjk->bik/dot_general | solution.py:34
  176.5 5.5 copy.83
  182.0 3.7 convolution_add_fusion.3
  187.3 31.4 %reduce-scatter.15.cloned.1.call-done = f32[1,128,256]{2,1,0:T(8,128)} async-done(((f32[8,128,256]{2,1,0:T(8,128)}), f32[1,128,256]{2,1,0:T(8,128)}) %reduce-scatter.15.cloned.1.call-update) | async-done | bytes 131088 | tf_op jit(solution)/shard_map/reduce_scatter | solution.py:39
  218.7 1.9 fusion.28
  220.7 2.8 gather_fusion.3
  223.6 10.6 %convolution_bitcast_fusion.8 = f32[32,128,256]{1,2,0:T(8,128)} fusion(f32[32,128,256]{2,1,0:T(8,128)} %gather_fusion.3, f32[1,1,6,32,128,128]{5,4,3,2,1,0:T(8,128)} %param.7), kind=kOutput, calls=%fused_computation.20 | convolution fusion | flops 1610612736 | bytes 10485760 | tf_op jit(solution)/shard_map/bij,bjk->bik/dot_general | solution.py:34
  234.1 5.5 copy.87
  239.7 3.8 fusion.92
  243.4 2.8 gather_fusion.4
  246.3 10.6 %convolution_bitcast_fusion.7 = f32[32,128,256]{1,2,0:T(8,128)} fusion(f32[32,128,256]{2,1,0:T(8,128)} %gather_fusion.4, f32[1,1,6,32,128,128]{5,4,3,2,1,0:T(8,128)} %param.7), kind=kOutput, calls=%fused_computation.19 | convolution fusion | flops 1610612736 | bytes 10485760 | tf_op jit(solution)/shard_map/bij,bjk->bik/dot_general | solution.py:34
  256.8 5.5 copy.89
  262.4 3.6 convolution_add_fusion.2
  266.0 4.4 gather_fusion.5
  270.4 11.0 %convolution_bitcast_fusion.6 = f32[32,128,256]{1,2,0:T(8,128)} fusion(f32[32,128,256]{2,1,0:T(8,128)} %gather_fusion.5, f32[1,1,6,32,128,128]{5,4,3,2,1,0:T(8,128)} %param.7), kind=kOutput, calls=%fused_computation.18 | convolution fusion | flops 1610612736 | bytes 10485760 | tf_op jit(solution)/shard_map/bij,bjk->bik/dot_general | solution.py:34
  281.4 5.5 copy.91
  286.9 3.7 convolution_add_fusion.1
  292.0 30.9 %reduce-scatter.17.cloned.1.call-done = f32[1,128,256]{2,1,0:T(8,128)} async-done(((f32[8,128,256]{2,1,0:T(8,128)}), f32[1,128,256]{2,1,0:T(8,128)}) %reduce-scatter.17.cloned.1.call-update) | async-done | bytes 131088 | tf_op jit(solution)/shard_map/reduce_scatter | solution.py:39
  326.5 21.1 %all-gather.19.cloned.1.call-done = f32[1024,256]{0,1:T(8,128)} async-done(((f32[128,256]{0,1:T(8,128)}), f32[1024,256]{0,1:T(8,128)}) %all-gather.19.cloned.1.call-update) | async-done | bytes 1048592 | tf_op jit(solution)/shard_map/all_gather | solution.py:80
  349.1 2.8 gather_fusion.6
  352.0 10.7 %convolution_bitcast_fusion.5 = f32[32,128,256]{1,2,0:T(8,128)} fusion(f32[32,128,256]{2,1,0:T(8,128)} %gather_fusion.6, f32[1,1,6,32,128,128]{5,4,3,2,1,0:T(8,128)} %param.7), kind=kOutput, calls=%fused_computation.17 | convolution fusion | flops 1610612736 | bytes 10485760 | tf_op jit(solution)/shard_map/bji,bjk->bik/dot_general | solution.py:62
  362.7 5.5 copy.96
  368.2 3.8 fusion.65
  372.1 2.6 copy.97
  374.7 75.2 %reduce-scatter.19.cloned.1.call-done = f32[1,128,256]{2,1,0:T(8,128)} async-done(((f32[16,128,256]{2,1,0:T(8,128)}), f32[1,128,256]{2,1,0:T(8,128)}) %reduce-scatter.19.cloned.1.call-update) | async-done | bytes 131088
  449.8 1.9 fusion.25
  451.9 2.8 gather_fusion.8
  454.7 10.8 %convolution_bitcast_fusion.3 = f32[32,128,256]{1,2,0:T(8,128)} fusion(f32[32,128,256]{2,1,0:T(8,128)} %gather_fusion.8, f32[1,1,6,32,128,128]{5,4,3,2,1,0:T(8,128)} %param.7), kind=kOutput, calls=%fused_computation.15 | convolution fusion | flops 1610612736 | bytes 10485760 | tf_op jit(solution)/shard_map/bji,bjk->bik/dot_general | solution.py:62
  465.5 5.5 copy.103
  471.0 3.9 all-gather.21.cloned.1.call-done
  476.4 2.9 gather_fusion.7
  479.3 10.6 %convolution_bitcast_fusion.4 = f32[32,128,256]{1,2,0:T(8,128)} fusion(f32[32,128,256]{2,1,0:T(8,128)} %gather_fusion.7, f32[1,1,6,32,128,128]{5,4,3,2,1,0:T(8,128)} %param.7), kind=kOutput, calls=%fused_computation.16 | convolution fusion | flops 1610612736 | bytes 10485760 | tf_op jit(solution)/shard_map/bji,bjk->bik/dot_general | solution.py:62
  489.9 5.7 copy.100
  495.6 3.9 fusion.61
  501.4 2.6 copy.104
  504.0 75.2 %reduce-scatter.21.cloned.1.call-done = f32[1,128,256]{2,1,0:T(8,128)} async-done(((f32[16,128,256]{2,1,0:T(8,128)}), f32[1,128,256]{2,1,0:T(8,128)}) %reduce-scatter.21.cloned.1.call-update) | async-done | bytes 131088
  579.2 1.9 fusion.24
  581.2 2.8 gather_fusion.11
  584.0 11.0 %convolution_bitcast_fusion = f32[32,128,256]{1,2,0:T(8,128)} fusion(f32[32,128,256]{2,1,0:T(8,128)} %gather_fusion.11, f32[1,1,6,32,128,128]{5,4,3,2,1,0:T(8,128)} %param.7), kind=kOutput, calls=%fused_computation.12 | convolution fusion | flops 1610612736 | bytes 10485760 | tf_op jit(solution)/shard_map/bji,bjk->bik/dot_general | solution.py:62
  595.0 5.5 copy.113
  600.5 2.8 gather_fusion.10
  603.3 10.6 %convolution_bitcast_fusion.1 = f32[32,128,256]{1,2,0:T(8,128)} fusion(f32[32,128,256]{2,1,0:T(8,128)} %gather_fusion.10, f32[1,1,6,32,128,128]{5,4,3,2,1,0:T(8,128)} %param.7), kind=kOutput, calls=%fused_computation.13 | convolution fusion | flops 1610612736 | bytes 10485760 | tf_op jit(solution)/shard_map/bji,bjk->bik/dot_general | solution.py:62
  614.0 5.5 copy.110
  619.5 3.7 fusion.72
  624.8 2.8 gather_fusion.9
  627.7 10.8 %convolution_bitcast_fusion.2 = f32[32,128,256]{1,2,0:T(8,128)} fusion(f32[32,128,256]{2,1,0:T(8,128)} %gather_fusion.9, f32[1,1,6,32,128,128]{5,4,3,2,1,0:T(8,128)} %param.7), kind=kOutput, calls=%fused_computation.14 | convolution fusion | flops 1610612736 | bytes 10485760 | tf_op jit(solution)/shard_map/bji,bjk->bik/dot_general | solution.py:62
  638.5 5.5 copy.107
  644.0 3.9 fusion.57
  647.9 2.1 add_add_fusion
  650.1 2.6 copy.114
  653.6 72.8 %reduce-scatter.23.cloned.1.call-done = f32[1,128,256]{2,1,0:T(8,128)} async-done(((f32[16,128,256]{2,1,0:T(8,128)}), f32[1,128,256]{2,1,0:T(8,128)}) %reduce-scatter.23.cloned.1.call-update) | async-done | bytes 131088
  (97 shorter events, 22.3 us)
Async XLA Ops:
  7.2 50.8 %all-gather.13.cloned.1.call-start = ((), (), s32[]{:S(2)}) async-start(), calls=%async_computation.9 | async-start | bytes 2228224 | tf_op jit(solution)/shard_map/all_gather | solution.py:52
  9.1 106.2 %reduce-scatter.13.cloned.1.call-start = ((), (), s32[]{:S(2)}) async-start(), calls=%async_computation.6 | async-start | bytes 1179648 | tf_op jit(solution)/shard_map/reduce_scatter | solution.py:39
  78.5 36.8 %copy-start.10 = (f32[4,1,1,128,128]{4,3,2,1,0:T(8,128)S(1)}, f32[4,1,1,128,128]{4,3,2,1,0:T(8,128)}, u32[]{:S(2)}) copy-start(f32[4,1,1,128,128]{4,3,2,1,0:T(8,128)} %param.6) | copy-start | bytes 786436
  78.5 39.0 %copy-start = (f32[2048,256]{1,0:T(8,128)S(1)}, f32[2048,256]{1,0:T(8,128)}, u32[]{:S(2)}) copy-start(f32[2048,256]{1,0:T(8,128)} %all-gather.13.cloned.1.call-done) | copy-start | bytes 6291460
  83.7 77.9 %all-gather.15.cloned.1.call-start = ((), (), s32[]{:S(2)}) async-start(), calls=%async_computation.10 | async-start | bytes 2228224 | tf_op jit(solution)/shard_map/all_gather | solution.py:52
  117.2 101.5 %reduce-scatter.15.cloned.1.call-start = ((), (), s32[]{:S(2)}) async-start(), calls=%async_computation.7 | async-start | bytes 1179648 | tf_op jit(solution)/shard_map/reduce_scatter | solution.py:39
  187.1 78.9 %all-gather.17.cloned.1.call-start = ((), (), s32[]{:S(2)}) async-start(), calls=%async_computation.11 | async-start | bytes 2228224 | tf_op jit(solution)/shard_map/all_gather | solution.py:52
  220.7 102.2 %reduce-scatter.17.cloned.1.call-start = ((), (), s32[]{:S(2)}) async-start(), calls=%async_computation.8 | async-start | bytes 1179648 | tf_op jit(solution)/shard_map/reduce_scatter | solution.py:39
  239.7 3.8 copy-start.1
  286.9 38.4 %copy-start.12 = (s32[1,1,6,32]{3,1,2,0:T(1,128)S(1)}, s32[1,1,6,32]{3,1,2,0:T(1,128)}, u32[]{:S(2)}) copy-start(s32[1,1,6,32]{3,1,2,0:T(1,128)} %param.9) | copy-start | bytes 2308
  286.9 39.0 %copy-start.13 = (s32[1,1,6,32]{3,1,2,0:T(1,128)S(1)}, s32[1,1,6,32]{3,1,2,0:T(1,128)}, u32[]{:S(2)}) copy-start(s32[1,1,6,32]{3,1,2,0:T(1,128)} %param.8) | copy-start | bytes 2308
  292.0 55.6 %all-gather.19.cloned.1.call-start = ((), (), s32[]{:S(2)}) async-start(), calls=%async_computation.12 | async-start | bytes 1179648 | tf_op jit(solution)/shard_map/all_gather | solution.py:80
  325.2 124.7 %reduce-scatter.19.cloned.1.call-start = ((), (), s32[]{:S(2)}) async-start(), calls=%async_computation.15 | async-start | bytes 2228224
  372.0 77.8 %copy-start.5 = (f32[256,128]{0,1:T(8,128)S(1)}, f32[256,128]{0,1:T(8,128)}, u32[]{:S(2)}) copy-start(f32[256,128]{0,1:T(8,128)} %fusion.28) | copy-start | bytes 393220
  372.0 77.8 %copy-start.11 = (f32[4,1,1,128,128]{4,3,2,1,0:T(8,128)S(1)}, f32[4,1,1,128,128]{4,3,2,1,0:T(8,128)}, u32[]{:S(2)}) copy-start(f32[4,1,1,128,128]{4,3,2,1,0:T(8,128)} %param.6) | copy-start | bytes 786436
  372.0 79.8 %copy-start.16 = (s32[32]{0:T(128)S(1)}, s32[32]{0:T(128)}, u32[]{:S(2)}) copy-start(s32[32]{0:T(128)} %get-tuple-element.24) | copy-start | bytes 388
  372.0 79.8 %copy-start.17 = (s32[32]{0:T(128)S(1)}, s32[32]{0:T(128)}, u32[]{:S(2)}) copy-start(s32[32]{0:T(128)} %get-tuple-element.25) | copy-start | bytes 388
  372.0 79.9 %copy-start.14 = (s32[32]{0:T(128)S(1)}, s32[32]{0:T(128)}, u32[]{:S(2)}) copy-start(s32[32]{0:T(128)} %get-tuple-element.22) | copy-start | bytes 388
  372.0 79.9 %copy-start.15 = (s32[32]{0:T(128)S(1)}, s32[32]{0:T(128)}, u32[]{:S(2)}) copy-start(s32[32]{0:T(128)} %get-tuple-element.26) | copy-start | bytes 388
  374.6 100.2 %all-gather.21.cloned.1.call-start = ((), (), s32[]{:S(2)}) async-start(), calls=%async_computation.13 | async-start | bytes 1179648 | tf_op jit(solution)/shard_map/all_gather | solution.py:80
  451.8 127.4 %reduce-scatter.21.cloned.1.call-start = ((), (), s32[]{:S(2)}) async-start(), calls=%async_computation.16 | async-start | bytes 2228224
  495.6 3.9 copy-start.3
  501.4 77.8 %copy-start.4 = (f32[256,128]{0,1:T(8,128)S(1)}, f32[256,128]{0,1:T(8,128)}, u32[]{:S(2)}) copy-start(f32[256,128]{0,1:T(8,128)} %fusion.30) | copy-start | bytes 393220
  504.0 119.3 %all-gather.23.cloned.1.call-start = ((), (), s32[]{:S(2)}) async-start(), calls=%async_computation.14 | async-start | bytes 1179648 | tf_op jit(solution)/shard_map/all_gather | solution.py:80
  581.1 145.2 %reduce-scatter.23.cloned.1.call-start = ((), (), s32[]{:S(2)}) async-start(), calls=%async_computation.17 | async-start | bytes 2228224
  614.0 5.5 copy-start.20
  614.0 5.5 copy-start.21
  638.4 5.5 copy-start.18
  638.5 5.5 copy-start.19
  644.0 4.0 copy-start.2
  650.0 2.7 copy-start.6
  650.1 77.6 %copy-start.7 = (f32[256,128]{1,0:T(8,128)S(1)}, f32[256,128]{1,0:T(8,128)}, u32[]{:S(2)}) copy-start(f32[256,128]{1,0:T(8,128)} %fusion.25) | copy-start | bytes 393220
  650.1 77.6 %copy-start.8 = (f32[256,128]{1,0:T(8,128)S(1)}, f32[256,128]{1,0:T(8,128)}, u32[]{:S(2)}) copy-start(f32[256,128]{1,0:T(8,128)} %fusion.24) | copy-start | bytes 393220
  650.1 77.6 %copy-start.9 = (f32[256,128]{1,0:T(8,128)S(1)}, f32[256,128]{1,0:T(8,128)}, u32[]{:S(2)}) copy-start(f32[256,128]{1,0:T(8,128)} %fusion.38) | copy-start | bytes 393220
Sparse Core Ops, SparseCore 0:
  10.7 47.2 all-gather.12
  83.8 31.4 reduce-scatter.12
  118.0 43.4 all-gather.14
  187.2 31.4 reduce-scatter.14
  220.8 43.4 all-gather.16
  292.1 30.7 reduce-scatter.16
  325.3 22.2 all-gather.18
  374.8 75.0 reduce-scatter.18
  451.9 22.8 all-gather.20
  504.1 75.0 reduce-scatter.20
  581.3 22.8 all-gather.22
  652.8 73.5 reduce-scatter.22
where the time goes:
time: 743 us; the launch traced here: 736 us
  waiting for transfers between devices  410 us (55%)
  matrix products  183 us (25%)
  local copies, waits for them, and re-layouts  123 us (17%)
  between operations  14.8 us (2%)
    unnamed x15, waiting for transfers between devices  223 us
    reduce_scatter x3, waiting for transfers between devices, body(): lax.psum_scatter(partial_value, 'prow', scatter_dimension=0, tiled=True)[0]  93.8 us
    all_gather x3, waiting for transfers between devices, body(): pools.append(lax.all_gather(current[None], 'pcol', axis=0, tiled=True))  68.3 us
    dot_general x6, matrix products, body(): product = jnp.einsum('bji,bjk->bik', panels[index], chosen, precision=best)  64.5 us
    dot_general x6, matrix products, body(): product = jnp.einsum('bij,bjk->bik', panels[index], chosen, precision=best)  63.8 us
    dot_general x6, local copies, waits for them, and re-layouts, body(): product = jnp.einsum('bji,bjk->bik', panels[index], chosen, precision=best)  33.2 us
    dot_general x6, local copies, waits for them, and re-layouts, body(): product = jnp.einsum('bij,bjk->bik', panels[index], chosen, precision=best)  33.1 us
    all_gather x3, waiting for transfers between devices, body(): columns[level] = lax.all_gather(current[None], 'prow', axis=0, tiled=True)  25 us
  transfers between devices with their start and end apart: 12, of which 10 were waited for; matrix products, arithmetic and copies ran while one was open for 18% of the time, Pallas kernels for 0%

commit v1 on v0

v1 whole, which is shorter than its diff:
```python
import functools

import jax
import jax.numpy as jnp
from jax import lax
from jax.experimental import pallas as pl
from jax.experimental.pallas import tpu as pltpu
from jax.sharding import PartitionSpec as P

W = 128
R = 256
LEV = 4
NZ, NC, NX, NY = 4, 2, 4, 4
CHUNK = 8
BOTH = ("prow", "pcol")


def pair_index(high, low):
    return high * (high - 1) // 2 + low


def device(z, c, x, y):
    return (z % NZ * NC + c) * NX * NY + x % NX * NY + y % NY


def shift_plane(value, step, phase):
    pairs = []
    for z in range(NZ):
        for c in range(NC):
            for x in range(NX):
                for y in range(NY):
                    if c == phase:
                        there = device(z, c, x + step, y)
                    else:
                        there = device(z, c, x, y + step)
                    pairs.append((device(z, c, x, y), there))
    return lax.ppermute(value, BOTH, pairs)


def shift_z(value, step):
    pairs = [(z * NC + c, (z + step) % NZ * NC + c) for z in range(NZ) for c in range(NC)]
    return lax.ppermute(value, "prow", pairs)


def swap_core(value):
    pairs = [(z * NC + c, z * NC + 1 - c) for z in range(NZ) for c in range(NC)]
    return lax.ppermute(value, "prow", pairs)


def split(value):
    high = value.astype(jnp.bfloat16)
    low = (value - high.astype(jnp.float32)).astype(jnp.bfloat16)
    return high, low


def pair_kernel(n_in, n_out, flip, has_init, slots, gathered, *refs):
    take, put, live = slots
    count = gathered
    vectors = refs[:count]
    blocks = refs[count]
    refs = refs[count + 1 :]
    init = refs[:n_out] if has_init else ()
    refs = refs[n_out:] if has_init else refs
    outs, (halves, total) = refs[:n_out], refs[n_out:]
    step = pl.program_id(0)

    @pl.when(step == 0)
    def _():
        per = n_in // count
        for k in range(n_in):
            high, low = split(vectors[k // per][k % per])
            halves[k, :W] = high
            halves[k, W:] = low
        per = total.shape[0] // n_out
        for k in range(n_out):
            if has_init:
                total[k * per : (k + 1) * per] = init[k][...]
            else:
                total[k * per : (k + 1) * per] = jnp.zeros((per, W, R), jnp.float32)

    for j in range(CHUNK):
        slot = step * CHUNK + j
        block = blocks[0, j]
        block = jnp.where(live[slot] > 0, block, 0.0)
        if flip:
            block = block.T
        high, low = split(block)
        left = jnp.concatenate(
            [jnp.concatenate([high, high], axis=1), jnp.concatenate([low, low], axis=1)], axis=0
        )
        product = jnp.dot(left, halves[take[slot]], preferred_element_type=jnp.float32)
        total[put[slot]] += product[:W] + product[W:]

    @pl.when(step == pl.num_programs(0) - 1)
    def _():
        per = total.shape[0] // n_out
        for k in range(n_out):
            outs[k][...] = total[k * per : (k + 1) * per]


def pair_product(index, flip, take, put, live, vectors, panels, init, n_out, total):
    n_in = sum(v.shape[0] for v in vectors)
    nb = panels.shape[1]
    per = total // n_out

    def kernel(take_ref, put_ref, live_ref, *refs):
        pair_kernel(n_in, n_out, flip, init is not None, (take_ref, put_ref, live_ref), len(vectors), *refs)

    def whole(step, *_):
        return (0, 0, 0)

    inits = [] if init is None else list(init)
    return pl.pallas_call(
        kernel,
        grid_spec=pltpu.PrefetchScalarGridSpec(
            num_scalar_prefetch=3,
            grid=(nb // CHUNK,),
            in_specs=[pl.BlockSpec(v.shape, whole) for v in vectors]
            + [pl.BlockSpec((1, CHUNK, W, W), lambda step, *_: (index, step, 0, 0))]
            + [pl.BlockSpec(v.shape, whole) for v in inits],
            out_specs=[pl.BlockSpec((per, W, R), whole)] * n_out,
            scratch_shapes=[
                pltpu.VMEM((n_in, 2 * W, R), jnp.bfloat16),
                pltpu.VMEM((total, W, R), jnp.float32),
            ],
        ),
        out_shape=[jax.ShapeDtypeStruct((per, W, R), jnp.float32)] * n_out,
        compiler_params=pltpu.CompilerParams(vmem_limit_bytes=40 * 1024 * 1024),
        cost_estimate=pl.CostEstimate(
            flops=nb * 8 * W * W * R, bytes_accessed=nb * W * W * 4, transcendentals=0
        ),
    )(take, put, live, *vectors, panels, *inits)


def solve_kernel(flip, terms, inverse, base, *refs):
    out = refs[-1]
    value = base[...]
    if terms:
        gone = refs[0][...]
        for ref in refs[1:terms]:
            gone = gone + ref[...]
        value = value - gone
    matrix = inverse[...]
    if flip:
        matrix = matrix.T
    out[...] = jnp.dot(
        matrix, value, precision=lax.Precision.HIGHEST, preferred_element_type=jnp.float32
    )


def solve(flip, inverse, base, gone):
    return pl.pallas_call(
        functools.partial(solve_kernel, flip, len(gone)),
        out_shape=jax.ShapeDtypeStruct((W, R), jnp.float32),
        cost_estimate=pl.CostEstimate(flops=12 * W * W * R, bytes_accessed=4 * W * R, transcendentals=0),
    )(inverse, base, *gone)


def gather_plane(value):
    units = jnp.stack([value] + [shift_plane(value, d, 0) for d in (1, 2, 3)])
    return [units] + [shift_plane(units, d, 1) for d in (1, 2, 3)]


def scatter_plane(groups):
    units = groups[0]
    for d in (1, 2, 3):
        units = units + shift_plane(groups[d], d, 0)
    return [units[0]] + [shift_plane(units[d], d, 1) for d in (1, 2, 3)]


def scatter_z(mine, other):
    units = mine + swap_core(other)
    return [units[0]] + [shift_z(units[d], d) for d in (1, 2, 3)]


def gather_z(value):
    units = jnp.stack([value] + [shift_z(value, d) for d in (1, 2, 3)])
    return [units, swap_core(units)]


def body(rhs, dinv, blocks, targets, sources):
    right = rhs[:, 0, 0]
    inverse = dinv[:, 0, 0]
    panels = blocks[0, 0]
    aims = targets[0, 0]
    anchor = sources[0, 0]
    row = lax.axis_index("prow")
    col = lax.axis_index("pcol")
    z, core = row // NC, row % NC
    x, y = col // NY, col % NY
    live = (aims >= 0).astype(jnp.int32)
    rows = jnp.maximum(aims, 0)
    off_x = (x - anchor // NY) % NX
    off_y = (y - anchor % NY) % NY
    near_x, near_y = (-off_x) % NX, (-off_y) % NY
    first = core == 0
    take_plane = jnp.where(first, off_y * NX + off_x, off_x * NY + off_y)
    put_plane = jnp.where(first, near_x * NY + near_y, near_y * NX + near_x)
    off_z = (z - rows // NC) % NZ
    across = (rows % NC != core).astype(jnp.int32) * NZ
    take_z = across + off_z
    put_z = across + (-off_z) % NZ

    def forth(high, low, vectors, init):
        index = pair_index(high, low)
        return pair_product(
            index, False, take_plane[index], put_z[index], live[index], vectors, panels, init, 2, 8
        )

    def back(high, low, vectors, init):
        index = pair_index(high, low)
        return pair_product(
            index, True, take_z[index], put_plane[index], live[index], vectors, panels, init, 4, 16
        )

    solved = [None] * LEV
    sums = [None] * LEV
    for level in range(LEV):
        gone = [] if level == 0 else scatter_z(*sums[level])
        solved[level] = solve(False, inverse[level], right[level], gone)
        if level + 1 < LEV:
            vectors = gather_plane(solved[level])
            for high in range(level + 1, LEV):
                sums[high] = forth(high, level, vectors, sums[high])
    result = [None] * LEV
    sums = [None] * LEV
    for level in reversed(range(LEV)):
        gone = [] if level == LEV - 1 else scatter_plane(sums[level])
        result[level] = solve(True, inverse[level], solved[level], gone)
        if level > 0:
            vectors = gather_z(result[level])
            for low in reversed(range(level)):
                sums[low] = back(level, low, vectors, sums[low])
    forward = jnp.stack(solved)[:, None, None]
    solution = jnp.stack(result)[:, None, None]
    return (forward, solution)


def solution(mesh):
    placed = (
        P(None, "prow", "pcol", None, None),
        P(None, "prow", "pcol", None, None),
        P("prow", "pcol", None, None, None, None),
        P("prow", "pcol", None, None),
        P("prow", "pcol", None, None),
    )
    return jax.shard_map(
        body,
        mesh=mesh,
        in_specs=placed,
        out_specs=(P(None, "prow", "pcol", None, None), P(None, "prow", "pcol", None, None)),
        check_vma=False,
    )
```

time: 743 us -> 311 us (0.42)
  waiting for transfers between devices: 410 us -> 142 us
  matrix products: 183 us -> 0 us
  local copies, waits for them, and re-layouts: 123 us -> 12.1 us
  starting transfers between devices: 0.88 us -> 72.5 us
  Pallas kernels: 0 us -> 70.9 us
  between operations: 14.8 us -> 1.04 us
    unnamed x15 -> x0, waiting for transfers between devices: 223 us -> none
    dot_general x32 -> x0, matrix products: 183 us -> none  [the longest x6 64.5 us: body(): product = jnp.einsum('bji,bjk->bik', panels[index], chosen, precision=best)]
    ppermute x0 -> x60, waiting for transfers between devices: none -> 142 us  [the longest x36 95.6 us: shift_plane(): return lax.ppermute(value, BOTH, pairs)]
    reduce_scatter x3 -> x0, waiting for transfers between devices: 93.8 us -> none  [body(): lax.psum_scatter(partial_value, 'prow', scatter_dimension=0, tiled=True)[0]]
    all_gather x6 -> x0, waiting for transfers between devices: 93.4 us -> none  [the longest x3 68.3 us: body(): pools.append(lax.all_gather(current[None], 'pcol', axis=0, tiled=True))]
    ppermute x0 -> x60, starting transfers between devices: none -> 72.5 us  [the longest x36 47.9 us: shift_plane(): return lax.ppermute(value, BOTH, pairs)]
    pallas_call x0 -> x20, Pallas kernels: none -> 70.9 us  [the longest x12 54.3 us: pair_product(): pl.pallas_call(kernel, grid_spec=pltpu.PrefetchScalarGridSpec(num_scalar_...]
    dot_general x15 -> x0, local copies, waits for them, and re-layouts: 70.3 us -> none  [the longest x6 33.2 us: body(): product = jnp.einsum('bji,bjk->bik', panels[index], chosen, precision=best)]
  transfers between devices with their start and end apart: 12 -> 60, of which waited for: 10 -> 49; matrix products, arithmetic and copies ran while one was open for 18% -> 1% of each run, Pallas kernels for 0% -> 9%
where the time goes in v1:
time: 311 us; the launch traced here: 309 us
  waiting for transfers between devices  142 us (46%)
  starting transfers between devices  72.5 us (23%)
  Pallas kernels  70.9 us (23%)
  local copies, waits for them, and re-layouts  12.1 us (4%)
  other arithmetic  10.9 us (4%)
    ppermute x36, waiting for transfers between devices, shift_plane(): return lax.ppermute(value, BOTH, pairs)  95.6 us
    pallas_call x12, Pallas kernels, pair_product(): pl.pallas_call(kernel, grid_spec=pltpu.PrefetchScalarGridSpec(num_scalar_...  54.3 us
    ppermute x36, starting transfers between devices, shift_plane(): return lax.ppermute(value, BOTH, pairs)  47.9 us
    ppermute x18, waiting for transfers between devices, shift_z(): return lax.ppermute(value, 'prow', pairs)  38.6 us
    ppermute x18, starting transfers between devices, shift_z(): return lax.ppermute(value, 'prow', pairs)  24 us
    pallas_call x8, Pallas kernels, solve(): pl.pallas_call(functools.partial(solve_kernel, flip, len(gone)), out_shap...  16.6 us
    ppermute x6, waiting for transfers between devices, swap_core(): return lax.ppermute(value, 'prow', pairs)  7.59 us
  transfers between devices with their start and end apart: 60, of which 49 were waited for; matrix products, arithmetic and copies ran while one was open for 1% of the time, Pallas kernels for 9%

profile of v1, /device:TPU:0, one launch (start us, length us, event | category | flops | bytes accessed | tf_op | source)
XLA Modules:
  0.0 309.3 jit_solution(11109307939126959172)
XLA Ops:
  6.0 2.8 collective-permute-start.2
  13.1 2.5 collective-permute-done.1
  19.5 2.9 collective-permute-start.4
  24.5 3.8 %collective-permute-done.3.refs_1_ = f32[4,128,256]{2,1,0:T(8,128)S(1)} collective-permute-done((f32[4,128,256]{2,1,0:T(8,128)S(1)}, f32[4,128,256]{2,1,0:T(8,128)S(1)}, u32[]{:S(2)}, u32[]{:S(2)}) %collective-permute-start.3) | collective-permute-done | bytes 524320 | tf_op jit(solution)/shard_map/ppermute | solution.py:37
  28.3 6.9 %collective-permute-done.4.refs_2_ = f32[4,128,256]{2,1,0:T(8,128)S(1)} collective-permute-done((f32[4,128,256]{2,1,0:T(8,128)S(1)}, f32[4,128,256]{2,1,0:T(8,128)S(1)}, u32[]{:S(2)}, u32[]{:S(2)}) %collective-permute-start.4) | collective-permute-done | bytes 524320 | tf_op jit(solution)/shard_map/ppermute | solution.py:37
  35.2 4.5 %shard_map.69 = (f32[4,128,256]{2,1,0:T(8,128)S(1)}, f32[4,128,256]{2,1,0:T(8,128)S(1)}) custom-call(s32[32]{0:T(128)S(1)} %get-tuple-element.142.take_ref, s32[32]{0:T(128)S(1)} %get-tuple-element.131.put_ref, s32[32]{0:T(128)S(1)} %get-tuple-element.125.live_ref, f32[4,128,256]{2,1,0:T(8,128)S(1)} %fusion.4.refs_0_, ...), custom_call_target="tpu_custom_call" | custom-call | flops 1073741824 | bytes 2097152 | tf_op jit(solution)/shard_map/pallas_call | solution.py:113
  42.4 1.9 collective-permute-start.7
  44.4 3.6 %collective-permute-start.8 = (f32[128,256]{1,0:T(8,128)S(1)}, f32[128,256]{1,0:T(8,128)S(1)}, u32[]{:S(2)}, u32[]{:S(2)}) collective-permute-start(f32[128,256]{1,0:T(8,128)S(1)} %get-tuple-element.97), channel_id=1, source_target_pairs={{0,64},{16,80},{32,96},{48,112},{64,0},{80,16},{96,32},{112,48},{1... | collective-permute-start | bytes 393224 | tf_op jit(solution)/shard_map/ppermute | solution.py:42
  50.3 4.0 %collective-permute-done.8.refs_2_ = f32[128,256]{1,0:T(8,128)S(1)} collective-permute-done((f32[128,256]{1,0:T(8,128)S(1)}, f32[128,256]{1,0:T(8,128)S(1)}, u32[]{:S(2)}, u32[]{:S(2)}) %collective-permute-start.8) | collective-permute-done | bytes 131104 | tf_op jit(solution)/shard_map/ppermute | solution.py:42
  55.0 2.1 shard_map.70.base
  59.3 3.0 collective-permute-done.12
  62.3 2.2 collective-permute-done.11
  68.4 2.1 collective-permute-start.14
  72.2 4.5 %shard_map.71 = (f32[4,128,256]{2,1,0:T(8,128)S(1)}, f32[4,128,256]{2,1,0:T(8,128)S(1)}) custom-call(s32[32]{0:T(128)S(1)} %get-tuple-element.144.take_ref, s32[32]{0:T(128)S(1)} %get-tuple-element.129.put_ref, s32[32]{0:T(128)S(1)} %get-tuple-element.123.live_ref, f32[4,128,256]{2,1,0:T(8,128)S(1)} %fusion.4.refs_0_, ...), custom_call_target="tpu_custom_call" | custom-call | flops 1073741824 | bytes 2097152 | tf_op jit(solution)/shard_map/pallas_call | solution.py:113
  77.2 6.1 %collective-permute-done.14.refs_2_ = f32[4,128,256]{2,1,0:T(8,128)S(1)} collective-permute-done((f32[4,128,256]{2,1,0:T(8,128)S(1)}, f32[4,128,256]{2,1,0:T(8,128)S(1)}, u32[]{:S(2)}, u32[]{:S(2)}) %collective-permute-start.14) | collective-permute-done | bytes 524320 | tf_op jit(solution)/shard_map/ppermute | solution.py:37
  83.7 4.4 %shard_map.72 = (f32[4,128,256]{2,1,0:T(8,128)S(1)}, f32[4,128,256]{2,1,0:T(8,128)S(1)}) custom-call(s32[32]{0:T(128)S(1)} %get-tuple-element.143.take_ref, s32[32]{0:T(128)S(1)} %get-tuple-element.130.put_ref, s32[32]{0:T(128)S(1)} %get-tuple-element.124.live_ref, f32[4,128,256]{2,1,0:T(8,128)S(1)} %pad_maximum_fusion.2.refs_0_, ...), custom_call_target="tpu_custom_call" | custom-call | flops 1073741824 | bytes 2097152 | tf_op jit(solution)/shard_map/pallas_call | solution.py:113
  92.7 2.4 collective-permute-start.18
  96.4 2.5 collective-permute-done.17.refs_1_
  98.9 2.5 collective-permute-done.18.refs_2_
  102.1 2.1 shard_map.73.base
  106.4 2.9 collective-permute-done.22
  109.4 2.8 collective-permute-done.21
  114.5 2.1 collective-permute-start.23
  116.5 2.1 collective-permute-start.24
  120.0 4.5 %shard_map.74 = (f32[4,128,256]{2,1,0:T(8,128)S(1)}, f32[4,128,256]{2,1,0:T(8,128)S(1)}) custom-call(s32[32]{0:T(128)S(1)} %get-tuple-element.147.take_ref, s32[32]{0:T(128)S(1)} %get-tuple-element.126.put_ref, s32[32]{0:T(128)S(1)} %get-tuple-element.120.live_ref, f32[4,128,256]{2,1,0:T(8,128)S(1)} %fusion.4.refs_0_, ...), custom_call_target="tpu_custom_call" | custom-call | flops 1073741824 | bytes 2097152 | tf_op jit(solution)/shard_map/pallas_call | solution.py:113
  124.5 4.4 %shard_map.75 = (f32[4,128,256]{2,1,0:T(8,128)S(1)}, f32[4,128,256]{2,1,0:T(8,128)S(1)}) custom-call(s32[32]{0:T(128)S(1)} %get-tuple-element.146.take_ref, s32[32]{0:T(128)S(1)} %get-tuple-element.127.put_ref, s32[32]{0:T(128)S(1)} %get-tuple-element.121.live_ref, f32[4,128,256]{2,1,0:T(8,128)S(1)} %pad_maximum_fusion.2.refs_0_, ...), custom_call_target="tpu_custom_call" | custom-call | flops 1073741824 | bytes 2097152 | tf_op jit(solution)/shard_map/pallas_call | solution.py:113
  129.0 2.4 collective-permute-done.24.refs_2_
  131.4 4.4 %shard_map.76 = (f32[4,128,256]{2,1,0:T(8,128)S(1)}, f32[4,128,256]{2,1,0:T(8,128)S(1)}) custom-call(s32[32]{0:T(128)S(1)} %get-tuple-element.145.take_ref, s32[32]{0:T(128)S(1)} %get-tuple-element.128.put_ref, s32[32]{0:T(128)S(1)} %get-tuple-element.122.live_ref, f32[4,128,256]{2,1,0:T(8,128)S(1)} %pad_maximum_fusion.3.refs_0_, ...), custom_call_target="tpu_custom_call" | custom-call | flops 1073741824 | bytes 2097152 | tf_op jit(solution)/shard_map/pallas_call | solution.py:113
  140.0 2.5 collective-permute-start.28
  143.3 2.2 collective-permute-done.27.refs_1_
  145.5 3.4 %collective-permute-done.28.refs_2_ = f32[128,256]{1,0:T(8,128)S(1)} collective-permute-done((f32[128,256]{1,0:T(8,128)S(1)}, f32[128,256]{1,0:T(8,128)S(1)}, u32[]{:S(2)}, u32[]{:S(2)}) %collective-permute-start.28) | collective-permute-done | bytes 131104 | tf_op jit(solution)/shard_map/ppermute | solution.py:42
  149.6 2.1 shard_map.77.base
  153.7 2.5 collective-permute-start.32
  157.0 5.1 %collective-permute-done.32 = f32[128,256]{1,0:T(8,128)S(1)} collective-permute-done((f32[128,256]{1,0:T(8,128)}, f32[128,256]{1,0:T(8,128)S(1)}, u32[]{:S(2)}, u32[]{:S(2)}) %collective-permute-start.32) | collective-permute-done | bytes 131104 | tf_op jit(solution)/shard_map/ppermute | solution.py:42
  162.1 2.2 collective-permute-done.31
  168.6 4.6 %shard_map.79 = (f32[4,128,256]{2,1,0:T(8,128)S(1)}, f32[4,128,256]{2,1,0:T(8,128)S(1)}, f32[4,128,256]{2,1,0:T(8,128)S(1)}, f32[4,128,256]{2,1,0:T(8,128)S(1)}) custom-call(s32[32]{0:T(128)S(1)} %get-tuple-element.150.take_ref, s32[32]{0:T(128)S(1)} %get-tuple-element.111.put_ref, s32[32]{0:T(128)S(1)} %get-tuple-element.122.live_ref, ...), custom_call_target="tpu_custom_call" | custom-call | flops 1073741824 | bytes 2097152 | tf_op jit(solution)/shard_map/pallas_call | solution.py:113
  175.6 6.9 %collective-permute-done.36 = f32[4,128,256]{2,1,0:T(8,128)S(1)} collective-permute-done((f32[4,128,256]{2,1,0:T(8,128)S(1)}, f32[4,128,256]{2,1,0:T(8,128)S(1)}, u32[]{:S(2)}, u32[]{:S(2)}) %collective-permute-start.36) | collective-permute-done | bytes 524320 | tf_op jit(solution)/shard_map/ppermute | solution.py:37
  182.4 2.2 collective-permute-done.35
  184.6 5.5 %collective-permute-done.34 = f32[4,128,256]{2,1,0:T(8,128)S(1)} collective-permute-done((f32[4,128,256]{2,1,0:T(8,128)S(1)}, f32[4,128,256]{2,1,0:T(8,128)S(1)}, u32[]{:S(2)}, u32[]{:S(2)}) %collective-permute-start.34) | collective-permute-done | bytes 524320 | tf_op jit(solution)/shard_map/ppermute | solution.py:37
  191.0 2.0 collective-permute-start.37
  192.9 2.1 collective-permute-start.38
  197.2 2.3 collective-permute-done.38.refs_2_
  200.7 2.2 shard_map.80
  205.2 3.7 %collective-permute-done.42 = f32[128,256]{1,0:T(8,128)S(1)} collective-permute-done((f32[128,256]{1,0:T(8,128)}, f32[128,256]{1,0:T(8,128)S(1)}, u32[]{:S(2)}, u32[]{:S(2)}) %collective-permute-start.42) | collective-permute-done | bytes 131104 | tf_op jit(solution)/shard_map/ppermute | solution.py:42
  208.9 2.2 collective-permute-done.41
  213.4 4.6 %shard_map.81 = (f32[4,128,256]{2,1,0:T(8,128)S(1)}, f32[4,128,256]{2,1,0:T(8,128)S(1)}, f32[4,128,256]{2,1,0:T(8,128)S(1)}, f32[4,128,256]{2,1,0:T(8,128)S(1)}) custom-call(s32[32]{0:T(128)S(1)} %get-tuple-element.151.take_ref, s32[32]{0:T(128)S(1)} %get-tuple-element.110.put_ref, s32[32]{0:T(128)S(1)} %get-tuple-element.121.live_ref, ...), custom_call_target="tpu_custom_call" | custom-call | flops 1073741824 | bytes 2097152 | tf_op jit(solution)/shard_map/pallas_call | solution.py:113
  218.0 4.6 %shard_map.82 = (f32[4,128,256]{2,1,0:T(8,128)S(1)}, f32[4,128,256]{2,1,0:T(8,128)S(1)}, f32[4,128,256]{2,1,0:T(8,128)S(1)}, f32[4,128,256]{2,1,0:T(8,128)S(1)}) custom-call(s32[32]{0:T(128)S(1)} %get-tuple-element.149.take_ref, s32[32]{0:T(128)S(1)} %get-tuple-element.112.put_ref, s32[32]{0:T(128)S(1)} %get-tuple-element.124.live_ref, ...), custom_call_target="tpu_custom_call" | custom-call | flops 1073741824 | bytes 2097152 | tf_op jit(solution)/shard_map/pallas_call | solution.py:113
  222.6 2.1 collective-permute-start.46
  225.7 11.4 %collective-permute-done.46 = f32[4,128,256]{2,1,0:T(8,128)S(1)} collective-permute-done((f32[4,128,256]{2,1,0:T(8,128)S(1)}, f32[4,128,256]{2,1,0:T(8,128)S(1)}, u32[]{:S(2)}, u32[]{:S(2)}) %collective-permute-start.46) | collective-permute-done | bytes 524320 | tf_op jit(solution)/shard_map/ppermute | solution.py:37
  237.1 3.9 %collective-permute-done.44 = f32[4,128,256]{2,1,0:T(8,128)S(1)} collective-permute-done((f32[4,128,256]{2,1,0:T(8,128)S(1)}, f32[4,128,256]{2,1,0:T(8,128)S(1)}, u32[]{:S(2)}, u32[]{:S(2)}) %collective-permute-start.44) | collective-permute-done | bytes 524320 | tf_op jit(solution)/shard_map/ppermute | solution.py:37
  242.1 2.4 collective-permute-start.48
  246.2 3.2 %collective-permute-done.47.refs_1_ = f32[128,256]{1,0:T(8,128)S(1)} collective-permute-done((f32[128,256]{1,0:T(8,128)S(1)}, f32[128,256]{1,0:T(8,128)S(1)}, u32[]{:S(2)}, u32[]{:S(2)}) %collective-permute-start.47) | collective-permute-done | bytes 131104 | tf_op jit(solution)/shard_map/ppermute | solution.py:37
  250.9 2.2 shard_map.83
  255.5 2.8 collective-permute-done.52
  258.3 2.6 collective-permute-done.51
  263.2 4.6 %shard_map.84 = (f32[4,128,256]{2,1,0:T(8,128)S(1)}, f32[4,128,256]{2,1,0:T(8,128)S(1)}, f32[4,128,256]{2,1,0:T(8,128)S(1)}, f32[4,128,256]{2,1,0:T(8,128)S(1)}) custom-call(s32[32]{0:T(128)S(1)} %get-tuple-element.153.take_ref, s32[32]{0:T(128)S(1)} %get-tuple-element.108.put_ref, s32[32]{0:T(128)S(1)} %get-tuple-element.120.live_ref, ...), custom_call_target="tpu_custom_call" | custom-call | flops 1073741824 | bytes 2097152 | tf_op jit(solution)/shard_map/pallas_call | solution.py:113
  267.8 4.6 %shard_map.85 = (f32[4,128,256]{2,1,0:T(8,128)S(1)}, f32[4,128,256]{2,1,0:T(8,128)S(1)}, f32[4,128,256]{2,1,0:T(8,128)S(1)}, f32[4,128,256]{2,1,0:T(8,128)S(1)}) custom-call(s32[32]{0:T(128)S(1)} %get-tuple-element.152.take_ref, s32[32]{0:T(128)S(1)} %get-tuple-element.109.put_ref, s32[32]{0:T(128)S(1)} %get-tuple-element.123.live_ref, ...), custom_call_target="tpu_custom_call" | custom-call | flops 1073741824 | bytes 2097152 | tf_op jit(solution)/shard_map/pallas_call | solution.py:113
  272.5 4.6 %shard_map.86 = (f32[4,128,256]{2,1,0:T(8,128)S(1)}, f32[4,128,256]{2,1,0:T(8,128)S(1)}, f32[4,128,256]{2,1,0:T(8,128)S(1)}, f32[4,128,256]{2,1,0:T(8,128)S(1)}) custom-call(s32[32]{0:T(128)S(1)} %get-tuple-element.148.take_ref, s32[32]{0:T(128)S(1)} %get-tuple-element.113.put_ref, s32[32]{0:T(128)S(1)} %get-tuple-element.125.live_ref, ...), custom_call_target="tpu_custom_call" | custom-call | flops 1073741824 | bytes 2097152 | tf_op jit(solution)/shard_map/pallas_call | solution.py:113
  277.1 2.1 collective-permute-start.56
  280.1 11.4 %collective-permute-done.56 = f32[4,128,256]{2,1,0:T(8,128)S(1)} collective-permute-done((f32[4,128,256]{2,1,0:T(8,128)S(1)}, f32[4,128,256]{2,1,0:T(8,128)S(1)}, u32[]{:S(2)}, u32[]{:S(2)}) %collective-permute-start.56) | collective-permute-done | bytes 524320 | tf_op jit(solution)/shard_map/ppermute | solution.py:37
  291.5 3.9 %collective-permute-done.54 = f32[4,128,256]{2,1,0:T(8,128)S(1)} collective-permute-done((f32[4,128,256]{2,1,0:T(8,128)S(1)}, f32[4,128,256]{2,1,0:T(8,128)S(1)}, u32[]{:S(2)}, u32[]{:S(2)}) %collective-permute-start.54) | collective-permute-done | bytes 524320 | tf_op jit(solution)/shard_map/ppermute | solution.py:37
  296.3 2.6 collective-permute-start.58
  300.7 3.2 %collective-permute-done.57.refs_1_ = f32[128,256]{1,0:T(8,128)S(1)} collective-permute-done((f32[128,256]{1,0:T(8,128)S(1)}, f32[128,256]{1,0:T(8,128)S(1)}, u32[]{:S(2)}, u32[]{:S(2)}) %collective-permute-start.57) | collective-permute-done | bytes 131104 | tf_op jit(solution)/shard_map/ppermute | solution.py:37
  305.4 2.2 shard_map.87
  (160 shorter events, 83.1 us)
Async XLA Ops:
  6.0 7.1 %collective-permute-start.2 = (f32[128,256]{1,0:T(8,128)}, f32[128,256]{1,0:T(8,128)S(1)}, u32[]{:S(2)}, u32[]{:S(2)}) collective-permute-start(f32[128,256]{1,0:T(8,128)} %shard_map.68.base), channel_id=1, source_target_pairs={{0,12},{1,13},{2,14},{3,15},{4,0},{5,1},{6,2},{7,3},{8,4},{9,5},{1... | collective-permute-start | bytes 393224 | tf_op jit(solution)/shard_map/ppermute | solution.py:37
  8.9 6.8 %collective-permute-start.1 = (f32[128,256]{1,0:T(8,128)}, f32[128,256]{1,0:T(8,128)S(1)}, u32[]{:S(2)}, u32[]{:S(2)}) collective-permute-start(f32[128,256]{1,0:T(8,128)} %shard_map.68.base), channel_id=1, source_target_pairs={{0,8},{1,9},{2,10},{3,11},{4,12},{5,13},{6,14},{7,15},{8,0},{9,1},... | collective-permute-start | bytes 393224 | tf_op jit(solution)/shard_map/ppermute | solution.py:37
  9.7 7.3 %collective-permute-start = (f32[128,256]{1,0:T(8,128)}, f32[128,256]{1,0:T(8,128)S(1)}, u32[]{:S(2)}, u32[]{:S(2)}) collective-permute-start(f32[128,256]{1,0:T(8,128)} %shard_map.68.base), channel_id=1, source_target_pairs={{0,4},{1,5},{2,6},{3,7},{4,8},{5,9},{6,10},{7,11},{8,12},{9,13},{1... | collective-permute-start | bytes 393224 | tf_op jit(solution)/shard_map/ppermute | solution.py:37
  17.9 10.5 %collective-permute-start.3 = (f32[4,128,256]{2,1,0:T(8,128)S(1)}, f32[4,128,256]{2,1,0:T(8,128)S(1)}, u32[]{:S(2)}, u32[]{:S(2)}) collective-permute-start(f32[4,128,256]{2,1,0:T(8,128)S(1)} %fusion.4.refs_0_), channel_id=1, source_target_pairs={{0,1},{1,2},{2,3},{3,0},{4,5},{5,6},{6,7},{7,4},{8,9},{9,10},{10,1... | collective-permute-start | bytes 1572872 | tf_op jit(solution)/shard_map/ppermute | solution.py:37
  19.5 15.7 %collective-permute-start.4 = (f32[4,128,256]{2,1,0:T(8,128)S(1)}, f32[4,128,256]{2,1,0:T(8,128)S(1)}, u32[]{:S(2)}, u32[]{:S(2)}) collective-permute-start(f32[4,128,256]{2,1,0:T(8,128)S(1)} %fusion.4.refs_0_), channel_id=1, source_target_pairs={{0,2},{1,3},{2,0},{3,1},{4,6},{5,7},{6,4},{7,5},{8,10},{9,11},{10,... | collective-permute-start | bytes 1572872 | tf_op jit(solution)/shard_map/ppermute | solution.py:37
  22.4 12.8 %collective-permute-start.5 = (f32[4,128,256]{2,1,0:T(8,128)S(1)}, f32[4,128,256]{2,1,0:T(8,128)S(1)}, u32[]{:S(2)}, u32[]{:S(2)}) collective-permute-start(f32[4,128,256]{2,1,0:T(8,128)S(1)} %fusion.4.refs_0_), channel_id=1, source_target_pairs={{0,3},{1,0},{2,1},{3,2},{4,7},{5,4},{6,5},{7,6},{8,11},{9,8},{10,9... | collective-permute-start | bytes 1572872 | tf_op jit(solution)/shard_map/ppermute | solution.py:37
  39.7 2.0 collective-permute-start.6
  42.4 7.8 %collective-permute-start.7 = (f32[128,256]{1,0:T(8,128)S(1)}, f32[128,256]{1,0:T(8,128)S(1)}, u32[]{:S(2)}, u32[]{:S(2)}) collective-permute-start(f32[128,256]{1,0:T(8,128)S(1)} %get-tuple-element.98), channel_id=1, source_target_pairs={{0,32},{16,48},{32,64},{48,80},{64,96},{80,112},{96,0},{112,16},{1... | collective-permute-start | bytes 393224 | tf_op jit(solution)/shard_map/ppermute | solution.py:42
  44.4 9.9 %collective-permute-start.8 = (f32[128,256]{1,0:T(8,128)S(1)}, f32[128,256]{1,0:T(8,128)S(1)}, u32[]{:S(2)}, u32[]{:S(2)}) collective-permute-start(f32[128,256]{1,0:T(8,128)S(1)} %get-tuple-element.97), channel_id=1, source_target_pairs={{0,64},{16,80},{32,96},{48,112},{64,0},{80,16},{96,32},{112,48},{1... | collective-permute-start | bytes 393224 | tf_op jit(solution)/shard_map/ppermute | solution.py:42
  47.9 6.3 %collective-permute-start.9 = (f32[128,256]{1,0:T(8,128)S(1)}, f32[128,256]{1,0:T(8,128)S(1)}, u32[]{:S(2)}, u32[]{:S(2)}) collective-permute-start(f32[128,256]{1,0:T(8,128)S(1)} %get-tuple-element.96), channel_id=1, source_target_pairs={{0,96},{16,112},{32,0},{48,16},{64,32},{80,48},{96,64},{112,80},{1... | collective-permute-start | bytes 393224 | tf_op jit(solution)/shard_map/ppermute | solution.py:42
  57.1 5.2 %collective-permute-start.12 = (f32[128,256]{1,0:T(8,128)}, f32[128,256]{1,0:T(8,128)S(1)}, u32[]{:S(2)}, u32[]{:S(2)}) collective-permute-start(f32[128,256]{1,0:T(8,128)} %shard_map.70.base), channel_id=1, source_target_pairs={{0,12},{1,13},{2,14},{3,15},{4,0},{5,1},{6,2},{7,3},{8,4},{9,5},{1... | collective-permute-start | bytes 393224 | tf_op jit(solution)/shard_map/ppermute | solution.py:37
  57.7 6.8 %collective-permute-start.11 = (f32[128,256]{1,0:T(8,128)}, f32[128,256]{1,0:T(8,128)S(1)}, u32[]{:S(2)}, u32[]{:S(2)}) collective-permute-start(f32[128,256]{1,0:T(8,128)} %shard_map.70.base), channel_id=1, source_target_pairs={{0,8},{1,9},{2,10},{3,11},{4,12},{5,13},{6,14},{7,15},{8,0},{9,1},... | collective-permute-start | bytes 393224 | tf_op jit(solution)/shard_map/ppermute | solution.py:37
  58.5 7.3 %collective-permute-start.10 = (f32[128,256]{1,0:T(8,128)}, f32[128,256]{1,0:T(8,128)S(1)}, u32[]{:S(2)}, u32[]{:S(2)}) collective-permute-start(f32[128,256]{1,0:T(8,128)} %shard_map.70.base), channel_id=1, source_target_pairs={{0,4},{1,5},{2,6},{3,7},{4,8},{5,9},{6,10},{7,11},{8,12},{9,13},{1... | collective-permute-start | bytes 393224 | tf_op jit(solution)/shard_map/ppermute | solution.py:37
  66.7 10.5 %collective-permute-start.13 = (f32[4,128,256]{2,1,0:T(8,128)S(1)}, f32[4,128,256]{2,1,0:T(8,128)S(1)}, u32[]{:S(2)}, u32[]{:S(2)}) collective-permute-start(f32[4,128,256]{2,1,0:T(8,128)S(1)} %pad_maximum_fusion.2.refs_0_), channel_id=1, source_target_pairs={{0,1},{1,2},{2,3},{3,0},{4,5},{5,6},{6,7},{7,4},{8,9},{9,10},{10,1... | collective-permute-start | bytes 1572872 | tf_op jit(solution)/shard_map/ppermute | solution.py:37
  68.4 14.9 %collective-permute-start.14 = (f32[4,128,256]{2,1,0:T(8,128)S(1)}, f32[4,128,256]{2,1,0:T(8,128)S(1)}, u32[]{:S(2)}, u32[]{:S(2)}) collective-permute-start(f32[4,128,256]{2,1,0:T(8,128)S(1)} %pad_maximum_fusion.2.refs_0_), channel_id=1, source_target_pairs={{0,2},{1,3},{2,0},{3,1},{4,6},{5,7},{6,4},{7,5},{8,10},{9,11},{10,... | collective-permute-start | bytes 1572872 | tf_op jit(solution)/shard_map/ppermute | solution.py:37
  70.5 13.2 %collective-permute-start.15 = (f32[4,128,256]{2,1,0:T(8,128)S(1)}, f32[4,128,256]{2,1,0:T(8,128)S(1)}, u32[]{:S(2)}, u32[]{:S(2)}) collective-permute-start(f32[4,128,256]{2,1,0:T(8,128)S(1)} %pad_maximum_fusion.2.refs_0_), channel_id=1, source_target_pairs={{0,3},{1,0},{2,1},{3,2},{4,7},{5,4},{6,5},{7,6},{8,11},{9,8},{10,9... | collective-permute-start | bytes 1572872 | tf_op jit(solution)/shard_map/ppermute | solution.py:37
  88.9 1.9 collective-permute-start.16
  91.6 7.3 %collective-permute-start.17 = (f32[128,256]{1,0:T(8,128)S(1)}, f32[128,256]{1,0:T(8,128)S(1)}, u32[]{:S(2)}, u32[]{:S(2)}) collective-permute-start(f32[128,256]{1,0:T(8,128)S(1)} %get-tuple-element.94), channel_id=1, source_target_pairs={{0,32},{16,48},{32,64},{48,80},{64,96},{80,112},{96,0},{112,16},{1... | collective-permute-start | bytes 393224 | tf_op jit(solution)/shard_map/ppermute | solution.py:42
  92.7 8.7 %collective-permute-start.18 = (f32[128,256]{1,0:T(8,128)S(1)}, f32[128,256]{1,0:T(8,128)S(1)}, u32[]{:S(2)}, u32[]{:S(2)}) collective-permute-start(f32[128,256]{1,0:T(8,128)S(1)} %get-tuple-element.93), channel_id=1, source_target_pairs={{0,64},{16,80},{32,96},{48,112},{64,0},{80,16},{96,32},{112,48},{1... | collective-permute-start | bytes 393224 | tf_op jit(solution)/shard_map/ppermute | solution.py:42
  95.1 6.8 %collective-permute-start.19 = (f32[128,256]{1,0:T(8,128)S(1)}, f32[128,256]{1,0:T(8,128)}, u32[]{:S(2)}, u32[]{:S(2)}) collective-permute-start(f32[128,256]{1,0:T(8,128)S(1)} %get-tuple-element.92), channel_id=1, source_target_pairs={{0,96},{16,112},{32,0},{48,16},{64,32},{80,48},{96,64},{112,80},{1... | collective-permute-start | bytes 393224 | tf_op jit(solution)/shard_map/ppermute | solution.py:42
  104.2 5.2 %collective-permute-start.22 = (f32[128,256]{1,0:T(8,128)}, f32[128,256]{1,0:T(8,128)S(1)}, u32[]{:S(2)}, u32[]{:S(2)}) collective-permute-start(f32[128,256]{1,0:T(8,128)} %shard_map.73.base), channel_id=1, source_target_pairs={{0,12},{1,13},{2,14},{3,15},{4,0},{5,1},{6,2},{7,3},{8,4},{9,5},{1... | collective-permute-start | bytes 393224 | tf_op jit(solution)/shard_map/ppermute | solution.py:37
  105.4 6.8 %collective-permute-start.21 = (f32[128,256]{1,0:T(8,128)}, f32[128,256]{1,0:T(8,128)S(1)}, u32[]{:S(2)}, u32[]{:S(2)}) collective-permute-start(f32[128,256]{1,0:T(8,128)} %shard_map.73.base), channel_id=1, source_target_pairs={{0,8},{1,9},{2,10},{3,11},{4,12},{5,13},{6,14},{7,15},{8,0},{9,1},... | collective-permute-start | bytes 393224 | tf_op jit(solution)/shard_map/ppermute | solution.py:37
  106.3 7.2 %collective-permute-start.20 = (f32[128,256]{1,0:T(8,128)}, f32[128,256]{1,0:T(8,128)S(1)}, u32[]{:S(2)}, u32[]{:S(2)}) collective-permute-start(f32[128,256]{1,0:T(8,128)} %shard_map.73.base), channel_id=1, source_target_pairs={{0,4},{1,5},{2,6},{3,7},{4,8},{5,9},{6,10},{7,11},{8,12},{9,13},{1... | collective-permute-start | bytes 393224 | tf_op jit(solution)/shard_map/ppermute | solution.py:37
  114.5 14.5 %collective-permute-start.23 = (f32[4,128,256]{2,1,0:T(8,128)S(1)}, f32[4,128,256]{2,1,0:T(8,128)S(1)}, u32[]{:S(2)}, u32[]{:S(2)}) collective-permute-start(f32[4,128,256]{2,1,0:T(8,128)S(1)} %pad_maximum_fusion.3.refs_0_), channel_id=1, source_target_pairs={{0,1},{1,2},{2,3},{3,0},{4,5},{5,6},{6,7},{7,4},{8,9},{9,10},{10,1... | collective-permute-start | bytes 1572872 | tf_op jit(solution)/shard_map/ppermute | solution.py:37
  116.5 14.9 %collective-permute-start.24 = (f32[4,128,256]{2,1,0:T(8,128)S(1)}, f32[4,128,256]{2,1,0:T(8,128)S(1)}, u32[]{:S(2)}, u32[]{:S(2)}) collective-permute-start(f32[4,128,256]{2,1,0:T(8,128)S(1)} %pad_maximum_fusion.3.refs_0_), channel_id=1, source_target_pairs={{0,2},{1,3},{2,0},{3,1},{4,6},{5,7},{6,4},{7,5},{8,10},{9,11},{10,... | collective-permute-start | bytes 1572872 | tf_op jit(solution)/shard_map/ppermute | solution.py:37
  118.6 12.8 %collective-permute-start.25 = (f32[4,128,256]{2,1,0:T(8,128)S(1)}, f32[4,128,256]{2,1,0:T(8,128)S(1)}, u32[]{:S(2)}, u32[]{:S(2)}) collective-permute-start(f32[4,128,256]{2,1,0:T(8,128)S(1)} %pad_maximum_fusion.3.refs_0_), channel_id=1, source_target_pairs={{0,3},{1,0},{2,1},{3,2},{4,7},{5,4},{6,5},{7,6},{8,11},{9,8},{10,9... | collective-permute-start | bytes 1572872 | tf_op jit(solution)/shard_map/ppermute | solution.py:37
  135.9 2.0 collective-permute-start.26
  138.7 6.8 %collective-permute-start.27 = (f32[128,256]{1,0:T(8,128)S(1)}, f32[128,256]{1,0:T(8,128)S(1)}, u32[]{:S(2)}, u32[]{:S(2)}) collective-permute-start(f32[128,256]{1,0:T(8,128)S(1)} %get-tuple-element.90), channel_id=1, source_target_pairs={{0,32},{16,48},{32,64},{48,80},{64,96},{80,112},{96,0},{112,16},{1... | collective-permute-start | bytes 393224 | tf_op jit(solution)/shard_map/ppermute | solution.py:42
  140.0 8.9 %collective-permute-start.28 = (f32[128,256]{1,0:T(8,128)S(1)}, f32[128,256]{1,0:T(8,128)S(1)}, u32[]{:S(2)}, u32[]{:S(2)}) collective-permute-start(f32[128,256]{1,0:T(8,128)S(1)} %get-tuple-element.89), channel_id=1, source_target_pairs={{0,64},{16,80},{32,96},{48,112},{64,0},{80,16},{96,32},{112,48},{1... | collective-permute-start | bytes 393224 | tf_op jit(solution)/shard_map/ppermute | solution.py:42
  142.6 6.3 %collective-permute-start.29 = (f32[128,256]{1,0:T(8,128)S(1)}, f32[128,256]{1,0:T(8,128)S(1)}, u32[]{:S(2)}, u32[]{:S(2)}) collective-permute-start(f32[128,256]{1,0:T(8,128)S(1)} %get-tuple-element.88), channel_id=1, source_target_pairs={{0,96},{16,112},{32,0},{48,16},{64,32},{80,48},{96,64},{112,80},{1... | collective-permute-start | bytes 393224 | tf_op jit(solution)/shard_map/ppermute | solution.py:42
  153.7 8.4 %collective-permute-start.32 = (f32[128,256]{1,0:T(8,128)}, f32[128,256]{1,0:T(8,128)S(1)}, u32[]{:S(2)}, u32[]{:S(2)}) collective-permute-start(f32[128,256]{1,0:T(8,128)} %shard_map.78), channel_id=1, source_target_pairs={{0,96},{16,112},{32,0},{48,16},{64,32},{80,48},{96,64},{112,80},{1... | collective-permute-start | bytes 393224 | tf_op jit(solution)/shard_map/ppermute | solution.py:42
  156.1 8.1 %collective-permute-start.31 = (f32[128,256]{1,0:T(8,128)}, f32[128,256]{1,0:T(8,128)S(1)}, u32[]{:S(2)}, u32[]{:S(2)}) collective-permute-start(f32[128,256]{1,0:T(8,128)} %shard_map.78), channel_id=1, source_target_pairs={{0,64},{16,80},{32,96},{48,112},{64,0},{80,16},{96,32},{112,48},{1... | collective-permute-start | bytes 393224 | tf_op jit(solution)/shard_map/ppermute | solution.py:42
  156.9 8.7 %collective-permute-start.30 = (f32[128,256]{1,0:T(8,128)}, f32[128,256]{1,0:T(8,128)S(1)}, u32[]{:S(2)}, u32[]{:S(2)}) collective-permute-start(f32[128,256]{1,0:T(8,128)} %shard_map.78), channel_id=1, source_target_pairs={{0,32},{16,48},{32,64},{48,80},{64,96},{80,112},{96,0},{112,16},{1... | collective-permute-start | bytes 393224 | tf_op jit(solution)/shard_map/ppermute | solution.py:42
  166.6 2.0 collective-permute-start.33
  173.2 9.2 %collective-permute-start.36 = (f32[4,128,256]{2,1,0:T(8,128)S(1)}, f32[4,128,256]{2,1,0:T(8,128)S(1)}, u32[]{:S(2)}, u32[]{:S(2)}) collective-permute-start(f32[4,128,256]{2,1,0:T(8,128)S(1)} %get-tuple-element.53), channel_id=1, source_target_pairs={{0,12},{1,13},{2,14},{3,15},{4,0},{5,1},{6,2},{7,3},{8,4},{9,5},{1... | collective-permute-start | bytes 1572872 | tf_op jit(solution)/shard_map/ppermute | solution.py:37
  173.8 10.8 %collective-permute-start.35 = (f32[4,128,256]{2,1,0:T(8,128)S(1)}, f32[4,128,256]{2,1,0:T(8,128)S(1)}, u32[]{:S(2)}, u32[]{:S(2)}) collective-permute-start(f32[4,128,256]{2,1,0:T(8,128)S(1)} %get-tuple-element.52), channel_id=1, source_target_pairs={{0,8},{1,9},{2,10},{3,11},{4,12},{5,13},{6,14},{7,15},{8,0},{9,1},... | collective-permute-start | bytes 1572872 | tf_op jit(solution)/shard_map/ppermute | solution.py:37
  174.7 15.4 %collective-permute-start.34 = (f32[4,128,256]{2,1,0:T(8,128)S(1)}, f32[4,128,256]{2,1,0:T(8,128)S(1)}, u32[]{:S(2)}, u32[]{:S(2)}) collective-permute-start(f32[4,128,256]{2,1,0:T(8,128)S(1)} %get-tuple-element.51), channel_id=1, source_target_pairs={{0,4},{1,5},{2,6},{3,7},{4,8},{5,9},{6,10},{7,11},{8,12},{9,13},{1... | collective-permute-start | bytes 1572872 | tf_op jit(solution)/shard_map/ppermute | solution.py:37
  191.0 6.2 %collective-permute-start.37 = (f32[128,256]{1,0:T(8,128)S(1)}, f32[128,256]{1,0:T(8,128)S(1)}, u32[]{:S(2)}, u32[]{:S(2)}) collective-permute-start(f32[128,256]{1,0:T(8,128)S(1)} %get-tuple-element.86), channel_id=1, source_target_pairs={{0,1},{1,2},{2,3},{3,0},{4,5},{5,6},{6,7},{7,4},{8,9},{9,10},{10,1... | collective-permute-start | bytes 393224 | tf_op jit(solution)/shard_map/ppermute | solution.py:37
  192.9 6.5 %collective-permute-start.38 = (f32[128,256]{1,0:T(8,128)S(1)}, f32[128,256]{1,0:T(8,128)S(1)}, u32[]{:S(2)}, u32[]{:S(2)}) collective-permute-start(f32[128,256]{1,0:T(8,128)S(1)} %get-tuple-element.85), channel_id=1, source_target_pairs={{0,2},{1,3},{2,0},{3,1},{4,6},{5,7},{6,4},{7,5},{8,10},{9,11},{10,... | collective-permute-start | bytes 393224 | tf_op jit(solution)/shard_map/ppermute | solution.py:37
  195.1 5.0 %collective-permute-start.39 = (f32[128,256]{1,0:T(8,128)S(1)}, f32[128,256]{1,0:T(8,128)S(1)}, u32[]{:S(2)}, u32[]{:S(2)}) collective-permute-start(f32[128,256]{1,0:T(8,128)S(1)} %get-tuple-element.84), channel_id=1, source_target_pairs={{0,3},{1,0},{2,1},{3,2},{4,7},{5,4},{6,5},{7,6},{8,11},{9,8},{10,9... | collective-permute-start | bytes 393224 | tf_op jit(solution)/shard_map/ppermute | solution.py:37
  202.8 6.1 %collective-permute-start.42 = (f32[128,256]{1,0:T(8,128)}, f32[128,256]{1,0:T(8,128)S(1)}, u32[]{:S(2)}, u32[]{:S(2)}) collective-permute-start(f32[128,256]{1,0:T(8,128)} %shard_map.80), channel_id=1, source_target_pairs={{0,96},{16,112},{32,0},{48,16},{64,32},{80,48},{96,64},{112,80},{1... | collective-permute-start | bytes 393224 | tf_op jit(solution)/shard_map/ppermute | solution.py:42
  203.4 7.7 %collective-permute-start.41 = (f32[128,256]{1,0:T(8,128)}, f32[128,256]{1,0:T(8,128)S(1)}, u32[]{:S(2)}, u32[]{:S(2)}) collective-permute-start(f32[128,256]{1,0:T(8,128)} %shard_map.80), channel_id=1, source_target_pairs={{0,64},{16,80},{32,96},{48,112},{64,0},{80,16},{96,32},{112,48},{1... | collective-permute-start | bytes 393224 | tf_op jit(solution)/shard_map/ppermute | solution.py:42
  204.3 7.8 %collective-permute-start.40 = (f32[128,256]{1,0:T(8,128)}, f32[128,256]{1,0:T(8,128)S(1)}, u32[]{:S(2)}, u32[]{:S(2)}) collective-permute-start(f32[128,256]{1,0:T(8,128)} %shard_map.80), channel_id=1, source_target_pairs={{0,32},{16,48},{32,64},{48,80},{64,96},{80,112},{96,0},{112,16},{1... | collective-permute-start | bytes 393224 | tf_op jit(solution)/shard_map/ppermute | solution.py:42
  213.0 4.9 %collective-permute-start.43 = (f32[4,128,256]{2,1,0:T(8,128)S(1)}, f32[4,128,256]{2,1,0:T(8,128)S(1)}, u32[]{:S(2)}, u32[]{:S(2)}) collective-permute-start(f32[4,128,256]{2,1,0:T(8,128)S(1)} %pad_maximum_fusion.5.refs_0_), channel_id=1, source_target_pairs={{0,16},{16,0},{32,48},{48,32},{64,80},{80,64},{96,112},{112,96},{1... | collective-permute-start | bytes 1572872 | tf_op jit(solution)/shard_map/ppermute | solution.py:47
  222.6 14.5 %collective-permute-start.46 = (f32[4,128,256]{2,1,0:T(8,128)S(1)}, f32[4,128,256]{2,1,0:T(8,128)S(1)}, u32[]{:S(2)}, u32[]{:S(2)}) collective-permute-start(f32[4,128,256]{2,1,0:T(8,128)S(1)} %get-tuple-element.61), channel_id=1, source_target_pairs={{0,12},{1,13},{2,14},{3,15},{4,0},{5,1},{6,2},{7,3},{8,4},{9,5},{1... | collective-permute-start | bytes 1572872 | tf_op jit(solution)/shard_map/ppermute | solution.py:37
  224.7 12.4 %collective-permute-start.45 = (f32[4,128,256]{2,1,0:T(8,128)S(1)}, f32[4,128,256]{2,1,0:T(8,128)S(1)}, u32[]{:S(2)}, u32[]{:S(2)}) collective-permute-start(f32[4,128,256]{2,1,0:T(8,128)S(1)} %get-tuple-element.60), channel_id=1, source_target_pairs={{0,8},{1,9},{2,10},{3,11},{4,12},{5,13},{6,14},{7,15},{8,0},{9,1},... | collective-permute-start | bytes 1572872 | tf_op jit(solution)/shard_map/ppermute | solution.py:37
  225.0 16.0 %collective-permute-start.44 = (f32[4,128,256]{2,1,0:T(8,128)S(1)}, f32[4,128,256]{2,1,0:T(8,128)S(1)}, u32[]{:S(2)}, u32[]{:S(2)}) collective-permute-start(f32[4,128,256]{2,1,0:T(8,128)S(1)} %get-tuple-element.59), channel_id=1, source_target_pairs={{0,4},{1,5},{2,6},{3,7},{4,8},{5,9},{6,10},{7,11},{8,12},{9,13},{1... | collective-permute-start | bytes 1572872 | tf_op jit(solution)/shard_map/ppermute | solution.py:37
  241.8 7.6 %collective-permute-start.47 = (f32[128,256]{1,0:T(8,128)S(1)}, f32[128,256]{1,0:T(8,128)S(1)}, u32[]{:S(2)}, u32[]{:S(2)}) collective-permute-start(f32[128,256]{1,0:T(8,128)S(1)} %get-tuple-element.82), channel_id=1, source_target_pairs={{0,1},{1,2},{2,3},{3,0},{4,5},{5,6},{6,7},{7,4},{8,9},{9,10},{10,1... | collective-permute-start | bytes 393224 | tf_op jit(solution)/shard_map/ppermute | solution.py:37
  242.1 7.3 %collective-permute-start.48 = (f32[128,256]{1,0:T(8,128)S(1)}, f32[128,256]{1,0:T(8,128)S(1)}, u32[]{:S(2)}, u32[]{:S(2)}) collective-permute-start(f32[128,256]{1,0:T(8,128)S(1)} %get-tuple-element.81), channel_id=1, source_target_pairs={{0,2},{1,3},{2,0},{3,1},{4,6},{5,7},{6,4},{7,5},{8,10},{9,11},{10,... | collective-permute-start | bytes 393224 | tf_op jit(solution)/shard_map/ppermute | solution.py:37
  244.5 5.8 %collective-permute-start.49 = (f32[128,256]{1,0:T(8,128)S(1)}, f32[128,256]{1,0:T(8,128)S(1)}, u32[]{:S(2)}, u32[]{:S(2)}) collective-permute-start(f32[128,256]{1,0:T(8,128)S(1)} %get-tuple-element.80), channel_id=1, source_target_pairs={{0,3},{1,0},{2,1},{3,2},{4,7},{5,4},{6,5},{7,6},{8,11},{9,8},{10,9... | collective-permute-start | bytes 393224 | tf_op jit(solution)/shard_map/ppermute | solution.py:37
  253.1 5.2 %collective-permute-start.52 = (f32[128,256]{1,0:T(8,128)}, f32[128,256]{1,0:T(8,128)S(1)}, u32[]{:S(2)}, u32[]{:S(2)}) collective-permute-start(f32[128,256]{1,0:T(8,128)} %shard_map.83), channel_id=1, source_target_pairs={{0,96},{16,112},{32,0},{48,16},{64,32},{80,48},{96,64},{112,80},{1... | collective-permute-start | bytes 393224 | tf_op jit(solution)/shard_map/ppermute | solution.py:42
  254.0 6.9 %collective-permute-start.51 = (f32[128,256]{1,0:T(8,128)}, f32[128,256]{1,0:T(8,128)S(1)}, u32[]{:S(2)}, u32[]{:S(2)}) collective-permute-start(f32[128,256]{1,0:T(8,128)} %shard_map.83), channel_id=1, source_target_pairs={{0,64},{16,80},{32,96},{48,112},{64,0},{80,16},{96,32},{112,48},{1... | collective-permute-start | bytes 393224 | tf_op jit(solution)/shard_map/ppermute | solution.py:42
  254.6 7.6 %collective-permute-start.50 = (f32[128,256]{1,0:T(8,128)}, f32[128,256]{1,0:T(8,128)S(1)}, u32[]{:S(2)}, u32[]{:S(2)}) collective-permute-start(f32[128,256]{1,0:T(8,128)} %shard_map.83), channel_id=1, source_target_pairs={{0,32},{16,48},{32,64},{48,80},{64,96},{80,112},{96,0},{112,16},{1... | collective-permute-start | bytes 393224 | tf_op jit(solution)/shard_map/ppermute | solution.py:42
  263.1 9.4 %collective-permute-start.53 = (f32[4,128,256]{2,1,0:T(8,128)S(1)}, f32[4,128,256]{2,1,0:T(8,128)S(1)}, u32[]{:S(2)}, u32[]{:S(2)}) collective-permute-start(f32[4,128,256]{2,1,0:T(8,128)S(1)} %pad_maximum_fusion.6.refs_0_), channel_id=1, source_target_pairs={{0,16},{16,0},{32,48},{48,32},{64,80},{80,64},{96,112},{112,96},{1... | collective-permute-start | bytes 1572872 | tf_op jit(solution)/shard_map/ppermute | solution.py:47
  272.4 27.5 %copy-start.4 = (f32[128,256]{1,0:T(8,128)S(1)}, f32[128,256]{1,0:T(8,128)}, u32[]{:S(2)}) copy-start(f32[128,256]{1,0:T(8,128)} %shard_map.68.base) | copy-start | bytes 393220
  272.4 35.1 %copy-start.8 = (f32[128,256]{1,0:T(8,128)S(1)}, f32[128,256]{1,0:T(8,128)}, u32[]{:S(2)}) copy-start(f32[128,256]{1,0:T(8,128)} %shard_map.78) | copy-start | bytes 393220
  272.4 35.1 %copy-start.9 = (f32[128,256]{1,0:T(8,128)S(1)}, f32[128,256]{1,0:T(8,128)}, u32[]{:S(2)}) copy-start(f32[128,256]{1,0:T(8,128)} %shard_map.80) | copy-start | bytes 393220
  272.4 35.1 %copy-start.10 = (f32[128,256]{1,0:T(8,128)S(1)}, f32[128,256]{1,0:T(8,128)}, u32[]{:S(2)}) copy-start(f32[128,256]{1,0:T(8,128)} %shard_map.83) | copy-start | bytes 393220
  277.1 14.5 %collective-permute-start.56 = (f32[4,128,256]{2,1,0:T(8,128)S(1)}, f32[4,128,256]{2,1,0:T(8,128)S(1)}, u32[]{:S(2)}, u32[]{:S(2)}) collective-permute-start(f32[4,128,256]{2,1,0:T(8,128)S(1)} %get-tuple-element.73), channel_id=1, source_target_pairs={{0,12},{1,13},{2,14},{3,15},{4,0},{5,1},{6,2},{7,3},{8,4},{9,5},{1... | collective-permute-start | bytes 1572872 | tf_op jit(solution)/shard_map/ppermute | solution.py:37
  279.2 12.4 %collective-permute-start.55 = (f32[4,128,256]{2,1,0:T(8,128)S(1)}, f32[4,128,256]{2,1,0:T(8,128)S(1)}, u32[]{:S(2)}, u32[]{:S(2)}) collective-permute-start(f32[4,128,256]{2,1,0:T(8,128)S(1)} %get-tuple-element.72), channel_id=1, source_target_pairs={{0,8},{1,9},{2,10},{3,11},{4,12},{5,13},{6,14},{7,15},{8,0},{9,1},... | collective-permute-start | bytes 1572872 | tf_op jit(solution)/shard_map/ppermute | solution.py:37
  279.5 16.0 %collective-permute-start.54 = (f32[4,128,256]{2,1,0:T(8,128)S(1)}, f32[4,128,256]{2,1,0:T(8,128)S(1)}, u32[]{:S(2)}, u32[]{:S(2)}) collective-permute-start(f32[4,128,256]{2,1,0:T(8,128)S(1)} %get-tuple-element.71), channel_id=1, source_target_pairs={{0,4},{1,5},{2,6},{3,7},{4,8},{5,9},{6,10},{7,11},{8,12},{9,13},{1... | collective-permute-start | bytes 1572872 | tf_op jit(solution)/shard_map/ppermute | solution.py:37
  296.3 7.6 %collective-permute-start.57 = (f32[128,256]{1,0:T(8,128)S(1)}, f32[128,256]{1,0:T(8,128)S(1)}, u32[]{:S(2)}, u32[]{:S(2)}) collective-permute-start(f32[128,256]{1,0:T(8,128)S(1)} %get-tuple-element.78), channel_id=1, source_target_pairs={{0,1},{1,2},{2,3},{3,0},{4,5},{5,6},{6,7},{7,4},{8,9},{9,10},{10,1... | collective-permute-start | bytes 393224 | tf_op jit(solution)/shard_map/ppermute | solution.py:37
  296.3 7.6 %collective-permute-start.58 = (f32[128,256]{1,0:T(8,128)S(1)}, f32[128,256]{1,0:T(8,128)S(1)}, u32[]{:S(2)}, u32[]{:S(2)}) collective-permute-start(f32[128,256]{1,0:T(8,128)S(1)} %get-tuple-element.77), channel_id=1, source_target_pairs={{0,2},{1,3},{2,0},{3,1},{4,6},{5,7},{6,4},{7,5},{8,10},{9,11},{10,... | collective-permute-start | bytes 393224 | tf_op jit(solution)/shard_map/ppermute | solution.py:37
  298.9 5.8 %collective-permute-start.59 = (f32[128,256]{1,0:T(8,128)S(1)}, f32[128,256]{1,0:T(8,128)S(1)}, u32[]{:S(2)}, u32[]{:S(2)}) collective-permute-start(f32[128,256]{1,0:T(8,128)S(1)} %get-tuple-element.76), channel_id=1, source_target_pairs={{0,3},{1,0},{2,1},{3,2},{4,7},{5,4},{6,5},{7,6},{8,11},{9,8},{10,9... | collective-permute-start | bytes 393224 | tf_op jit(solution)/shard_map/ppermute | solution.py:37
  (24 other events, 150.8 us)

commit v2 on v1

v2 whole, which is shorter than its diff:
```python
import functools

import jax
import jax.numpy as jnp
from jax import lax
from jax.experimental import pallas as pl
from jax.experimental.pallas import tpu as pltpu
from jax.sharding import PartitionSpec as P

W = 128
R = 256
LEV = 4
NZ, NC, NX, NY = 4, 2, 4, 4
BOTH = ("prow", "pcol")
PLAIN = (1, 2, 3)
FAR_FIRST = (2, 1, 3)


def pair_index(high, low):
    return high * (high - 1) // 2 + low


def device(z, c, x, y):
    return (z % NZ * NC + c) * NX * NY + x % NX * NY + y % NY


def shift_plane(value, step, phase):
    pairs = []
    for z in range(NZ):
        for c in range(NC):
            for x in range(NX):
                for y in range(NY):
                    if c == phase:
                        there = device(z, c, x + step, y)
                    else:
                        there = device(z, c, x, y + step)
                    pairs.append((device(z, c, x, y), there))
    return lax.ppermute(value, BOTH, pairs)


def shift_z(value, step):
    pairs = [(z * NC + c, (z + step) % NZ * NC + c) for z in range(NZ) for c in range(NC)]
    return lax.ppermute(value, "prow", pairs)


def swap_core(value):
    pairs = [(z * NC + c, z * NC + 1 - c) for z in range(NZ) for c in range(NC)]
    return lax.ppermute(value, "prow", pairs)


def split(value):
    high = value.astype(jnp.bfloat16)
    low = (value - high.astype(jnp.float32)).astype(jnp.bfloat16)
    return high, low


def near(value):
    return pltpu.with_memory_space_constraint(value, pltpu.VMEM)


def far(value):
    return pltpu.with_memory_space_constraint(value, pltpu.HBM)


def fast_call(kernel, shapes, operands, scalars, scratch, flops):
    return pl.pallas_call(
        kernel,
        in_specs=[pl.BlockSpec(memory_space=pltpu.SMEM)] * len(scalars)
        + [pl.BlockSpec(memory_space=pltpu.VMEM)] * len(operands),
        out_specs=[pl.BlockSpec(memory_space=pltpu.VMEM)] * len(shapes),
        out_shape=[pltpu.VMEM(shape, jnp.float32) for shape in shapes],
        scratch_shapes=scratch,
        compiler_params=pltpu.CompilerParams(vmem_limit_bytes=16 * 1024 * 1024),
        cost_estimate=pl.CostEstimate(flops=flops, bytes_accessed=4096, transcendentals=0),
    )(*scalars, *[near(value) for value in operands])


def pair_kernel(index, n_in, n_out, flip, has_init, waits, take, put, live, *refs):
    vectors, refs = refs[:n_in], refs[n_in:]
    blocks, refs = refs[0], refs[1:]
    init, refs = (refs[:n_out], refs[n_out:]) if has_init else ((), refs)
    refs = refs[waits:]
    outs, halves, total = refs[:n_out], refs[n_out], refs[n_out + 1]
    per = vectors[0].shape[0]
    for k in range(n_in * per):
        high, low = split(vectors[k // per][k % per])
        halves[k, :W] = high
        halves[k, W:] = low
    per = outs[0].shape[0]
    for k in range(n_out):
        if has_init:
            total[k * per : (k + 1) * per] = init[k][...]
        else:
            total[k * per : (k + 1) * per] = jnp.zeros((per, W, R), jnp.float32)
    for slot in range(blocks.shape[1]):
        block = jnp.where(live[slot] > 0, blocks[index, slot], 0.0)
        if flip:
            block = block.T
        high, low = split(block)
        left = jnp.concatenate(
            [jnp.concatenate([high, high], axis=1), jnp.concatenate([low, low], axis=1)], axis=0
        )
        product = jnp.dot(left, halves[take[slot]], preferred_element_type=jnp.float32)
        total[put[slot]] += product[:W] + product[W:]
    for k in range(n_out):
        outs[k][...] = total[k * per : (k + 1) * per]


def pair_product(index, flip, scalars, vectors, blocks, init, after, n_out, total):
    n_in = len(vectors)
    units = n_in * vectors[0].shape[0]
    return fast_call(
        functools.partial(pair_kernel, index, n_in, n_out, flip, init is not None, len(after)),
        [(total // n_out, W, R)] * n_out,
        [*vectors, blocks, *(init or ()), *after],
        scalars,
        [pltpu.VMEM((units, 2 * W, R), jnp.bfloat16), pltpu.VMEM((total, W, R), jnp.float32)],
        blocks.shape[1] * 8 * W * W * R,
    )


def dot(left, right):
    return jnp.dot(
        left, right, precision=lax.Precision.HIGHEST, preferred_element_type=jnp.float32
    )


def solve_kernel(level, flip, stacked, terms, inverse, base, *refs):
    value = base[level] if stacked else base[...]
    if terms:
        gone = refs[0][...]
        for ref in refs[1:terms]:
            gone = gone + ref[...]
        value = value - gone
    outs = refs[terms:]
    for flipped, out in zip(flip, outs):
        matrix = inverse[level]
        value = dot(matrix.T if flipped else matrix, value)
        out[...] = value


def solve(level, flip, inverse, base, gone):
    return fast_call(
        functools.partial(solve_kernel, level, flip, base.ndim == 3, len(gone)),
        [(W, R)] * len(flip),
        [inverse, base, *gone],
        [],
        [],
        12 * W * W * R,
    )


def add_kernel(terms, waits, *refs):
    for k, out in enumerate(refs[terms + waits :]):
        value = refs[0][k]
        for ref in refs[1:terms]:
            value = value + ref[k]
        out[...] = value


def add_units(parts, after):
    return fast_call(
        functools.partial(add_kernel, len(parts), len(after)),
        [(W, R)] * 4,
        [*parts, *after],
        [],
        [],
        len(parts) * 4 * W * R,
    )


def first_kernel(inverse, base, out, matrix, value, sems):
    copies = [
        pltpu.make_async_copy(inverse.at[0], matrix, sems.at[0]),
        pltpu.make_async_copy(base.at[0], value, sems.at[1]),
    ]
    for copy in copies:
        copy.start()
    for copy in copies:
        copy.wait()
    out[...] = dot(matrix[...], value[...])


def first_solve(inverse, base):
    return pl.pallas_call(
        first_kernel,
        in_specs=[pl.BlockSpec(memory_space=pl.ANY)] * 2,
        out_specs=pl.BlockSpec(memory_space=pltpu.VMEM),
        out_shape=pltpu.VMEM((W, R), jnp.float32),
        scratch_shapes=[
            pltpu.VMEM((W, W), jnp.float32),
            pltpu.VMEM((W, R), jnp.float32),
            pltpu.SemaphoreType.DMA((2,)),
        ],
        compiler_params=pltpu.CompilerParams(vmem_limit_bytes=16 * 1024 * 1024),
    )(far(inverse), far(base))


def load_kernel(blocks, after, out, sems):
    copies = [
        pltpu.make_async_copy(blocks.at[k], out.at[k], sems.at[k]) for k in range(blocks.shape[0])
    ]
    for copy in copies:
        copy.start()
    for copy in copies:
        copy.wait()


def load(blocks, after):
    return pl.pallas_call(
        load_kernel,
        in_specs=[pl.BlockSpec(memory_space=pl.ANY), pl.BlockSpec(memory_space=pltpu.VMEM)],
        out_specs=pl.BlockSpec(memory_space=pltpu.VMEM),
        out_shape=pltpu.VMEM(blocks.shape, jnp.float32),
        scratch_shapes=[pltpu.SemaphoreType.DMA((blocks.shape[0],))],
        compiler_params=pltpu.CompilerParams(vmem_limit_bytes=16 * 1024 * 1024),
        cost_estimate=pl.CostEstimate(
            flops=0, bytes_accessed=blocks.size * 4, transcendentals=0
        ),
    )(far(blocks), near(after))


def gather_plane(value):
    units = jnp.stack([value] + [shift_plane(value, d, 0) for d in PLAIN])
    return [units] + [shift_plane(units, d, 1) for d in PLAIN]


def scatter_plane(groups, beside):
    first = [shift_plane(groups[k], d, 0) for k, d in enumerate(FAR_FIRST, 1)]
    units = add_units([groups[0]] + first, beside(first[0]))
    return [units[0]] + [shift_plane(units[d], d, 1) for d in PLAIN]


def scatter_z(mine, other):
    units = add_units([mine, swap_core(other)], [])
    return [units[0]] + [shift_z(units[d], d) for d in PLAIN]


def gather_z(value):
    units = jnp.stack([value] + [shift_z(value, d) for d in PLAIN])
    return [units, swap_core(units)]


def place(offset, order):
    spot = jnp.zeros_like(offset)
    for k, d in enumerate(order, 1):
        spot = jnp.where(offset == d, k, spot)
    return spot


def body(rhs, dinv, blocks, targets, sources):
    right = rhs[:, 0, 0]
    inverse = dinv[:, 0, 0]
    aims = targets[0, 0]
    anchor = sources[0, 0]
    row = lax.axis_index("prow")
    col = lax.axis_index("pcol")
    z, core = row // NC, row % NC
    x, y = col // NY, col % NY
    live = (aims >= 0).astype(jnp.int32)
    rows = jnp.maximum(aims, 0)
    off_x = (x - anchor // NY) % NX
    off_y = (y - anchor % NY) % NY
    off_z = (z - rows // NC) % NZ
    first = core == 0
    to_x, to_y, to_z = (-off_x) % NX, (-off_y) % NY, (-off_z) % NZ
    take_plane = jnp.where(first, off_y * NX + off_x, off_x * NY + off_y)
    put_plane = jnp.where(
        first, place(to_x, FAR_FIRST) * NY + to_y, place(to_y, FAR_FIRST) * NX + to_x
    )
    across = (rows % NC != core).astype(jnp.int32) * NZ
    take_z = across + off_z
    put_z = across + to_z

    def forth(high, low, vectors, init):
        index = pair_index(high, low)
        scalars = (take_plane[index], put_z[index], live[index])
        return pair_product(index, False, scalars, vectors, panels, init, (), 2, 8)

    def back(high, low, vectors, init, after):
        index = pair_index(high, low)
        scalars = (take_z[index], put_plane[index], live[index])
        return pair_product(index, True, scalars, vectors, panels, init, after, 4, 16)

    top = LEV - 1
    solved = [None] * LEV
    result = [None] * LEV
    sums = [None] * LEV
    for level in range(LEV):
        gone = [] if level == 0 else scatter_z(*sums[level])
        if level == top:
            solved[level], result[level] = solve(level, (False, True), inverse, right, gone)
            break
        if level == 0:
            solved[level] = first_solve(inverse, right)
        else:
            (solved[level],) = solve(level, (False,), inverse, right, gone)
        vectors = gather_plane(solved[level])
        if level == 0:
            panels = load(blocks[0, 0], vectors[0])
        for high in range(level + 1, LEV):
            sums[high] = forth(high, level, vectors, sums[high])
    sums = [None] * LEV
    for level in reversed(range(1, LEV)):
        vectors = gather_z(result[level])

        def beside(held):
            done = []
            for low in reversed(range(level - 1)):
                sums[low] = back(level, low, vectors, sums[low], (held,))
                done += sums[low][:1]
            return done

        gone = scatter_plane(back(level, level - 1, vectors, sums[level - 1], ()), beside)
        (result[level - 1],) = solve(level - 1, (True,), inverse, solved[level - 1], gone)
    forward = jnp.stack(solved)[:, None, None]
    solution = jnp.stack(result)[:, None, None]
    return (forward, solution)


def solution(mesh):
    placed = (
        P(None, "prow", "pcol", None, None),
        P(None, "prow", "pcol", None, None),
        P("prow", "pcol", None, None, None, None),
        P("prow", "pcol", None, None),
        P("prow", "pcol", None, None),
    )
    return jax.shard_map(
        body,
        mesh=mesh,
        in_specs=placed,
        out_specs=(P(None, "prow", "pcol", None, None), P(None, "prow", "pcol", None, None)),
        check_vma=False,
    )
```

time: 311 us -> 260 us (0.84)
  Pallas kernels: 70.9 us -> 35.5 us
  starting transfers between devices: 72.5 us -> 98.7 us
  waiting for transfers between devices: 142 us -> 116 us
  local copies, waits for them, and re-layouts: 12.1 us -> 0.04 us
  other arithmetic: 10.9 us -> 3.99 us
    pallas_call x20 -> x26, Pallas kernels: 70.9 us -> 35.5 us  [the longest x24 29.6 us: fast_call(): pl.pallas_call(kernel, in_specs=[pl.BlockSpec(memory_space=pltpu.SMEM)] *...]
    ppermute x36, waiting for transfers between devices: 95.6 us -> 75.2 us  [shift_plane(): return lax.ppermute(value, BOTH, pairs)]
    ppermute x36, starting transfers between devices: 47.9 us -> 67.7 us  [shift_plane(): return lax.ppermute(value, BOTH, pairs)]
    ppermute x18, waiting for transfers between devices: 38.6 us -> 29.6 us  [shift_z(): return lax.ppermute(value, 'prow', pairs)]
    squeeze x11 -> x3, local copies, waits for them, and re-layouts: 7.75 us -> 0.02 us  [the longest x2 0.01 us: forth(): scalars = (take_plane[index], put_z[index], live[index])]
    ppermute x18, starting transfers between devices: 24 us -> 30.5 us  [shift_z(): return lax.ppermute(value, 'prow', pairs)]
    another operation x6, other arithmetic: 5.63 us -> 0.21 us  [the longest x3 0.1 us: gather_z(): units = jnp.stack([value] + [shift_z(value, d) for d in PLAIN])]
    unnamed x56 -> x4, local copies, waits for them, and re-layouts: 4.37 us -> 0.01 us
  transfers between devices with their start and end apart: 60 -> 60, of which waited for: 49 -> 50; matrix products, arithmetic and copies ran while one was open for 1% -> 1% of each run, Pallas kernels for 9% -> 7%
where the time goes in v2:
time: 260 us; the launch traced here: 256 us
  waiting for transfers between devices  116 us (45%)
  starting transfers between devices  98.7 us (38%)
  Pallas kernels  35.5 us (14%)
  other arithmetic  3.99 us (2%)
    ppermute x36, waiting for transfers between devices, shift_plane(): return lax.ppermute(value, BOTH, pairs)  75.2 us
    ppermute x36, starting transfers between devices, shift_plane(): return lax.ppermute(value, BOTH, pairs)  67.7 us
    ppermute x18, starting transfers between devices, shift_z(): return lax.ppermute(value, 'prow', pairs)  30.5 us
    ppermute x18, waiting for transfers between devices, shift_z(): return lax.ppermute(value, 'prow', pairs)  29.6 us
    pallas_call x24, Pallas kernels, fast_call(): pl.pallas_call(kernel, in_specs=[pl.BlockSpec(memory_space=pltpu.SMEM)] *...  29.6 us
    ppermute x6, waiting for transfers between devices, swap_core(): return lax.ppermute(value, 'prow', pairs)  11.4 us
  transfers between devices with their start and end apart: 60, of which 50 were waited for; matrix products, arithmetic and copies ran while one was open for 1% of the time, Pallas kernels for 7%

profile of v2, /device:TPU:0, one launch (start us, length us, event | category | flops | bytes accessed | tf_op | source)
XLA Modules:
  0.0 255.7 jit_solution(15225991551981171160)
XLA Ops:
  1.9 3.2 %collective-permute-start.1 = (f32[128,256]{1,0:T(8,128)S(1)}, f32[128,256]{1,0:T(8,128)S(1)}, u32[]{:S(2)}, u32[]{:S(2)}) collective-permute-start(f32[128,256]{1,0:T(8,128)S(1)} %shard_map.68.base), channel_id=1, source_target_pairs={{0,8},{1,9},{2,10},{3,11},{4,12},{5,13},{6,14},{7,15},{8,0},{9,1},... | collective-permute-start | bytes 393224 | tf_op jit(solution)/shard_map/ppermute | solution.py:38
  10.0 2.4 collective-permute-done
  14.0 2.9 %collective-permute-start.4 = (f32[4,128,256]{2,1,0:T(8,128)S(1)}, f32[4,128,256]{2,1,0:T(8,128)S(1)}, u32[]{:S(2)}, u32[]{:S(2)}) collective-permute-start(f32[4,128,256]{2,1,0:T(8,128)S(1)} %fusion.4.after.refs_0_), channel_id=1, source_target_pairs={{0,2},{1,3},{2,0},{3,1},{4,6},{5,7},{6,4},{7,5},{8,10},{9,11},{10,... | collective-permute-start | bytes 1572872 | tf_op jit(solution)/shard_map/ppermute | solution.py:38
  19.0 4.7 %shard_map.69.refs_4_.refs_2_ = f32[6,32,128,128]{3,2,1,0:T(8,128)S(1)} custom-call(f32[6,32,128,128]{3,2,1,0:T(8,128)} %bitcast.202, f32[4,128,256]{2,1,0:T(8,128)S(1)} %fusion.4.after.refs_0_), custom_call_target="tpu_custom_call" | custom-call | bytes 12582912 | tf_op jit(solution)/shard_map/pallas_call | solution.py:210
  23.8 5.9 %collective-permute-done.4.refs_2_ = f32[4,128,256]{2,1,0:T(8,128)S(1)} collective-permute-done((f32[4,128,256]{2,1,0:T(8,128)S(1)}, f32[4,128,256]{2,1,0:T(8,128)S(1)}, u32[]{:S(2)}, u32[]{:S(2)}) %collective-permute-start.4) | collective-permute-done | bytes 524320 | tf_op jit(solution)/shard_map/ppermute | solution.py:38
  29.7 2.2 shard_map.70
  32.1 1.9 collective-permute-done.6.refs_1_
  34.0 2.0 collective-permute-start.7
  36.0 3.6 %collective-permute-start.8 = (f32[128,256]{1,0:T(8,128)S(1)}, f32[128,256]{1,0:T(8,128)S(1)}, u32[]{:S(2)}, u32[]{:S(2)}) collective-permute-start(f32[128,256]{1,0:T(8,128)S(1)} %get-tuple-element.68), channel_id=1, source_target_pairs={{0,64},{16,80},{32,96},{48,112},{64,0},{80,16},{96,32},{112,48},{1... | collective-permute-start | bytes 393224 | tf_op jit(solution)/shard_map/ppermute | solution.py:43
  41.9 4.0 %collective-permute-done.8.refs_2_ = f32[128,256]{1,0:T(8,128)S(1)} collective-permute-done((f32[128,256]{1,0:T(8,128)S(1)}, f32[128,256]{1,0:T(8,128)S(1)}, u32[]{:S(2)}, u32[]{:S(2)}) %collective-permute-start.8) | collective-permute-done | bytes 131104 | tf_op jit(solution)/shard_map/ppermute | solution.py:43
  46.3 1.7 collective-permute-start.11
  49.5 4.3 %collective-permute-done.10 = f32[128,256]{1,0:T(8,128)S(1)} collective-permute-done((f32[128,256]{1,0:T(8,128)S(1)}, f32[128,256]{1,0:T(8,128)S(1)}, u32[]{:S(2)}, u32[]{:S(2)}) %collective-permute-start.10) | collective-permute-done | bytes 131104 | tf_op jit(solution)/shard_map/ppermute | solution.py:38
  56.5 2.1 collective-permute-start.14
  58.6 1.7 collective-permute-start.15
  60.4 2.2 shard_map.73
  62.6 2.7 %collective-permute-done.13.refs_1_ = f32[4,128,256]{2,1,0:T(8,128)S(1)} collective-permute-done((f32[4,128,256]{2,1,0:T(8,128)S(1)}, f32[4,128,256]{2,1,0:T(8,128)S(1)}, u32[]{:S(2)}, u32[]{:S(2)}) %collective-permute-start.13) | collective-permute-done | bytes 524320 | tf_op jit(solution)/shard_map/ppermute | solution.py:38
  65.3 6.1 %collective-permute-done.14.refs_2_ = f32[4,128,256]{2,1,0:T(8,128)S(1)} collective-permute-done((f32[4,128,256]{2,1,0:T(8,128)S(1)}, f32[4,128,256]{2,1,0:T(8,128)S(1)}, u32[]{:S(2)}, u32[]{:S(2)}) %collective-permute-start.14) | collective-permute-done | bytes 524320 | tf_op jit(solution)/shard_map/ppermute | solution.py:38
  71.8 2.2 shard_map.74
  74.1 1.9 collective-permute-done.16.refs_1_
  77.4 2.4 collective-permute-start.18
  81.3 2.0 collective-permute-done.17.refs_1_
  83.3 2.8 %collective-permute-done.18.refs_2_ = f32[128,256]{1,0:T(8,128)S(1)} collective-permute-done((f32[128,256]{1,0:T(8,128)S(1)}, f32[128,256]{1,0:T(8,128)S(1)}, u32[]{:S(2)}, u32[]{:S(2)}) %collective-permute-start.18) | collective-permute-done | bytes 131104 | tf_op jit(solution)/shard_map/ppermute | solution.py:43
  87.2 3.2 %collective-permute-start.21 = (f32[128,256]{1,0:T(8,128)S(1)}, f32[128,256]{1,0:T(8,128)S(1)}, u32[]{:S(2)}, u32[]{:S(2)}) collective-permute-start(f32[128,256]{1,0:T(8,128)S(1)} %shard_map.76.base), channel_id=1, source_target_pairs={{0,8},{1,9},{2,10},{3,11},{4,12},{5,13},{6,14},{7,15},{8,0},{9,1},... | collective-permute-start | bytes 393224 | tf_op jit(solution)/shard_map/ppermute | solution.py:38
  90.5 2.4 collective-permute-done.20
  92.8 2.0 collective-permute-done.21
  95.5 2.0 collective-permute-start.23
  97.5 2.1 collective-permute-start.24
  101.0 2.2 shard_map.77
  103.3 2.2 shard_map.78
  105.9 6.5 %collective-permute-done.24.refs_2_ = f32[4,128,256]{2,1,0:T(8,128)S(1)} collective-permute-done((f32[4,128,256]{2,1,0:T(8,128)S(1)}, f32[4,128,256]{2,1,0:T(8,128)S(1)}, u32[]{:S(2)}, u32[]{:S(2)}) %collective-permute-start.24) | collective-permute-done | bytes 524320 | tf_op jit(solution)/shard_map/ppermute | solution.py:38
  112.4 2.2 shard_map.79
  114.8 1.9 collective-permute-done.26.refs_1_
  118.4 2.5 collective-permute-start.28
  121.7 1.9 collective-permute-done.27.refs_1_
  123.5 3.7 %collective-permute-done.28.refs_2_ = f32[128,256]{1,0:T(8,128)S(1)} collective-permute-done((f32[128,256]{1,0:T(8,128)S(1)}, f32[128,256]{1,0:T(8,128)S(1)}, u32[]{:S(2)}, u32[]{:S(2)}) %collective-permute-start.28) | collective-permute-done | bytes 131104 | tf_op jit(solution)/shard_map/ppermute | solution.py:43
  129.3 2.5 collective-permute-start.31
  132.6 2.2 collective-permute-done.30
  134.8 2.9 %collective-permute-done.31 = f32[128,256]{1,0:T(8,128)S(1)} collective-permute-done((f32[128,256]{1,0:T(8,128)S(1)}, f32[128,256]{1,0:T(8,128)S(1)}, u32[]{:S(2)}, u32[]{:S(2)}) %collective-permute-start.31) | collective-permute-done | bytes 131104 | tf_op jit(solution)/shard_map/ppermute | solution.py:43
  137.9 1.9 collective-permute-done.33.refs_1_
  139.8 2.2 shard_map.82
  142.0 10.4 %collective-permute-start.34 = (f32[4,128,256]{2,1,0:T(8,128)S(1)}, f32[4,128,256]{2,1,0:T(8,128)S(1)}, u32[]{:S(2)}, u32[]{:S(2)}) collective-permute-start(f32[4,128,256]{2,1,0:T(8,128)S(1)} %get-tuple-element.91), channel_id=1, source_target_pairs={{0,8},{1,9},{2,10},{3,11},{4,12},{5,13},{6,14},{7,15},{8,0},{9,1},... | collective-permute-start | bytes 1572872 | tf_op jit(solution)/shard_map/ppermute | solution.py:38
  155.7 6.0 %collective-permute-done.34.refs_3_.refs_1_ = f32[4,128,256]{2,1,0:T(8,128)S(1)} collective-permute-done((f32[4,128,256]{2,1,0:T(8,128)S(1)}, f32[4,128,256]{2,1,0:T(8,128)S(1)}, u32[]{:S(2)}, u32[]{:S(2)}) %collective-permute-start.34) | collective-permute-done | bytes 524320 | tf_op jit(solution)/shard_map/ppermute | solution.py:38
  161.7 2.2 shard_map.84
  164.0 2.3 shard_map.83
  167.4 2.1 collective-permute-start.37
  169.4 2.1 collective-permute-start.38
  173.6 2.3 collective-permute-done.38.refs_2_
  178.2 2.4 collective-permute-start.41
  183.1 1.8 collective-permute-done.41
  185.7 1.9 collective-permute-done.43.refs_1_
  187.6 2.2 shard_map.87
  194.7 6.0 %collective-permute-done.44.refs_7_.refs_1_ = f32[4,128,256]{2,1,0:T(8,128)S(1)} collective-permute-done((f32[4,128,256]{2,1,0:T(8,128)S(1)}, f32[4,128,256]{2,1,0:T(8,128)S(1)}, u32[]{:S(2)}, u32[]{:S(2)}) %collective-permute-start.44) | collective-permute-done | bytes 524320 | tf_op jit(solution)/shard_map/ppermute | solution.py:38
  200.7 2.2 shard_map.88
  203.0 3.3 %collective-permute-done.45.refs_2_ = f32[4,128,256]{2,1,0:T(8,128)S(1)} collective-permute-done((f32[4,128,256]{2,1,0:T(8,128)S(1)}, f32[4,128,256]{2,1,0:T(8,128)S(1)}, u32[]{:S(2)}, u32[]{:S(2)}) %collective-permute-start.45) | collective-permute-done | bytes 524320 | tf_op jit(solution)/shard_map/ppermute | solution.py:38
  207.9 2.7 %collective-permute-start.48 = (f32[128,256]{1,0:T(8,128)S(1)}, f32[128,256]{1,0:T(8,128)S(1)}, u32[]{:S(2)}, u32[]{:S(2)}) collective-permute-start(f32[128,256]{1,0:T(8,128)S(1)} %get-tuple-element.113), channel_id=1, source_target_pairs={{0,2},{1,3},{2,0},{3,1},{4,6},{5,7},{6,4},{7,5},{8,10},{9,11},{10,... | collective-permute-start | bytes 393224 | tf_op jit(solution)/shard_map/ppermute | solution.py:38
  212.6 2.2 collective-permute-done.48.refs_2_
  217.3 2.7 %collective-permute-start.51 = (f32[128,256]{1,0:T(8,128)S(1)}, f32[128,256]{1,0:T(8,128)S(1)}, u32[]{:S(2)}, u32[]{:S(2)}) collective-permute-start(f32[128,256]{1,0:T(8,128)S(1)} %shard_map.90), channel_id=1, source_target_pairs={{0,64},{16,80},{32,96},{48,112},{64,0},{80,16},{96,32},{112,48},{1... | collective-permute-start | bytes 393224 | tf_op jit(solution)/shard_map/ppermute | solution.py:43
  220.5 1.8 collective-permute-done.50
  222.3 2.1 collective-permute-done.51
  225.1 1.9 collective-permute-done.53.refs_1_
  227.0 2.2 shard_map.91
  234.1 6.0 %collective-permute-done.54.refs_1_ = f32[4,128,256]{2,1,0:T(8,128)S(1)} collective-permute-done((f32[4,128,256]{2,1,0:T(8,128)S(1)}, f32[4,128,256]{2,1,0:T(8,128)S(1)}, u32[]{:S(2)}, u32[]{:S(2)}) %collective-permute-start.54) | collective-permute-done | bytes 524320 | tf_op jit(solution)/shard_map/ppermute | solution.py:38
  240.1 5.5 %collective-permute-done.55.refs_2_ = f32[4,128,256]{2,1,0:T(8,128)S(1)} collective-permute-done((f32[4,128,256]{2,1,0:T(8,128)S(1)}, f32[4,128,256]{2,1,0:T(8,128)S(1)}, u32[]{:S(2)}, u32[]{:S(2)}) %collective-permute-start.55) | collective-permute-done | bytes 524320 | tf_op jit(solution)/shard_map/ppermute | solution.py:38
  246.7 2.6 %collective-permute-start.58 = (f32[128,256]{1,0:T(8,128)S(1)}, f32[128,256]{1,0:T(8,128)S(1)}, u32[]{:S(2)}, u32[]{:S(2)}) collective-permute-start(f32[128,256]{1,0:T(8,128)S(1)} %get-tuple-element.124), channel_id=1, source_target_pairs={{0,2},{1,3},{2,0},{3,1},{4,6},{5,7},{6,4},{7,5},{8,10},{9,11},{10,... | collective-permute-start | bytes 393224 | tf_op jit(solution)/shard_map/ppermute | solution.py:38
  (100 shorter events, 65.7 us)
Async XLA Ops:
  1.9 6.6 %collective-permute-start.1 = (f32[128,256]{1,0:T(8,128)S(1)}, f32[128,256]{1,0:T(8,128)S(1)}, u32[]{:S(2)}, u32[]{:S(2)}) collective-permute-start(f32[128,256]{1,0:T(8,128)S(1)} %shard_map.68.base), channel_id=1, source_target_pairs={{0,8},{1,9},{2,10},{3,11},{4,12},{5,13},{6,14},{7,15},{8,0},{9,1},... | collective-permute-start | bytes 393224 | tf_op jit(solution)/shard_map/ppermute | solution.py:38
  5.0 5.0 %collective-permute-start.2 = (f32[128,256]{1,0:T(8,128)S(1)}, f32[128,256]{1,0:T(8,128)S(1)}, u32[]{:S(2)}, u32[]{:S(2)}) collective-permute-start(f32[128,256]{1,0:T(8,128)S(1)} %shard_map.68.base), channel_id=1, source_target_pairs={{0,12},{1,13},{2,14},{3,15},{4,0},{5,1},{6,2},{7,3},{8,4},{9,5},{1... | collective-permute-start | bytes 393224 | tf_op jit(solution)/shard_map/ppermute | solution.py:38
  6.2 6.2 %collective-permute-start = (f32[128,256]{1,0:T(8,128)S(1)}, f32[128,256]{1,0:T(8,128)S(1)}, u32[]{:S(2)}, u32[]{:S(2)}) collective-permute-start(f32[128,256]{1,0:T(8,128)S(1)} %shard_map.68.base), channel_id=1, source_target_pairs={{0,4},{1,5},{2,6},{3,7},{4,8},{5,9},{6,10},{7,11},{8,12},{9,13},{1... | collective-permute-start | bytes 393224 | tf_op jit(solution)/shard_map/ppermute | solution.py:38
  12.4 11.4 %collective-permute-start.3 = (f32[4,128,256]{2,1,0:T(8,128)S(1)}, f32[4,128,256]{2,1,0:T(8,128)S(1)}, u32[]{:S(2)}, u32[]{:S(2)}) collective-permute-start(f32[4,128,256]{2,1,0:T(8,128)S(1)} %fusion.4.after.refs_0_), channel_id=1, source_target_pairs={{0,1},{1,2},{2,3},{3,0},{4,5},{5,6},{6,7},{7,4},{8,9},{9,10},{10,1... | collective-permute-start | bytes 1572872 | tf_op jit(solution)/shard_map/ppermute | solution.py:38
  14.0 15.7 %collective-permute-start.4 = (f32[4,128,256]{2,1,0:T(8,128)S(1)}, f32[4,128,256]{2,1,0:T(8,128)S(1)}, u32[]{:S(2)}, u32[]{:S(2)}) collective-permute-start(f32[4,128,256]{2,1,0:T(8,128)S(1)} %fusion.4.after.refs_0_), channel_id=1, source_target_pairs={{0,2},{1,3},{2,0},{3,1},{4,6},{5,7},{6,4},{7,5},{8,10},{9,11},{10,... | collective-permute-start | bytes 1572872 | tf_op jit(solution)/shard_map/ppermute | solution.py:38
  17.0 12.8 %collective-permute-start.5 = (f32[4,128,256]{2,1,0:T(8,128)S(1)}, f32[4,128,256]{2,1,0:T(8,128)S(1)}, u32[]{:S(2)}, u32[]{:S(2)}) collective-permute-start(f32[4,128,256]{2,1,0:T(8,128)S(1)} %fusion.4.after.refs_0_), channel_id=1, source_target_pairs={{0,3},{1,0},{2,1},{3,2},{4,7},{5,4},{6,5},{7,6},{8,11},{9,8},{10,9... | collective-permute-start | bytes 1572872 | tf_op jit(solution)/shard_map/ppermute | solution.py:38
  23.8 22.1 %copy-start = (f32[4,1,1,128,128]{4,3,2,1,0:T(8,128)S(1)}, f32[4,1,1,128,128]{4,3,2,1,0:T(8,128)}, u32[]{:S(2)}) copy-start(f32[4,1,1,128,128]{4,3,2,1,0:T(8,128)} %param.6) | copy-start | bytes 786436
  23.8 22.1 %copy-start.1 = (f32[4,1,1,128,256]{4,3,2,1,0:T(8,128)S(1)}, f32[4,1,1,128,256]{4,3,2,1,0:T(8,128)}, u32[]{:S(2)}) copy-start(f32[4,1,1,128,256]{4,3,2,1,0:T(8,128)} %param.5) | copy-start | bytes 1572868
  32.0 2.0 collective-permute-start.6
  34.0 7.9 %collective-permute-start.7 = (f32[128,256]{1,0:T(8,128)S(1)}, f32[128,256]{1,0:T(8,128)S(1)}, u32[]{:S(2)}, u32[]{:S(2)}) collective-permute-start(f32[128,256]{1,0:T(8,128)S(1)} %get-tuple-element.67), channel_id=1, source_target_pairs={{0,32},{16,48},{32,64},{48,80},{64,96},{80,112},{96,0},{112,16},{1... | collective-permute-start | bytes 393224 | tf_op jit(solution)/shard_map/ppermute | solution.py:43
  36.0 9.9 %collective-permute-start.8 = (f32[128,256]{1,0:T(8,128)S(1)}, f32[128,256]{1,0:T(8,128)S(1)}, u32[]{:S(2)}, u32[]{:S(2)}) collective-permute-start(f32[128,256]{1,0:T(8,128)S(1)} %get-tuple-element.68), channel_id=1, source_target_pairs={{0,64},{16,80},{32,96},{48,112},{64,0},{80,16},{96,32},{112,48},{1... | collective-permute-start | bytes 393224 | tf_op jit(solution)/shard_map/ppermute | solution.py:43
  39.6 6.3 %collective-permute-start.9 = (f32[128,256]{1,0:T(8,128)S(1)}, f32[128,256]{1,0:T(8,128)S(1)}, u32[]{:S(2)}, u32[]{:S(2)}) collective-permute-start(f32[128,256]{1,0:T(8,128)S(1)} %get-tuple-element.69), channel_id=1, source_target_pairs={{0,96},{16,112},{32,0},{48,16},{64,32},{80,48},{96,64},{112,80},{1... | collective-permute-start | bytes 393224 | tf_op jit(solution)/shard_map/ppermute | solution.py:43
  46.2 7.7 %collective-permute-start.10 = (f32[128,256]{1,0:T(8,128)S(1)}, f32[128,256]{1,0:T(8,128)S(1)}, u32[]{:S(2)}, u32[]{:S(2)}) collective-permute-start(f32[128,256]{1,0:T(8,128)S(1)} %shard_map.72.base), channel_id=1, source_target_pairs={{0,4},{1,5},{2,6},{3,7},{4,8},{5,9},{6,10},{7,11},{8,12},{9,13},{1... | collective-permute-start | bytes 393224 | tf_op jit(solution)/shard_map/ppermute | solution.py:38
  46.3 7.6 %collective-permute-start.11 = (f32[128,256]{1,0:T(8,128)S(1)}, f32[128,256]{1,0:T(8,128)S(1)}, u32[]{:S(2)}, u32[]{:S(2)}) collective-permute-start(f32[128,256]{1,0:T(8,128)S(1)} %shard_map.72.base), channel_id=1, source_target_pairs={{0,8},{1,9},{2,10},{3,11},{4,12},{5,13},{6,14},{7,15},{8,0},{9,1},... | collective-permute-start | bytes 393224 | tf_op jit(solution)/shard_map/ppermute | solution.py:38
  48.0 6.7 %collective-permute-start.12 = (f32[128,256]{1,0:T(8,128)S(1)}, f32[128,256]{1,0:T(8,128)S(1)}, u32[]{:S(2)}, u32[]{:S(2)}) collective-permute-start(f32[128,256]{1,0:T(8,128)S(1)} %shard_map.72.base), channel_id=1, source_target_pairs={{0,12},{1,13},{2,14},{3,15},{4,0},{5,1},{6,2},{7,3},{8,4},{9,5},{1... | collective-permute-start | bytes 393224 | tf_op jit(solution)/shard_map/ppermute | solution.py:38
  54.8 10.5 %collective-permute-start.13 = (f32[4,128,256]{2,1,0:T(8,128)S(1)}, f32[4,128,256]{2,1,0:T(8,128)S(1)}, u32[]{:S(2)}, u32[]{:S(2)}) collective-permute-start(f32[4,128,256]{2,1,0:T(8,128)S(1)} %pad_maximum_fusion.2.refs_0_), channel_id=1, source_target_pairs={{0,1},{1,2},{2,3},{3,0},{4,5},{5,6},{6,7},{7,4},{8,9},{9,10},{10,1... | collective-permute-start | bytes 1572872 | tf_op jit(solution)/shard_map/ppermute | solution.py:38
  56.5 14.9 %collective-permute-start.14 = (f32[4,128,256]{2,1,0:T(8,128)S(1)}, f32[4,128,256]{2,1,0:T(8,128)S(1)}, u32[]{:S(2)}, u32[]{:S(2)}) collective-permute-start(f32[4,128,256]{2,1,0:T(8,128)S(1)} %pad_maximum_fusion.2.refs_0_), channel_id=1, source_target_pairs={{0,2},{1,3},{2,0},{3,1},{4,6},{5,7},{6,4},{7,5},{8,10},{9,11},{10,... | collective-permute-start | bytes 1572872 | tf_op jit(solution)/shard_map/ppermute | solution.py:38
  58.6 13.2 %collective-permute-start.15 = (f32[4,128,256]{2,1,0:T(8,128)S(1)}, f32[4,128,256]{2,1,0:T(8,128)S(1)}, u32[]{:S(2)}, u32[]{:S(2)}) collective-permute-start(f32[4,128,256]{2,1,0:T(8,128)S(1)} %pad_maximum_fusion.2.refs_0_), channel_id=1, source_target_pairs={{0,3},{1,0},{2,1},{3,2},{4,7},{5,4},{6,5},{7,6},{8,11},{9,8},{10,9... | collective-permute-start | bytes 1572872 | tf_op jit(solution)/shard_map/ppermute | solution.py:38
  74.0 2.0 collective-permute-start.16
  76.1 7.2 %collective-permute-start.17 = (f32[128,256]{1,0:T(8,128)S(1)}, f32[128,256]{1,0:T(8,128)S(1)}, u32[]{:S(2)}, u32[]{:S(2)}) collective-permute-start(f32[128,256]{1,0:T(8,128)S(1)} %get-tuple-element.75), channel_id=1, source_target_pairs={{0,32},{16,48},{32,64},{48,80},{64,96},{80,112},{96,0},{112,16},{1... | collective-permute-start | bytes 393224 | tf_op jit(solution)/shard_map/ppermute | solution.py:43
  77.4 8.7 %collective-permute-start.18 = (f32[128,256]{1,0:T(8,128)S(1)}, f32[128,256]{1,0:T(8,128)S(1)}, u32[]{:S(2)}, u32[]{:S(2)}) collective-permute-start(f32[128,256]{1,0:T(8,128)S(1)} %get-tuple-element.76), channel_id=1, source_target_pairs={{0,64},{16,80},{32,96},{48,112},{64,0},{80,16},{96,32},{112,48},{1... | collective-permute-start | bytes 393224 | tf_op jit(solution)/shard_map/ppermute | solution.py:43
  79.8 6.5 %collective-permute-start.19 = (f32[128,256]{1,0:T(8,128)S(1)}, f32[128,256]{1,0:T(8,128)S(1)}, u32[]{:S(2)}, u32[]{:S(2)}) collective-permute-start(f32[128,256]{1,0:T(8,128)S(1)} %get-tuple-element.77), channel_id=1, source_target_pairs={{0,96},{16,112},{32,0},{48,16},{64,32},{80,48},{96,64},{112,80},{1... | collective-permute-start | bytes 393224 | tf_op jit(solution)/shard_map/ppermute | solution.py:43
  86.6 6.2 %collective-permute-start.20 = (f32[128,256]{1,0:T(8,128)S(1)}, f32[128,256]{1,0:T(8,128)S(1)}, u32[]{:S(2)}, u32[]{:S(2)}) collective-permute-start(f32[128,256]{1,0:T(8,128)S(1)} %shard_map.76.base), channel_id=1, source_target_pairs={{0,4},{1,5},{2,6},{3,7},{4,8},{5,9},{6,10},{7,11},{8,12},{9,13},{1... | collective-permute-start | bytes 393224 | tf_op jit(solution)/shard_map/ppermute | solution.py:38
  87.2 7.6 %collective-permute-start.21 = (f32[128,256]{1,0:T(8,128)S(1)}, f32[128,256]{1,0:T(8,128)S(1)}, u32[]{:S(2)}, u32[]{:S(2)}) collective-permute-start(f32[128,256]{1,0:T(8,128)S(1)} %shard_map.76.base), channel_id=1, source_target_pairs={{0,8},{1,9},{2,10},{3,11},{4,12},{5,13},{6,14},{7,15},{8,0},{9,1},... | collective-permute-start | bytes 393224 | tf_op jit(solution)/shard_map/ppermute | solution.py:38
  90.4 5.0 %collective-permute-start.22 = (f32[128,256]{1,0:T(8,128)S(1)}, f32[128,256]{1,0:T(8,128)S(1)}, u32[]{:S(2)}, u32[]{:S(2)}) collective-permute-start(f32[128,256]{1,0:T(8,128)S(1)} %shard_map.76.base), channel_id=1, source_target_pairs={{0,12},{1,13},{2,14},{3,15},{4,0},{5,1},{6,2},{7,3},{8,4},{9,5},{1... | collective-permute-start | bytes 393224 | tf_op jit(solution)/shard_map/ppermute | solution.py:38
  95.5 10.5 %collective-permute-start.23 = (f32[4,128,256]{2,1,0:T(8,128)S(1)}, f32[4,128,256]{2,1,0:T(8,128)S(1)}, u32[]{:S(2)}, u32[]{:S(2)}) collective-permute-start(f32[4,128,256]{2,1,0:T(8,128)S(1)} %pad_maximum_fusion.3.refs_0_), channel_id=1, source_target_pairs={{0,1},{1,2},{2,3},{3,0},{4,5},{5,6},{6,7},{7,4},{8,9},{9,10},{10,1... | collective-permute-start | bytes 1572872 | tf_op jit(solution)/shard_map/ppermute | solution.py:38
  97.5 14.9 %collective-permute-start.24 = (f32[4,128,256]{2,1,0:T(8,128)S(1)}, f32[4,128,256]{2,1,0:T(8,128)S(1)}, u32[]{:S(2)}, u32[]{:S(2)}) collective-permute-start(f32[4,128,256]{2,1,0:T(8,128)S(1)} %pad_maximum_fusion.3.refs_0_), channel_id=1, source_target_pairs={{0,2},{1,3},{2,0},{3,1},{4,6},{5,7},{6,4},{7,5},{8,10},{9,11},{10,... | collective-permute-start | bytes 1572872 | tf_op jit(solution)/shard_map/ppermute | solution.py:38
  99.6 12.8 %collective-permute-start.25 = (f32[4,128,256]{2,1,0:T(8,128)S(1)}, f32[4,128,256]{2,1,0:T(8,128)S(1)}, u32[]{:S(2)}, u32[]{:S(2)}) collective-permute-start(f32[4,128,256]{2,1,0:T(8,128)S(1)} %pad_maximum_fusion.3.refs_0_), channel_id=1, source_target_pairs={{0,3},{1,0},{2,1},{3,2},{4,7},{5,4},{6,5},{7,6},{8,11},{9,8},{10,9... | collective-permute-start | bytes 1572872 | tf_op jit(solution)/shard_map/ppermute | solution.py:38
  114.7 2.0 collective-permute-start.26
  116.7 6.8 %collective-permute-start.27 = (f32[128,256]{1,0:T(8,128)S(1)}, f32[128,256]{1,0:T(8,128)S(1)}, u32[]{:S(2)}, u32[]{:S(2)}) collective-permute-start(f32[128,256]{1,0:T(8,128)S(1)} %get-tuple-element.85), channel_id=1, source_target_pairs={{0,32},{16,48},{32,64},{48,80},{64,96},{80,112},{96,0},{112,16},{1... | collective-permute-start | bytes 393224 | tf_op jit(solution)/shard_map/ppermute | solution.py:43
  118.4 8.8 %collective-permute-start.28 = (f32[128,256]{1,0:T(8,128)S(1)}, f32[128,256]{1,0:T(8,128)S(1)}, u32[]{:S(2)}, u32[]{:S(2)}) collective-permute-start(f32[128,256]{1,0:T(8,128)S(1)} %get-tuple-element.86), channel_id=1, source_target_pairs={{0,64},{16,80},{32,96},{48,112},{64,0},{80,16},{96,32},{112,48},{1... | collective-permute-start | bytes 393224 | tf_op jit(solution)/shard_map/ppermute | solution.py:43
  120.9 6.3 %collective-permute-start.29 = (f32[128,256]{1,0:T(8,128)S(1)}, f32[128,256]{1,0:T(8,128)S(1)}, u32[]{:S(2)}, u32[]{:S(2)}) collective-permute-start(f32[128,256]{1,0:T(8,128)S(1)} %get-tuple-element.87), channel_id=1, source_target_pairs={{0,96},{16,112},{32,0},{48,16},{64,32},{80,48},{96,64},{112,80},{1... | collective-permute-start | bytes 393224 | tf_op jit(solution)/shard_map/ppermute | solution.py:43
  127.9 6.8 %collective-permute-start.30 = (f32[128,256]{1,0:T(8,128)S(1)}, f32[128,256]{1,0:T(8,128)S(1)}, u32[]{:S(2)}, u32[]{:S(2)}) collective-permute-start(f32[128,256]{1,0:T(8,128)S(1)} %get-tuple-element.89), channel_id=1, source_target_pairs={{0,32},{16,48},{32,64},{48,80},{64,96},{80,112},{96,0},{112,16},{1... | collective-permute-start | bytes 393224 | tf_op jit(solution)/shard_map/ppermute | solution.py:43
  129.3 8.4 %collective-permute-start.31 = (f32[128,256]{1,0:T(8,128)S(1)}, f32[128,256]{1,0:T(8,128)S(1)}, u32[]{:S(2)}, u32[]{:S(2)}) collective-permute-start(f32[128,256]{1,0:T(8,128)S(1)} %get-tuple-element.89), channel_id=1, source_target_pairs={{0,64},{16,80},{32,96},{48,112},{64,0},{80,16},{96,32},{112,48},{1... | collective-permute-start | bytes 393224 | tf_op jit(solution)/shard_map/ppermute | solution.py:43
  131.8 6.0 %collective-permute-start.32 = (f32[128,256]{1,0:T(8,128)S(1)}, f32[128,256]{1,0:T(8,128)S(1)}, u32[]{:S(2)}, u32[]{:S(2)}) collective-permute-start(f32[128,256]{1,0:T(8,128)S(1)} %get-tuple-element.89), channel_id=1, source_target_pairs={{0,96},{16,112},{32,0},{48,16},{64,32},{80,48},{96,64},{112,80},{1... | collective-permute-start | bytes 393224 | tf_op jit(solution)/shard_map/ppermute | solution.py:43
  137.8 2.0 collective-permute-start.33
  142.0 19.7 %collective-permute-start.34 = (f32[4,128,256]{2,1,0:T(8,128)S(1)}, f32[4,128,256]{2,1,0:T(8,128)S(1)}, u32[]{:S(2)}, u32[]{:S(2)}) collective-permute-start(f32[4,128,256]{2,1,0:T(8,128)S(1)} %get-tuple-element.91), channel_id=1, source_target_pairs={{0,8},{1,9},{2,10},{3,11},{4,12},{5,13},{6,14},{7,15},{8,0},{9,1},... | collective-permute-start | bytes 1572872 | tf_op jit(solution)/shard_map/ppermute | solution.py:38
  152.5 14.8 %collective-permute-start.35 = (f32[4,128,256]{2,1,0:T(8,128)S(1)}, f32[4,128,256]{2,1,0:T(8,128)S(1)}, u32[]{:S(2)}, u32[]{:S(2)}) collective-permute-start(f32[4,128,256]{2,1,0:T(8,128)S(1)} %get-tuple-element.92), channel_id=1, source_target_pairs={{0,4},{1,5},{2,6},{3,7},{4,8},{5,9},{6,10},{7,11},{8,12},{9,13},{1... | collective-permute-start | bytes 1572872 | tf_op jit(solution)/shard_map/ppermute | solution.py:38
  154.2 13.1 %collective-permute-start.36 = (f32[4,128,256]{2,1,0:T(8,128)S(1)}, f32[4,128,256]{2,1,0:T(8,128)S(1)}, u32[]{:S(2)}, u32[]{:S(2)}) collective-permute-start(f32[4,128,256]{2,1,0:T(8,128)S(1)} %get-tuple-element.93), channel_id=1, source_target_pairs={{0,12},{1,13},{2,14},{3,15},{4,0},{5,1},{6,2},{7,3},{8,4},{9,5},{1... | collective-permute-start | bytes 1572872 | tf_op jit(solution)/shard_map/ppermute | solution.py:38
  167.4 6.2 %collective-permute-start.37 = (f32[128,256]{1,0:T(8,128)S(1)}, f32[128,256]{1,0:T(8,128)S(1)}, u32[]{:S(2)}, u32[]{:S(2)}) collective-permute-start(f32[128,256]{1,0:T(8,128)S(1)} %get-tuple-element.97), channel_id=1, source_target_pairs={{0,1},{1,2},{2,3},{3,0},{4,5},{5,6},{6,7},{7,4},{8,9},{9,10},{10,1... | collective-permute-start | bytes 393224 | tf_op jit(solution)/shard_map/ppermute | solution.py:38
  169.4 6.5 %collective-permute-start.38 = (f32[128,256]{1,0:T(8,128)S(1)}, f32[128,256]{1,0:T(8,128)S(1)}, u32[]{:S(2)}, u32[]{:S(2)}) collective-permute-start(f32[128,256]{1,0:T(8,128)S(1)} %get-tuple-element.98), channel_id=1, source_target_pairs={{0,2},{1,3},{2,0},{3,1},{4,6},{5,7},{6,4},{7,5},{8,10},{9,11},{10,... | collective-permute-start | bytes 393224 | tf_op jit(solution)/shard_map/ppermute | solution.py:38
  171.6 5.0 %collective-permute-start.39 = (f32[128,256]{1,0:T(8,128)S(1)}, f32[128,256]{1,0:T(8,128)S(1)}, u32[]{:S(2)}, u32[]{:S(2)}) collective-permute-start(f32[128,256]{1,0:T(8,128)S(1)} %get-tuple-element.99), channel_id=1, source_target_pairs={{0,3},{1,0},{2,1},{3,2},{4,7},{5,4},{6,5},{7,6},{8,11},{9,8},{10,9... | collective-permute-start | bytes 393224 | tf_op jit(solution)/shard_map/ppermute | solution.py:38
  176.9 6.2 %collective-permute-start.40 = (f32[128,256]{1,0:T(8,128)S(1)}, f32[128,256]{1,0:T(8,128)S(1)}, u32[]{:S(2)}, u32[]{:S(2)}) collective-permute-start(f32[128,256]{1,0:T(8,128)S(1)} %shard_map.86), channel_id=1, source_target_pairs={{0,32},{16,48},{32,64},{48,80},{64,96},{80,112},{96,0},{112,16},{1... | collective-permute-start | bytes 393224 | tf_op jit(solution)/shard_map/ppermute | solution.py:43
  178.2 6.7 %collective-permute-start.41 = (f32[128,256]{1,0:T(8,128)S(1)}, f32[128,256]{1,0:T(8,128)S(1)}, u32[]{:S(2)}, u32[]{:S(2)}) collective-permute-start(f32[128,256]{1,0:T(8,128)S(1)} %shard_map.86), channel_id=1, source_target_pairs={{0,64},{16,80},{32,96},{48,112},{64,0},{80,16},{96,32},{112,48},{1... | collective-permute-start | bytes 393224 | tf_op jit(solution)/shard_map/ppermute | solution.py:43
  180.6 5.0 %collective-permute-start.42 = (f32[128,256]{1,0:T(8,128)S(1)}, f32[128,256]{1,0:T(8,128)S(1)}, u32[]{:S(2)}, u32[]{:S(2)}) collective-permute-start(f32[128,256]{1,0:T(8,128)S(1)} %shard_map.86), channel_id=1, source_target_pairs={{0,96},{16,112},{32,0},{48,16},{64,32},{80,48},{96,64},{112,80},{1... | collective-permute-start | bytes 393224 | tf_op jit(solution)/shard_map/ppermute | solution.py:43
  185.6 2.0 collective-permute-start.43
  189.8 10.9 %collective-permute-start.44 = (f32[4,128,256]{2,1,0:T(8,128)S(1)}, f32[4,128,256]{2,1,0:T(8,128)S(1)}, u32[]{:S(2)}, u32[]{:S(2)}) collective-permute-start(f32[4,128,256]{2,1,0:T(8,128)S(1)} %get-tuple-element.104), channel_id=1, source_target_pairs={{0,8},{1,9},{2,10},{3,11},{4,12},{5,13},{6,14},{7,15},{8,0},{9,1},... | collective-permute-start | bytes 1572872 | tf_op jit(solution)/shard_map/ppermute | solution.py:38
  191.4 14.8 %collective-permute-start.45 = (f32[4,128,256]{2,1,0:T(8,128)S(1)}, f32[4,128,256]{2,1,0:T(8,128)S(1)}, u32[]{:S(2)}, u32[]{:S(2)}) collective-permute-start(f32[4,128,256]{2,1,0:T(8,128)S(1)} %get-tuple-element.105), channel_id=1, source_target_pairs={{0,4},{1,5},{2,6},{3,7},{4,8},{5,9},{6,10},{7,11},{8,12},{9,13},{1... | collective-permute-start | bytes 1572872 | tf_op jit(solution)/shard_map/ppermute | solution.py:38
  193.1 13.1 %collective-permute-start.46 = (f32[4,128,256]{2,1,0:T(8,128)S(1)}, f32[4,128,256]{2,1,0:T(8,128)S(1)}, u32[]{:S(2)}, u32[]{:S(2)}) collective-permute-start(f32[4,128,256]{2,1,0:T(8,128)S(1)} %get-tuple-element.106), channel_id=1, source_target_pairs={{0,12},{1,13},{2,14},{3,15},{4,0},{5,1},{6,2},{7,3},{8,4},{9,5},{1... | collective-permute-start | bytes 1572872 | tf_op jit(solution)/shard_map/ppermute | solution.py:38
  206.4 6.2 %collective-permute-start.47 = (f32[128,256]{1,0:T(8,128)S(1)}, f32[128,256]{1,0:T(8,128)S(1)}, u32[]{:S(2)}, u32[]{:S(2)}) collective-permute-start(f32[128,256]{1,0:T(8,128)S(1)} %get-tuple-element.112), channel_id=1, source_target_pairs={{0,1},{1,2},{2,3},{3,0},{4,5},{5,6},{6,7},{7,4},{8,9},{9,10},{10,1... | collective-permute-start | bytes 393224 | tf_op jit(solution)/shard_map/ppermute | solution.py:38
  207.9 7.0 %collective-permute-start.48 = (f32[128,256]{1,0:T(8,128)S(1)}, f32[128,256]{1,0:T(8,128)S(1)}, u32[]{:S(2)}, u32[]{:S(2)}) collective-permute-start(f32[128,256]{1,0:T(8,128)S(1)} %get-tuple-element.113), channel_id=1, source_target_pairs={{0,2},{1,3},{2,0},{3,1},{4,6},{5,7},{6,4},{7,5},{8,10},{9,11},{10,... | collective-permute-start | bytes 393224 | tf_op jit(solution)/shard_map/ppermute | solution.py:38
  210.5 5.2 %collective-permute-start.49 = (f32[128,256]{1,0:T(8,128)S(1)}, f32[128,256]{1,0:T(8,128)S(1)}, u32[]{:S(2)}, u32[]{:S(2)}) collective-permute-start(f32[128,256]{1,0:T(8,128)S(1)} %get-tuple-element.114), channel_id=1, source_target_pairs={{0,3},{1,0},{2,1},{3,2},{4,7},{5,4},{6,5},{7,6},{8,11},{9,8},{10,9... | collective-permute-start | bytes 393224 | tf_op jit(solution)/shard_map/ppermute | solution.py:38
  216.0 6.2 %collective-permute-start.50 = (f32[128,256]{1,0:T(8,128)S(1)}, f32[128,256]{1,0:T(8,128)S(1)}, u32[]{:S(2)}, u32[]{:S(2)}) collective-permute-start(f32[128,256]{1,0:T(8,128)S(1)} %shard_map.90), channel_id=1, source_target_pairs={{0,32},{16,48},{32,64},{48,80},{64,96},{80,112},{96,0},{112,16},{1... | collective-permute-start | bytes 393224 | tf_op jit(solution)/shard_map/ppermute | solution.py:43
  217.3 7.1 %collective-permute-start.51 = (f32[128,256]{1,0:T(8,128)S(1)}, f32[128,256]{1,0:T(8,128)S(1)}, u32[]{:S(2)}, u32[]{:S(2)}) collective-permute-start(f32[128,256]{1,0:T(8,128)S(1)} %shard_map.90), channel_id=1, source_target_pairs={{0,64},{16,80},{32,96},{48,112},{64,0},{80,16},{96,32},{112,48},{1... | collective-permute-start | bytes 393224 | tf_op jit(solution)/shard_map/ppermute | solution.py:43
  220.0 5.0 %collective-permute-start.52 = (f32[128,256]{1,0:T(8,128)S(1)}, f32[128,256]{1,0:T(8,128)S(1)}, u32[]{:S(2)}, u32[]{:S(2)}) collective-permute-start(f32[128,256]{1,0:T(8,128)S(1)} %shard_map.90), channel_id=1, source_target_pairs={{0,96},{16,112},{32,0},{48,16},{64,32},{80,48},{96,64},{112,80},{1... | collective-permute-start | bytes 393224 | tf_op jit(solution)/shard_map/ppermute | solution.py:43
  225.0 2.0 collective-permute-start.53
  229.2 10.9 %collective-permute-start.54 = (f32[4,128,256]{2,1,0:T(8,128)S(1)}, f32[4,128,256]{2,1,0:T(8,128)S(1)}, u32[]{:S(2)}, u32[]{:S(2)}) collective-permute-start(f32[4,128,256]{2,1,0:T(8,128)S(1)} %get-tuple-element.119), channel_id=1, source_target_pairs={{0,8},{1,9},{2,10},{3,11},{4,12},{5,13},{6,14},{7,15},{8,0},{9,1},... | collective-permute-start | bytes 1572872 | tf_op jit(solution)/shard_map/ppermute | solution.py:38
  230.9 14.7 %collective-permute-start.55 = (f32[4,128,256]{2,1,0:T(8,128)S(1)}, f32[4,128,256]{2,1,0:T(8,128)S(1)}, u32[]{:S(2)}, u32[]{:S(2)}) collective-permute-start(f32[4,128,256]{2,1,0:T(8,128)S(1)} %get-tuple-element.120), channel_id=1, source_target_pairs={{0,4},{1,5},{2,6},{3,7},{4,8},{5,9},{6,10},{7,11},{8,12},{9,13},{1... | collective-permute-start | bytes 1572872 | tf_op jit(solution)/shard_map/ppermute | solution.py:38
  232.5 13.1 %collective-permute-start.56 = (f32[4,128,256]{2,1,0:T(8,128)S(1)}, f32[4,128,256]{2,1,0:T(8,128)S(1)}, u32[]{:S(2)}, u32[]{:S(2)}) collective-permute-start(f32[4,128,256]{2,1,0:T(8,128)S(1)} %get-tuple-element.121), channel_id=1, source_target_pairs={{0,12},{1,13},{2,14},{3,15},{4,0},{5,1},{6,2},{7,3},{8,4},{9,5},{1... | collective-permute-start | bytes 1572872 | tf_op jit(solution)/shard_map/ppermute | solution.py:38
  245.7 6.2 %collective-permute-start.57 = (f32[128,256]{1,0:T(8,128)S(1)}, f32[128,256]{1,0:T(8,128)S(1)}, u32[]{:S(2)}, u32[]{:S(2)}) collective-permute-start(f32[128,256]{1,0:T(8,128)S(1)} %get-tuple-element.123), channel_id=1, source_target_pairs={{0,1},{1,2},{2,3},{3,0},{4,5},{5,6},{6,7},{7,4},{8,9},{9,10},{10,1... | collective-permute-start | bytes 393224 | tf_op jit(solution)/shard_map/ppermute | solution.py:38
  246.7 7.0 %collective-permute-start.58 = (f32[128,256]{1,0:T(8,128)S(1)}, f32[128,256]{1,0:T(8,128)S(1)}, u32[]{:S(2)}, u32[]{:S(2)}) collective-permute-start(f32[128,256]{1,0:T(8,128)S(1)} %get-tuple-element.124), channel_id=1, source_target_pairs={{0,2},{1,3},{2,0},{3,1},{4,6},{5,7},{6,4},{7,5},{8,10},{9,11},{10,... | collective-permute-start | bytes 393224 | tf_op jit(solution)/shard_map/ppermute | solution.py:38
  249.3 5.0 %collective-permute-start.59 = (f32[128,256]{1,0:T(8,128)S(1)}, f32[128,256]{1,0:T(8,128)S(1)}, u32[]{:S(2)}, u32[]{:S(2)}) collective-permute-start(f32[128,256]{1,0:T(8,128)S(1)} %get-tuple-element.125), channel_id=1, source_target_pairs={{0,3},{1,0},{2,1},{3,2},{4,7},{5,4},{6,5},{7,6},{8,11},{9,8},{10,9... | collective-permute-start | bytes 393224 | tf_op jit(solution)/shard_map/ppermute | solution.py:38

commit v3 on v2

--- a/solution.py
+++ b/solution.py
@@ -12,6 +12,7 @@
 LEV = 4
 NZ, NC, NX, NY = 4, 2, 4, 4
 BOTH = ("prow", "pcol")
+UNROLL = 16
 PLAIN = (1, 2, 3)
 FAR_FIRST = (2, 1, 3)
 
@@ -82,28 +83,43 @@
     refs = refs[waits:]
     outs, halves, total = refs[:n_out], refs[n_out], refs[n_out + 1]
     per = vectors[0].shape[0]
-    for k in range(n_in * per):
-        high, low = split(vectors[k // per][k % per])
-        halves[k, :W] = high
-        halves[k, W:] = low
+    for k in range(n_in):
+
+        @pl.loop(0, per)
+        def _(unit, k=k):
+            high, low = split(vectors[k][unit])
+            halves[k * per + unit, :W] = high
+            halves[k * per + unit, W:] = low
+
     per = outs[0].shape[0]
     for k in range(n_out):
-        if has_init:
-            total[k * per : (k + 1) * per] = init[k][...]
-        else:
-            total[k * per : (k + 1) * per] = jnp.zeros((per, W, R), jnp.float32)
-    for slot in range(blocks.shape[1]):
-        block = jnp.where(live[slot] > 0, blocks[index, slot], 0.0)
-        if flip:
-            block = block.T
-        high, low = split(block)
-        left = jnp.concatenate(
-            [jnp.concatenate([high, high], axis=1), jnp.concatenate([low, low], axis=1)], axis=0
-        )
-        product = jnp.dot(left, halves[take[slot]], preferred_element_type=jnp.float32)
-        total[put[slot]] += product[:W] + product[W:]
+
+        @pl.loop(0, per)
+        def _(unit, k=k):
+            if has_init:
+                total[k * per + unit] = init[k][unit]
+            else:
+                total[k * per + unit] = jnp.zeros((W, R), jnp.float32)
+
+    @pl.loop(0, blocks.shape[1], step=UNROLL)
+    def _(start):
+        for j in range(UNROLL):
+            slot = start + j
+            block = jnp.where(live[slot] > 0, blocks[index, slot], 0.0)
+            if flip:
+                block = block.T
+            high, low = split(block)
+            left = jnp.concatenate(
+                [jnp.concatenate([high, high], axis=1), jnp.concatenate([low, low], axis=1)], axis=0
+            )
+            product = jnp.dot(left, halves[take[slot]], preferred_element_type=jnp.float32)
+            total[put[slot]] += product[:W] + product[W:]
+
     for k in range(n_out):
-        outs[k][...] = total[k * per : (k + 1) * per]
+
+        @pl.loop(0, per)
+        def _(unit, k=k):
+            outs[k][unit] = total[k * per + unit]
 
 
 def pair_product(index, flip, scalars, vectors, blocks, init, after, n_out, total):

time: 260 us -> 249 us (0.958); the launches traced: 256 us -> 249 us
  starting transfers between devices: 98.7 us -> 89.8 us
  Pallas kernels: 35.5 us -> 39.4 us
    ppermute x36, starting transfers between devices: 67.7 us -> 58.7 us  [shift_plane(): return lax.ppermute(value, BOTH, pairs)]
    pallas_call x24, Pallas kernels: 29.6 us -> 33.5 us  [fast_call(): pl.pallas_call(kernel, in_specs=[pl.BlockSpec(memory_space=pltpu.SMEM)] *...]
  transfers between devices with their start and end apart: 60 -> 60, of which waited for: 50 -> 49; matrix products, arithmetic and copies ran while one was open for 1% -> 1% of each run, Pallas kernels for 7% -> 8%
where the time goes in v3:
time: 249 us
  waiting for transfers between devices  114 us (46%)
  starting transfers between devices  89.8 us (36%)
  Pallas kernels  39.4 us (16%)
  other arithmetic  3.99 us (2%)
    ppermute x36, waiting for transfers between devices, shift_plane(): return lax.ppermute(value, BOTH, pairs)  73.2 us
    ppermute x36, starting transfers between devices, shift_plane(): return lax.ppermute(value, BOTH, pairs)  58.7 us
    pallas_call x24, Pallas kernels, fast_call(): pl.pallas_call(kernel, in_specs=[pl.BlockSpec(memory_space=pltpu.SMEM)] *...  33.5 us
    ppermute x18, starting transfers between devices, shift_z(): return lax.ppermute(value, 'prow', pairs)  30.4 us
    ppermute x18, waiting for transfers between devices, shift_z(): return lax.ppermute(value, 'prow', pairs)  29.7 us
    ppermute x6, waiting for transfers between devices, swap_core(): return lax.ppermute(value, 'prow', pairs)  11.4 us
  transfers between devices with their start and end apart: 60, of which 49 were waited for; matrix products, arithmetic and copies ran while one was open for 1% of the time, Pallas kernels for 8%

profile of v3, /device:TPU:0, one launch (start us, length us, event | category | flops | bytes accessed | tf_op | source)
XLA Modules:
  0.0 248.6 jit_solution(6032773031689596596)
XLA Ops:
  1.9 3.2 %collective-permute-start.1 = (f32[128,256]{1,0:T(8,128)S(1)}, f32[128,256]{1,0:T(8,128)S(1)}, u32[]{:S(2)}, u32[]{:S(2)}) collective-permute-start(f32[128,256]{1,0:T(8,128)S(1)} %shard_map.68.base), channel_id=1, source_target_pairs={{0,8},{1,9},{2,10},{3,11},{4,12},{5,13},{6,14},{7,15},{8,0},{9,1},... | collective-permute-start | bytes 393224 | tf_op jit(solution)/shard_map/ppermute | solution.py:39
  10.0 2.4 collective-permute-done
  14.1 2.9 %collective-permute-start.4 = (f32[4,128,256]{2,1,0:T(8,128)S(1)}, f32[4,128,256]{2,1,0:T(8,128)S(1)}, u32[]{:S(2)}, u32[]{:S(2)}) collective-permute-start(f32[4,128,256]{2,1,0:T(8,128)S(1)} %fusion.4.after.refs_0_), channel_id=1, source_target_pairs={{0,2},{1,3},{2,0},{3,1},{4,6},{5,7},{6,4},{7,5},{8,10},{9,11},{10,... | collective-permute-start | bytes 1572872 | tf_op jit(solution)/shard_map/ppermute | solution.py:39
  19.0 4.7 %shard_map.69.refs_4_.refs_2_ = f32[6,32,128,128]{3,2,1,0:T(8,128)S(1)} custom-call(f32[6,32,128,128]{3,2,1,0:T(8,128)} %bitcast.202, f32[4,128,256]{2,1,0:T(8,128)S(1)} %fusion.4.after.refs_0_), custom_call_target="tpu_custom_call" | custom-call | bytes 12582912 | tf_op jit(solution)/shard_map/pallas_call | solution.py:226
  23.8 5.9 %collective-permute-done.4.refs_2_ = f32[4,128,256]{2,1,0:T(8,128)S(1)} collective-permute-done((f32[4,128,256]{2,1,0:T(8,128)S(1)}, f32[4,128,256]{2,1,0:T(8,128)S(1)}, u32[]{:S(2)}, u32[]{:S(2)}) %collective-permute-start.4) | collective-permute-done | bytes 524320 | tf_op jit(solution)/shard_map/ppermute | solution.py:39
  29.7 2.5 %shard_map.70 = (f32[4,128,256]{2,1,0:T(8,128)S(1)}, f32[4,128,256]{2,1,0:T(8,128)S(1)}) custom-call(s32[32]{0:T(128)S(1)} %get-tuple-element.162.take, s32[32]{0:T(128)S(1)} %get-tuple-element.151.put, s32[32]{0:T(128)S(1)} %get-tuple-element.145.live, f32[4,128,256]{2,1,0:T(8,128)S(1)} %fusion.4.after.refs_0_, ...), custom_call_target="tpu_custom_call" | custom-call | flops 1073741824 | bytes 4096 | tf_op jit(solution)/shard_map/pallas_call | solution.py:67
  32.3 1.9 collective-permute-done.6.refs_1_
  34.3 2.0 collective-permute-start.7
  36.3 3.6 %collective-permute-start.8 = (f32[128,256]{1,0:T(8,128)S(1)}, f32[128,256]{1,0:T(8,128)S(1)}, u32[]{:S(2)}, u32[]{:S(2)}) collective-permute-start(f32[128,256]{1,0:T(8,128)S(1)} %get-tuple-element.68), channel_id=1, source_target_pairs={{0,64},{16,80},{32,96},{48,112},{64,0},{80,16},{96,32},{112,48},{1... | collective-permute-start | bytes 393224 | tf_op jit(solution)/shard_map/ppermute | solution.py:44
  42.2 4.0 %collective-permute-done.8.refs_2_ = f32[128,256]{1,0:T(8,128)S(1)} collective-permute-done((f32[128,256]{1,0:T(8,128)S(1)}, f32[128,256]{1,0:T(8,128)S(1)}, u32[]{:S(2)}, u32[]{:S(2)}) %collective-permute-start.8) | collective-permute-done | bytes 131104 | tf_op jit(solution)/shard_map/ppermute | solution.py:44
  46.6 1.7 collective-permute-start.11
  49.8 4.3 %collective-permute-done.10 = f32[128,256]{1,0:T(8,128)S(1)} collective-permute-done((f32[128,256]{1,0:T(8,128)S(1)}, f32[128,256]{1,0:T(8,128)S(1)}, u32[]{:S(2)}, u32[]{:S(2)}) %collective-permute-start.10) | collective-permute-done | bytes 131104 | tf_op jit(solution)/shard_map/ppermute | solution.py:39
  56.8 2.1 collective-permute-start.14
  58.9 1.7 collective-permute-start.15
  60.6 2.5 %shard_map.73 = (f32[4,128,256]{2,1,0:T(8,128)S(1)}, f32[4,128,256]{2,1,0:T(8,128)S(1)}) custom-call(s32[32]{0:T(128)S(1)} %get-tuple-element.164.take, s32[32]{0:T(128)S(1)} %get-tuple-element.149.put, s32[32]{0:T(128)S(1)} %get-tuple-element.143.live, f32[4,128,256]{2,1,0:T(8,128)S(1)} %fusion.4.after.refs_0_, ...), custom_call_target="tpu_custom_call" | custom-call | flops 1073741824 | bytes 4096 | tf_op jit(solution)/shard_map/pallas_call | solution.py:67
  63.1 2.4 collective-permute-done.13.refs_1_
  65.5 6.1 %collective-permute-done.14.refs_2_ = f32[4,128,256]{2,1,0:T(8,128)S(1)} collective-permute-done((f32[4,128,256]{2,1,0:T(8,128)S(1)}, f32[4,128,256]{2,1,0:T(8,128)S(1)}, u32[]{:S(2)}, u32[]{:S(2)}) %collective-permute-start.14) | collective-permute-done | bytes 524320 | tf_op jit(solution)/shard_map/ppermute | solution.py:39
  72.1 2.5 %shard_map.74 = (f32[4,128,256]{2,1,0:T(8,128)S(1)}, f32[4,128,256]{2,1,0:T(8,128)S(1)}) custom-call(s32[32]{0:T(128)S(1)} %get-tuple-element.163.take, s32[32]{0:T(128)S(1)} %get-tuple-element.150.put, s32[32]{0:T(128)S(1)} %get-tuple-element.144.live, f32[4,128,256]{2,1,0:T(8,128)S(1)} %pad_maximum_fusion.2.refs_0_, ...), custom_call_target="tpu_custom_call" | custom-call | flops 1073741824 | bytes 4096 | tf_op jit(solution)/shard_map/pallas_call | solution.py:67
  74.7 1.9 collective-permute-done.16.refs_1_
  77.9 2.4 collective-permute-start.18
  81.6 2.3 collective-permute-done.17.refs_1_
  83.9 2.8 %collective-permute-done.18.refs_2_ = f32[128,256]{1,0:T(8,128)S(1)} collective-permute-done((f32[128,256]{1,0:T(8,128)S(1)}, f32[128,256]{1,0:T(8,128)S(1)}, u32[]{:S(2)}, u32[]{:S(2)}) %collective-permute-start.18) | collective-permute-done | bytes 131104 | tf_op jit(solution)/shard_map/ppermute | solution.py:44
  87.8 3.2 %collective-permute-start.21 = (f32[128,256]{1,0:T(8,128)S(1)}, f32[128,256]{1,0:T(8,128)S(1)}, u32[]{:S(2)}, u32[]{:S(2)}) collective-permute-start(f32[128,256]{1,0:T(8,128)S(1)} %shard_map.76.base), channel_id=1, source_target_pairs={{0,8},{1,9},{2,10},{3,11},{4,12},{5,13},{6,14},{7,15},{8,0},{9,1},... | collective-permute-start | bytes 393224 | tf_op jit(solution)/shard_map/ppermute | solution.py:39
  91.0 2.4 collective-permute-done.20
  93.4 2.0 collective-permute-done.21
  96.0 2.0 collective-permute-start.23
  98.0 2.1 collective-permute-start.24
  101.5 2.5 %shard_map.77 = (f32[4,128,256]{2,1,0:T(8,128)S(1)}, f32[4,128,256]{2,1,0:T(8,128)S(1)}) custom-call(s32[32]{0:T(128)S(1)} %get-tuple-element.167.take, s32[32]{0:T(128)S(1)} %get-tuple-element.146.put, s32[32]{0:T(128)S(1)} %get-tuple-element.140.live, f32[4,128,256]{2,1,0:T(8,128)S(1)} %fusion.4.after.refs_0_, ...), custom_call_target="tpu_custom_call" | custom-call | flops 1073741824 | bytes 4096 | tf_op jit(solution)/shard_map/pallas_call | solution.py:67
  104.1 2.5 %shard_map.78 = (f32[4,128,256]{2,1,0:T(8,128)S(1)}, f32[4,128,256]{2,1,0:T(8,128)S(1)}) custom-call(s32[32]{0:T(128)S(1)} %get-tuple-element.166.take, s32[32]{0:T(128)S(1)} %get-tuple-element.147.put, s32[32]{0:T(128)S(1)} %get-tuple-element.141.live, f32[4,128,256]{2,1,0:T(8,128)S(1)} %pad_maximum_fusion.2.refs_0_, ...), custom_call_target="tpu_custom_call" | custom-call | flops 1073741824 | bytes 4096 | tf_op jit(solution)/shard_map/pallas_call | solution.py:67
  106.6 6.4 %collective-permute-done.24.refs_2_ = f32[4,128,256]{2,1,0:T(8,128)S(1)} collective-permute-done((f32[4,128,256]{2,1,0:T(8,128)S(1)}, f32[4,128,256]{2,1,0:T(8,128)S(1)}, u32[]{:S(2)}, u32[]{:S(2)}) %collective-permute-start.24) | collective-permute-done | bytes 524320 | tf_op jit(solution)/shard_map/ppermute | solution.py:39
  113.0 2.5 %shard_map.79 = (f32[4,128,256]{2,1,0:T(8,128)S(1)}, f32[4,128,256]{2,1,0:T(8,128)S(1)}) custom-call(s32[32]{0:T(128)S(1)} %get-tuple-element.165.take, s32[32]{0:T(128)S(1)} %get-tuple-element.148.put, s32[32]{0:T(128)S(1)} %get-tuple-element.142.live, f32[4,128,256]{2,1,0:T(8,128)S(1)} %pad_maximum_fusion.3.refs_0_, ...), custom_call_target="tpu_custom_call" | custom-call | flops 1073741824 | bytes 4096 | tf_op jit(solution)/shard_map/pallas_call | solution.py:67
  115.6 1.9 collective-permute-done.26.refs_1_
  119.2 2.5 %collective-permute-start.28 = (f32[128,256]{1,0:T(8,128)S(1)}, f32[128,256]{1,0:T(8,128)S(1)}, u32[]{:S(2)}, u32[]{:S(2)}) collective-permute-start(f32[128,256]{1,0:T(8,128)S(1)} %get-tuple-element.86), channel_id=1, source_target_pairs={{0,64},{16,80},{32,96},{48,112},{64,0},{80,16},{96,32},{112,48},{1... | collective-permute-start | bytes 393224 | tf_op jit(solution)/shard_map/ppermute | solution.py:44
  122.5 1.9 collective-permute-done.27.refs_1_
  124.4 3.7 %collective-permute-done.28.refs_2_ = f32[128,256]{1,0:T(8,128)S(1)} collective-permute-done((f32[128,256]{1,0:T(8,128)S(1)}, f32[128,256]{1,0:T(8,128)S(1)}, u32[]{:S(2)}, u32[]{:S(2)}) %collective-permute-start.28) | collective-permute-done | bytes 131104 | tf_op jit(solution)/shard_map/ppermute | solution.py:44
  130.1 2.5 %collective-permute-start.31 = (f32[128,256]{1,0:T(8,128)S(1)}, f32[128,256]{1,0:T(8,128)S(1)}, u32[]{:S(2)}, u32[]{:S(2)}) collective-permute-start(f32[128,256]{1,0:T(8,128)S(1)} %get-tuple-element.89), channel_id=1, source_target_pairs={{0,64},{16,80},{32,96},{48,112},{64,0},{80,16},{96,32},{112,48},{1... | collective-permute-start | bytes 393224 | tf_op jit(solution)/shard_map/ppermute | solution.py:44
  133.4 2.2 collective-permute-done.30
  135.6 2.9 %collective-permute-done.31 = f32[128,256]{1,0:T(8,128)S(1)} collective-permute-done((f32[128,256]{1,0:T(8,128)S(1)}, f32[128,256]{1,0:T(8,128)S(1)}, u32[]{:S(2)}, u32[]{:S(2)}) %collective-permute-start.31) | collective-permute-done | bytes 131104 | tf_op jit(solution)/shard_map/ppermute | solution.py:44
  138.7 1.9 collective-permute-done.33.refs_1_
  140.6 2.6 %shard_map.82 = (f32[4,128,256]{2,1,0:T(8,128)S(1)}, f32[4,128,256]{2,1,0:T(8,128)S(1)}, f32[4,128,256]{2,1,0:T(8,128)S(1)}, f32[4,128,256]{2,1,0:T(8,128)S(1)}) custom-call(s32[32]{0:T(128)S(1)} %get-tuple-element.169.take, s32[32]{0:T(128)S(1)} %get-tuple-element.132.put, s32[32]{0:T(128)S(1)} %get-tuple-element.142.live, ...), custom_call_target="tpu_custom_call" | custom-call | flops 1073741824 | bytes 4096 | tf_op jit(solution)/shard_map/pallas_call | solution.py:67
  144.8 1.7 collective-permute-start.35
  148.1 6.0 %collective-permute-done.34.refs_3_.refs_1_ = f32[4,128,256]{2,1,0:T(8,128)S(1)} collective-permute-done((f32[4,128,256]{2,1,0:T(8,128)S(1)}, f32[4,128,256]{2,1,0:T(8,128)S(1)}, u32[]{:S(2)}, u32[]{:S(2)}) %collective-permute-start.34) | collective-permute-done | bytes 524320 | tf_op jit(solution)/shard_map/ppermute | solution.py:39
  154.1 2.6 %shard_map.84 = (f32[4,128,256]{2,1,0:T(8,128)S(1)}, f32[4,128,256]{2,1,0:T(8,128)S(1)}, f32[4,128,256]{2,1,0:T(8,128)S(1)}, f32[4,128,256]{2,1,0:T(8,128)S(1)}) custom-call(s32[32]{0:T(128)S(1)} %get-tuple-element.171.take, s32[32]{0:T(128)S(1)} %get-tuple-element.130.put, s32[32]{0:T(128)S(1)} %get-tuple-element.140.live, ...), custom_call_target="tpu_custom_call" | custom-call | flops 1073741824 | bytes 4096 | tf_op jit(solution)/shard_map/pallas_call | solution.py:67
  156.7 2.6 %shard_map.83 = (f32[4,128,256]{2,1,0:T(8,128)S(1)}, f32[4,128,256]{2,1,0:T(8,128)S(1)}, f32[4,128,256]{2,1,0:T(8,128)S(1)}, f32[4,128,256]{2,1,0:T(8,128)S(1)}) custom-call(s32[32]{0:T(128)S(1)} %get-tuple-element.170.take, s32[32]{0:T(128)S(1)} %get-tuple-element.131.put, s32[32]{0:T(128)S(1)} %get-tuple-element.141.live, ...), custom_call_target="tpu_custom_call" | custom-call | flops 1073741824 | bytes 4096 | tf_op jit(solution)/shard_map/pallas_call | solution.py:67
  159.8 2.1 collective-permute-start.37
  161.8 2.1 collective-permute-start.38
  166.0 2.3 collective-permute-done.38.refs_2_
  170.6 2.4 collective-permute-start.41
  175.4 1.9 collective-permute-done.41
  178.3 1.9 collective-permute-done.43.refs_1_
  180.2 2.6 %shard_map.87 = (f32[4,128,256]{2,1,0:T(8,128)S(1)}, f32[4,128,256]{2,1,0:T(8,128)S(1)}, f32[4,128,256]{2,1,0:T(8,128)S(1)}, f32[4,128,256]{2,1,0:T(8,128)S(1)}) custom-call(s32[32]{0:T(128)S(1)} %get-tuple-element.168.take, s32[32]{0:T(128)S(1)} %get-tuple-element.133.put, s32[32]{0:T(128)S(1)} %get-tuple-element.144.live, ...), custom_call_target="tpu_custom_call" | custom-call | flops 1073741824 | bytes 4096 | tf_op jit(solution)/shard_map/pallas_call | solution.py:67
  184.4 1.7 collective-permute-start.45
  187.6 6.0 %collective-permute-done.44.refs_7_.refs_1_ = f32[4,128,256]{2,1,0:T(8,128)S(1)} collective-permute-done((f32[4,128,256]{2,1,0:T(8,128)S(1)}, f32[4,128,256]{2,1,0:T(8,128)S(1)}, u32[]{:S(2)}, u32[]{:S(2)}) %collective-permute-start.44) | collective-permute-done | bytes 524320 | tf_op jit(solution)/shard_map/ppermute | solution.py:39
  193.7 2.6 %shard_map.88 = (f32[4,128,256]{2,1,0:T(8,128)S(1)}, f32[4,128,256]{2,1,0:T(8,128)S(1)}, f32[4,128,256]{2,1,0:T(8,128)S(1)}, f32[4,128,256]{2,1,0:T(8,128)S(1)}) custom-call(s32[32]{0:T(128)S(1)} %get-tuple-element.172.take, s32[32]{0:T(128)S(1)} %get-tuple-element.129.put, s32[32]{0:T(128)S(1)} %get-tuple-element.143.live, ...), custom_call_target="tpu_custom_call" | custom-call | flops 1073741824 | bytes 4096 | tf_op jit(solution)/shard_map/pallas_call | solution.py:67
  196.3 2.9 %collective-permute-done.45.refs_2_ = f32[4,128,256]{2,1,0:T(8,128)S(1)} collective-permute-done((f32[4,128,256]{2,1,0:T(8,128)S(1)}, f32[4,128,256]{2,1,0:T(8,128)S(1)}, u32[]{:S(2)}, u32[]{:S(2)}) %collective-permute-start.45) | collective-permute-done | bytes 524320 | tf_op jit(solution)/shard_map/ppermute | solution.py:39
  200.8 2.6 %collective-permute-start.48 = (f32[128,256]{1,0:T(8,128)S(1)}, f32[128,256]{1,0:T(8,128)S(1)}, u32[]{:S(2)}, u32[]{:S(2)}) collective-permute-start(f32[128,256]{1,0:T(8,128)S(1)} %get-tuple-element.113), channel_id=1, source_target_pairs={{0,2},{1,3},{2,0},{3,1},{4,6},{5,7},{6,4},{7,5},{8,10},{9,11},{10,... | collective-permute-start | bytes 393224 | tf_op jit(solution)/shard_map/ppermute | solution.py:39
  205.6 2.2 collective-permute-done.48.refs_2_
  210.1 2.7 %collective-permute-start.51 = (f32[128,256]{1,0:T(8,128)S(1)}, f32[128,256]{1,0:T(8,128)S(1)}, u32[]{:S(2)}, u32[]{:S(2)}) collective-permute-start(f32[128,256]{1,0:T(8,128)S(1)} %shard_map.90), channel_id=1, source_target_pairs={{0,64},{16,80},{32,96},{48,112},{64,0},{80,16},{96,32},{112,48},{1... | collective-permute-start | bytes 393224 | tf_op jit(solution)/shard_map/ppermute | solution.py:44
  215.0 2.1 collective-permute-done.51
  217.9 1.9 collective-permute-done.53.refs_1_
  219.8 2.6 %shard_map.91 = (f32[4,128,256]{2,1,0:T(8,128)S(1)}, f32[4,128,256]{2,1,0:T(8,128)S(1)}, f32[4,128,256]{2,1,0:T(8,128)S(1)}, f32[4,128,256]{2,1,0:T(8,128)S(1)}) custom-call(s32[32]{0:T(128)S(1)} %get-tuple-element.173.take, s32[32]{0:T(128)S(1)} %get-tuple-element.128.put, s32[32]{0:T(128)S(1)} %get-tuple-element.145.live, ...), custom_call_target="tpu_custom_call" | custom-call | flops 1073741824 | bytes 4096 | tf_op jit(solution)/shard_map/pallas_call | solution.py:67
  227.2 6.1 %collective-permute-done.54.refs_1_ = f32[4,128,256]{2,1,0:T(8,128)S(1)} collective-permute-done((f32[4,128,256]{2,1,0:T(8,128)S(1)}, f32[4,128,256]{2,1,0:T(8,128)S(1)}, u32[]{:S(2)}, u32[]{:S(2)}) %collective-permute-start.54) | collective-permute-done | bytes 524320 | tf_op jit(solution)/shard_map/ppermute | solution.py:39
  233.3 5.5 %collective-permute-done.55.refs_2_ = f32[4,128,256]{2,1,0:T(8,128)S(1)} collective-permute-done((f32[4,128,256]{2,1,0:T(8,128)S(1)}, f32[4,128,256]{2,1,0:T(8,128)S(1)}, u32[]{:S(2)}, u32[]{:S(2)}) %collective-permute-start.55) | collective-permute-done | bytes 524320 | tf_op jit(solution)/shard_map/ppermute | solution.py:39
  240.0 2.5 collective-permute-start.58
  (100 shorter events, 64.4 us)
Async XLA Ops:
  1.9 6.6 %collective-permute-start.1 = (f32[128,256]{1,0:T(8,128)S(1)}, f32[128,256]{1,0:T(8,128)S(1)}, u32[]{:S(2)}, u32[]{:S(2)}) collective-permute-start(f32[128,256]{1,0:T(8,128)S(1)} %shard_map.68.base), channel_id=1, source_target_pairs={{0,8},{1,9},{2,10},{3,11},{4,12},{5,13},{6,14},{7,15},{8,0},{9,1},... | collective-permute-start | bytes 393224 | tf_op jit(solution)/shard_map/ppermute | solution.py:39
  5.0 5.0 %collective-permute-start.2 = (f32[128,256]{1,0:T(8,128)S(1)}, f32[128,256]{1,0:T(8,128)S(1)}, u32[]{:S(2)}, u32[]{:S(2)}) collective-permute-start(f32[128,256]{1,0:T(8,128)S(1)} %shard_map.68.base), channel_id=1, source_target_pairs={{0,12},{1,13},{2,14},{3,15},{4,0},{5,1},{6,2},{7,3},{8,4},{9,5},{1... | collective-permute-start | bytes 393224 | tf_op jit(solution)/shard_map/ppermute | solution.py:39
  6.2 6.2 %collective-permute-start = (f32[128,256]{1,0:T(8,128)S(1)}, f32[128,256]{1,0:T(8,128)S(1)}, u32[]{:S(2)}, u32[]{:S(2)}) collective-permute-start(f32[128,256]{1,0:T(8,128)S(1)} %shard_map.68.base), channel_id=1, source_target_pairs={{0,4},{1,5},{2,6},{3,7},{4,8},{5,9},{6,10},{7,11},{8,12},{9,13},{1... | collective-permute-start | bytes 393224 | tf_op jit(solution)/shard_map/ppermute | solution.py:39
  12.4 11.4 %collective-permute-start.3 = (f32[4,128,256]{2,1,0:T(8,128)S(1)}, f32[4,128,256]{2,1,0:T(8,128)S(1)}, u32[]{:S(2)}, u32[]{:S(2)}) collective-permute-start(f32[4,128,256]{2,1,0:T(8,128)S(1)} %fusion.4.after.refs_0_), channel_id=1, source_target_pairs={{0,1},{1,2},{2,3},{3,0},{4,5},{5,6},{6,7},{7,4},{8,9},{9,10},{10,1... | collective-permute-start | bytes 1572872 | tf_op jit(solution)/shard_map/ppermute | solution.py:39
  14.1 15.7 %collective-permute-start.4 = (f32[4,128,256]{2,1,0:T(8,128)S(1)}, f32[4,128,256]{2,1,0:T(8,128)S(1)}, u32[]{:S(2)}, u32[]{:S(2)}) collective-permute-start(f32[4,128,256]{2,1,0:T(8,128)S(1)} %fusion.4.after.refs_0_), channel_id=1, source_target_pairs={{0,2},{1,3},{2,0},{3,1},{4,6},{5,7},{6,4},{7,5},{8,10},{9,11},{10,... | collective-permute-start | bytes 1572872 | tf_op jit(solution)/shard_map/ppermute | solution.py:39
  17.0 12.8 %collective-permute-start.5 = (f32[4,128,256]{2,1,0:T(8,128)S(1)}, f32[4,128,256]{2,1,0:T(8,128)S(1)}, u32[]{:S(2)}, u32[]{:S(2)}) collective-permute-start(f32[4,128,256]{2,1,0:T(8,128)S(1)} %fusion.4.after.refs_0_), channel_id=1, source_target_pairs={{0,3},{1,0},{2,1},{3,2},{4,7},{5,4},{6,5},{7,6},{8,11},{9,8},{10,9... | collective-permute-start | bytes 1572872 | tf_op jit(solution)/shard_map/ppermute | solution.py:39
  23.8 22.4 %copy-start = (f32[4,1,1,128,128]{4,3,2,1,0:T(8,128)S(1)}, f32[4,1,1,128,128]{4,3,2,1,0:T(8,128)}, u32[]{:S(2)}) copy-start(f32[4,1,1,128,128]{4,3,2,1,0:T(8,128)} %param.6) | copy-start | bytes 786436
  23.8 22.4 %copy-start.1 = (f32[4,1,1,128,256]{4,3,2,1,0:T(8,128)S(1)}, f32[4,1,1,128,256]{4,3,2,1,0:T(8,128)}, u32[]{:S(2)}) copy-start(f32[4,1,1,128,256]{4,3,2,1,0:T(8,128)} %param.5) | copy-start | bytes 1572868
  32.2 2.0 collective-permute-start.6
  34.3 7.9 %collective-permute-start.7 = (f32[128,256]{1,0:T(8,128)S(1)}, f32[128,256]{1,0:T(8,128)S(1)}, u32[]{:S(2)}, u32[]{:S(2)}) collective-permute-start(f32[128,256]{1,0:T(8,128)S(1)} %get-tuple-element.67), channel_id=1, source_target_pairs={{0,32},{16,48},{32,64},{48,80},{64,96},{80,112},{96,0},{112,16},{1... | collective-permute-start | bytes 393224 | tf_op jit(solution)/shard_map/ppermute | solution.py:44
  36.3 9.9 %collective-permute-start.8 = (f32[128,256]{1,0:T(8,128)S(1)}, f32[128,256]{1,0:T(8,128)S(1)}, u32[]{:S(2)}, u32[]{:S(2)}) collective-permute-start(f32[128,256]{1,0:T(8,128)S(1)} %get-tuple-element.68), channel_id=1, source_target_pairs={{0,64},{16,80},{32,96},{48,112},{64,0},{80,16},{96,32},{112,48},{1... | collective-permute-start | bytes 393224 | tf_op jit(solution)/shard_map/ppermute | solution.py:44
  39.9 6.3 %collective-permute-start.9 = (f32[128,256]{1,0:T(8,128)S(1)}, f32[128,256]{1,0:T(8,128)S(1)}, u32[]{:S(2)}, u32[]{:S(2)}) collective-permute-start(f32[128,256]{1,0:T(8,128)S(1)} %get-tuple-element.69), channel_id=1, source_target_pairs={{0,96},{16,112},{32,0},{48,16},{64,32},{80,48},{96,64},{112,80},{1... | collective-permute-start | bytes 393224 | tf_op jit(solution)/shard_map/ppermute | solution.py:44
  46.5 7.7 %collective-permute-start.10 = (f32[128,256]{1,0:T(8,128)S(1)}, f32[128,256]{1,0:T(8,128)S(1)}, u32[]{:S(2)}, u32[]{:S(2)}) collective-permute-start(f32[128,256]{1,0:T(8,128)S(1)} %shard_map.72.base), channel_id=1, source_target_pairs={{0,4},{1,5},{2,6},{3,7},{4,8},{5,9},{6,10},{7,11},{8,12},{9,13},{1... | collective-permute-start | bytes 393224 | tf_op jit(solution)/shard_map/ppermute | solution.py:39
  46.6 7.6 %collective-permute-start.11 = (f32[128,256]{1,0:T(8,128)S(1)}, f32[128,256]{1,0:T(8,128)S(1)}, u32[]{:S(2)}, u32[]{:S(2)}) collective-permute-start(f32[128,256]{1,0:T(8,128)S(1)} %shard_map.72.base), channel_id=1, source_target_pairs={{0,8},{1,9},{2,10},{3,11},{4,12},{5,13},{6,14},{7,15},{8,0},{9,1},... | collective-permute-start | bytes 393224 | tf_op jit(solution)/shard_map/ppermute | solution.py:39
  48.3 6.7 %collective-permute-start.12 = (f32[128,256]{1,0:T(8,128)S(1)}, f32[128,256]{1,0:T(8,128)S(1)}, u32[]{:S(2)}, u32[]{:S(2)}) collective-permute-start(f32[128,256]{1,0:T(8,128)S(1)} %shard_map.72.base), channel_id=1, source_target_pairs={{0,12},{1,13},{2,14},{3,15},{4,0},{5,1},{6,2},{7,3},{8,4},{9,5},{1... | collective-permute-start | bytes 393224 | tf_op jit(solution)/shard_map/ppermute | solution.py:39
  55.1 10.5 %collective-permute-start.13 = (f32[4,128,256]{2,1,0:T(8,128)S(1)}, f32[4,128,256]{2,1,0:T(8,128)S(1)}, u32[]{:S(2)}, u32[]{:S(2)}) collective-permute-start(f32[4,128,256]{2,1,0:T(8,128)S(1)} %pad_maximum_fusion.2.refs_0_), channel_id=1, source_target_pairs={{0,1},{1,2},{2,3},{3,0},{4,5},{5,6},{6,7},{7,4},{8,9},{9,10},{10,1... | collective-permute-start | bytes 1572872 | tf_op jit(solution)/shard_map/ppermute | solution.py:39
  56.8 14.9 %collective-permute-start.14 = (f32[4,128,256]{2,1,0:T(8,128)S(1)}, f32[4,128,256]{2,1,0:T(8,128)S(1)}, u32[]{:S(2)}, u32[]{:S(2)}) collective-permute-start(f32[4,128,256]{2,1,0:T(8,128)S(1)} %pad_maximum_fusion.2.refs_0_), channel_id=1, source_target_pairs={{0,2},{1,3},{2,0},{3,1},{4,6},{5,7},{6,4},{7,5},{8,10},{9,11},{10,... | collective-permute-start | bytes 1572872 | tf_op jit(solution)/shard_map/ppermute | solution.py:39
  58.9 13.2 %collective-permute-start.15 = (f32[4,128,256]{2,1,0:T(8,128)S(1)}, f32[4,128,256]{2,1,0:T(8,128)S(1)}, u32[]{:S(2)}, u32[]{:S(2)}) collective-permute-start(f32[4,128,256]{2,1,0:T(8,128)S(1)} %pad_maximum_fusion.2.refs_0_), channel_id=1, source_target_pairs={{0,3},{1,0},{2,1},{3,2},{4,7},{5,4},{6,5},{7,6},{8,11},{9,8},{10,9... | collective-permute-start | bytes 1572872 | tf_op jit(solution)/shard_map/ppermute | solution.py:39
  74.6 2.0 collective-permute-start.16
  76.6 7.2 %collective-permute-start.17 = (f32[128,256]{1,0:T(8,128)S(1)}, f32[128,256]{1,0:T(8,128)S(1)}, u32[]{:S(2)}, u32[]{:S(2)}) collective-permute-start(f32[128,256]{1,0:T(8,128)S(1)} %get-tuple-element.75), channel_id=1, source_target_pairs={{0,32},{16,48},{32,64},{48,80},{64,96},{80,112},{96,0},{112,16},{1... | collective-permute-start | bytes 393224 | tf_op jit(solution)/shard_map/ppermute | solution.py:44
  77.9 8.7 %collective-permute-start.18 = (f32[128,256]{1,0:T(8,128)S(1)}, f32[128,256]{1,0:T(8,128)S(1)}, u32[]{:S(2)}, u32[]{:S(2)}) collective-permute-start(f32[128,256]{1,0:T(8,128)S(1)} %get-tuple-element.76), channel_id=1, source_target_pairs={{0,64},{16,80},{32,96},{48,112},{64,0},{80,16},{96,32},{112,48},{1... | collective-permute-start | bytes 393224 | tf_op jit(solution)/shard_map/ppermute | solution.py:44
  80.3 6.5 %collective-permute-start.19 = (f32[128,256]{1,0:T(8,128)S(1)}, f32[128,256]{1,0:T(8,128)S(1)}, u32[]{:S(2)}, u32[]{:S(2)}) collective-permute-start(f32[128,256]{1,0:T(8,128)S(1)} %get-tuple-element.77), channel_id=1, source_target_pairs={{0,96},{16,112},{32,0},{48,16},{64,32},{80,48},{96,64},{112,80},{1... | collective-permute-start | bytes 393224 | tf_op jit(solution)/shard_map/ppermute | solution.py:44
  87.1 6.2 %collective-permute-start.20 = (f32[128,256]{1,0:T(8,128)S(1)}, f32[128,256]{1,0:T(8,128)S(1)}, u32[]{:S(2)}, u32[]{:S(2)}) collective-permute-start(f32[128,256]{1,0:T(8,128)S(1)} %shard_map.76.base), channel_id=1, source_target_pairs={{0,4},{1,5},{2,6},{3,7},{4,8},{5,9},{6,10},{7,11},{8,12},{9,13},{1... | collective-permute-start | bytes 393224 | tf_op jit(solution)/shard_map/ppermute | solution.py:39
  87.8 7.6 %collective-permute-start.21 = (f32[128,256]{1,0:T(8,128)S(1)}, f32[128,256]{1,0:T(8,128)S(1)}, u32[]{:S(2)}, u32[]{:S(2)}) collective-permute-start(f32[128,256]{1,0:T(8,128)S(1)} %shard_map.76.base), channel_id=1, source_target_pairs={{0,8},{1,9},{2,10},{3,11},{4,12},{5,13},{6,14},{7,15},{8,0},{9,1},... | collective-permute-start | bytes 393224 | tf_op jit(solution)/shard_map/ppermute | solution.py:39
  91.0 5.0 %collective-permute-start.22 = (f32[128,256]{1,0:T(8,128)S(1)}, f32[128,256]{1,0:T(8,128)S(1)}, u32[]{:S(2)}, u32[]{:S(2)}) collective-permute-start(f32[128,256]{1,0:T(8,128)S(1)} %shard_map.76.base), channel_id=1, source_target_pairs={{0,12},{1,13},{2,14},{3,15},{4,0},{5,1},{6,2},{7,3},{8,4},{9,5},{1... | collective-permute-start | bytes 393224 | tf_op jit(solution)/shard_map/ppermute | solution.py:39
  96.0 10.6 %collective-permute-start.23 = (f32[4,128,256]{2,1,0:T(8,128)S(1)}, f32[4,128,256]{2,1,0:T(8,128)S(1)}, u32[]{:S(2)}, u32[]{:S(2)}) collective-permute-start(f32[4,128,256]{2,1,0:T(8,128)S(1)} %pad_maximum_fusion.3.refs_0_), channel_id=1, source_target_pairs={{0,1},{1,2},{2,3},{3,0},{4,5},{5,6},{6,7},{7,4},{8,9},{9,10},{10,1... | collective-permute-start | bytes 1572872 | tf_op jit(solution)/shard_map/ppermute | solution.py:39
  98.0 14.9 %collective-permute-start.24 = (f32[4,128,256]{2,1,0:T(8,128)S(1)}, f32[4,128,256]{2,1,0:T(8,128)S(1)}, u32[]{:S(2)}, u32[]{:S(2)}) collective-permute-start(f32[4,128,256]{2,1,0:T(8,128)S(1)} %pad_maximum_fusion.3.refs_0_), channel_id=1, source_target_pairs={{0,2},{1,3},{2,0},{3,1},{4,6},{5,7},{6,4},{7,5},{8,10},{9,11},{10,... | collective-permute-start | bytes 1572872 | tf_op jit(solution)/shard_map/ppermute | solution.py:39
  100.2 12.8 %collective-permute-start.25 = (f32[4,128,256]{2,1,0:T(8,128)S(1)}, f32[4,128,256]{2,1,0:T(8,128)S(1)}, u32[]{:S(2)}, u32[]{:S(2)}) collective-permute-start(f32[4,128,256]{2,1,0:T(8,128)S(1)} %pad_maximum_fusion.3.refs_0_), channel_id=1, source_target_pairs={{0,3},{1,0},{2,1},{3,2},{4,7},{5,4},{6,5},{7,6},{8,11},{9,8},{10,9... | collective-permute-start | bytes 1572872 | tf_op jit(solution)/shard_map/ppermute | solution.py:39
  115.5 2.0 collective-permute-start.26
  117.5 6.8 %collective-permute-start.27 = (f32[128,256]{1,0:T(8,128)S(1)}, f32[128,256]{1,0:T(8,128)S(1)}, u32[]{:S(2)}, u32[]{:S(2)}) collective-permute-start(f32[128,256]{1,0:T(8,128)S(1)} %get-tuple-element.85), channel_id=1, source_target_pairs={{0,32},{16,48},{32,64},{48,80},{64,96},{80,112},{96,0},{112,16},{1... | collective-permute-start | bytes 393224 | tf_op jit(solution)/shard_map/ppermute | solution.py:44
  119.2 8.8 %collective-permute-start.28 = (f32[128,256]{1,0:T(8,128)S(1)}, f32[128,256]{1,0:T(8,128)S(1)}, u32[]{:S(2)}, u32[]{:S(2)}) collective-permute-start(f32[128,256]{1,0:T(8,128)S(1)} %get-tuple-element.86), channel_id=1, source_target_pairs={{0,64},{16,80},{32,96},{48,112},{64,0},{80,16},{96,32},{112,48},{1... | collective-permute-start | bytes 393224 | tf_op jit(solution)/shard_map/ppermute | solution.py:44
  121.7 6.3 %collective-permute-start.29 = (f32[128,256]{1,0:T(8,128)S(1)}, f32[128,256]{1,0:T(8,128)S(1)}, u32[]{:S(2)}, u32[]{:S(2)}) collective-permute-start(f32[128,256]{1,0:T(8,128)S(1)} %get-tuple-element.87), channel_id=1, source_target_pairs={{0,96},{16,112},{32,0},{48,16},{64,32},{80,48},{96,64},{112,80},{1... | collective-permute-start | bytes 393224 | tf_op jit(solution)/shard_map/ppermute | solution.py:44
  128.8 6.8 %collective-permute-start.30 = (f32[128,256]{1,0:T(8,128)S(1)}, f32[128,256]{1,0:T(8,128)S(1)}, u32[]{:S(2)}, u32[]{:S(2)}) collective-permute-start(f32[128,256]{1,0:T(8,128)S(1)} %get-tuple-element.89), channel_id=1, source_target_pairs={{0,32},{16,48},{32,64},{48,80},{64,96},{80,112},{96,0},{112,16},{1... | collective-permute-start | bytes 393224 | tf_op jit(solution)/shard_map/ppermute | solution.py:44
  130.1 8.4 %collective-permute-start.31 = (f32[128,256]{1,0:T(8,128)S(1)}, f32[128,256]{1,0:T(8,128)S(1)}, u32[]{:S(2)}, u32[]{:S(2)}) collective-permute-start(f32[128,256]{1,0:T(8,128)S(1)} %get-tuple-element.89), channel_id=1, source_target_pairs={{0,64},{16,80},{32,96},{48,112},{64,0},{80,16},{96,32},{112,48},{1... | collective-permute-start | bytes 393224 | tf_op jit(solution)/shard_map/ppermute | solution.py:44
  132.6 5.9 %collective-permute-start.32 = (f32[128,256]{1,0:T(8,128)S(1)}, f32[128,256]{1,0:T(8,128)S(1)}, u32[]{:S(2)}, u32[]{:S(2)}) collective-permute-start(f32[128,256]{1,0:T(8,128)S(1)} %get-tuple-element.89), channel_id=1, source_target_pairs={{0,96},{16,112},{32,0},{48,16},{64,32},{80,48},{96,64},{112,80},{1... | collective-permute-start | bytes 393224 | tf_op jit(solution)/shard_map/ppermute | solution.py:44
  138.6 2.0 collective-permute-start.33
  143.2 10.9 %collective-permute-start.34 = (f32[4,128,256]{2,1,0:T(8,128)S(1)}, f32[4,128,256]{2,1,0:T(8,128)S(1)}, u32[]{:S(2)}, u32[]{:S(2)}) collective-permute-start(f32[4,128,256]{2,1,0:T(8,128)S(1)} %get-tuple-element.91), channel_id=1, source_target_pairs={{0,8},{1,9},{2,10},{3,11},{4,12},{5,13},{6,14},{7,15},{8,0},{9,1},... | collective-permute-start | bytes 1572872 | tf_op jit(solution)/shard_map/ppermute | solution.py:39
  144.8 14.8 %collective-permute-start.35 = (f32[4,128,256]{2,1,0:T(8,128)S(1)}, f32[4,128,256]{2,1,0:T(8,128)S(1)}, u32[]{:S(2)}, u32[]{:S(2)}) collective-permute-start(f32[4,128,256]{2,1,0:T(8,128)S(1)} %get-tuple-element.92), channel_id=1, source_target_pairs={{0,4},{1,5},{2,6},{3,7},{4,8},{5,9},{6,10},{7,11},{8,12},{9,13},{1... | collective-permute-start | bytes 1572872 | tf_op jit(solution)/shard_map/ppermute | solution.py:39
  146.5 13.1 %collective-permute-start.36 = (f32[4,128,256]{2,1,0:T(8,128)S(1)}, f32[4,128,256]{2,1,0:T(8,128)S(1)}, u32[]{:S(2)}, u32[]{:S(2)}) collective-permute-start(f32[4,128,256]{2,1,0:T(8,128)S(1)} %get-tuple-element.93), channel_id=1, source_target_pairs={{0,12},{1,13},{2,14},{3,15},{4,0},{5,1},{6,2},{7,3},{8,4},{9,5},{1... | collective-permute-start | bytes 1572872 | tf_op jit(solution)/shard_map/ppermute | solution.py:39
  159.8 6.2 %collective-permute-start.37 = (f32[128,256]{1,0:T(8,128)S(1)}, f32[128,256]{1,0:T(8,128)S(1)}, u32[]{:S(2)}, u32[]{:S(2)}) collective-permute-start(f32[128,256]{1,0:T(8,128)S(1)} %get-tuple-element.97), channel_id=1, source_target_pairs={{0,1},{1,2},{2,3},{3,0},{4,5},{5,6},{6,7},{7,4},{8,9},{9,10},{10,1... | collective-permute-start | bytes 393224 | tf_op jit(solution)/shard_map/ppermute | solution.py:39
  161.8 6.5 %collective-permute-start.38 = (f32[128,256]{1,0:T(8,128)S(1)}, f32[128,256]{1,0:T(8,128)S(1)}, u32[]{:S(2)}, u32[]{:S(2)}) collective-permute-start(f32[128,256]{1,0:T(8,128)S(1)} %get-tuple-element.98), channel_id=1, source_target_pairs={{0,2},{1,3},{2,0},{3,1},{4,6},{5,7},{6,4},{7,5},{8,10},{9,11},{10,... | collective-permute-start | bytes 393224 | tf_op jit(solution)/shard_map/ppermute | solution.py:39
  163.9 5.0 %collective-permute-start.39 = (f32[128,256]{1,0:T(8,128)S(1)}, f32[128,256]{1,0:T(8,128)S(1)}, u32[]{:S(2)}, u32[]{:S(2)}) collective-permute-start(f32[128,256]{1,0:T(8,128)S(1)} %get-tuple-element.99), channel_id=1, source_target_pairs={{0,3},{1,0},{2,1},{3,2},{4,7},{5,4},{6,5},{7,6},{8,11},{9,8},{10,9... | collective-permute-start | bytes 393224 | tf_op jit(solution)/shard_map/ppermute | solution.py:39
  169.2 6.2 %collective-permute-start.40 = (f32[128,256]{1,0:T(8,128)S(1)}, f32[128,256]{1,0:T(8,128)S(1)}, u32[]{:S(2)}, u32[]{:S(2)}) collective-permute-start(f32[128,256]{1,0:T(8,128)S(1)} %shard_map.86), channel_id=1, source_target_pairs={{0,32},{16,48},{32,64},{48,80},{64,96},{80,112},{96,0},{112,16},{1... | collective-permute-start | bytes 393224 | tf_op jit(solution)/shard_map/ppermute | solution.py:44
  170.6 6.7 %collective-permute-start.41 = (f32[128,256]{1,0:T(8,128)S(1)}, f32[128,256]{1,0:T(8,128)S(1)}, u32[]{:S(2)}, u32[]{:S(2)}) collective-permute-start(f32[128,256]{1,0:T(8,128)S(1)} %shard_map.86), channel_id=1, source_target_pairs={{0,64},{16,80},{32,96},{48,112},{64,0},{80,16},{96,32},{112,48},{1... | collective-permute-start | bytes 393224 | tf_op jit(solution)/shard_map/ppermute | solution.py:44
  173.0 5.0 %collective-permute-start.42 = (f32[128,256]{1,0:T(8,128)S(1)}, f32[128,256]{1,0:T(8,128)S(1)}, u32[]{:S(2)}, u32[]{:S(2)}) collective-permute-start(f32[128,256]{1,0:T(8,128)S(1)} %shard_map.86), channel_id=1, source_target_pairs={{0,96},{16,112},{32,0},{48,16},{64,32},{80,48},{96,64},{112,80},{1... | collective-permute-start | bytes 393224 | tf_op jit(solution)/shard_map/ppermute | solution.py:44
  178.0 2.2 collective-permute-start.43
  182.8 10.9 %collective-permute-start.44 = (f32[4,128,256]{2,1,0:T(8,128)S(1)}, f32[4,128,256]{2,1,0:T(8,128)S(1)}, u32[]{:S(2)}, u32[]{:S(2)}) collective-permute-start(f32[4,128,256]{2,1,0:T(8,128)S(1)} %get-tuple-element.104), channel_id=1, source_target_pairs={{0,8},{1,9},{2,10},{3,11},{4,12},{5,13},{6,14},{7,15},{8,0},{9,1},... | collective-permute-start | bytes 1572872 | tf_op jit(solution)/shard_map/ppermute | solution.py:39
  184.4 14.8 %collective-permute-start.45 = (f32[4,128,256]{2,1,0:T(8,128)S(1)}, f32[4,128,256]{2,1,0:T(8,128)S(1)}, u32[]{:S(2)}, u32[]{:S(2)}) collective-permute-start(f32[4,128,256]{2,1,0:T(8,128)S(1)} %get-tuple-element.105), channel_id=1, source_target_pairs={{0,4},{1,5},{2,6},{3,7},{4,8},{5,9},{6,10},{7,11},{8,12},{9,13},{1... | collective-permute-start | bytes 1572872 | tf_op jit(solution)/shard_map/ppermute | solution.py:39
  186.1 13.1 %collective-permute-start.46 = (f32[4,128,256]{2,1,0:T(8,128)S(1)}, f32[4,128,256]{2,1,0:T(8,128)S(1)}, u32[]{:S(2)}, u32[]{:S(2)}) collective-permute-start(f32[4,128,256]{2,1,0:T(8,128)S(1)} %get-tuple-element.106), channel_id=1, source_target_pairs={{0,12},{1,13},{2,14},{3,15},{4,0},{5,1},{6,2},{7,3},{8,4},{9,5},{1... | collective-permute-start | bytes 1572872 | tf_op jit(solution)/shard_map/ppermute | solution.py:39
  199.3 6.2 %collective-permute-start.47 = (f32[128,256]{1,0:T(8,128)S(1)}, f32[128,256]{1,0:T(8,128)S(1)}, u32[]{:S(2)}, u32[]{:S(2)}) collective-permute-start(f32[128,256]{1,0:T(8,128)S(1)} %get-tuple-element.112), channel_id=1, source_target_pairs={{0,1},{1,2},{2,3},{3,0},{4,5},{5,6},{6,7},{7,4},{8,9},{9,10},{10,1... | collective-permute-start | bytes 393224 | tf_op jit(solution)/shard_map/ppermute | solution.py:39
  200.8 7.0 %collective-permute-start.48 = (f32[128,256]{1,0:T(8,128)S(1)}, f32[128,256]{1,0:T(8,128)S(1)}, u32[]{:S(2)}, u32[]{:S(2)}) collective-permute-start(f32[128,256]{1,0:T(8,128)S(1)} %get-tuple-element.113), channel_id=1, source_target_pairs={{0,2},{1,3},{2,0},{3,1},{4,6},{5,7},{6,4},{7,5},{8,10},{9,11},{10,... | collective-permute-start | bytes 393224 | tf_op jit(solution)/shard_map/ppermute | solution.py:39
  203.5 5.0 %collective-permute-start.49 = (f32[128,256]{1,0:T(8,128)S(1)}, f32[128,256]{1,0:T(8,128)S(1)}, u32[]{:S(2)}, u32[]{:S(2)}) collective-permute-start(f32[128,256]{1,0:T(8,128)S(1)} %get-tuple-element.114), channel_id=1, source_target_pairs={{0,3},{1,0},{2,1},{3,2},{4,7},{5,4},{6,5},{7,6},{8,11},{9,8},{10,9... | collective-permute-start | bytes 393224 | tf_op jit(solution)/shard_map/ppermute | solution.py:39
  208.8 6.2 %collective-permute-start.50 = (f32[128,256]{1,0:T(8,128)S(1)}, f32[128,256]{1,0:T(8,128)S(1)}, u32[]{:S(2)}, u32[]{:S(2)}) collective-permute-start(f32[128,256]{1,0:T(8,128)S(1)} %shard_map.90), channel_id=1, source_target_pairs={{0,32},{16,48},{32,64},{48,80},{64,96},{80,112},{96,0},{112,16},{1... | collective-permute-start | bytes 393224 | tf_op jit(solution)/shard_map/ppermute | solution.py:44
  210.1 7.1 %collective-permute-start.51 = (f32[128,256]{1,0:T(8,128)S(1)}, f32[128,256]{1,0:T(8,128)S(1)}, u32[]{:S(2)}, u32[]{:S(2)}) collective-permute-start(f32[128,256]{1,0:T(8,128)S(1)} %shard_map.90), channel_id=1, source_target_pairs={{0,64},{16,80},{32,96},{48,112},{64,0},{80,16},{96,32},{112,48},{1... | collective-permute-start | bytes 393224 | tf_op jit(solution)/shard_map/ppermute | solution.py:44
  212.8 5.0 %collective-permute-start.52 = (f32[128,256]{1,0:T(8,128)S(1)}, f32[128,256]{1,0:T(8,128)S(1)}, u32[]{:S(2)}, u32[]{:S(2)}) collective-permute-start(f32[128,256]{1,0:T(8,128)S(1)} %shard_map.90), channel_id=1, source_target_pairs={{0,96},{16,112},{32,0},{48,16},{64,32},{80,48},{96,64},{112,80},{1... | collective-permute-start | bytes 393224 | tf_op jit(solution)/shard_map/ppermute | solution.py:44
  217.8 2.0 collective-permute-start.53
  222.4 10.9 %collective-permute-start.54 = (f32[4,128,256]{2,1,0:T(8,128)S(1)}, f32[4,128,256]{2,1,0:T(8,128)S(1)}, u32[]{:S(2)}, u32[]{:S(2)}) collective-permute-start(f32[4,128,256]{2,1,0:T(8,128)S(1)} %get-tuple-element.119), channel_id=1, source_target_pairs={{0,8},{1,9},{2,10},{3,11},{4,12},{5,13},{6,14},{7,15},{8,0},{9,1},... | collective-permute-start | bytes 1572872 | tf_op jit(solution)/shard_map/ppermute | solution.py:39
  224.0 14.8 %collective-permute-start.55 = (f32[4,128,256]{2,1,0:T(8,128)S(1)}, f32[4,128,256]{2,1,0:T(8,128)S(1)}, u32[]{:S(2)}, u32[]{:S(2)}) collective-permute-start(f32[4,128,256]{2,1,0:T(8,128)S(1)} %get-tuple-element.120), channel_id=1, source_target_pairs={{0,4},{1,5},{2,6},{3,7},{4,8},{5,9},{6,10},{7,11},{8,12},{9,13},{1... | collective-permute-start | bytes 1572872 | tf_op jit(solution)/shard_map/ppermute | solution.py:39
  225.7 13.1 %collective-permute-start.56 = (f32[4,128,256]{2,1,0:T(8,128)S(1)}, f32[4,128,256]{2,1,0:T(8,128)S(1)}, u32[]{:S(2)}, u32[]{:S(2)}) collective-permute-start(f32[4,128,256]{2,1,0:T(8,128)S(1)} %get-tuple-element.121), channel_id=1, source_target_pairs={{0,12},{1,13},{2,14},{3,15},{4,0},{5,1},{6,2},{7,3},{8,4},{9,5},{1... | collective-permute-start | bytes 1572872 | tf_op jit(solution)/shard_map/ppermute | solution.py:39
  238.9 6.2 %collective-permute-start.57 = (f32[128,256]{1,0:T(8,128)S(1)}, f32[128,256]{1,0:T(8,128)S(1)}, u32[]{:S(2)}, u32[]{:S(2)}) collective-permute-start(f32[128,256]{1,0:T(8,128)S(1)} %get-tuple-element.123), channel_id=1, source_target_pairs={{0,1},{1,2},{2,3},{3,0},{4,5},{5,6},{6,7},{7,4},{8,9},{9,10},{10,1... | collective-permute-start | bytes 393224 | tf_op jit(solution)/shard_map/ppermute | solution.py:39
  240.0 6.8 %collective-permute-start.58 = (f32[128,256]{1,0:T(8,128)S(1)}, f32[128,256]{1,0:T(8,128)S(1)}, u32[]{:S(2)}, u32[]{:S(2)}) collective-permute-start(f32[128,256]{1,0:T(8,128)S(1)} %get-tuple-element.124), channel_id=1, source_target_pairs={{0,2},{1,3},{2,0},{3,1},{4,6},{5,7},{6,4},{7,5},{8,10},{9,11},{10,... | collective-permute-start | bytes 393224 | tf_op jit(solution)/shard_map/ppermute | solution.py:39
  242.5 5.0 %collective-permute-start.59 = (f32[128,256]{1,0:T(8,128)S(1)}, f32[128,256]{1,0:T(8,128)S(1)}, u32[]{:S(2)}, u32[]{:S(2)}) collective-permute-start(f32[128,256]{1,0:T(8,128)S(1)} %get-tuple-element.125), channel_id=1, source_target_pairs={{0,3},{1,0},{2,1},{3,2},{4,7},{5,4},{6,5},{7,6},{8,11},{9,8},{10,9... | collective-permute-start | bytes 393224 | tf_op jit(solution)/shard_map/ppermute | solution.py:39

commit v4 on v3

--- a/solution.py
+++ b/solution.py
@@ -13,8 +13,7 @@
 NZ, NC, NX, NY = 4, 2, 4, 4
 BOTH = ("prow", "pcol")
 UNROLL = 16
-PLAIN = (1, 2, 3)
-FAR_FIRST = (2, 1, 3)
+ORDER = (2, 1, 3)
 
 
 def pair_index(high, low):
@@ -237,29 +236,29 @@
 
 
 def gather_plane(value):
-    units = jnp.stack([value] + [shift_plane(value, d, 0) for d in PLAIN])
-    return [units] + [shift_plane(units, d, 1) for d in PLAIN]
+    units = jnp.stack([value] + [shift_plane(value, d, 0) for d in ORDER])
+    return [units] + [shift_plane(units, d, 1) for d in ORDER]
 
 
 def scatter_plane(groups, beside):
-    first = [shift_plane(groups[k], d, 0) for k, d in enumerate(FAR_FIRST, 1)]
+    first = [shift_plane(groups[k], d, 0) for k, d in enumerate(ORDER, 1)]
     units = add_units([groups[0]] + first, beside(first[0]))
-    return [units[0]] + [shift_plane(units[d], d, 1) for d in PLAIN]
+    return [units[0]] + [shift_plane(units[k], d, 1) for k, d in enumerate(ORDER, 1)]
 
 
 def scatter_z(mine, other):
     units = add_units([mine, swap_core(other)], [])
-    return [units[0]] + [shift_z(units[d], d) for d in PLAIN]
+    return [units[0]] + [shift_z(units[k], d) for k, d in enumerate(ORDER, 1)]
 
 
 def gather_z(value):
-    units = jnp.stack([value] + [shift_z(value, d) for d in PLAIN])
+    units = jnp.stack([value] + [shift_z(value, d) for d in ORDER])
     return [units, swap_core(units)]
 
 
-def place(offset, order):
+def place(offset):
     spot = jnp.zeros_like(offset)
-    for k, d in enumerate(order, 1):
+    for k, d in enumerate(ORDER, 1):
         spot = jnp.where(offset == d, k, spot)
     return spot
 
@@ -279,13 +278,12 @@
     off_y = (y - anchor % NY) % NY
     off_z = (z - rows // NC) % NZ
     first = core == 0
-    to_x, to_y, to_z = (-off_x) % NX, (-off_y) % NY, (-off_z) % NZ
-    take_plane = jnp.where(first, off_y * NX + off_x, off_x * NY + off_y)
-    put_plane = jnp.where(
-        first, place(to_x, FAR_FIRST) * NY + to_y, place(to_y, FAR_FIRST) * NX + to_x
-    )
+    from_x, from_y, from_z = [place(v) for v in (off_x, off_y, off_z)]
+    to_x, to_y, to_z = [place((-v) % 4) for v in (off_x, off_y, off_z)]
+    take_plane = jnp.where(first, from_y * NX + from_x, from_x * NY + from_y)
+    put_plane = jnp.where(first, to_x * NY + to_y, to_y * NX + to_x)
     across = (rows % NC != core).astype(jnp.int32) * NZ
-    take_z = across + off_z
+    take_z = across + from_z
     put_z = across + to_z
 
     def forth(high, low, vectors, init):

time: 249 us -> 243 us (0.976)
  waiting for transfers between devices: 114 us -> 105 us
  starting transfers between devices: 89.8 us -> 93.6 us
    ppermute x18, waiting for transfers between devices: 29.7 us -> 24.8 us  [shift_z(): return lax.ppermute(value, 'prow', pairs)]
    ppermute x36, waiting for transfers between devices: 73.2 us -> 68.9 us  [shift_plane(): return lax.ppermute(value, BOTH, pairs)]
    ppermute x18, starting transfers between devices: 30.4 us -> 33.2 us  [shift_z(): return lax.ppermute(value, 'prow', pairs)]
where the time goes in v4:
time: 243 us
  waiting for transfers between devices  105 us (43%)
  starting transfers between devices  93.6 us (39%)
  Pallas kernels  39.4 us (16%)
  other arithmetic  4 us (2%)
    ppermute x36, waiting for transfers between devices, shift_plane(): return lax.ppermute(value, BOTH, pairs)  68.9 us
    ppermute x36, starting transfers between devices, shift_plane(): return lax.ppermute(value, BOTH, pairs)  59.7 us
    pallas_call x24, Pallas kernels, fast_call(): pl.pallas_call(kernel, in_specs=[pl.BlockSpec(memory_space=pltpu.SMEM)] *...  33.4 us
    ppermute x18, starting transfers between devices, shift_z(): return lax.ppermute(value, 'prow', pairs)  33.2 us
    ppermute x18, waiting for transfers between devices, shift_z(): return lax.ppermute(value, 'prow', pairs)  24.8 us
    ppermute x6, waiting for transfers between devices, swap_core(): return lax.ppermute(value, 'prow', pairs)  11.4 us
  transfers between devices with their start and end apart: 60, of which 49 were waited for; matrix products, arithmetic and copies ran while one was open for 1% of the time, Pallas kernels for 8%

profile of v4, /device:TPU:0, one launch (start us, length us, event | category | flops | bytes accessed | tf_op | source)
XLA Modules:
  0.0 243.1 jit_solution(8561021832211339833)
XLA Ops:
  5.2 1.9 collective-permute-start
  8.5 3.2 %collective-permute-done = f32[128,256]{1,0:T(8,128)S(1)} collective-permute-done((f32[128,256]{1,0:T(8,128)S(1)}, f32[128,256]{1,0:T(8,128)S(1)}, u32[]{:S(2)}, u32[]{:S(2)}) %collective-permute-start) | collective-permute-done | bytes 131104 | tf_op jit(solution)/shard_map/ppermute | solution.py:38
  11.7 3.4 %collective-permute-start.3 = (f32[4,128,256]{2,1,0:T(8,128)S(1)}, f32[4,128,256]{2,1,0:T(8,128)S(1)}, u32[]{:S(2)}, u32[]{:S(2)}) collective-permute-start(f32[4,128,256]{2,1,0:T(8,128)S(1)} %fusion.4.after.refs_0_), channel_id=1, source_target_pairs={{0,2},{1,3},{2,0},{3,1},{4,6},{5,7},{6,4},{7,5},{8,10},{9,11},{10,... | collective-permute-start | bytes 1572872 | tf_op jit(solution)/shard_map/ppermute | solution.py:38
  15.7 2.6 %collective-permute-start.5 = (f32[4,128,256]{2,1,0:T(8,128)S(1)}, f32[4,128,256]{2,1,0:T(8,128)S(1)}, u32[]{:S(2)}, u32[]{:S(2)}) collective-permute-start(f32[4,128,256]{2,1,0:T(8,128)S(1)} %fusion.4.after.refs_0_), channel_id=1, source_target_pairs={{0,3},{1,0},{2,1},{3,2},{4,7},{5,4},{6,5},{7,6},{8,11},{9,8},{10,9... | collective-permute-start | bytes 1572872 | tf_op jit(solution)/shard_map/ppermute | solution.py:38
  19.0 4.7 %shard_map.69.refs_4_.refs_2_ = f32[6,32,128,128]{3,2,1,0:T(8,128)S(1)} custom-call(f32[6,32,128,128]{3,2,1,0:T(8,128)} %bitcast.202, f32[4,128,256]{2,1,0:T(8,128)S(1)} %fusion.4.after.refs_0_), custom_call_target="tpu_custom_call" | custom-call | bytes 12582912 | tf_op jit(solution)/shard_map/pallas_call | solution.py:225
  23.8 4.3 %collective-permute-done.4.refs_2_ = f32[4,128,256]{2,1,0:T(8,128)S(1)} collective-permute-done((f32[4,128,256]{2,1,0:T(8,128)S(1)}, f32[4,128,256]{2,1,0:T(8,128)S(1)}, u32[]{:S(2)}, u32[]{:S(2)}) %collective-permute-start.4) | collective-permute-done | bytes 524320 | tf_op jit(solution)/shard_map/ppermute | solution.py:38
  28.5 2.5 %shard_map.70 = (f32[4,128,256]{2,1,0:T(8,128)S(1)}, f32[4,128,256]{2,1,0:T(8,128)S(1)}) custom-call(s32[32]{0:T(128)S(1)} %get-tuple-element.162.take, s32[32]{0:T(128)S(1)} %get-tuple-element.151.put, s32[32]{0:T(128)S(1)} %get-tuple-element.145.live, f32[4,128,256]{2,1,0:T(8,128)S(1)} %fusion.4.after.refs_0_, ...), custom_call_target="tpu_custom_call" | custom-call | flops 1073741824 | bytes 4096 | tf_op jit(solution)/shard_map/pallas_call | solution.py:66
  31.1 1.9 collective-permute-done.6.refs_1_
  33.1 4.0 %collective-permute-start.7 = (f32[128,256]{1,0:T(8,128)S(1)}, f32[128,256]{1,0:T(8,128)S(1)}, u32[]{:S(2)}, u32[]{:S(2)}) collective-permute-start(f32[128,256]{1,0:T(8,128)S(1)} %get-tuple-element.67), channel_id=1, source_target_pairs={{0,64},{16,80},{32,96},{48,112},{64,0},{80,16},{96,32},{112,48},{1... | collective-permute-start | bytes 393224 | tf_op jit(solution)/shard_map/ppermute | solution.py:43
  38.1 2.2 collective-permute-start.9
  41.3 2.5 %collective-permute-done.8.refs_2_ = f32[128,256]{1,0:T(8,128)S(1)} collective-permute-done((f32[128,256]{1,0:T(8,128)S(1)}, f32[128,256]{1,0:T(8,128)S(1)}, u32[]{:S(2)}, u32[]{:S(2)}) %collective-permute-start.8) | collective-permute-done | bytes 131104 | tf_op jit(solution)/shard_map/ppermute | solution.py:43
  44.7 1.9 collective-permute-start.10
  47.2 2.6 %collective-permute-start.12 = (f32[128,256]{1,0:T(8,128)S(1)}, f32[128,256]{1,0:T(8,128)S(1)}, u32[]{:S(2)}, u32[]{:S(2)}) collective-permute-start(f32[128,256]{1,0:T(8,128)S(1)} %shard_map.72.base), channel_id=1, source_target_pairs={{0,12},{1,13},{2,14},{3,15},{4,0},{5,1},{6,2},{7,3},{8,4},{9,5},{1... | collective-permute-start | bytes 393224 | tf_op jit(solution)/shard_map/ppermute | solution.py:38
  52.8 2.1 collective-permute-start.13
  56.4 1.8 collective-permute-start.15
  58.1 2.5 %shard_map.73 = (f32[4,128,256]{2,1,0:T(8,128)S(1)}, f32[4,128,256]{2,1,0:T(8,128)S(1)}) custom-call(s32[32]{0:T(128)S(1)} %get-tuple-element.164.take, s32[32]{0:T(128)S(1)} %get-tuple-element.149.put, s32[32]{0:T(128)S(1)} %get-tuple-element.143.live, f32[4,128,256]{2,1,0:T(8,128)S(1)} %fusion.4.after.refs_0_, ...), custom_call_target="tpu_custom_call" | custom-call | flops 1073741824 | bytes 4096 | tf_op jit(solution)/shard_map/pallas_call | solution.py:66
  60.7 3.0 %collective-permute-done.13.refs_1_ = f32[4,128,256]{2,1,0:T(8,128)S(1)} collective-permute-done((f32[4,128,256]{2,1,0:T(8,128)S(1)}, f32[4,128,256]{2,1,0:T(8,128)S(1)}, u32[]{:S(2)}, u32[]{:S(2)}) %collective-permute-start.13) | collective-permute-done | bytes 524320 | tf_op jit(solution)/shard_map/ppermute | solution.py:38
  63.7 5.5 %collective-permute-done.14.refs_2_ = f32[4,128,256]{2,1,0:T(8,128)S(1)} collective-permute-done((f32[4,128,256]{2,1,0:T(8,128)S(1)}, f32[4,128,256]{2,1,0:T(8,128)S(1)}, u32[]{:S(2)}, u32[]{:S(2)}) %collective-permute-start.14) | collective-permute-done | bytes 524320 | tf_op jit(solution)/shard_map/ppermute | solution.py:38
  69.2 2.5 %shard_map.74 = (f32[4,128,256]{2,1,0:T(8,128)S(1)}, f32[4,128,256]{2,1,0:T(8,128)S(1)}) custom-call(s32[32]{0:T(128)S(1)} %get-tuple-element.163.take, s32[32]{0:T(128)S(1)} %get-tuple-element.150.put, s32[32]{0:T(128)S(1)} %get-tuple-element.144.live, f32[4,128,256]{2,1,0:T(8,128)S(1)} %pad_maximum_fusion.2.refs_0_, ...), custom_call_target="tpu_custom_call" | custom-call | flops 1073741824 | bytes 4096 | tf_op jit(solution)/shard_map/pallas_call | solution.py:66
  71.8 1.9 collective-permute-done.16.refs_1_
  73.7 2.2 collective-permute-start.17
  79.1 2.5 %collective-permute-done.17.refs_1_ = f32[128,256]{1,0:T(8,128)S(1)} collective-permute-done((f32[128,256]{1,0:T(8,128)S(1)}, f32[128,256]{1,0:T(8,128)S(1)}, u32[]{:S(2)}, u32[]{:S(2)}) %collective-permute-start.17) | collective-permute-done | bytes 131104 | tf_op jit(solution)/shard_map/ppermute | solution.py:43
  81.7 2.0 collective-permute-done.18.refs_2_
  84.1 1.8 collective-permute-start.20
  85.9 2.4 collective-permute-start.21
  93.3 2.1 collective-permute-start.23
  96.8 1.8 collective-permute-start.25
  98.6 2.5 %shard_map.77 = (f32[4,128,256]{2,1,0:T(8,128)S(1)}, f32[4,128,256]{2,1,0:T(8,128)S(1)}) custom-call(s32[32]{0:T(128)S(1)} %get-tuple-element.167.take, s32[32]{0:T(128)S(1)} %get-tuple-element.146.put, s32[32]{0:T(128)S(1)} %get-tuple-element.140.live, f32[4,128,256]{2,1,0:T(8,128)S(1)} %fusion.4.after.refs_0_, ...), custom_call_target="tpu_custom_call" | custom-call | flops 1073741824 | bytes 4096 | tf_op jit(solution)/shard_map/pallas_call | solution.py:66
  101.1 2.5 %shard_map.78 = (f32[4,128,256]{2,1,0:T(8,128)S(1)}, f32[4,128,256]{2,1,0:T(8,128)S(1)}) custom-call(s32[32]{0:T(128)S(1)} %get-tuple-element.166.take, s32[32]{0:T(128)S(1)} %get-tuple-element.147.put, s32[32]{0:T(128)S(1)} %get-tuple-element.141.live, f32[4,128,256]{2,1,0:T(8,128)S(1)} %pad_maximum_fusion.2.refs_0_, ...), custom_call_target="tpu_custom_call" | custom-call | flops 1073741824 | bytes 4096 | tf_op jit(solution)/shard_map/pallas_call | solution.py:66
  104.1 5.5 %collective-permute-done.24.refs_2_ = f32[4,128,256]{2,1,0:T(8,128)S(1)} collective-permute-done((f32[4,128,256]{2,1,0:T(8,128)S(1)}, f32[4,128,256]{2,1,0:T(8,128)S(1)}, u32[]{:S(2)}, u32[]{:S(2)}) %collective-permute-start.24) | collective-permute-done | bytes 524320 | tf_op jit(solution)/shard_map/ppermute | solution.py:38
  109.6 2.5 %shard_map.79 = (f32[4,128,256]{2,1,0:T(8,128)S(1)}, f32[4,128,256]{2,1,0:T(8,128)S(1)}) custom-call(s32[32]{0:T(128)S(1)} %get-tuple-element.165.take, s32[32]{0:T(128)S(1)} %get-tuple-element.148.put, s32[32]{0:T(128)S(1)} %get-tuple-element.142.live, f32[4,128,256]{2,1,0:T(8,128)S(1)} %pad_maximum_fusion.3.refs_0_, ...), custom_call_target="tpu_custom_call" | custom-call | flops 1073741824 | bytes 4096 | tf_op jit(solution)/shard_map/pallas_call | solution.py:66
  112.3 1.9 collective-permute-done.26.refs_1_
  114.2 2.1 collective-permute-start.27
  119.5 2.6 %collective-permute-done.27.refs_1_ = f32[128,256]{1,0:T(8,128)S(1)} collective-permute-done((f32[128,256]{1,0:T(8,128)S(1)}, f32[128,256]{1,0:T(8,128)S(1)}, u32[]{:S(2)}, u32[]{:S(2)}) %collective-permute-start.27) | collective-permute-done | bytes 131104 | tf_op jit(solution)/shard_map/ppermute | solution.py:43
  122.1 2.0 collective-permute-done.28.refs_2_
  124.8 2.1 collective-permute-start.30
  130.1 2.7 %collective-permute-done.30 = f32[128,256]{1,0:T(8,128)S(1)} collective-permute-done((f32[128,256]{1,0:T(8,128)S(1)}, f32[128,256]{1,0:T(8,128)S(1)}, u32[]{:S(2)}, u32[]{:S(2)}) %collective-permute-start.30) | collective-permute-done | bytes 131104 | tf_op jit(solution)/shard_map/ppermute | solution.py:43
  134.6 1.9 collective-permute-done.33.refs_1_
  136.5 2.6 %shard_map.82 = (f32[4,128,256]{2,1,0:T(8,128)S(1)}, f32[4,128,256]{2,1,0:T(8,128)S(1)}, f32[4,128,256]{2,1,0:T(8,128)S(1)}, f32[4,128,256]{2,1,0:T(8,128)S(1)}) custom-call(s32[32]{0:T(128)S(1)} %get-tuple-element.169.take, s32[32]{0:T(128)S(1)} %get-tuple-element.132.put, s32[32]{0:T(128)S(1)} %get-tuple-element.142.live, ...), custom_call_target="tpu_custom_call" | custom-call | flops 1073741824 | bytes 4096 | tf_op jit(solution)/shard_map/pallas_call | solution.py:66
  139.9 2.2 collective-permute-start.35
  143.1 6.9 %collective-permute-done.34.refs_3_.refs_1_ = f32[4,128,256]{2,1,0:T(8,128)S(1)} collective-permute-done((f32[4,128,256]{2,1,0:T(8,128)S(1)}, f32[4,128,256]{2,1,0:T(8,128)S(1)}, u32[]{:S(2)}, u32[]{:S(2)}) %collective-permute-start.34) | collective-permute-done | bytes 524320 | tf_op jit(solution)/shard_map/ppermute | solution.py:38
  150.0 2.6 %shard_map.84 = (f32[4,128,256]{2,1,0:T(8,128)S(1)}, f32[4,128,256]{2,1,0:T(8,128)S(1)}, f32[4,128,256]{2,1,0:T(8,128)S(1)}, f32[4,128,256]{2,1,0:T(8,128)S(1)}) custom-call(s32[32]{0:T(128)S(1)} %get-tuple-element.171.take, s32[32]{0:T(128)S(1)} %get-tuple-element.130.put, s32[32]{0:T(128)S(1)} %get-tuple-element.140.live, ...), custom_call_target="tpu_custom_call" | custom-call | flops 1073741824 | bytes 4096 | tf_op jit(solution)/shard_map/pallas_call | solution.py:66
  152.7 2.6 %shard_map.83 = (f32[4,128,256]{2,1,0:T(8,128)S(1)}, f32[4,128,256]{2,1,0:T(8,128)S(1)}, f32[4,128,256]{2,1,0:T(8,128)S(1)}, f32[4,128,256]{2,1,0:T(8,128)S(1)}) custom-call(s32[32]{0:T(128)S(1)} %get-tuple-element.170.take, s32[32]{0:T(128)S(1)} %get-tuple-element.131.put, s32[32]{0:T(128)S(1)} %get-tuple-element.141.live, ...), custom_call_target="tpu_custom_call" | custom-call | flops 1073741824 | bytes 4096 | tf_op jit(solution)/shard_map/pallas_call | solution.py:66
  155.7 2.1 collective-permute-start.37
  159.2 1.8 collective-permute-start.39
  162.2 1.7 collective-permute-done.38.refs_2_
  164.5 1.8 collective-permute-start.40
  166.3 1.8 collective-permute-start.41
  173.5 1.9 collective-permute-done.43.refs_1_
  175.4 2.6 %shard_map.87 = (f32[4,128,256]{2,1,0:T(8,128)S(1)}, f32[4,128,256]{2,1,0:T(8,128)S(1)}, f32[4,128,256]{2,1,0:T(8,128)S(1)}, f32[4,128,256]{2,1,0:T(8,128)S(1)}) custom-call(s32[32]{0:T(128)S(1)} %get-tuple-element.168.take, s32[32]{0:T(128)S(1)} %get-tuple-element.133.put, s32[32]{0:T(128)S(1)} %get-tuple-element.144.live, ...), custom_call_target="tpu_custom_call" | custom-call | flops 1073741824 | bytes 4096 | tf_op jit(solution)/shard_map/pallas_call | solution.py:66
  178.8 2.2 collective-permute-start.45
  182.0 6.9 %collective-permute-done.44.refs_7_.refs_1_ = f32[4,128,256]{2,1,0:T(8,128)S(1)} collective-permute-done((f32[4,128,256]{2,1,0:T(8,128)S(1)}, f32[4,128,256]{2,1,0:T(8,128)S(1)}, u32[]{:S(2)}, u32[]{:S(2)}) %collective-permute-start.44) | collective-permute-done | bytes 524320 | tf_op jit(solution)/shard_map/ppermute | solution.py:38
  188.9 2.6 %shard_map.88 = (f32[4,128,256]{2,1,0:T(8,128)S(1)}, f32[4,128,256]{2,1,0:T(8,128)S(1)}, f32[4,128,256]{2,1,0:T(8,128)S(1)}, f32[4,128,256]{2,1,0:T(8,128)S(1)}) custom-call(s32[32]{0:T(128)S(1)} %get-tuple-element.172.take, s32[32]{0:T(128)S(1)} %get-tuple-element.129.put, s32[32]{0:T(128)S(1)} %get-tuple-element.143.live, ...), custom_call_target="tpu_custom_call" | custom-call | flops 1073741824 | bytes 4096 | tf_op jit(solution)/shard_map/pallas_call | solution.py:66
  191.5 2.9 %collective-permute-done.45.refs_2_ = f32[4,128,256]{2,1,0:T(8,128)S(1)} collective-permute-done((f32[4,128,256]{2,1,0:T(8,128)S(1)}, f32[4,128,256]{2,1,0:T(8,128)S(1)}, u32[]{:S(2)}, u32[]{:S(2)}) %collective-permute-start.45) | collective-permute-done | bytes 524320 | tf_op jit(solution)/shard_map/ppermute | solution.py:38
  194.6 2.1 collective-permute-start.47
  196.6 1.9 collective-permute-start.48
  203.8 1.7 collective-permute-start.50
  205.5 1.8 collective-permute-start.51
  212.4 1.9 collective-permute-done.53.refs_1_
  214.3 2.6 %shard_map.91 = (f32[4,128,256]{2,1,0:T(8,128)S(1)}, f32[4,128,256]{2,1,0:T(8,128)S(1)}, f32[4,128,256]{2,1,0:T(8,128)S(1)}, f32[4,128,256]{2,1,0:T(8,128)S(1)}) custom-call(s32[32]{0:T(128)S(1)} %get-tuple-element.173.take, s32[32]{0:T(128)S(1)} %get-tuple-element.128.put, s32[32]{0:T(128)S(1)} %get-tuple-element.145.live, ...), custom_call_target="tpu_custom_call" | custom-call | flops 1073741824 | bytes 4096 | tf_op jit(solution)/shard_map/pallas_call | solution.py:66
  217.7 2.2 collective-permute-start.55
  221.0 6.8 %collective-permute-done.54.refs_1_ = f32[4,128,256]{2,1,0:T(8,128)S(1)} collective-permute-done((f32[4,128,256]{2,1,0:T(8,128)S(1)}, f32[4,128,256]{2,1,0:T(8,128)S(1)}, u32[]{:S(2)}, u32[]{:S(2)}) %collective-permute-start.54) | collective-permute-done | bytes 524320 | tf_op jit(solution)/shard_map/ppermute | solution.py:38
  227.8 5.5 %collective-permute-done.55.refs_2_ = f32[4,128,256]{2,1,0:T(8,128)S(1)} collective-permute-done((f32[4,128,256]{2,1,0:T(8,128)S(1)}, f32[4,128,256]{2,1,0:T(8,128)S(1)}, u32[]{:S(2)}, u32[]{:S(2)}) %collective-permute-start.55) | collective-permute-done | bytes 524320 | tf_op jit(solution)/shard_map/ppermute | solution.py:38
  234.6 2.4 collective-permute-start.58
  (100 shorter events, 68.1 us)
Async XLA Ops:
  1.9 6.6 %collective-permute-start.1 = (f32[128,256]{1,0:T(8,128)S(1)}, f32[128,256]{1,0:T(8,128)S(1)}, u32[]{:S(2)}, u32[]{:S(2)}) collective-permute-start(f32[128,256]{1,0:T(8,128)S(1)} %shard_map.68.base), channel_id=1, source_target_pairs={{0,4},{1,5},{2,6},{3,7},{4,8},{5,9},{6,10},{7,11},{8,12},{9,13},{1... | collective-permute-start | bytes 393224 | tf_op jit(solution)/shard_map/ppermute | solution.py:38
  3.5 5.0 %collective-permute-start.2 = (f32[128,256]{1,0:T(8,128)S(1)}, f32[128,256]{1,0:T(8,128)S(1)}, u32[]{:S(2)}, u32[]{:S(2)}) collective-permute-start(f32[128,256]{1,0:T(8,128)S(1)} %shard_map.68.base), channel_id=1, source_target_pairs={{0,12},{1,13},{2,14},{3,15},{4,0},{5,1},{6,2},{7,3},{8,4},{9,5},{1... | collective-permute-start | bytes 393224 | tf_op jit(solution)/shard_map/ppermute | solution.py:38
  5.2 6.5 %collective-permute-start = (f32[128,256]{1,0:T(8,128)S(1)}, f32[128,256]{1,0:T(8,128)S(1)}, u32[]{:S(2)}, u32[]{:S(2)}) collective-permute-start(f32[128,256]{1,0:T(8,128)S(1)} %shard_map.68.base), channel_id=1, source_target_pairs={{0,8},{1,9},{2,10},{3,11},{4,12},{5,13},{6,14},{7,15},{8,0},{9,1},... | collective-permute-start | bytes 393224 | tf_op jit(solution)/shard_map/ppermute | solution.py:38
  11.7 12.1 %collective-permute-start.3 = (f32[4,128,256]{2,1,0:T(8,128)S(1)}, f32[4,128,256]{2,1,0:T(8,128)S(1)}, u32[]{:S(2)}, u32[]{:S(2)}) collective-permute-start(f32[4,128,256]{2,1,0:T(8,128)S(1)} %fusion.4.after.refs_0_), channel_id=1, source_target_pairs={{0,2},{1,3},{2,0},{3,1},{4,6},{5,7},{6,4},{7,5},{8,10},{9,11},{10,... | collective-permute-start | bytes 1572872 | tf_op jit(solution)/shard_map/ppermute | solution.py:38
  15.0 13.0 %collective-permute-start.4 = (f32[4,128,256]{2,1,0:T(8,128)S(1)}, f32[4,128,256]{2,1,0:T(8,128)S(1)}, u32[]{:S(2)}, u32[]{:S(2)}) collective-permute-start(f32[4,128,256]{2,1,0:T(8,128)S(1)} %fusion.4.after.refs_0_), channel_id=1, source_target_pairs={{0,1},{1,2},{2,3},{3,0},{4,5},{5,6},{6,7},{7,4},{8,9},{9,10},{10,1... | collective-permute-start | bytes 1572872 | tf_op jit(solution)/shard_map/ppermute | solution.py:38
  15.7 12.8 %collective-permute-start.5 = (f32[4,128,256]{2,1,0:T(8,128)S(1)}, f32[4,128,256]{2,1,0:T(8,128)S(1)}, u32[]{:S(2)}, u32[]{:S(2)}) collective-permute-start(f32[4,128,256]{2,1,0:T(8,128)S(1)} %fusion.4.after.refs_0_), channel_id=1, source_target_pairs={{0,3},{1,0},{2,1},{3,2},{4,7},{5,4},{6,5},{7,6},{8,11},{9,8},{10,9... | collective-permute-start | bytes 1572872 | tf_op jit(solution)/shard_map/ppermute | solution.py:38
  23.7 20.6 %copy-start = (f32[4,1,1,128,128]{4,3,2,1,0:T(8,128)S(1)}, f32[4,1,1,128,128]{4,3,2,1,0:T(8,128)}, u32[]{:S(2)}) copy-start(f32[4,1,1,128,128]{4,3,2,1,0:T(8,128)} %param.6) | copy-start | bytes 786436
  23.7 20.6 %copy-start.1 = (f32[4,1,1,128,256]{4,3,2,1,0:T(8,128)S(1)}, f32[4,1,1,128,256]{4,3,2,1,0:T(8,128)}, u32[]{:S(2)}) copy-start(f32[4,1,1,128,256]{4,3,2,1,0:T(8,128)} %param.5) | copy-start | bytes 1572868
  31.0 2.0 collective-permute-start.6
  33.1 8.2 %collective-permute-start.7 = (f32[128,256]{1,0:T(8,128)S(1)}, f32[128,256]{1,0:T(8,128)S(1)}, u32[]{:S(2)}, u32[]{:S(2)}) collective-permute-start(f32[128,256]{1,0:T(8,128)S(1)} %get-tuple-element.67), channel_id=1, source_target_pairs={{0,64},{16,80},{32,96},{48,112},{64,0},{80,16},{96,32},{112,48},{1... | collective-permute-start | bytes 393224 | tf_op jit(solution)/shard_map/ppermute | solution.py:43
  37.0 6.8 %collective-permute-start.8 = (f32[128,256]{1,0:T(8,128)S(1)}, f32[128,256]{1,0:T(8,128)S(1)}, u32[]{:S(2)}, u32[]{:S(2)}) collective-permute-start(f32[128,256]{1,0:T(8,128)S(1)} %get-tuple-element.68), channel_id=1, source_target_pairs={{0,32},{16,48},{32,64},{48,80},{64,96},{80,112},{96,0},{112,16},{1... | collective-permute-start | bytes 393224 | tf_op jit(solution)/shard_map/ppermute | solution.py:43
  38.1 6.3 %collective-permute-start.9 = (f32[128,256]{1,0:T(8,128)S(1)}, f32[128,256]{1,0:T(8,128)S(1)}, u32[]{:S(2)}, u32[]{:S(2)}) collective-permute-start(f32[128,256]{1,0:T(8,128)S(1)} %get-tuple-element.69), channel_id=1, source_target_pairs={{0,96},{16,112},{32,0},{48,16},{64,32},{80,48},{96,64},{112,80},{1... | collective-permute-start | bytes 393224 | tf_op jit(solution)/shard_map/ppermute | solution.py:43
  44.7 6.6 %collective-permute-start.10 = (f32[128,256]{1,0:T(8,128)S(1)}, f32[128,256]{1,0:T(8,128)S(1)}, u32[]{:S(2)}, u32[]{:S(2)}) collective-permute-start(f32[128,256]{1,0:T(8,128)S(1)} %shard_map.72.base), channel_id=1, source_target_pairs={{0,8},{1,9},{2,10},{3,11},{4,12},{5,13},{6,14},{7,15},{8,0},{9,1},... | collective-permute-start | bytes 393224 | tf_op jit(solution)/shard_map/ppermute | solution.py:38
  46.6 6.2 %collective-permute-start.11 = (f32[128,256]{1,0:T(8,128)S(1)}, f32[128,256]{1,0:T(8,128)S(1)}, u32[]{:S(2)}, u32[]{:S(2)}) collective-permute-start(f32[128,256]{1,0:T(8,128)S(1)} %shard_map.72.base), channel_id=1, source_target_pairs={{0,4},{1,5},{2,6},{3,7},{4,8},{5,9},{6,10},{7,11},{8,12},{9,13},{1... | collective-permute-start | bytes 393224 | tf_op jit(solution)/shard_map/ppermute | solution.py:38
  47.2 5.6 %collective-permute-start.12 = (f32[128,256]{1,0:T(8,128)S(1)}, f32[128,256]{1,0:T(8,128)S(1)}, u32[]{:S(2)}, u32[]{:S(2)}) collective-permute-start(f32[128,256]{1,0:T(8,128)S(1)} %shard_map.72.base), channel_id=1, source_target_pairs={{0,12},{1,13},{2,14},{3,15},{4,0},{5,1},{6,2},{7,3},{8,4},{9,5},{1... | collective-permute-start | bytes 393224 | tf_op jit(solution)/shard_map/ppermute | solution.py:38
  52.8 10.9 %collective-permute-start.13 = (f32[4,128,256]{2,1,0:T(8,128)S(1)}, f32[4,128,256]{2,1,0:T(8,128)S(1)}, u32[]{:S(2)}, u32[]{:S(2)}) collective-permute-start(f32[4,128,256]{2,1,0:T(8,128)S(1)} %pad_maximum_fusion.2.refs_0_), channel_id=1, source_target_pairs={{0,2},{1,3},{2,0},{3,1},{4,6},{5,7},{6,4},{7,5},{8,10},{9,11},{10,... | collective-permute-start | bytes 1572872 | tf_op jit(solution)/shard_map/ppermute | solution.py:38
  54.9 14.3 %collective-permute-start.14 = (f32[4,128,256]{2,1,0:T(8,128)S(1)}, f32[4,128,256]{2,1,0:T(8,128)S(1)}, u32[]{:S(2)}, u32[]{:S(2)}) collective-permute-start(f32[4,128,256]{2,1,0:T(8,128)S(1)} %pad_maximum_fusion.2.refs_0_), channel_id=1, source_target_pairs={{0,1},{1,2},{2,3},{3,0},{4,5},{5,6},{6,7},{7,4},{8,9},{9,10},{10,1... | collective-permute-start | bytes 1572872 | tf_op jit(solution)/shard_map/ppermute | solution.py:38
  56.4 12.8 %collective-permute-start.15 = (f32[4,128,256]{2,1,0:T(8,128)S(1)}, f32[4,128,256]{2,1,0:T(8,128)S(1)}, u32[]{:S(2)}, u32[]{:S(2)}) collective-permute-start(f32[4,128,256]{2,1,0:T(8,128)S(1)} %pad_maximum_fusion.2.refs_0_), channel_id=1, source_target_pairs={{0,3},{1,0},{2,1},{3,2},{4,7},{5,4},{6,5},{7,6},{8,11},{9,8},{10,9... | collective-permute-start | bytes 1572872 | tf_op jit(solution)/shard_map/ppermute | solution.py:38
  71.7 2.0 collective-permute-start.16
  73.7 7.9 %collective-permute-start.17 = (f32[128,256]{1,0:T(8,128)S(1)}, f32[128,256]{1,0:T(8,128)S(1)}, u32[]{:S(2)}, u32[]{:S(2)}) collective-permute-start(f32[128,256]{1,0:T(8,128)S(1)} %get-tuple-element.75), channel_id=1, source_target_pairs={{0,64},{16,80},{32,96},{48,112},{64,0},{80,16},{96,32},{112,48},{1... | collective-permute-start | bytes 393224 | tf_op jit(solution)/shard_map/ppermute | solution.py:43
  75.9 7.8 %collective-permute-start.18 = (f32[128,256]{1,0:T(8,128)S(1)}, f32[128,256]{1,0:T(8,128)S(1)}, u32[]{:S(2)}, u32[]{:S(2)}) collective-permute-start(f32[128,256]{1,0:T(8,128)S(1)} %get-tuple-element.76), channel_id=1, source_target_pairs={{0,32},{16,48},{32,64},{48,80},{64,96},{80,112},{96,0},{112,16},{1... | collective-permute-start | bytes 393224 | tf_op jit(solution)/shard_map/ppermute | solution.py:43
  77.5 6.3 %collective-permute-start.19 = (f32[128,256]{1,0:T(8,128)S(1)}, f32[128,256]{1,0:T(8,128)S(1)}, u32[]{:S(2)}, u32[]{:S(2)}) collective-permute-start(f32[128,256]{1,0:T(8,128)S(1)} %get-tuple-element.77), channel_id=1, source_target_pairs={{0,96},{16,112},{32,0},{48,16},{64,32},{80,48},{96,64},{112,80},{1... | collective-permute-start | bytes 393224 | tf_op jit(solution)/shard_map/ppermute | solution.py:43
  84.1 6.6 %collective-permute-start.20 = (f32[128,256]{1,0:T(8,128)S(1)}, f32[128,256]{1,0:T(8,128)S(1)}, u32[]{:S(2)}, u32[]{:S(2)}) collective-permute-start(f32[128,256]{1,0:T(8,128)S(1)} %shard_map.76.base), channel_id=1, source_target_pairs={{0,8},{1,9},{2,10},{3,11},{4,12},{5,13},{6,14},{7,15},{8,0},{9,1},... | collective-permute-start | bytes 393224 | tf_op jit(solution)/shard_map/ppermute | solution.py:38
  85.9 6.2 %collective-permute-start.21 = (f32[128,256]{1,0:T(8,128)S(1)}, f32[128,256]{1,0:T(8,128)S(1)}, u32[]{:S(2)}, u32[]{:S(2)}) collective-permute-start(f32[128,256]{1,0:T(8,128)S(1)} %shard_map.76.base), channel_id=1, source_target_pairs={{0,4},{1,5},{2,6},{3,7},{4,8},{5,9},{6,10},{7,11},{8,12},{9,13},{1... | collective-permute-start | bytes 393224 | tf_op jit(solution)/shard_map/ppermute | solution.py:38
  88.2 5.0 %collective-permute-start.22 = (f32[128,256]{1,0:T(8,128)S(1)}, f32[128,256]{1,0:T(8,128)S(1)}, u32[]{:S(2)}, u32[]{:S(2)}) collective-permute-start(f32[128,256]{1,0:T(8,128)S(1)} %shard_map.76.base), channel_id=1, source_target_pairs={{0,12},{1,13},{2,14},{3,15},{4,0},{5,1},{6,2},{7,3},{8,4},{9,5},{1... | collective-permute-start | bytes 393224 | tf_op jit(solution)/shard_map/ppermute | solution.py:38
  93.3 10.9 %collective-permute-start.23 = (f32[4,128,256]{2,1,0:T(8,128)S(1)}, f32[4,128,256]{2,1,0:T(8,128)S(1)}, u32[]{:S(2)}, u32[]{:S(2)}) collective-permute-start(f32[4,128,256]{2,1,0:T(8,128)S(1)} %pad_maximum_fusion.3.refs_0_), channel_id=1, source_target_pairs={{0,2},{1,3},{2,0},{3,1},{4,6},{5,7},{6,4},{7,5},{8,10},{9,11},{10,... | collective-permute-start | bytes 1572872 | tf_op jit(solution)/shard_map/ppermute | solution.py:38
  95.4 14.3 %collective-permute-start.24 = (f32[4,128,256]{2,1,0:T(8,128)S(1)}, f32[4,128,256]{2,1,0:T(8,128)S(1)}, u32[]{:S(2)}, u32[]{:S(2)}) collective-permute-start(f32[4,128,256]{2,1,0:T(8,128)S(1)} %pad_maximum_fusion.3.refs_0_), channel_id=1, source_target_pairs={{0,1},{1,2},{2,3},{3,0},{4,5},{5,6},{6,7},{7,4},{8,9},{9,10},{10,1... | collective-permute-start | bytes 1572872 | tf_op jit(solution)/shard_map/ppermute | solution.py:38
  96.8 12.8 %collective-permute-start.25 = (f32[4,128,256]{2,1,0:T(8,128)S(1)}, f32[4,128,256]{2,1,0:T(8,128)S(1)}, u32[]{:S(2)}, u32[]{:S(2)}) collective-permute-start(f32[4,128,256]{2,1,0:T(8,128)S(1)} %pad_maximum_fusion.3.refs_0_), channel_id=1, source_target_pairs={{0,3},{1,0},{2,1},{3,2},{4,7},{5,4},{6,5},{7,6},{8,11},{9,8},{10,9... | collective-permute-start | bytes 1572872 | tf_op jit(solution)/shard_map/ppermute | solution.py:38
  112.2 2.0 collective-permute-start.26
  114.2 7.9 %collective-permute-start.27 = (f32[128,256]{1,0:T(8,128)S(1)}, f32[128,256]{1,0:T(8,128)S(1)}, u32[]{:S(2)}, u32[]{:S(2)}) collective-permute-start(f32[128,256]{1,0:T(8,128)S(1)} %get-tuple-element.85), channel_id=1, source_target_pairs={{0,64},{16,80},{32,96},{48,112},{64,0},{80,16},{96,32},{112,48},{1... | collective-permute-start | bytes 393224 | tf_op jit(solution)/shard_map/ppermute | solution.py:43
  116.3 7.9 %collective-permute-start.28 = (f32[128,256]{1,0:T(8,128)S(1)}, f32[128,256]{1,0:T(8,128)S(1)}, u32[]{:S(2)}, u32[]{:S(2)}) collective-permute-start(f32[128,256]{1,0:T(8,128)S(1)} %get-tuple-element.86), channel_id=1, source_target_pairs={{0,32},{16,48},{32,64},{48,80},{64,96},{80,112},{96,0},{112,16},{1... | collective-permute-start | bytes 393224 | tf_op jit(solution)/shard_map/ppermute | solution.py:43
  117.8 6.3 %collective-permute-start.29 = (f32[128,256]{1,0:T(8,128)S(1)}, f32[128,256]{1,0:T(8,128)S(1)}, u32[]{:S(2)}, u32[]{:S(2)}) collective-permute-start(f32[128,256]{1,0:T(8,128)S(1)} %get-tuple-element.87), channel_id=1, source_target_pairs={{0,96},{16,112},{32,0},{48,16},{64,32},{80,48},{96,64},{112,80},{1... | collective-permute-start | bytes 393224 | tf_op jit(solution)/shard_map/ppermute | solution.py:43
  124.8 8.0 %collective-permute-start.30 = (f32[128,256]{1,0:T(8,128)S(1)}, f32[128,256]{1,0:T(8,128)S(1)}, u32[]{:S(2)}, u32[]{:S(2)}) collective-permute-start(f32[128,256]{1,0:T(8,128)S(1)} %get-tuple-element.89), channel_id=1, source_target_pairs={{0,64},{16,80},{32,96},{48,112},{64,0},{80,16},{96,32},{112,48},{1... | collective-permute-start | bytes 393224 | tf_op jit(solution)/shard_map/ppermute | solution.py:43
  126.9 7.6 %collective-permute-start.31 = (f32[128,256]{1,0:T(8,128)S(1)}, f32[128,256]{1,0:T(8,128)S(1)}, u32[]{:S(2)}, u32[]{:S(2)}) collective-permute-start(f32[128,256]{1,0:T(8,128)S(1)} %get-tuple-element.89), channel_id=1, source_target_pairs={{0,32},{16,48},{32,64},{48,80},{64,96},{80,112},{96,0},{112,16},{1... | collective-permute-start | bytes 393224 | tf_op jit(solution)/shard_map/ppermute | solution.py:43
  128.4 6.0 %collective-permute-start.32 = (f32[128,256]{1,0:T(8,128)S(1)}, f32[128,256]{1,0:T(8,128)S(1)}, u32[]{:S(2)}, u32[]{:S(2)}) collective-permute-start(f32[128,256]{1,0:T(8,128)S(1)} %get-tuple-element.89), channel_id=1, source_target_pairs={{0,96},{16,112},{32,0},{48,16},{64,32},{80,48},{96,64},{112,80},{1... | collective-permute-start | bytes 393224 | tf_op jit(solution)/shard_map/ppermute | solution.py:43
  134.5 2.0 collective-permute-start.33
  139.2 10.9 %collective-permute-start.34 = (f32[4,128,256]{2,1,0:T(8,128)S(1)}, f32[4,128,256]{2,1,0:T(8,128)S(1)}, u32[]{:S(2)}, u32[]{:S(2)}) collective-permute-start(f32[4,128,256]{2,1,0:T(8,128)S(1)} %get-tuple-element.91), channel_id=1, source_target_pairs={{0,8},{1,9},{2,10},{3,11},{4,12},{5,13},{6,14},{7,15},{8,0},{9,1},... | collective-permute-start | bytes 1572872 | tf_op jit(solution)/shard_map/ppermute | solution.py:38
  139.9 15.6 %collective-permute-start.35 = (f32[4,128,256]{2,1,0:T(8,128)S(1)}, f32[4,128,256]{2,1,0:T(8,128)S(1)}, u32[]{:S(2)}, u32[]{:S(2)}) collective-permute-start(f32[4,128,256]{2,1,0:T(8,128)S(1)} %get-tuple-element.92), channel_id=1, source_target_pairs={{0,4},{1,5},{2,6},{3,7},{4,8},{5,9},{6,10},{7,11},{8,12},{9,13},{1... | collective-permute-start | bytes 1572872 | tf_op jit(solution)/shard_map/ppermute | solution.py:38
  142.1 13.4 %collective-permute-start.36 = (f32[4,128,256]{2,1,0:T(8,128)S(1)}, f32[4,128,256]{2,1,0:T(8,128)S(1)}, u32[]{:S(2)}, u32[]{:S(2)}) collective-permute-start(f32[4,128,256]{2,1,0:T(8,128)S(1)} %get-tuple-element.93), channel_id=1, source_target_pairs={{0,12},{1,13},{2,14},{3,15},{4,0},{5,1},{6,2},{7,3},{8,4},{9,5},{1... | collective-permute-start | bytes 1572872 | tf_op jit(solution)/shard_map/ppermute | solution.py:38
  155.7 6.6 %collective-permute-start.37 = (f32[128,256]{1,0:T(8,128)S(1)}, f32[128,256]{1,0:T(8,128)S(1)}, u32[]{:S(2)}, u32[]{:S(2)}) collective-permute-start(f32[128,256]{1,0:T(8,128)S(1)} %get-tuple-element.97), channel_id=1, source_target_pairs={{0,2},{1,3},{2,0},{3,1},{4,6},{5,7},{6,4},{7,5},{8,10},{9,11},{10,... | collective-permute-start | bytes 393224 | tf_op jit(solution)/shard_map/ppermute | solution.py:38
  157.7 6.2 %collective-permute-start.38 = (f32[128,256]{1,0:T(8,128)S(1)}, f32[128,256]{1,0:T(8,128)S(1)}, u32[]{:S(2)}, u32[]{:S(2)}) collective-permute-start(f32[128,256]{1,0:T(8,128)S(1)} %get-tuple-element.98), channel_id=1, source_target_pairs={{0,1},{1,2},{2,3},{3,0},{4,5},{5,6},{6,7},{7,4},{8,9},{9,10},{10,1... | collective-permute-start | bytes 393224 | tf_op jit(solution)/shard_map/ppermute | solution.py:38
  159.2 5.0 %collective-permute-start.39 = (f32[128,256]{1,0:T(8,128)S(1)}, f32[128,256]{1,0:T(8,128)S(1)}, u32[]{:S(2)}, u32[]{:S(2)}) collective-permute-start(f32[128,256]{1,0:T(8,128)S(1)} %get-tuple-element.99), channel_id=1, source_target_pairs={{0,3},{1,0},{2,1},{3,2},{4,7},{5,4},{6,5},{7,6},{8,11},{9,8},{10,9... | collective-permute-start | bytes 393224 | tf_op jit(solution)/shard_map/ppermute | solution.py:38
  164.5 6.6 %collective-permute-start.40 = (f32[128,256]{1,0:T(8,128)S(1)}, f32[128,256]{1,0:T(8,128)S(1)}, u32[]{:S(2)}, u32[]{:S(2)}) collective-permute-start(f32[128,256]{1,0:T(8,128)S(1)} %shard_map.86), channel_id=1, source_target_pairs={{0,64},{16,80},{32,96},{48,112},{64,0},{80,16},{96,32},{112,48},{1... | collective-permute-start | bytes 393224 | tf_op jit(solution)/shard_map/ppermute | solution.py:43
  166.3 6.2 %collective-permute-start.41 = (f32[128,256]{1,0:T(8,128)S(1)}, f32[128,256]{1,0:T(8,128)S(1)}, u32[]{:S(2)}, u32[]{:S(2)}) collective-permute-start(f32[128,256]{1,0:T(8,128)S(1)} %shard_map.86), channel_id=1, source_target_pairs={{0,32},{16,48},{32,64},{48,80},{64,96},{80,112},{96,0},{112,16},{1... | collective-permute-start | bytes 393224 | tf_op jit(solution)/shard_map/ppermute | solution.py:43
  168.2 5.0 %collective-permute-start.42 = (f32[128,256]{1,0:T(8,128)S(1)}, f32[128,256]{1,0:T(8,128)S(1)}, u32[]{:S(2)}, u32[]{:S(2)}) collective-permute-start(f32[128,256]{1,0:T(8,128)S(1)} %shard_map.86), channel_id=1, source_target_pairs={{0,96},{16,112},{32,0},{48,16},{64,32},{80,48},{96,64},{112,80},{1... | collective-permute-start | bytes 393224 | tf_op jit(solution)/shard_map/ppermute | solution.py:43
  173.2 2.2 collective-permute-start.43
  178.0 10.9 %collective-permute-start.44 = (f32[4,128,256]{2,1,0:T(8,128)S(1)}, f32[4,128,256]{2,1,0:T(8,128)S(1)}, u32[]{:S(2)}, u32[]{:S(2)}) collective-permute-start(f32[4,128,256]{2,1,0:T(8,128)S(1)} %get-tuple-element.104), channel_id=1, source_target_pairs={{0,8},{1,9},{2,10},{3,11},{4,12},{5,13},{6,14},{7,15},{8,0},{9,1},... | collective-permute-start | bytes 1572872 | tf_op jit(solution)/shard_map/ppermute | solution.py:38
  178.8 15.6 %collective-permute-start.45 = (f32[4,128,256]{2,1,0:T(8,128)S(1)}, f32[4,128,256]{2,1,0:T(8,128)S(1)}, u32[]{:S(2)}, u32[]{:S(2)}) collective-permute-start(f32[4,128,256]{2,1,0:T(8,128)S(1)} %get-tuple-element.105), channel_id=1, source_target_pairs={{0,4},{1,5},{2,6},{3,7},{4,8},{5,9},{6,10},{7,11},{8,12},{9,13},{1... | collective-permute-start | bytes 1572872 | tf_op jit(solution)/shard_map/ppermute | solution.py:38
  181.0 13.4 %collective-permute-start.46 = (f32[4,128,256]{2,1,0:T(8,128)S(1)}, f32[4,128,256]{2,1,0:T(8,128)S(1)}, u32[]{:S(2)}, u32[]{:S(2)}) collective-permute-start(f32[4,128,256]{2,1,0:T(8,128)S(1)} %get-tuple-element.106), channel_id=1, source_target_pairs={{0,12},{1,13},{2,14},{3,15},{4,0},{5,1},{6,2},{7,3},{8,4},{9,5},{1... | collective-permute-start | bytes 1572872 | tf_op jit(solution)/shard_map/ppermute | solution.py:38
  194.6 6.6 %collective-permute-start.47 = (f32[128,256]{1,0:T(8,128)S(1)}, f32[128,256]{1,0:T(8,128)S(1)}, u32[]{:S(2)}, u32[]{:S(2)}) collective-permute-start(f32[128,256]{1,0:T(8,128)S(1)} %get-tuple-element.112), channel_id=1, source_target_pairs={{0,2},{1,3},{2,0},{3,1},{4,6},{5,7},{6,4},{7,5},{8,10},{9,11},{10,... | collective-permute-start | bytes 393224 | tf_op jit(solution)/shard_map/ppermute | solution.py:38
  196.6 6.2 %collective-permute-start.48 = (f32[128,256]{1,0:T(8,128)S(1)}, f32[128,256]{1,0:T(8,128)S(1)}, u32[]{:S(2)}, u32[]{:S(2)}) collective-permute-start(f32[128,256]{1,0:T(8,128)S(1)} %get-tuple-element.113), channel_id=1, source_target_pairs={{0,1},{1,2},{2,3},{3,0},{4,5},{5,6},{6,7},{7,4},{8,9},{9,10},{10,1... | collective-permute-start | bytes 393224 | tf_op jit(solution)/shard_map/ppermute | solution.py:38
  198.5 5.0 %collective-permute-start.49 = (f32[128,256]{1,0:T(8,128)S(1)}, f32[128,256]{1,0:T(8,128)S(1)}, u32[]{:S(2)}, u32[]{:S(2)}) collective-permute-start(f32[128,256]{1,0:T(8,128)S(1)} %get-tuple-element.114), channel_id=1, source_target_pairs={{0,3},{1,0},{2,1},{3,2},{4,7},{5,4},{6,5},{7,6},{8,11},{9,8},{10,9... | collective-permute-start | bytes 393224 | tf_op jit(solution)/shard_map/ppermute | solution.py:38
  203.8 6.6 %collective-permute-start.50 = (f32[128,256]{1,0:T(8,128)S(1)}, f32[128,256]{1,0:T(8,128)S(1)}, u32[]{:S(2)}, u32[]{:S(2)}) collective-permute-start(f32[128,256]{1,0:T(8,128)S(1)} %shard_map.90), channel_id=1, source_target_pairs={{0,64},{16,80},{32,96},{48,112},{64,0},{80,16},{96,32},{112,48},{1... | collective-permute-start | bytes 393224 | tf_op jit(solution)/shard_map/ppermute | solution.py:43
  205.5 6.3 %collective-permute-start.51 = (f32[128,256]{1,0:T(8,128)S(1)}, f32[128,256]{1,0:T(8,128)S(1)}, u32[]{:S(2)}, u32[]{:S(2)}) collective-permute-start(f32[128,256]{1,0:T(8,128)S(1)} %shard_map.90), channel_id=1, source_target_pairs={{0,32},{16,48},{32,64},{48,80},{64,96},{80,112},{96,0},{112,16},{1... | collective-permute-start | bytes 393224 | tf_op jit(solution)/shard_map/ppermute | solution.py:43
  207.3 5.0 %collective-permute-start.52 = (f32[128,256]{1,0:T(8,128)S(1)}, f32[128,256]{1,0:T(8,128)S(1)}, u32[]{:S(2)}, u32[]{:S(2)}) collective-permute-start(f32[128,256]{1,0:T(8,128)S(1)} %shard_map.90), channel_id=1, source_target_pairs={{0,96},{16,112},{32,0},{48,16},{64,32},{80,48},{96,64},{112,80},{1... | collective-permute-start | bytes 393224 | tf_op jit(solution)/shard_map/ppermute | solution.py:43
  212.3 2.0 collective-permute-start.53
  216.9 10.9 %collective-permute-start.54 = (f32[4,128,256]{2,1,0:T(8,128)S(1)}, f32[4,128,256]{2,1,0:T(8,128)S(1)}, u32[]{:S(2)}, u32[]{:S(2)}) collective-permute-start(f32[4,128,256]{2,1,0:T(8,128)S(1)} %get-tuple-element.119), channel_id=1, source_target_pairs={{0,8},{1,9},{2,10},{3,11},{4,12},{5,13},{6,14},{7,15},{8,0},{9,1},... | collective-permute-start | bytes 1572872 | tf_op jit(solution)/shard_map/ppermute | solution.py:38
  217.7 15.6 %collective-permute-start.55 = (f32[4,128,256]{2,1,0:T(8,128)S(1)}, f32[4,128,256]{2,1,0:T(8,128)S(1)}, u32[]{:S(2)}, u32[]{:S(2)}) collective-permute-start(f32[4,128,256]{2,1,0:T(8,128)S(1)} %get-tuple-element.120), channel_id=1, source_target_pairs={{0,4},{1,5},{2,6},{3,7},{4,8},{5,9},{6,10},{7,11},{8,12},{9,13},{1... | collective-permute-start | bytes 1572872 | tf_op jit(solution)/shard_map/ppermute | solution.py:38
  219.9 13.4 %collective-permute-start.56 = (f32[4,128,256]{2,1,0:T(8,128)S(1)}, f32[4,128,256]{2,1,0:T(8,128)S(1)}, u32[]{:S(2)}, u32[]{:S(2)}) collective-permute-start(f32[4,128,256]{2,1,0:T(8,128)S(1)} %get-tuple-element.121), channel_id=1, source_target_pairs={{0,12},{1,13},{2,14},{3,15},{4,0},{5,1},{6,2},{7,3},{8,4},{9,5},{1... | collective-permute-start | bytes 1572872 | tf_op jit(solution)/shard_map/ppermute | solution.py:38
  233.4 6.6 %collective-permute-start.57 = (f32[128,256]{1,0:T(8,128)S(1)}, f32[128,256]{1,0:T(8,128)S(1)}, u32[]{:S(2)}, u32[]{:S(2)}) collective-permute-start(f32[128,256]{1,0:T(8,128)S(1)} %get-tuple-element.123), channel_id=1, source_target_pairs={{0,2},{1,3},{2,0},{3,1},{4,6},{5,7},{6,4},{7,5},{8,10},{9,11},{10,... | collective-permute-start | bytes 393224 | tf_op jit(solution)/shard_map/ppermute | solution.py:38
  234.6 6.8 %collective-permute-start.58 = (f32[128,256]{1,0:T(8,128)S(1)}, f32[128,256]{1,0:T(8,128)S(1)}, u32[]{:S(2)}, u32[]{:S(2)}) collective-permute-start(f32[128,256]{1,0:T(8,128)S(1)} %get-tuple-element.124), channel_id=1, source_target_pairs={{0,1},{1,2},{2,3},{3,0},{4,5},{5,6},{6,7},{7,4},{8,9},{9,10},{10,1... | collective-permute-start | bytes 393224 | tf_op jit(solution)/shard_map/ppermute | solution.py:38
  237.0 5.0 %collective-permute-start.59 = (f32[128,256]{1,0:T(8,128)S(1)}, f32[128,256]{1,0:T(8,128)S(1)}, u32[]{:S(2)}, u32[]{:S(2)}) collective-permute-start(f32[128,256]{1,0:T(8,128)S(1)} %get-tuple-element.125), channel_id=1, source_target_pairs={{0,3},{1,0},{2,1},{3,2},{4,7},{5,4},{6,5},{7,6},{8,11},{9,8},{10,9... | collective-permute-start | bytes 393224 | tf_op jit(solution)/shard_map/ppermute | solution.py:38

commit v5 on v4

--- a/solution.py
+++ b/solution.py
@@ -12,7 +12,7 @@
 LEV = 4
 NZ, NC, NX, NY = 4, 2, 4, 4
 BOTH = ("prow", "pcol")
-UNROLL = 16
+WHOLE, SHORT = 32, 8
 ORDER = (2, 1, 3)
 
 
@@ -75,7 +75,7 @@
     )(*scalars, *[near(value) for value in operands])
 
 
-def pair_kernel(index, n_in, n_out, flip, has_init, waits, take, put, live, *refs):
+def pair_kernel(index, unroll, n_in, n_out, flip, has_init, waits, take, put, live, *refs):
     vectors, refs = refs[:n_in], refs[n_in:]
     blocks, refs = refs[0], refs[1:]
     init, refs = (refs[:n_out], refs[n_out:]) if has_init else ((), refs)
@@ -100,9 +100,9 @@
             else:
                 total[k * per + unit] = jnp.zeros((W, R), jnp.float32)
 
-    @pl.loop(0, blocks.shape[1], step=UNROLL)
+    @pl.loop(0, blocks.shape[1], step=unroll)
     def _(start):
-        for j in range(UNROLL):
+        for j in range(unroll):
             slot = start + j
             block = jnp.where(live[slot] > 0, blocks[index, slot], 0.0)
             if flip:
@@ -121,11 +121,11 @@
             outs[k][unit] = total[k * per + unit]
 
 
-def pair_product(index, flip, scalars, vectors, blocks, init, after, n_out, total):
+def pair_product(index, unroll, flip, scalars, vectors, blocks, init, after, n_out, total):
     n_in = len(vectors)
     units = n_in * vectors[0].shape[0]
     return fast_call(
-        functools.partial(pair_kernel, index, n_in, n_out, flip, init is not None, len(after)),
+        functools.partial(pair_kernel, index, unroll, n_in, n_out, flip, init is not None, len(after)),
         [(total // n_out, W, R)] * n_out,
         [*vectors, blocks, *(init or ()), *after],
         scalars,
@@ -289,12 +289,14 @@
     def forth(high, low, vectors, init):
         index = pair_index(high, low)
         scalars = (take_plane[index], put_z[index], live[index])
-        return pair_product(index, False, scalars, vectors, panels, init, (), 2, 8)
+        unroll = WHOLE if high == low + 1 else SHORT
+        return pair_product(index, unroll, False, scalars, vectors, panels, init, (), 2, 8)
 
     def back(high, low, vectors, init, after):
         index = pair_index(high, low)
         scalars = (take_z[index], put_plane[index], live[index])
-        return pair_product(index, True, scalars, vectors, panels, init, after, 4, 16)
+        unroll = WHOLE if high == low + 1 else SHORT
+        return pair_product(index, unroll, True, scalars, vectors, panels, init, after, 4, 16)
 
     top = LEV - 1
     solved = [None] * LEV

time: 243 us -> 243 us (level)
  transfers between devices with their start and end apart: 60 -> 60, of which waited for: 49 -> 47; matrix products, arithmetic and copies ran while one was open for 1% -> 1% of each run, Pallas kernels for 8% -> 9%
where the time goes in v5:
time: 243 us; the launch traced here: 242 us
  waiting for transfers between devices  103 us (42%)
  starting transfers between devices  93.5 us (38%)
  Pallas kernels  40.5 us (17%)
  other arithmetic  4 us (2%)
    ppermute x36, waiting for transfers between devices, shift_plane(): return lax.ppermute(value, BOTH, pairs)  67.1 us
    ppermute x36, starting transfers between devices, shift_plane(): return lax.ppermute(value, BOTH, pairs)  59.7 us
    pallas_call x24, Pallas kernels, fast_call(): pl.pallas_call(kernel, in_specs=[pl.BlockSpec(memory_space=pltpu.SMEM)] *...  34.6 us
    ppermute x18, starting transfers between devices, shift_z(): return lax.ppermute(value, 'prow', pairs)  33.2 us
    ppermute x18, waiting for transfers between devices, shift_z(): return lax.ppermute(value, 'prow', pairs)  24.9 us
    ppermute x6, waiting for transfers between devices, swap_core(): return lax.ppermute(value, 'prow', pairs)  11.4 us
  transfers between devices with their start and end apart: 60, of which 47 were waited for; matrix products, arithmetic and copies ran while one was open for 1% of the time, Pallas kernels for 9%

profile of v5, /device:TPU:0, one launch (start us, length us, event | category | flops | bytes accessed | tf_op | source)
XLA Modules:
  0.0 242.4 jit_solution(5013771907710387265)
XLA Ops:
  5.2 1.9 collective-permute-start
  8.5 3.2 %collective-permute-done = f32[128,256]{1,0:T(8,128)S(1)} collective-permute-done((f32[128,256]{1,0:T(8,128)S(1)}, f32[128,256]{1,0:T(8,128)S(1)}, u32[]{:S(2)}, u32[]{:S(2)}) %collective-permute-start) | collective-permute-done | bytes 131104 | tf_op jit(solution)/shard_map/ppermute | solution.py:38
  11.7 3.4 %collective-permute-start.3 = (f32[4,128,256]{2,1,0:T(8,128)S(1)}, f32[4,128,256]{2,1,0:T(8,128)S(1)}, u32[]{:S(2)}, u32[]{:S(2)}) collective-permute-start(f32[4,128,256]{2,1,0:T(8,128)S(1)} %fusion.4.after.refs_0_), channel_id=1, source_target_pairs={{0,2},{1,3},{2,0},{3,1},{4,6},{5,7},{6,4},{7,5},{8,10},{9,11},{10,... | collective-permute-start | bytes 1572872 | tf_op jit(solution)/shard_map/ppermute | solution.py:38
  15.7 2.6 %collective-permute-start.5 = (f32[4,128,256]{2,1,0:T(8,128)S(1)}, f32[4,128,256]{2,1,0:T(8,128)S(1)}, u32[]{:S(2)}, u32[]{:S(2)}) collective-permute-start(f32[4,128,256]{2,1,0:T(8,128)S(1)} %fusion.4.after.refs_0_), channel_id=1, source_target_pairs={{0,3},{1,0},{2,1},{3,2},{4,7},{5,4},{6,5},{7,6},{8,11},{9,8},{10,9... | collective-permute-start | bytes 1572872 | tf_op jit(solution)/shard_map/ppermute | solution.py:38
  19.0 4.7 %shard_map.69.refs_4_.refs_2_ = f32[6,32,128,128]{3,2,1,0:T(8,128)S(1)} custom-call(f32[6,32,128,128]{3,2,1,0:T(8,128)} %bitcast.202, f32[4,128,256]{2,1,0:T(8,128)S(1)} %fusion.4.after.refs_0_), custom_call_target="tpu_custom_call" | custom-call | bytes 12582912 | tf_op jit(solution)/shard_map/pallas_call | solution.py:225
  23.8 4.3 %collective-permute-done.4.refs_2_ = f32[4,128,256]{2,1,0:T(8,128)S(1)} collective-permute-done((f32[4,128,256]{2,1,0:T(8,128)S(1)}, f32[4,128,256]{2,1,0:T(8,128)S(1)}, u32[]{:S(2)}, u32[]{:S(2)}) %collective-permute-start.4) | collective-permute-done | bytes 524320 | tf_op jit(solution)/shard_map/ppermute | solution.py:38
  28.5 2.3 shard_map.70
  31.0 1.9 collective-permute-done.6.refs_1_
  32.9 4.0 %collective-permute-start.7 = (f32[128,256]{1,0:T(8,128)S(1)}, f32[128,256]{1,0:T(8,128)S(1)}, u32[]{:S(2)}, u32[]{:S(2)}) collective-permute-start(f32[128,256]{1,0:T(8,128)S(1)} %get-tuple-element.67), channel_id=1, source_target_pairs={{0,64},{16,80},{32,96},{48,112},{64,0},{80,16},{96,32},{112,48},{1... | collective-permute-start | bytes 393224 | tf_op jit(solution)/shard_map/ppermute | solution.py:43
  37.9 2.2 collective-permute-start.9
  41.2 2.5 %collective-permute-done.8.refs_2_ = f32[128,256]{1,0:T(8,128)S(1)} collective-permute-done((f32[128,256]{1,0:T(8,128)S(1)}, f32[128,256]{1,0:T(8,128)S(1)}, u32[]{:S(2)}, u32[]{:S(2)}) %collective-permute-start.8) | collective-permute-done | bytes 131104 | tf_op jit(solution)/shard_map/ppermute | solution.py:43
  44.5 1.9 collective-permute-start.10
  47.0 2.6 %collective-permute-start.12 = (f32[128,256]{1,0:T(8,128)S(1)}, f32[128,256]{1,0:T(8,128)S(1)}, u32[]{:S(2)}, u32[]{:S(2)}) collective-permute-start(f32[128,256]{1,0:T(8,128)S(1)} %shard_map.72.base), channel_id=1, source_target_pairs={{0,12},{1,13},{2,14},{3,15},{4,0},{5,1},{6,2},{7,3},{8,4},{9,5},{1... | collective-permute-start | bytes 393224 | tf_op jit(solution)/shard_map/ppermute | solution.py:38
  52.6 2.1 collective-permute-start.13
  56.2 1.8 collective-permute-start.15
  58.0 2.9 %shard_map.73 = (f32[4,128,256]{2,1,0:T(8,128)S(1)}, f32[4,128,256]{2,1,0:T(8,128)S(1)}) custom-call(s32[32]{0:T(128)S(1)} %get-tuple-element.164.take, s32[32]{0:T(128)S(1)} %get-tuple-element.149.put, s32[32]{0:T(128)S(1)} %get-tuple-element.143.live, f32[4,128,256]{2,1,0:T(8,128)S(1)} %fusion.4.after.refs_0_, ...), custom_call_target="tpu_custom_call" | custom-call | flops 1073741824 | bytes 4096 | tf_op jit(solution)/shard_map/pallas_call | solution.py:66
  60.8 2.7 %collective-permute-done.13.refs_1_ = f32[4,128,256]{2,1,0:T(8,128)S(1)} collective-permute-done((f32[4,128,256]{2,1,0:T(8,128)S(1)}, f32[4,128,256]{2,1,0:T(8,128)S(1)}, u32[]{:S(2)}, u32[]{:S(2)}) %collective-permute-start.13) | collective-permute-done | bytes 524320 | tf_op jit(solution)/shard_map/ppermute | solution.py:38
  63.5 5.5 %collective-permute-done.14.refs_2_ = f32[4,128,256]{2,1,0:T(8,128)S(1)} collective-permute-done((f32[4,128,256]{2,1,0:T(8,128)S(1)}, f32[4,128,256]{2,1,0:T(8,128)S(1)}, u32[]{:S(2)}, u32[]{:S(2)}) %collective-permute-start.14) | collective-permute-done | bytes 524320 | tf_op jit(solution)/shard_map/ppermute | solution.py:38
  69.0 2.3 shard_map.74
  71.5 1.9 collective-permute-done.16.refs_1_
  73.4 2.2 collective-permute-start.17
  78.8 2.5 %collective-permute-done.17.refs_1_ = f32[128,256]{1,0:T(8,128)S(1)} collective-permute-done((f32[128,256]{1,0:T(8,128)S(1)}, f32[128,256]{1,0:T(8,128)S(1)}, u32[]{:S(2)}, u32[]{:S(2)}) %collective-permute-start.17) | collective-permute-done | bytes 131104 | tf_op jit(solution)/shard_map/ppermute | solution.py:43
  81.3 2.0 collective-permute-done.18.refs_2_
  83.7 1.8 collective-permute-start.20
  85.5 2.4 collective-permute-start.21
  92.9 2.3 collective-permute-start.23
  96.7 1.8 collective-permute-start.25
  98.5 2.9 %shard_map.77 = (f32[4,128,256]{2,1,0:T(8,128)S(1)}, f32[4,128,256]{2,1,0:T(8,128)S(1)}) custom-call(s32[32]{0:T(128)S(1)} %get-tuple-element.167.take, s32[32]{0:T(128)S(1)} %get-tuple-element.146.put, s32[32]{0:T(128)S(1)} %get-tuple-element.140.live, f32[4,128,256]{2,1,0:T(8,128)S(1)} %fusion.4.after.refs_0_, ...), custom_call_target="tpu_custom_call" | custom-call | flops 1073741824 | bytes 4096 | tf_op jit(solution)/shard_map/pallas_call | solution.py:66
  101.3 2.9 %shard_map.78 = (f32[4,128,256]{2,1,0:T(8,128)S(1)}, f32[4,128,256]{2,1,0:T(8,128)S(1)}) custom-call(s32[32]{0:T(128)S(1)} %get-tuple-element.166.take, s32[32]{0:T(128)S(1)} %get-tuple-element.147.put, s32[32]{0:T(128)S(1)} %get-tuple-element.141.live, f32[4,128,256]{2,1,0:T(8,128)S(1)} %pad_maximum_fusion.2.refs_0_, ...), custom_call_target="tpu_custom_call" | custom-call | flops 1073741824 | bytes 4096 | tf_op jit(solution)/shard_map/pallas_call | solution.py:66
  104.2 5.3 %collective-permute-done.24.refs_2_ = f32[4,128,256]{2,1,0:T(8,128)S(1)} collective-permute-done((f32[4,128,256]{2,1,0:T(8,128)S(1)}, f32[4,128,256]{2,1,0:T(8,128)S(1)}, u32[]{:S(2)}, u32[]{:S(2)}) %collective-permute-start.24) | collective-permute-done | bytes 524320 | tf_op jit(solution)/shard_map/ppermute | solution.py:38
  109.5 2.3 shard_map.79
  111.9 1.9 collective-permute-done.26.refs_1_
  113.9 2.1 collective-permute-start.27
  119.2 2.6 %collective-permute-done.27.refs_1_ = f32[128,256]{1,0:T(8,128)S(1)} collective-permute-done((f32[128,256]{1,0:T(8,128)S(1)}, f32[128,256]{1,0:T(8,128)S(1)}, u32[]{:S(2)}, u32[]{:S(2)}) %collective-permute-start.27) | collective-permute-done | bytes 131104 | tf_op jit(solution)/shard_map/ppermute | solution.py:43
  121.8 2.0 collective-permute-done.28.refs_2_
  124.5 2.1 collective-permute-start.30
  129.8 2.7 %collective-permute-done.30 = f32[128,256]{1,0:T(8,128)S(1)} collective-permute-done((f32[128,256]{1,0:T(8,128)S(1)}, f32[128,256]{1,0:T(8,128)S(1)}, u32[]{:S(2)}, u32[]{:S(2)}) %collective-permute-start.30) | collective-permute-done | bytes 131104 | tf_op jit(solution)/shard_map/ppermute | solution.py:43
  134.3 1.9 collective-permute-done.33.refs_1_
  136.2 2.4 shard_map.82
  139.3 2.2 collective-permute-start.35
  142.6 6.9 %collective-permute-done.34.refs_3_.refs_1_ = f32[4,128,256]{2,1,0:T(8,128)S(1)} collective-permute-done((f32[4,128,256]{2,1,0:T(8,128)S(1)}, f32[4,128,256]{2,1,0:T(8,128)S(1)}, u32[]{:S(2)}, u32[]{:S(2)}) %collective-permute-start.34) | collective-permute-done | bytes 524320 | tf_op jit(solution)/shard_map/ppermute | solution.py:38
  149.4 3.0 %shard_map.84 = (f32[4,128,256]{2,1,0:T(8,128)S(1)}, f32[4,128,256]{2,1,0:T(8,128)S(1)}, f32[4,128,256]{2,1,0:T(8,128)S(1)}, f32[4,128,256]{2,1,0:T(8,128)S(1)}) custom-call(s32[32]{0:T(128)S(1)} %get-tuple-element.171.take, s32[32]{0:T(128)S(1)} %get-tuple-element.130.put, s32[32]{0:T(128)S(1)} %get-tuple-element.140.live, ...), custom_call_target="tpu_custom_call" | custom-call | flops 1073741824 | bytes 4096 | tf_op jit(solution)/shard_map/pallas_call | solution.py:66
  152.5 3.1 %shard_map.83 = (f32[4,128,256]{2,1,0:T(8,128)S(1)}, f32[4,128,256]{2,1,0:T(8,128)S(1)}, f32[4,128,256]{2,1,0:T(8,128)S(1)}, f32[4,128,256]{2,1,0:T(8,128)S(1)}) custom-call(s32[32]{0:T(128)S(1)} %get-tuple-element.170.take, s32[32]{0:T(128)S(1)} %get-tuple-element.131.put, s32[32]{0:T(128)S(1)} %get-tuple-element.141.live, ...), custom_call_target="tpu_custom_call" | custom-call | flops 1073741824 | bytes 4096 | tf_op jit(solution)/shard_map/pallas_call | solution.py:66
  155.7 2.1 collective-permute-start.37
  159.3 1.8 collective-permute-start.39
  162.3 1.7 collective-permute-done.38.refs_2_
  164.6 1.8 collective-permute-start.40
  166.4 1.9 collective-permute-start.41
  173.4 1.9 collective-permute-done.43.refs_1_
  175.3 2.4 shard_map.87
  178.4 2.2 collective-permute-start.45
  181.6 6.9 %collective-permute-done.44.refs_7_.refs_1_ = f32[4,128,256]{2,1,0:T(8,128)S(1)} collective-permute-done((f32[4,128,256]{2,1,0:T(8,128)S(1)}, f32[4,128,256]{2,1,0:T(8,128)S(1)}, u32[]{:S(2)}, u32[]{:S(2)}) %collective-permute-start.44) | collective-permute-done | bytes 524320 | tf_op jit(solution)/shard_map/ppermute | solution.py:38
  188.5 3.1 %shard_map.88 = (f32[4,128,256]{2,1,0:T(8,128)S(1)}, f32[4,128,256]{2,1,0:T(8,128)S(1)}, f32[4,128,256]{2,1,0:T(8,128)S(1)}, f32[4,128,256]{2,1,0:T(8,128)S(1)}) custom-call(s32[32]{0:T(128)S(1)} %get-tuple-element.172.take, s32[32]{0:T(128)S(1)} %get-tuple-element.129.put, s32[32]{0:T(128)S(1)} %get-tuple-element.143.live, ...), custom_call_target="tpu_custom_call" | custom-call | flops 1073741824 | bytes 4096 | tf_op jit(solution)/shard_map/pallas_call | solution.py:66
  191.6 2.4 %collective-permute-done.45.refs_2_ = f32[4,128,256]{2,1,0:T(8,128)S(1)} collective-permute-done((f32[4,128,256]{2,1,0:T(8,128)S(1)}, f32[4,128,256]{2,1,0:T(8,128)S(1)}, u32[]{:S(2)}, u32[]{:S(2)}) %collective-permute-start.45) | collective-permute-done | bytes 524320 | tf_op jit(solution)/shard_map/ppermute | solution.py:38
  194.2 2.1 collective-permute-start.47
  196.2 1.9 collective-permute-start.48
  203.4 1.8 collective-permute-start.50
  205.2 1.8 collective-permute-start.51
  212.0 1.9 collective-permute-done.53.refs_1_
  213.9 2.4 shard_map.91
  217.1 2.2 collective-permute-start.55
  220.3 6.9 %collective-permute-done.54.refs_1_ = f32[4,128,256]{2,1,0:T(8,128)S(1)} collective-permute-done((f32[4,128,256]{2,1,0:T(8,128)S(1)}, f32[4,128,256]{2,1,0:T(8,128)S(1)}, u32[]{:S(2)}, u32[]{:S(2)}) %collective-permute-start.54) | collective-permute-done | bytes 524320 | tf_op jit(solution)/shard_map/ppermute | solution.py:38
  227.2 5.5 %collective-permute-done.55.refs_2_ = f32[4,128,256]{2,1,0:T(8,128)S(1)} collective-permute-done((f32[4,128,256]{2,1,0:T(8,128)S(1)}, f32[4,128,256]{2,1,0:T(8,128)S(1)}, u32[]{:S(2)}, u32[]{:S(2)}) %collective-permute-start.55) | collective-permute-done | bytes 524320 | tf_op jit(solution)/shard_map/ppermute | solution.py:38
  233.9 2.4 collective-permute-start.58
  (100 shorter events, 67.0 us)
Async XLA Ops:
  1.9 6.6 %collective-permute-start.1 = (f32[128,256]{1,0:T(8,128)S(1)}, f32[128,256]{1,0:T(8,128)S(1)}, u32[]{:S(2)}, u32[]{:S(2)}) collective-permute-start(f32[128,256]{1,0:T(8,128)S(1)} %shard_map.68.base), channel_id=1, source_target_pairs={{0,4},{1,5},{2,6},{3,7},{4,8},{5,9},{6,10},{7,11},{8,12},{9,13},{1... | collective-permute-start | bytes 393224 | tf_op jit(solution)/shard_map/ppermute | solution.py:38
  3.5 5.0 %collective-permute-start.2 = (f32[128,256]{1,0:T(8,128)S(1)}, f32[128,256]{1,0:T(8,128)S(1)}, u32[]{:S(2)}, u32[]{:S(2)}) collective-permute-start(f32[128,256]{1,0:T(8,128)S(1)} %shard_map.68.base), channel_id=1, source_target_pairs={{0,12},{1,13},{2,14},{3,15},{4,0},{5,1},{6,2},{7,3},{8,4},{9,5},{1... | collective-permute-start | bytes 393224 | tf_op jit(solution)/shard_map/ppermute | solution.py:38
  5.2 6.5 %collective-permute-start = (f32[128,256]{1,0:T(8,128)S(1)}, f32[128,256]{1,0:T(8,128)S(1)}, u32[]{:S(2)}, u32[]{:S(2)}) collective-permute-start(f32[128,256]{1,0:T(8,128)S(1)} %shard_map.68.base), channel_id=1, source_target_pairs={{0,8},{1,9},{2,10},{3,11},{4,12},{5,13},{6,14},{7,15},{8,0},{9,1},... | collective-permute-start | bytes 393224 | tf_op jit(solution)/shard_map/ppermute | solution.py:38
  11.7 12.1 %collective-permute-start.3 = (f32[4,128,256]{2,1,0:T(8,128)S(1)}, f32[4,128,256]{2,1,0:T(8,128)S(1)}, u32[]{:S(2)}, u32[]{:S(2)}) collective-permute-start(f32[4,128,256]{2,1,0:T(8,128)S(1)} %fusion.4.after.refs_0_), channel_id=1, source_target_pairs={{0,2},{1,3},{2,0},{3,1},{4,6},{5,7},{6,4},{7,5},{8,10},{9,11},{10,... | collective-permute-start | bytes 1572872 | tf_op jit(solution)/shard_map/ppermute | solution.py:38
  15.0 13.0 %collective-permute-start.4 = (f32[4,128,256]{2,1,0:T(8,128)S(1)}, f32[4,128,256]{2,1,0:T(8,128)S(1)}, u32[]{:S(2)}, u32[]{:S(2)}) collective-permute-start(f32[4,128,256]{2,1,0:T(8,128)S(1)} %fusion.4.after.refs_0_), channel_id=1, source_target_pairs={{0,1},{1,2},{2,3},{3,0},{4,5},{5,6},{6,7},{7,4},{8,9},{9,10},{10,1... | collective-permute-start | bytes 1572872 | tf_op jit(solution)/shard_map/ppermute | solution.py:38
  15.7 12.8 %collective-permute-start.5 = (f32[4,128,256]{2,1,0:T(8,128)S(1)}, f32[4,128,256]{2,1,0:T(8,128)S(1)}, u32[]{:S(2)}, u32[]{:S(2)}) collective-permute-start(f32[4,128,256]{2,1,0:T(8,128)S(1)} %fusion.4.after.refs_0_), channel_id=1, source_target_pairs={{0,3},{1,0},{2,1},{3,2},{4,7},{5,4},{6,5},{7,6},{8,11},{9,8},{10,9... | collective-permute-start | bytes 1572872 | tf_op jit(solution)/shard_map/ppermute | solution.py:38
  23.7 20.5 %copy-start = (f32[4,1,1,128,128]{4,3,2,1,0:T(8,128)S(1)}, f32[4,1,1,128,128]{4,3,2,1,0:T(8,128)}, u32[]{:S(2)}) copy-start(f32[4,1,1,128,128]{4,3,2,1,0:T(8,128)} %param.6) | copy-start | bytes 786436
  23.7 20.5 %copy-start.1 = (f32[4,1,1,128,256]{4,3,2,1,0:T(8,128)S(1)}, f32[4,1,1,128,256]{4,3,2,1,0:T(8,128)}, u32[]{:S(2)}) copy-start(f32[4,1,1,128,256]{4,3,2,1,0:T(8,128)} %param.5) | copy-start | bytes 1572868
  30.9 2.0 collective-permute-start.6
  32.9 8.2 %collective-permute-start.7 = (f32[128,256]{1,0:T(8,128)S(1)}, f32[128,256]{1,0:T(8,128)S(1)}, u32[]{:S(2)}, u32[]{:S(2)}) collective-permute-start(f32[128,256]{1,0:T(8,128)S(1)} %get-tuple-element.67), channel_id=1, source_target_pairs={{0,64},{16,80},{32,96},{48,112},{64,0},{80,16},{96,32},{112,48},{1... | collective-permute-start | bytes 393224 | tf_op jit(solution)/shard_map/ppermute | solution.py:43
  36.9 6.8 %collective-permute-start.8 = (f32[128,256]{1,0:T(8,128)S(1)}, f32[128,256]{1,0:T(8,128)S(1)}, u32[]{:S(2)}, u32[]{:S(2)}) collective-permute-start(f32[128,256]{1,0:T(8,128)S(1)} %get-tuple-element.68), channel_id=1, source_target_pairs={{0,32},{16,48},{32,64},{48,80},{64,96},{80,112},{96,0},{112,16},{1... | collective-permute-start | bytes 393224 | tf_op jit(solution)/shard_map/ppermute | solution.py:43
  37.9 6.3 %collective-permute-start.9 = (f32[128,256]{1,0:T(8,128)S(1)}, f32[128,256]{1,0:T(8,128)S(1)}, u32[]{:S(2)}, u32[]{:S(2)}) collective-permute-start(f32[128,256]{1,0:T(8,128)S(1)} %get-tuple-element.69), channel_id=1, source_target_pairs={{0,96},{16,112},{32,0},{48,16},{64,32},{80,48},{96,64},{112,80},{1... | collective-permute-start | bytes 393224 | tf_op jit(solution)/shard_map/ppermute | solution.py:43
  44.5 6.6 %collective-permute-start.10 = (f32[128,256]{1,0:T(8,128)S(1)}, f32[128,256]{1,0:T(8,128)S(1)}, u32[]{:S(2)}, u32[]{:S(2)}) collective-permute-start(f32[128,256]{1,0:T(8,128)S(1)} %shard_map.72.base), channel_id=1, source_target_pairs={{0,8},{1,9},{2,10},{3,11},{4,12},{5,13},{6,14},{7,15},{8,0},{9,1},... | collective-permute-start | bytes 393224 | tf_op jit(solution)/shard_map/ppermute | solution.py:38
  46.4 6.2 %collective-permute-start.11 = (f32[128,256]{1,0:T(8,128)S(1)}, f32[128,256]{1,0:T(8,128)S(1)}, u32[]{:S(2)}, u32[]{:S(2)}) collective-permute-start(f32[128,256]{1,0:T(8,128)S(1)} %shard_map.72.base), channel_id=1, source_target_pairs={{0,4},{1,5},{2,6},{3,7},{4,8},{5,9},{6,10},{7,11},{8,12},{9,13},{1... | collective-permute-start | bytes 393224 | tf_op jit(solution)/shard_map/ppermute | solution.py:38
  47.0 5.6 %collective-permute-start.12 = (f32[128,256]{1,0:T(8,128)S(1)}, f32[128,256]{1,0:T(8,128)S(1)}, u32[]{:S(2)}, u32[]{:S(2)}) collective-permute-start(f32[128,256]{1,0:T(8,128)S(1)} %shard_map.72.base), channel_id=1, source_target_pairs={{0,12},{1,13},{2,14},{3,15},{4,0},{5,1},{6,2},{7,3},{8,4},{9,5},{1... | collective-permute-start | bytes 393224 | tf_op jit(solution)/shard_map/ppermute | solution.py:38
  52.6 10.9 %collective-permute-start.13 = (f32[4,128,256]{2,1,0:T(8,128)S(1)}, f32[4,128,256]{2,1,0:T(8,128)S(1)}, u32[]{:S(2)}, u32[]{:S(2)}) collective-permute-start(f32[4,128,256]{2,1,0:T(8,128)S(1)} %pad_maximum_fusion.2.refs_0_), channel_id=1, source_target_pairs={{0,2},{1,3},{2,0},{3,1},{4,6},{5,7},{6,4},{7,5},{8,10},{9,11},{10,... | collective-permute-start | bytes 1572872 | tf_op jit(solution)/shard_map/ppermute | solution.py:38
  54.7 14.3 %collective-permute-start.14 = (f32[4,128,256]{2,1,0:T(8,128)S(1)}, f32[4,128,256]{2,1,0:T(8,128)S(1)}, u32[]{:S(2)}, u32[]{:S(2)}) collective-permute-start(f32[4,128,256]{2,1,0:T(8,128)S(1)} %pad_maximum_fusion.2.refs_0_), channel_id=1, source_target_pairs={{0,1},{1,2},{2,3},{3,0},{4,5},{5,6},{6,7},{7,4},{8,9},{9,10},{10,1... | collective-permute-start | bytes 1572872 | tf_op jit(solution)/shard_map/ppermute | solution.py:38
  56.2 12.8 %collective-permute-start.15 = (f32[4,128,256]{2,1,0:T(8,128)S(1)}, f32[4,128,256]{2,1,0:T(8,128)S(1)}, u32[]{:S(2)}, u32[]{:S(2)}) collective-permute-start(f32[4,128,256]{2,1,0:T(8,128)S(1)} %pad_maximum_fusion.2.refs_0_), channel_id=1, source_target_pairs={{0,3},{1,0},{2,1},{3,2},{4,7},{5,4},{6,5},{7,6},{8,11},{9,8},{10,9... | collective-permute-start | bytes 1572872 | tf_op jit(solution)/shard_map/ppermute | solution.py:38
  71.4 2.0 collective-permute-start.16
  73.4 7.9 %collective-permute-start.17 = (f32[128,256]{1,0:T(8,128)S(1)}, f32[128,256]{1,0:T(8,128)S(1)}, u32[]{:S(2)}, u32[]{:S(2)}) collective-permute-start(f32[128,256]{1,0:T(8,128)S(1)} %get-tuple-element.75), channel_id=1, source_target_pairs={{0,64},{16,80},{32,96},{48,112},{64,0},{80,16},{96,32},{112,48},{1... | collective-permute-start | bytes 393224 | tf_op jit(solution)/shard_map/ppermute | solution.py:43
  75.6 7.8 %collective-permute-start.18 = (f32[128,256]{1,0:T(8,128)S(1)}, f32[128,256]{1,0:T(8,128)S(1)}, u32[]{:S(2)}, u32[]{:S(2)}) collective-permute-start(f32[128,256]{1,0:T(8,128)S(1)} %get-tuple-element.76), channel_id=1, source_target_pairs={{0,32},{16,48},{32,64},{48,80},{64,96},{80,112},{96,0},{112,16},{1... | collective-permute-start | bytes 393224 | tf_op jit(solution)/shard_map/ppermute | solution.py:43
  77.1 6.3 %collective-permute-start.19 = (f32[128,256]{1,0:T(8,128)S(1)}, f32[128,256]{1,0:T(8,128)S(1)}, u32[]{:S(2)}, u32[]{:S(2)}) collective-permute-start(f32[128,256]{1,0:T(8,128)S(1)} %get-tuple-element.77), channel_id=1, source_target_pairs={{0,96},{16,112},{32,0},{48,16},{64,32},{80,48},{96,64},{112,80},{1... | collective-permute-start | bytes 393224 | tf_op jit(solution)/shard_map/ppermute | solution.py:43
  83.7 6.6 %collective-permute-start.20 = (f32[128,256]{1,0:T(8,128)S(1)}, f32[128,256]{1,0:T(8,128)S(1)}, u32[]{:S(2)}, u32[]{:S(2)}) collective-permute-start(f32[128,256]{1,0:T(8,128)S(1)} %shard_map.76.base), channel_id=1, source_target_pairs={{0,8},{1,9},{2,10},{3,11},{4,12},{5,13},{6,14},{7,15},{8,0},{9,1},... | collective-permute-start | bytes 393224 | tf_op jit(solution)/shard_map/ppermute | solution.py:38
  85.5 6.2 %collective-permute-start.21 = (f32[128,256]{1,0:T(8,128)S(1)}, f32[128,256]{1,0:T(8,128)S(1)}, u32[]{:S(2)}, u32[]{:S(2)}) collective-permute-start(f32[128,256]{1,0:T(8,128)S(1)} %shard_map.76.base), channel_id=1, source_target_pairs={{0,4},{1,5},{2,6},{3,7},{4,8},{5,9},{6,10},{7,11},{8,12},{9,13},{1... | collective-permute-start | bytes 393224 | tf_op jit(solution)/shard_map/ppermute | solution.py:38
  87.9 5.0 %collective-permute-start.22 = (f32[128,256]{1,0:T(8,128)S(1)}, f32[128,256]{1,0:T(8,128)S(1)}, u32[]{:S(2)}, u32[]{:S(2)}) collective-permute-start(f32[128,256]{1,0:T(8,128)S(1)} %shard_map.76.base), channel_id=1, source_target_pairs={{0,12},{1,13},{2,14},{3,15},{4,0},{5,1},{6,2},{7,3},{8,4},{9,5},{1... | collective-permute-start | bytes 393224 | tf_op jit(solution)/shard_map/ppermute | solution.py:38
  92.9 11.3 %collective-permute-start.23 = (f32[4,128,256]{2,1,0:T(8,128)S(1)}, f32[4,128,256]{2,1,0:T(8,128)S(1)}, u32[]{:S(2)}, u32[]{:S(2)}) collective-permute-start(f32[4,128,256]{2,1,0:T(8,128)S(1)} %pad_maximum_fusion.3.refs_0_), channel_id=1, source_target_pairs={{0,2},{1,3},{2,0},{3,1},{4,6},{5,7},{6,4},{7,5},{8,10},{9,11},{10,... | collective-permute-start | bytes 1572872 | tf_op jit(solution)/shard_map/ppermute | solution.py:38
  95.2 14.3 %collective-permute-start.24 = (f32[4,128,256]{2,1,0:T(8,128)S(1)}, f32[4,128,256]{2,1,0:T(8,128)S(1)}, u32[]{:S(2)}, u32[]{:S(2)}) collective-permute-start(f32[4,128,256]{2,1,0:T(8,128)S(1)} %pad_maximum_fusion.3.refs_0_), channel_id=1, source_target_pairs={{0,1},{1,2},{2,3},{3,0},{4,5},{5,6},{6,7},{7,4},{8,9},{9,10},{10,1... | collective-permute-start | bytes 1572872 | tf_op jit(solution)/shard_map/ppermute | solution.py:38
  96.7 12.8 %collective-permute-start.25 = (f32[4,128,256]{2,1,0:T(8,128)S(1)}, f32[4,128,256]{2,1,0:T(8,128)S(1)}, u32[]{:S(2)}, u32[]{:S(2)}) collective-permute-start(f32[4,128,256]{2,1,0:T(8,128)S(1)} %pad_maximum_fusion.3.refs_0_), channel_id=1, source_target_pairs={{0,3},{1,0},{2,1},{3,2},{4,7},{5,4},{6,5},{7,6},{8,11},{9,8},{10,9... | collective-permute-start | bytes 1572872 | tf_op jit(solution)/shard_map/ppermute | solution.py:38
  111.8 2.0 collective-permute-start.26
  113.9 7.9 %collective-permute-start.27 = (f32[128,256]{1,0:T(8,128)S(1)}, f32[128,256]{1,0:T(8,128)S(1)}, u32[]{:S(2)}, u32[]{:S(2)}) collective-permute-start(f32[128,256]{1,0:T(8,128)S(1)} %get-tuple-element.85), channel_id=1, source_target_pairs={{0,64},{16,80},{32,96},{48,112},{64,0},{80,16},{96,32},{112,48},{1... | collective-permute-start | bytes 393224 | tf_op jit(solution)/shard_map/ppermute | solution.py:43
  115.9 7.9 %collective-permute-start.28 = (f32[128,256]{1,0:T(8,128)S(1)}, f32[128,256]{1,0:T(8,128)S(1)}, u32[]{:S(2)}, u32[]{:S(2)}) collective-permute-start(f32[128,256]{1,0:T(8,128)S(1)} %get-tuple-element.86), channel_id=1, source_target_pairs={{0,32},{16,48},{32,64},{48,80},{64,96},{80,112},{96,0},{112,16},{1... | collective-permute-start | bytes 393224 | tf_op jit(solution)/shard_map/ppermute | solution.py:43
  117.5 6.3 %collective-permute-start.29 = (f32[128,256]{1,0:T(8,128)S(1)}, f32[128,256]{1,0:T(8,128)S(1)}, u32[]{:S(2)}, u32[]{:S(2)}) collective-permute-start(f32[128,256]{1,0:T(8,128)S(1)} %get-tuple-element.87), channel_id=1, source_target_pairs={{0,96},{16,112},{32,0},{48,16},{64,32},{80,48},{96,64},{112,80},{1... | collective-permute-start | bytes 393224 | tf_op jit(solution)/shard_map/ppermute | solution.py:43
  124.5 8.0 %collective-permute-start.30 = (f32[128,256]{1,0:T(8,128)S(1)}, f32[128,256]{1,0:T(8,128)S(1)}, u32[]{:S(2)}, u32[]{:S(2)}) collective-permute-start(f32[128,256]{1,0:T(8,128)S(1)} %get-tuple-element.89), channel_id=1, source_target_pairs={{0,64},{16,80},{32,96},{48,112},{64,0},{80,16},{96,32},{112,48},{1... | collective-permute-start | bytes 393224 | tf_op jit(solution)/shard_map/ppermute | solution.py:43
  126.6 7.6 %collective-permute-start.31 = (f32[128,256]{1,0:T(8,128)S(1)}, f32[128,256]{1,0:T(8,128)S(1)}, u32[]{:S(2)}, u32[]{:S(2)}) collective-permute-start(f32[128,256]{1,0:T(8,128)S(1)} %get-tuple-element.89), channel_id=1, source_target_pairs={{0,32},{16,48},{32,64},{48,80},{64,96},{80,112},{96,0},{112,16},{1... | collective-permute-start | bytes 393224 | tf_op jit(solution)/shard_map/ppermute | solution.py:43
  128.1 6.0 %collective-permute-start.32 = (f32[128,256]{1,0:T(8,128)S(1)}, f32[128,256]{1,0:T(8,128)S(1)}, u32[]{:S(2)}, u32[]{:S(2)}) collective-permute-start(f32[128,256]{1,0:T(8,128)S(1)} %get-tuple-element.89), channel_id=1, source_target_pairs={{0,96},{16,112},{32,0},{48,16},{64,32},{80,48},{96,64},{112,80},{1... | collective-permute-start | bytes 393224 | tf_op jit(solution)/shard_map/ppermute | solution.py:43
  134.2 2.0 collective-permute-start.33
  138.6 10.9 %collective-permute-start.34 = (f32[4,128,256]{2,1,0:T(8,128)S(1)}, f32[4,128,256]{2,1,0:T(8,128)S(1)}, u32[]{:S(2)}, u32[]{:S(2)}) collective-permute-start(f32[4,128,256]{2,1,0:T(8,128)S(1)} %get-tuple-element.91), channel_id=1, source_target_pairs={{0,8},{1,9},{2,10},{3,11},{4,12},{5,13},{6,14},{7,15},{8,0},{9,1},... | collective-permute-start | bytes 1572872 | tf_op jit(solution)/shard_map/ppermute | solution.py:38
  139.3 16.2 %collective-permute-start.35 = (f32[4,128,256]{2,1,0:T(8,128)S(1)}, f32[4,128,256]{2,1,0:T(8,128)S(1)}, u32[]{:S(2)}, u32[]{:S(2)}) collective-permute-start(f32[4,128,256]{2,1,0:T(8,128)S(1)} %get-tuple-element.92), channel_id=1, source_target_pairs={{0,4},{1,5},{2,6},{3,7},{4,8},{5,9},{6,10},{7,11},{8,12},{9,13},{1... | collective-permute-start | bytes 1572872 | tf_op jit(solution)/shard_map/ppermute | solution.py:38
  141.6 14.0 %collective-permute-start.36 = (f32[4,128,256]{2,1,0:T(8,128)S(1)}, f32[4,128,256]{2,1,0:T(8,128)S(1)}, u32[]{:S(2)}, u32[]{:S(2)}) collective-permute-start(f32[4,128,256]{2,1,0:T(8,128)S(1)} %get-tuple-element.93), channel_id=1, source_target_pairs={{0,12},{1,13},{2,14},{3,15},{4,0},{5,1},{6,2},{7,3},{8,4},{9,5},{1... | collective-permute-start | bytes 1572872 | tf_op jit(solution)/shard_map/ppermute | solution.py:38
  155.7 6.6 %collective-permute-start.37 = (f32[128,256]{1,0:T(8,128)S(1)}, f32[128,256]{1,0:T(8,128)S(1)}, u32[]{:S(2)}, u32[]{:S(2)}) collective-permute-start(f32[128,256]{1,0:T(8,128)S(1)} %get-tuple-element.97), channel_id=1, source_target_pairs={{0,2},{1,3},{2,0},{3,1},{4,6},{5,7},{6,4},{7,5},{8,10},{9,11},{10,... | collective-permute-start | bytes 393224 | tf_op jit(solution)/shard_map/ppermute | solution.py:38
  157.8 6.2 %collective-permute-start.38 = (f32[128,256]{1,0:T(8,128)S(1)}, f32[128,256]{1,0:T(8,128)S(1)}, u32[]{:S(2)}, u32[]{:S(2)}) collective-permute-start(f32[128,256]{1,0:T(8,128)S(1)} %get-tuple-element.98), channel_id=1, source_target_pairs={{0,1},{1,2},{2,3},{3,0},{4,5},{5,6},{6,7},{7,4},{8,9},{9,10},{10,1... | collective-permute-start | bytes 393224 | tf_op jit(solution)/shard_map/ppermute | solution.py:38
  159.3 5.0 %collective-permute-start.39 = (f32[128,256]{1,0:T(8,128)S(1)}, f32[128,256]{1,0:T(8,128)S(1)}, u32[]{:S(2)}, u32[]{:S(2)}) collective-permute-start(f32[128,256]{1,0:T(8,128)S(1)} %get-tuple-element.99), channel_id=1, source_target_pairs={{0,3},{1,0},{2,1},{3,2},{4,7},{5,4},{6,5},{7,6},{8,11},{9,8},{10,9... | collective-permute-start | bytes 393224 | tf_op jit(solution)/shard_map/ppermute | solution.py:38
  164.6 6.6 %collective-permute-start.40 = (f32[128,256]{1,0:T(8,128)S(1)}, f32[128,256]{1,0:T(8,128)S(1)}, u32[]{:S(2)}, u32[]{:S(2)}) collective-permute-start(f32[128,256]{1,0:T(8,128)S(1)} %shard_map.86), channel_id=1, source_target_pairs={{0,64},{16,80},{32,96},{48,112},{64,0},{80,16},{96,32},{112,48},{1... | collective-permute-start | bytes 393224 | tf_op jit(solution)/shard_map/ppermute | solution.py:43
  166.4 6.2 %collective-permute-start.41 = (f32[128,256]{1,0:T(8,128)S(1)}, f32[128,256]{1,0:T(8,128)S(1)}, u32[]{:S(2)}, u32[]{:S(2)}) collective-permute-start(f32[128,256]{1,0:T(8,128)S(1)} %shard_map.86), channel_id=1, source_target_pairs={{0,32},{16,48},{32,64},{48,80},{64,96},{80,112},{96,0},{112,16},{1... | collective-permute-start | bytes 393224 | tf_op jit(solution)/shard_map/ppermute | solution.py:43
  168.3 5.0 %collective-permute-start.42 = (f32[128,256]{1,0:T(8,128)S(1)}, f32[128,256]{1,0:T(8,128)S(1)}, u32[]{:S(2)}, u32[]{:S(2)}) collective-permute-start(f32[128,256]{1,0:T(8,128)S(1)} %shard_map.86), channel_id=1, source_target_pairs={{0,96},{16,112},{32,0},{48,16},{64,32},{80,48},{96,64},{112,80},{1... | collective-permute-start | bytes 393224 | tf_op jit(solution)/shard_map/ppermute | solution.py:43
  173.3 2.0 collective-permute-start.43
  177.6 10.9 %collective-permute-start.44 = (f32[4,128,256]{2,1,0:T(8,128)S(1)}, f32[4,128,256]{2,1,0:T(8,128)S(1)}, u32[]{:S(2)}, u32[]{:S(2)}) collective-permute-start(f32[4,128,256]{2,1,0:T(8,128)S(1)} %get-tuple-element.104), channel_id=1, source_target_pairs={{0,8},{1,9},{2,10},{3,11},{4,12},{5,13},{6,14},{7,15},{8,0},{9,1},... | collective-permute-start | bytes 1572872 | tf_op jit(solution)/shard_map/ppermute | solution.py:38
  178.4 15.6 %collective-permute-start.45 = (f32[4,128,256]{2,1,0:T(8,128)S(1)}, f32[4,128,256]{2,1,0:T(8,128)S(1)}, u32[]{:S(2)}, u32[]{:S(2)}) collective-permute-start(f32[4,128,256]{2,1,0:T(8,128)S(1)} %get-tuple-element.105), channel_id=1, source_target_pairs={{0,4},{1,5},{2,6},{3,7},{4,8},{5,9},{6,10},{7,11},{8,12},{9,13},{1... | collective-permute-start | bytes 1572872 | tf_op jit(solution)/shard_map/ppermute | solution.py:38
  180.6 13.4 %collective-permute-start.46 = (f32[4,128,256]{2,1,0:T(8,128)S(1)}, f32[4,128,256]{2,1,0:T(8,128)S(1)}, u32[]{:S(2)}, u32[]{:S(2)}) collective-permute-start(f32[4,128,256]{2,1,0:T(8,128)S(1)} %get-tuple-element.106), channel_id=1, source_target_pairs={{0,12},{1,13},{2,14},{3,15},{4,0},{5,1},{6,2},{7,3},{8,4},{9,5},{1... | collective-permute-start | bytes 1572872 | tf_op jit(solution)/shard_map/ppermute | solution.py:38
  194.2 6.6 %collective-permute-start.47 = (f32[128,256]{1,0:T(8,128)S(1)}, f32[128,256]{1,0:T(8,128)S(1)}, u32[]{:S(2)}, u32[]{:S(2)}) collective-permute-start(f32[128,256]{1,0:T(8,128)S(1)} %get-tuple-element.112), channel_id=1, source_target_pairs={{0,2},{1,3},{2,0},{3,1},{4,6},{5,7},{6,4},{7,5},{8,10},{9,11},{10,... | collective-permute-start | bytes 393224 | tf_op jit(solution)/shard_map/ppermute | solution.py:38
  196.2 6.2 %collective-permute-start.48 = (f32[128,256]{1,0:T(8,128)S(1)}, f32[128,256]{1,0:T(8,128)S(1)}, u32[]{:S(2)}, u32[]{:S(2)}) collective-permute-start(f32[128,256]{1,0:T(8,128)S(1)} %get-tuple-element.113), channel_id=1, source_target_pairs={{0,1},{1,2},{2,3},{3,0},{4,5},{5,6},{6,7},{7,4},{8,9},{9,10},{10,1... | collective-permute-start | bytes 393224 | tf_op jit(solution)/shard_map/ppermute | solution.py:38
  198.1 5.0 %collective-permute-start.49 = (f32[128,256]{1,0:T(8,128)S(1)}, f32[128,256]{1,0:T(8,128)S(1)}, u32[]{:S(2)}, u32[]{:S(2)}) collective-permute-start(f32[128,256]{1,0:T(8,128)S(1)} %get-tuple-element.114), channel_id=1, source_target_pairs={{0,3},{1,0},{2,1},{3,2},{4,7},{5,4},{6,5},{7,6},{8,11},{9,8},{10,9... | collective-permute-start | bytes 393224 | tf_op jit(solution)/shard_map/ppermute | solution.py:38
  203.4 6.6 %collective-permute-start.50 = (f32[128,256]{1,0:T(8,128)S(1)}, f32[128,256]{1,0:T(8,128)S(1)}, u32[]{:S(2)}, u32[]{:S(2)}) collective-permute-start(f32[128,256]{1,0:T(8,128)S(1)} %shard_map.90), channel_id=1, source_target_pairs={{0,64},{16,80},{32,96},{48,112},{64,0},{80,16},{96,32},{112,48},{1... | collective-permute-start | bytes 393224 | tf_op jit(solution)/shard_map/ppermute | solution.py:43
  205.2 6.2 %collective-permute-start.51 = (f32[128,256]{1,0:T(8,128)S(1)}, f32[128,256]{1,0:T(8,128)S(1)}, u32[]{:S(2)}, u32[]{:S(2)}) collective-permute-start(f32[128,256]{1,0:T(8,128)S(1)} %shard_map.90), channel_id=1, source_target_pairs={{0,32},{16,48},{32,64},{48,80},{64,96},{80,112},{96,0},{112,16},{1... | collective-permute-start | bytes 393224 | tf_op jit(solution)/shard_map/ppermute | solution.py:43
  206.9 5.0 %collective-permute-start.52 = (f32[128,256]{1,0:T(8,128)S(1)}, f32[128,256]{1,0:T(8,128)S(1)}, u32[]{:S(2)}, u32[]{:S(2)}) collective-permute-start(f32[128,256]{1,0:T(8,128)S(1)} %shard_map.90), channel_id=1, source_target_pairs={{0,96},{16,112},{32,0},{48,16},{64,32},{80,48},{96,64},{112,80},{1... | collective-permute-start | bytes 393224 | tf_op jit(solution)/shard_map/ppermute | solution.py:43
  211.9 2.0 collective-permute-start.53
  216.3 10.9 %collective-permute-start.54 = (f32[4,128,256]{2,1,0:T(8,128)S(1)}, f32[4,128,256]{2,1,0:T(8,128)S(1)}, u32[]{:S(2)}, u32[]{:S(2)}) collective-permute-start(f32[4,128,256]{2,1,0:T(8,128)S(1)} %get-tuple-element.119), channel_id=1, source_target_pairs={{0,8},{1,9},{2,10},{3,11},{4,12},{5,13},{6,14},{7,15},{8,0},{9,1},... | collective-permute-start | bytes 1572872 | tf_op jit(solution)/shard_map/ppermute | solution.py:38
  217.1 15.7 %collective-permute-start.55 = (f32[4,128,256]{2,1,0:T(8,128)S(1)}, f32[4,128,256]{2,1,0:T(8,128)S(1)}, u32[]{:S(2)}, u32[]{:S(2)}) collective-permute-start(f32[4,128,256]{2,1,0:T(8,128)S(1)} %get-tuple-element.120), channel_id=1, source_target_pairs={{0,4},{1,5},{2,6},{3,7},{4,8},{5,9},{6,10},{7,11},{8,12},{9,13},{1... | collective-permute-start | bytes 1572872 | tf_op jit(solution)/shard_map/ppermute | solution.py:38
  219.3 13.4 %collective-permute-start.56 = (f32[4,128,256]{2,1,0:T(8,128)S(1)}, f32[4,128,256]{2,1,0:T(8,128)S(1)}, u32[]{:S(2)}, u32[]{:S(2)}) collective-permute-start(f32[4,128,256]{2,1,0:T(8,128)S(1)} %get-tuple-element.121), channel_id=1, source_target_pairs={{0,12},{1,13},{2,14},{3,15},{4,0},{5,1},{6,2},{7,3},{8,4},{9,5},{1... | collective-permute-start | bytes 1572872 | tf_op jit(solution)/shard_map/ppermute | solution.py:38
  232.8 6.6 %collective-permute-start.57 = (f32[128,256]{1,0:T(8,128)S(1)}, f32[128,256]{1,0:T(8,128)S(1)}, u32[]{:S(2)}, u32[]{:S(2)}) collective-permute-start(f32[128,256]{1,0:T(8,128)S(1)} %get-tuple-element.123), channel_id=1, source_target_pairs={{0,2},{1,3},{2,0},{3,1},{4,6},{5,7},{6,4},{7,5},{8,10},{9,11},{10,... | collective-permute-start | bytes 393224 | tf_op jit(solution)/shard_map/ppermute | solution.py:38
  233.9 6.8 %collective-permute-start.58 = (f32[128,256]{1,0:T(8,128)S(1)}, f32[128,256]{1,0:T(8,128)S(1)}, u32[]{:S(2)}, u32[]{:S(2)}) collective-permute-start(f32[128,256]{1,0:T(8,128)S(1)} %get-tuple-element.124), channel_id=1, source_target_pairs={{0,1},{1,2},{2,3},{3,0},{4,5},{5,6},{6,7},{7,4},{8,9},{9,10},{10,1... | collective-permute-start | bytes 393224 | tf_op jit(solution)/shard_map/ppermute | solution.py:38
  236.3 5.0 %collective-permute-start.59 = (f32[128,256]{1,0:T(8,128)S(1)}, f32[128,256]{1,0:T(8,128)S(1)}, u32[]{:S(2)}, u32[]{:S(2)}) collective-permute-start(f32[128,256]{1,0:T(8,128)S(1)} %get-tuple-element.125), channel_id=1, source_target_pairs={{0,3},{1,0},{2,1},{3,2},{4,7},{5,4},{6,5},{7,6},{8,11},{9,8},{10,9... | collective-permute-start | bytes 393224 | tf_op jit(solution)/shard_map/ppermute | solution.py:38

commit v6 on v5

--- a/solution.py
+++ b/solution.py
@@ -12,7 +12,7 @@
 LEV = 4
 NZ, NC, NX, NY = 4, 2, 4, 4
 BOTH = ("prow", "pcol")
-WHOLE, SHORT = 32, 8
+WHOLE, HALF, SHORT = 32, 16, 8
 ORDER = (2, 1, 3)
 
 
@@ -295,7 +295,7 @@
     def back(high, low, vectors, init, after):
         index = pair_index(high, low)
         scalars = (take_z[index], put_plane[index], live[index])
-        unroll = WHOLE if high == low + 1 else SHORT
+        unroll = WHOLE if high == low + 1 else HALF if high == LEV - 1 else SHORT
         return pair_product(index, unroll, True, scalars, vectors, panels, init, after, 4, 16)
 
     top = LEV - 1

time: 243 us -> 242 us (level)
  transfers between devices with their start and end apart: 60 -> 60, of which waited for: 47 -> 48; matrix products, arithmetic and copies ran while one was open for 1% -> 1% of each run, Pallas kernels for 9% -> 9%
where the time goes in v6:
time: 242 us
  waiting for transfers between devices  104 us (43%)
  starting transfers between devices  93.6 us (39%)
  Pallas kernels  39.6 us (16%)
  other arithmetic  4 us (2%)
    ppermute x36, waiting for transfers between devices, shift_plane(): return lax.ppermute(value, BOTH, pairs)  67.3 us
    ppermute x36, starting transfers between devices, shift_plane(): return lax.ppermute(value, BOTH, pairs)  59.9 us
    pallas_call x24, Pallas kernels, fast_call(): pl.pallas_call(kernel, in_specs=[pl.BlockSpec(memory_space=pltpu.SMEM)] *...  33.7 us
    ppermute x18, starting transfers between devices, shift_z(): return lax.ppermute(value, 'prow', pairs)  33.2 us
    ppermute x18, waiting for transfers between devices, shift_z(): return lax.ppermute(value, 'prow', pairs)  24.8 us
    ppermute x6, waiting for transfers between devices, swap_core(): return lax.ppermute(value, 'prow', pairs)  11.4 us
  transfers between devices with their start and end apart: 60, of which 48 were waited for; matrix products, arithmetic and copies ran while one was open for 1% of the time, Pallas kernels for 9%

profile of v6, /device:TPU:0, one launch (start us, length us, event | category | flops | bytes accessed | tf_op | source)
XLA Modules:
  0.0 241.8 jit_solution(15186912318698306337)
XLA Ops:
  5.2 1.9 collective-permute-start
  8.5 3.2 %collective-permute-done = f32[128,256]{1,0:T(8,128)S(1)} collective-permute-done((f32[128,256]{1,0:T(8,128)S(1)}, f32[128,256]{1,0:T(8,128)S(1)}, u32[]{:S(2)}, u32[]{:S(2)}) %collective-permute-start) | collective-permute-done | bytes 131104 | tf_op jit(solution)/shard_map/ppermute | solution.py:38
  11.7 3.4 %collective-permute-start.3 = (f32[4,128,256]{2,1,0:T(8,128)S(1)}, f32[4,128,256]{2,1,0:T(8,128)S(1)}, u32[]{:S(2)}, u32[]{:S(2)}) collective-permute-start(f32[4,128,256]{2,1,0:T(8,128)S(1)} %fusion.4.after.refs_0_), channel_id=1, source_target_pairs={{0,2},{1,3},{2,0},{3,1},{4,6},{5,7},{6,4},{7,5},{8,10},{9,11},{10,... | collective-permute-start | bytes 1572872 | tf_op jit(solution)/shard_map/ppermute | solution.py:38
  15.7 2.6 %collective-permute-start.5 = (f32[4,128,256]{2,1,0:T(8,128)S(1)}, f32[4,128,256]{2,1,0:T(8,128)S(1)}, u32[]{:S(2)}, u32[]{:S(2)}) collective-permute-start(f32[4,128,256]{2,1,0:T(8,128)S(1)} %fusion.4.after.refs_0_), channel_id=1, source_target_pairs={{0,3},{1,0},{2,1},{3,2},{4,7},{5,4},{6,5},{7,6},{8,11},{9,8},{10,9... | collective-permute-start | bytes 1572872 | tf_op jit(solution)/shard_map/ppermute | solution.py:38
  19.0 4.7 %shard_map.69.refs_4_.refs_2_ = f32[6,32,128,128]{3,2,1,0:T(8,128)S(1)} custom-call(f32[6,32,128,128]{3,2,1,0:T(8,128)} %bitcast.202, f32[4,128,256]{2,1,0:T(8,128)S(1)} %fusion.4.after.refs_0_), custom_call_target="tpu_custom_call" | custom-call | bytes 12582912 | tf_op jit(solution)/shard_map/pallas_call | solution.py:225
  23.8 4.3 %collective-permute-done.4.refs_2_ = f32[4,128,256]{2,1,0:T(8,128)S(1)} collective-permute-done((f32[4,128,256]{2,1,0:T(8,128)S(1)}, f32[4,128,256]{2,1,0:T(8,128)S(1)}, u32[]{:S(2)}, u32[]{:S(2)}) %collective-permute-start.4) | collective-permute-done | bytes 524320 | tf_op jit(solution)/shard_map/ppermute | solution.py:38
  28.5 2.3 shard_map.70
  31.0 1.9 collective-permute-done.6.refs_1_
  32.9 4.0 %collective-permute-start.7 = (f32[128,256]{1,0:T(8,128)S(1)}, f32[128,256]{1,0:T(8,128)S(1)}, u32[]{:S(2)}, u32[]{:S(2)}) collective-permute-start(f32[128,256]{1,0:T(8,128)S(1)} %get-tuple-element.67), channel_id=1, source_target_pairs={{0,64},{16,80},{32,96},{48,112},{64,0},{80,16},{96,32},{112,48},{1... | collective-permute-start | bytes 393224 | tf_op jit(solution)/shard_map/ppermute | solution.py:43
  37.9 2.2 collective-permute-start.9
  41.2 2.5 %collective-permute-done.8.refs_2_ = f32[128,256]{1,0:T(8,128)S(1)} collective-permute-done((f32[128,256]{1,0:T(8,128)S(1)}, f32[128,256]{1,0:T(8,128)S(1)}, u32[]{:S(2)}, u32[]{:S(2)}) %collective-permute-start.8) | collective-permute-done | bytes 131104 | tf_op jit(solution)/shard_map/ppermute | solution.py:43
  44.5 1.9 collective-permute-start.10
  47.0 2.6 %collective-permute-start.12 = (f32[128,256]{1,0:T(8,128)S(1)}, f32[128,256]{1,0:T(8,128)S(1)}, u32[]{:S(2)}, u32[]{:S(2)}) collective-permute-start(f32[128,256]{1,0:T(8,128)S(1)} %shard_map.72.base), channel_id=1, source_target_pairs={{0,12},{1,13},{2,14},{3,15},{4,0},{5,1},{6,2},{7,3},{8,4},{9,5},{1... | collective-permute-start | bytes 393224 | tf_op jit(solution)/shard_map/ppermute | solution.py:38
  52.6 2.1 collective-permute-start.13
  56.2 1.8 collective-permute-start.15
  58.0 2.9 %shard_map.73 = (f32[4,128,256]{2,1,0:T(8,128)S(1)}, f32[4,128,256]{2,1,0:T(8,128)S(1)}) custom-call(s32[32]{0:T(128)S(1)} %get-tuple-element.164.take, s32[32]{0:T(128)S(1)} %get-tuple-element.149.put, s32[32]{0:T(128)S(1)} %get-tuple-element.143.live, f32[4,128,256]{2,1,0:T(8,128)S(1)} %fusion.4.after.refs_0_, ...), custom_call_target="tpu_custom_call" | custom-call | flops 1073741824 | bytes 4096 | tf_op jit(solution)/shard_map/pallas_call | solution.py:66
  60.8 2.7 %collective-permute-done.13.refs_1_ = f32[4,128,256]{2,1,0:T(8,128)S(1)} collective-permute-done((f32[4,128,256]{2,1,0:T(8,128)S(1)}, f32[4,128,256]{2,1,0:T(8,128)S(1)}, u32[]{:S(2)}, u32[]{:S(2)}) %collective-permute-start.13) | collective-permute-done | bytes 524320 | tf_op jit(solution)/shard_map/ppermute | solution.py:38
  63.5 5.5 %collective-permute-done.14.refs_2_ = f32[4,128,256]{2,1,0:T(8,128)S(1)} collective-permute-done((f32[4,128,256]{2,1,0:T(8,128)S(1)}, f32[4,128,256]{2,1,0:T(8,128)S(1)}, u32[]{:S(2)}, u32[]{:S(2)}) %collective-permute-start.14) | collective-permute-done | bytes 524320 | tf_op jit(solution)/shard_map/ppermute | solution.py:38
  69.0 2.3 shard_map.74
  71.5 1.9 collective-permute-done.16.refs_1_
  73.4 2.2 collective-permute-start.17
  78.8 2.5 %collective-permute-done.17.refs_1_ = f32[128,256]{1,0:T(8,128)S(1)} collective-permute-done((f32[128,256]{1,0:T(8,128)S(1)}, f32[128,256]{1,0:T(8,128)S(1)}, u32[]{:S(2)}, u32[]{:S(2)}) %collective-permute-start.17) | collective-permute-done | bytes 131104 | tf_op jit(solution)/shard_map/ppermute | solution.py:43
  81.3 2.0 collective-permute-done.18.refs_2_
  83.7 1.8 collective-permute-start.20
  85.5 2.4 collective-permute-start.21
  92.9 2.3 collective-permute-start.23
  96.7 1.8 collective-permute-start.25
  98.5 2.9 %shard_map.77 = (f32[4,128,256]{2,1,0:T(8,128)S(1)}, f32[4,128,256]{2,1,0:T(8,128)S(1)}) custom-call(s32[32]{0:T(128)S(1)} %get-tuple-element.167.take, s32[32]{0:T(128)S(1)} %get-tuple-element.146.put, s32[32]{0:T(128)S(1)} %get-tuple-element.140.live, f32[4,128,256]{2,1,0:T(8,128)S(1)} %fusion.4.after.refs_0_, ...), custom_call_target="tpu_custom_call" | custom-call | flops 1073741824 | bytes 4096 | tf_op jit(solution)/shard_map/pallas_call | solution.py:66
  101.3 2.9 %shard_map.78 = (f32[4,128,256]{2,1,0:T(8,128)S(1)}, f32[4,128,256]{2,1,0:T(8,128)S(1)}) custom-call(s32[32]{0:T(128)S(1)} %get-tuple-element.166.take, s32[32]{0:T(128)S(1)} %get-tuple-element.147.put, s32[32]{0:T(128)S(1)} %get-tuple-element.141.live, f32[4,128,256]{2,1,0:T(8,128)S(1)} %pad_maximum_fusion.2.refs_0_, ...), custom_call_target="tpu_custom_call" | custom-call | flops 1073741824 | bytes 4096 | tf_op jit(solution)/shard_map/pallas_call | solution.py:66
  104.2 5.3 %collective-permute-done.24.refs_2_ = f32[4,128,256]{2,1,0:T(8,128)S(1)} collective-permute-done((f32[4,128,256]{2,1,0:T(8,128)S(1)}, f32[4,128,256]{2,1,0:T(8,128)S(1)}, u32[]{:S(2)}, u32[]{:S(2)}) %collective-permute-start.24) | collective-permute-done | bytes 524320 | tf_op jit(solution)/shard_map/ppermute | solution.py:38
  109.5 2.3 shard_map.79
  111.9 1.9 collective-permute-done.26.refs_1_
  113.9 2.1 collective-permute-start.27
  119.2 2.6 %collective-permute-done.27.refs_1_ = f32[128,256]{1,0:T(8,128)S(1)} collective-permute-done((f32[128,256]{1,0:T(8,128)S(1)}, f32[128,256]{1,0:T(8,128)S(1)}, u32[]{:S(2)}, u32[]{:S(2)}) %collective-permute-start.27) | collective-permute-done | bytes 131104 | tf_op jit(solution)/shard_map/ppermute | solution.py:43
  121.8 2.0 collective-permute-done.28.refs_2_
  124.5 2.1 collective-permute-start.30
  129.8 2.7 %collective-permute-done.30 = f32[128,256]{1,0:T(8,128)S(1)} collective-permute-done((f32[128,256]{1,0:T(8,128)S(1)}, f32[128,256]{1,0:T(8,128)S(1)}, u32[]{:S(2)}, u32[]{:S(2)}) %collective-permute-start.30) | collective-permute-done | bytes 131104 | tf_op jit(solution)/shard_map/ppermute | solution.py:43
  134.3 1.9 collective-permute-done.33.refs_1_
  136.2 2.4 shard_map.82
  139.3 2.2 collective-permute-start.35
  142.6 6.9 %collective-permute-done.34.refs_3_.refs_1_ = f32[4,128,256]{2,1,0:T(8,128)S(1)} collective-permute-done((f32[4,128,256]{2,1,0:T(8,128)S(1)}, f32[4,128,256]{2,1,0:T(8,128)S(1)}, u32[]{:S(2)}, u32[]{:S(2)}) %collective-permute-start.34) | collective-permute-done | bytes 524320 | tf_op jit(solution)/shard_map/ppermute | solution.py:38
  149.5 2.6 %shard_map.84 = (f32[4,128,256]{2,1,0:T(8,128)S(1)}, f32[4,128,256]{2,1,0:T(8,128)S(1)}, f32[4,128,256]{2,1,0:T(8,128)S(1)}, f32[4,128,256]{2,1,0:T(8,128)S(1)}) custom-call(s32[32]{0:T(128)S(1)} %get-tuple-element.171.take, s32[32]{0:T(128)S(1)} %get-tuple-element.130.put, s32[32]{0:T(128)S(1)} %get-tuple-element.140.live, ...), custom_call_target="tpu_custom_call" | custom-call | flops 1073741824 | bytes 4096 | tf_op jit(solution)/shard_map/pallas_call | solution.py:66
  152.1 2.6 %shard_map.83 = (f32[4,128,256]{2,1,0:T(8,128)S(1)}, f32[4,128,256]{2,1,0:T(8,128)S(1)}, f32[4,128,256]{2,1,0:T(8,128)S(1)}, f32[4,128,256]{2,1,0:T(8,128)S(1)}) custom-call(s32[32]{0:T(128)S(1)} %get-tuple-element.170.take, s32[32]{0:T(128)S(1)} %get-tuple-element.131.put, s32[32]{0:T(128)S(1)} %get-tuple-element.141.live, ...), custom_call_target="tpu_custom_call" | custom-call | flops 1073741824 | bytes 4096 | tf_op jit(solution)/shard_map/pallas_call | solution.py:66
  155.1 2.1 collective-permute-start.37
  158.7 1.8 collective-permute-start.39
  161.7 1.7 collective-permute-done.38.refs_2_
  164.0 1.8 collective-permute-start.40
  165.8 1.8 collective-permute-start.41
  172.7 1.9 collective-permute-done.43.refs_1_
  174.6 2.4 shard_map.87
  177.8 2.2 collective-permute-start.45
  181.0 6.8 %collective-permute-done.44.refs_7_.refs_1_ = f32[4,128,256]{2,1,0:T(8,128)S(1)} collective-permute-done((f32[4,128,256]{2,1,0:T(8,128)S(1)}, f32[4,128,256]{2,1,0:T(8,128)S(1)}, u32[]{:S(2)}, u32[]{:S(2)}) %collective-permute-start.44) | collective-permute-done | bytes 524320 | tf_op jit(solution)/shard_map/ppermute | solution.py:38
  187.8 3.1 %shard_map.88 = (f32[4,128,256]{2,1,0:T(8,128)S(1)}, f32[4,128,256]{2,1,0:T(8,128)S(1)}, f32[4,128,256]{2,1,0:T(8,128)S(1)}, f32[4,128,256]{2,1,0:T(8,128)S(1)}) custom-call(s32[32]{0:T(128)S(1)} %get-tuple-element.172.take, s32[32]{0:T(128)S(1)} %get-tuple-element.129.put, s32[32]{0:T(128)S(1)} %get-tuple-element.143.live, ...), custom_call_target="tpu_custom_call" | custom-call | flops 1073741824 | bytes 4096 | tf_op jit(solution)/shard_map/pallas_call | solution.py:66
  190.9 2.4 %collective-permute-done.45.refs_2_ = f32[4,128,256]{2,1,0:T(8,128)S(1)} collective-permute-done((f32[4,128,256]{2,1,0:T(8,128)S(1)}, f32[4,128,256]{2,1,0:T(8,128)S(1)}, u32[]{:S(2)}, u32[]{:S(2)}) %collective-permute-start.45) | collective-permute-done | bytes 524320 | tf_op jit(solution)/shard_map/ppermute | solution.py:38
  193.5 2.1 collective-permute-start.47
  195.6 1.9 collective-permute-start.48
  200.1 1.8 collective-permute-done.48.refs_2_
  204.5 1.8 collective-permute-start.51
  211.4 1.9 collective-permute-done.53.refs_1_
  213.3 2.4 shard_map.91
  216.4 2.2 collective-permute-start.55
  219.7 6.8 %collective-permute-done.54.refs_1_ = f32[4,128,256]{2,1,0:T(8,128)S(1)} collective-permute-done((f32[4,128,256]{2,1,0:T(8,128)S(1)}, f32[4,128,256]{2,1,0:T(8,128)S(1)}, u32[]{:S(2)}, u32[]{:S(2)}) %collective-permute-start.54) | collective-permute-done | bytes 524320 | tf_op jit(solution)/shard_map/ppermute | solution.py:38
  226.5 5.5 %collective-permute-done.55.refs_2_ = f32[4,128,256]{2,1,0:T(8,128)S(1)} collective-permute-done((f32[4,128,256]{2,1,0:T(8,128)S(1)}, f32[4,128,256]{2,1,0:T(8,128)S(1)}, u32[]{:S(2)}, u32[]{:S(2)}) %collective-permute-start.55) | collective-permute-done | bytes 524320 | tf_op jit(solution)/shard_map/ppermute | solution.py:38
  233.3 2.4 collective-permute-start.58
  (100 shorter events, 67.3 us)
Async XLA Ops:
  1.9 6.6 %collective-permute-start.1 = (f32[128,256]{1,0:T(8,128)S(1)}, f32[128,256]{1,0:T(8,128)S(1)}, u32[]{:S(2)}, u32[]{:S(2)}) collective-permute-start(f32[128,256]{1,0:T(8,128)S(1)} %shard_map.68.base), channel_id=1, source_target_pairs={{0,4},{1,5},{2,6},{3,7},{4,8},{5,9},{6,10},{7,11},{8,12},{9,13},{1... | collective-permute-start | bytes 393224 | tf_op jit(solution)/shard_map/ppermute | solution.py:38
  3.5 5.0 %collective-permute-start.2 = (f32[128,256]{1,0:T(8,128)S(1)}, f32[128,256]{1,0:T(8,128)S(1)}, u32[]{:S(2)}, u32[]{:S(2)}) collective-permute-start(f32[128,256]{1,0:T(8,128)S(1)} %shard_map.68.base), channel_id=1, source_target_pairs={{0,12},{1,13},{2,14},{3,15},{4,0},{5,1},{6,2},{7,3},{8,4},{9,5},{1... | collective-permute-start | bytes 393224 | tf_op jit(solution)/shard_map/ppermute | solution.py:38
  5.2 6.5 %collective-permute-start = (f32[128,256]{1,0:T(8,128)S(1)}, f32[128,256]{1,0:T(8,128)S(1)}, u32[]{:S(2)}, u32[]{:S(2)}) collective-permute-start(f32[128,256]{1,0:T(8,128)S(1)} %shard_map.68.base), channel_id=1, source_target_pairs={{0,8},{1,9},{2,10},{3,11},{4,12},{5,13},{6,14},{7,15},{8,0},{9,1},... | collective-permute-start | bytes 393224 | tf_op jit(solution)/shard_map/ppermute | solution.py:38
  11.7 12.1 %collective-permute-start.3 = (f32[4,128,256]{2,1,0:T(8,128)S(1)}, f32[4,128,256]{2,1,0:T(8,128)S(1)}, u32[]{:S(2)}, u32[]{:S(2)}) collective-permute-start(f32[4,128,256]{2,1,0:T(8,128)S(1)} %fusion.4.after.refs_0_), channel_id=1, source_target_pairs={{0,2},{1,3},{2,0},{3,1},{4,6},{5,7},{6,4},{7,5},{8,10},{9,11},{10,... | collective-permute-start | bytes 1572872 | tf_op jit(solution)/shard_map/ppermute | solution.py:38
  15.0 13.0 %collective-permute-start.4 = (f32[4,128,256]{2,1,0:T(8,128)S(1)}, f32[4,128,256]{2,1,0:T(8,128)S(1)}, u32[]{:S(2)}, u32[]{:S(2)}) collective-permute-start(f32[4,128,256]{2,1,0:T(8,128)S(1)} %fusion.4.after.refs_0_), channel_id=1, source_target_pairs={{0,1},{1,2},{2,3},{3,0},{4,5},{5,6},{6,7},{7,4},{8,9},{9,10},{10,1... | collective-permute-start | bytes 1572872 | tf_op jit(solution)/shard_map/ppermute | solution.py:38
  15.7 12.8 %collective-permute-start.5 = (f32[4,128,256]{2,1,0:T(8,128)S(1)}, f32[4,128,256]{2,1,0:T(8,128)S(1)}, u32[]{:S(2)}, u32[]{:S(2)}) collective-permute-start(f32[4,128,256]{2,1,0:T(8,128)S(1)} %fusion.4.after.refs_0_), channel_id=1, source_target_pairs={{0,3},{1,0},{2,1},{3,2},{4,7},{5,4},{6,5},{7,6},{8,11},{9,8},{10,9... | collective-permute-start | bytes 1572872 | tf_op jit(solution)/shard_map/ppermute | solution.py:38
  23.7 20.5 %copy-start = (f32[4,1,1,128,128]{4,3,2,1,0:T(8,128)S(1)}, f32[4,1,1,128,128]{4,3,2,1,0:T(8,128)}, u32[]{:S(2)}) copy-start(f32[4,1,1,128,128]{4,3,2,1,0:T(8,128)} %param.6) | copy-start | bytes 786436
  23.7 20.5 %copy-start.1 = (f32[4,1,1,128,256]{4,3,2,1,0:T(8,128)S(1)}, f32[4,1,1,128,256]{4,3,2,1,0:T(8,128)}, u32[]{:S(2)}) copy-start(f32[4,1,1,128,256]{4,3,2,1,0:T(8,128)} %param.5) | copy-start | bytes 1572868
  30.9 2.0 collective-permute-start.6
  32.9 8.2 %collective-permute-start.7 = (f32[128,256]{1,0:T(8,128)S(1)}, f32[128,256]{1,0:T(8,128)S(1)}, u32[]{:S(2)}, u32[]{:S(2)}) collective-permute-start(f32[128,256]{1,0:T(8,128)S(1)} %get-tuple-element.67), channel_id=1, source_target_pairs={{0,64},{16,80},{32,96},{48,112},{64,0},{80,16},{96,32},{112,48},{1... | collective-permute-start | bytes 393224 | tf_op jit(solution)/shard_map/ppermute | solution.py:43
  36.9 6.8 %collective-permute-start.8 = (f32[128,256]{1,0:T(8,128)S(1)}, f32[128,256]{1,0:T(8,128)S(1)}, u32[]{:S(2)}, u32[]{:S(2)}) collective-permute-start(f32[128,256]{1,0:T(8,128)S(1)} %get-tuple-element.68), channel_id=1, source_target_pairs={{0,32},{16,48},{32,64},{48,80},{64,96},{80,112},{96,0},{112,16},{1... | collective-permute-start | bytes 393224 | tf_op jit(solution)/shard_map/ppermute | solution.py:43
  37.9 6.3 %collective-permute-start.9 = (f32[128,256]{1,0:T(8,128)S(1)}, f32[128,256]{1,0:T(8,128)S(1)}, u32[]{:S(2)}, u32[]{:S(2)}) collective-permute-start(f32[128,256]{1,0:T(8,128)S(1)} %get-tuple-element.69), channel_id=1, source_target_pairs={{0,96},{16,112},{32,0},{48,16},{64,32},{80,48},{96,64},{112,80},{1... | collective-permute-start | bytes 393224 | tf_op jit(solution)/shard_map/ppermute | solution.py:43
  44.5 6.6 %collective-permute-start.10 = (f32[128,256]{1,0:T(8,128)S(1)}, f32[128,256]{1,0:T(8,128)S(1)}, u32[]{:S(2)}, u32[]{:S(2)}) collective-permute-start(f32[128,256]{1,0:T(8,128)S(1)} %shard_map.72.base), channel_id=1, source_target_pairs={{0,8},{1,9},{2,10},{3,11},{4,12},{5,13},{6,14},{7,15},{8,0},{9,1},... | collective-permute-start | bytes 393224 | tf_op jit(solution)/shard_map/ppermute | solution.py:38
  46.4 6.2 %collective-permute-start.11 = (f32[128,256]{1,0:T(8,128)S(1)}, f32[128,256]{1,0:T(8,128)S(1)}, u32[]{:S(2)}, u32[]{:S(2)}) collective-permute-start(f32[128,256]{1,0:T(8,128)S(1)} %shard_map.72.base), channel_id=1, source_target_pairs={{0,4},{1,5},{2,6},{3,7},{4,8},{5,9},{6,10},{7,11},{8,12},{9,13},{1... | collective-permute-start | bytes 393224 | tf_op jit(solution)/shard_map/ppermute | solution.py:38
  47.0 5.6 %collective-permute-start.12 = (f32[128,256]{1,0:T(8,128)S(1)}, f32[128,256]{1,0:T(8,128)S(1)}, u32[]{:S(2)}, u32[]{:S(2)}) collective-permute-start(f32[128,256]{1,0:T(8,128)S(1)} %shard_map.72.base), channel_id=1, source_target_pairs={{0,12},{1,13},{2,14},{3,15},{4,0},{5,1},{6,2},{7,3},{8,4},{9,5},{1... | collective-permute-start | bytes 393224 | tf_op jit(solution)/shard_map/ppermute | solution.py:38
  52.6 10.9 %collective-permute-start.13 = (f32[4,128,256]{2,1,0:T(8,128)S(1)}, f32[4,128,256]{2,1,0:T(8,128)S(1)}, u32[]{:S(2)}, u32[]{:S(2)}) collective-permute-start(f32[4,128,256]{2,1,0:T(8,128)S(1)} %pad_maximum_fusion.2.refs_0_), channel_id=1, source_target_pairs={{0,2},{1,3},{2,0},{3,1},{4,6},{5,7},{6,4},{7,5},{8,10},{9,11},{10,... | collective-permute-start | bytes 1572872 | tf_op jit(solution)/shard_map/ppermute | solution.py:38
  54.7 14.3 %collective-permute-start.14 = (f32[4,128,256]{2,1,0:T(8,128)S(1)}, f32[4,128,256]{2,1,0:T(8,128)S(1)}, u32[]{:S(2)}, u32[]{:S(2)}) collective-permute-start(f32[4,128,256]{2,1,0:T(8,128)S(1)} %pad_maximum_fusion.2.refs_0_), channel_id=1, source_target_pairs={{0,1},{1,2},{2,3},{3,0},{4,5},{5,6},{6,7},{7,4},{8,9},{9,10},{10,1... | collective-permute-start | bytes 1572872 | tf_op jit(solution)/shard_map/ppermute | solution.py:38
  56.2 12.8 %collective-permute-start.15 = (f32[4,128,256]{2,1,0:T(8,128)S(1)}, f32[4,128,256]{2,1,0:T(8,128)S(1)}, u32[]{:S(2)}, u32[]{:S(2)}) collective-permute-start(f32[4,128,256]{2,1,0:T(8,128)S(1)} %pad_maximum_fusion.2.refs_0_), channel_id=1, source_target_pairs={{0,3},{1,0},{2,1},{3,2},{4,7},{5,4},{6,5},{7,6},{8,11},{9,8},{10,9... | collective-permute-start | bytes 1572872 | tf_op jit(solution)/shard_map/ppermute | solution.py:38
  71.4 2.0 collective-permute-start.16
  73.4 7.9 %collective-permute-start.17 = (f32[128,256]{1,0:T(8,128)S(1)}, f32[128,256]{1,0:T(8,128)S(1)}, u32[]{:S(2)}, u32[]{:S(2)}) collective-permute-start(f32[128,256]{1,0:T(8,128)S(1)} %get-tuple-element.75), channel_id=1, source_target_pairs={{0,64},{16,80},{32,96},{48,112},{64,0},{80,16},{96,32},{112,48},{1... | collective-permute-start | bytes 393224 | tf_op jit(solution)/shard_map/ppermute | solution.py:43
  75.6 7.8 %collective-permute-start.18 = (f32[128,256]{1,0:T(8,128)S(1)}, f32[128,256]{1,0:T(8,128)S(1)}, u32[]{:S(2)}, u32[]{:S(2)}) collective-permute-start(f32[128,256]{1,0:T(8,128)S(1)} %get-tuple-element.76), channel_id=1, source_target_pairs={{0,32},{16,48},{32,64},{48,80},{64,96},{80,112},{96,0},{112,16},{1... | collective-permute-start | bytes 393224 | tf_op jit(solution)/shard_map/ppermute | solution.py:43
  77.1 6.3 %collective-permute-start.19 = (f32[128,256]{1,0:T(8,128)S(1)}, f32[128,256]{1,0:T(8,128)S(1)}, u32[]{:S(2)}, u32[]{:S(2)}) collective-permute-start(f32[128,256]{1,0:T(8,128)S(1)} %get-tuple-element.77), channel_id=1, source_target_pairs={{0,96},{16,112},{32,0},{48,16},{64,32},{80,48},{96,64},{112,80},{1... | collective-permute-start | bytes 393224 | tf_op jit(solution)/shard_map/ppermute | solution.py:43
  83.7 6.6 %collective-permute-start.20 = (f32[128,256]{1,0:T(8,128)S(1)}, f32[128,256]{1,0:T(8,128)S(1)}, u32[]{:S(2)}, u32[]{:S(2)}) collective-permute-start(f32[128,256]{1,0:T(8,128)S(1)} %shard_map.76.base), channel_id=1, source_target_pairs={{0,8},{1,9},{2,10},{3,11},{4,12},{5,13},{6,14},{7,15},{8,0},{9,1},... | collective-permute-start | bytes 393224 | tf_op jit(solution)/shard_map/ppermute | solution.py:38
  85.5 6.2 %collective-permute-start.21 = (f32[128,256]{1,0:T(8,128)S(1)}, f32[128,256]{1,0:T(8,128)S(1)}, u32[]{:S(2)}, u32[]{:S(2)}) collective-permute-start(f32[128,256]{1,0:T(8,128)S(1)} %shard_map.76.base), channel_id=1, source_target_pairs={{0,4},{1,5},{2,6},{3,7},{4,8},{5,9},{6,10},{7,11},{8,12},{9,13},{1... | collective-permute-start | bytes 393224 | tf_op jit(solution)/shard_map/ppermute | solution.py:38
  87.9 5.0 %collective-permute-start.22 = (f32[128,256]{1,0:T(8,128)S(1)}, f32[128,256]{1,0:T(8,128)S(1)}, u32[]{:S(2)}, u32[]{:S(2)}) collective-permute-start(f32[128,256]{1,0:T(8,128)S(1)} %shard_map.76.base), channel_id=1, source_target_pairs={{0,12},{1,13},{2,14},{3,15},{4,0},{5,1},{6,2},{7,3},{8,4},{9,5},{1... | collective-permute-start | bytes 393224 | tf_op jit(solution)/shard_map/ppermute | solution.py:38
  92.9 11.3 %collective-permute-start.23 = (f32[4,128,256]{2,1,0:T(8,128)S(1)}, f32[4,128,256]{2,1,0:T(8,128)S(1)}, u32[]{:S(2)}, u32[]{:S(2)}) collective-permute-start(f32[4,128,256]{2,1,0:T(8,128)S(1)} %pad_maximum_fusion.3.refs_0_), channel_id=1, source_target_pairs={{0,2},{1,3},{2,0},{3,1},{4,6},{5,7},{6,4},{7,5},{8,10},{9,11},{10,... | collective-permute-start | bytes 1572872 | tf_op jit(solution)/shard_map/ppermute | solution.py:38
  95.2 14.3 %collective-permute-start.24 = (f32[4,128,256]{2,1,0:T(8,128)S(1)}, f32[4,128,256]{2,1,0:T(8,128)S(1)}, u32[]{:S(2)}, u32[]{:S(2)}) collective-permute-start(f32[4,128,256]{2,1,0:T(8,128)S(1)} %pad_maximum_fusion.3.refs_0_), channel_id=1, source_target_pairs={{0,1},{1,2},{2,3},{3,0},{4,5},{5,6},{6,7},{7,4},{8,9},{9,10},{10,1... | collective-permute-start | bytes 1572872 | tf_op jit(solution)/shard_map/ppermute | solution.py:38
  96.7 12.8 %collective-permute-start.25 = (f32[4,128,256]{2,1,0:T(8,128)S(1)}, f32[4,128,256]{2,1,0:T(8,128)S(1)}, u32[]{:S(2)}, u32[]{:S(2)}) collective-permute-start(f32[4,128,256]{2,1,0:T(8,128)S(1)} %pad_maximum_fusion.3.refs_0_), channel_id=1, source_target_pairs={{0,3},{1,0},{2,1},{3,2},{4,7},{5,4},{6,5},{7,6},{8,11},{9,8},{10,9... | collective-permute-start | bytes 1572872 | tf_op jit(solution)/shard_map/ppermute | solution.py:38
  111.8 2.0 collective-permute-start.26
  113.9 7.9 %collective-permute-start.27 = (f32[128,256]{1,0:T(8,128)S(1)}, f32[128,256]{1,0:T(8,128)S(1)}, u32[]{:S(2)}, u32[]{:S(2)}) collective-permute-start(f32[128,256]{1,0:T(8,128)S(1)} %get-tuple-element.85), channel_id=1, source_target_pairs={{0,64},{16,80},{32,96},{48,112},{64,0},{80,16},{96,32},{112,48},{1... | collective-permute-start | bytes 393224 | tf_op jit(solution)/shard_map/ppermute | solution.py:43
  115.9 7.9 %collective-permute-start.28 = (f32[128,256]{1,0:T(8,128)S(1)}, f32[128,256]{1,0:T(8,128)S(1)}, u32[]{:S(2)}, u32[]{:S(2)}) collective-permute-start(f32[128,256]{1,0:T(8,128)S(1)} %get-tuple-element.86), channel_id=1, source_target_pairs={{0,32},{16,48},{32,64},{48,80},{64,96},{80,112},{96,0},{112,16},{1... | collective-permute-start | bytes 393224 | tf_op jit(solution)/shard_map/ppermute | solution.py:43
  117.5 6.3 %collective-permute-start.29 = (f32[128,256]{1,0:T(8,128)S(1)}, f32[128,256]{1,0:T(8,128)S(1)}, u32[]{:S(2)}, u32[]{:S(2)}) collective-permute-start(f32[128,256]{1,0:T(8,128)S(1)} %get-tuple-element.87), channel_id=1, source_target_pairs={{0,96},{16,112},{32,0},{48,16},{64,32},{80,48},{96,64},{112,80},{1... | collective-permute-start | bytes 393224 | tf_op jit(solution)/shard_map/ppermute | solution.py:43
  124.5 8.0 %collective-permute-start.30 = (f32[128,256]{1,0:T(8,128)S(1)}, f32[128,256]{1,0:T(8,128)S(1)}, u32[]{:S(2)}, u32[]{:S(2)}) collective-permute-start(f32[128,256]{1,0:T(8,128)S(1)} %get-tuple-element.89), channel_id=1, source_target_pairs={{0,64},{16,80},{32,96},{48,112},{64,0},{80,16},{96,32},{112,48},{1... | collective-permute-start | bytes 393224 | tf_op jit(solution)/shard_map/ppermute | solution.py:43
  126.6 7.6 %collective-permute-start.31 = (f32[128,256]{1,0:T(8,128)S(1)}, f32[128,256]{1,0:T(8,128)S(1)}, u32[]{:S(2)}, u32[]{:S(2)}) collective-permute-start(f32[128,256]{1,0:T(8,128)S(1)} %get-tuple-element.89), channel_id=1, source_target_pairs={{0,32},{16,48},{32,64},{48,80},{64,96},{80,112},{96,0},{112,16},{1... | collective-permute-start | bytes 393224 | tf_op jit(solution)/shard_map/ppermute | solution.py:43
  128.1 6.0 %collective-permute-start.32 = (f32[128,256]{1,0:T(8,128)S(1)}, f32[128,256]{1,0:T(8,128)S(1)}, u32[]{:S(2)}, u32[]{:S(2)}) collective-permute-start(f32[128,256]{1,0:T(8,128)S(1)} %get-tuple-element.89), channel_id=1, source_target_pairs={{0,96},{16,112},{32,0},{48,16},{64,32},{80,48},{96,64},{112,80},{1... | collective-permute-start | bytes 393224 | tf_op jit(solution)/shard_map/ppermute | solution.py:43
  134.2 2.0 collective-permute-start.33
  138.6 10.9 %collective-permute-start.34 = (f32[4,128,256]{2,1,0:T(8,128)S(1)}, f32[4,128,256]{2,1,0:T(8,128)S(1)}, u32[]{:S(2)}, u32[]{:S(2)}) collective-permute-start(f32[4,128,256]{2,1,0:T(8,128)S(1)} %get-tuple-element.91), channel_id=1, source_target_pairs={{0,8},{1,9},{2,10},{3,11},{4,12},{5,13},{6,14},{7,15},{8,0},{9,1},... | collective-permute-start | bytes 1572872 | tf_op jit(solution)/shard_map/ppermute | solution.py:38
  139.3 15.6 %collective-permute-start.35 = (f32[4,128,256]{2,1,0:T(8,128)S(1)}, f32[4,128,256]{2,1,0:T(8,128)S(1)}, u32[]{:S(2)}, u32[]{:S(2)}) collective-permute-start(f32[4,128,256]{2,1,0:T(8,128)S(1)} %get-tuple-element.92), channel_id=1, source_target_pairs={{0,4},{1,5},{2,6},{3,7},{4,8},{5,9},{6,10},{7,11},{8,12},{9,13},{1... | collective-permute-start | bytes 1572872 | tf_op jit(solution)/shard_map/ppermute | solution.py:38
  141.6 13.4 %collective-permute-start.36 = (f32[4,128,256]{2,1,0:T(8,128)S(1)}, f32[4,128,256]{2,1,0:T(8,128)S(1)}, u32[]{:S(2)}, u32[]{:S(2)}) collective-permute-start(f32[4,128,256]{2,1,0:T(8,128)S(1)} %get-tuple-element.93), channel_id=1, source_target_pairs={{0,12},{1,13},{2,14},{3,15},{4,0},{5,1},{6,2},{7,3},{8,4},{9,5},{1... | collective-permute-start | bytes 1572872 | tf_op jit(solution)/shard_map/ppermute | solution.py:38
  155.1 6.6 %collective-permute-start.37 = (f32[128,256]{1,0:T(8,128)S(1)}, f32[128,256]{1,0:T(8,128)S(1)}, u32[]{:S(2)}, u32[]{:S(2)}) collective-permute-start(f32[128,256]{1,0:T(8,128)S(1)} %get-tuple-element.97), channel_id=1, source_target_pairs={{0,2},{1,3},{2,0},{3,1},{4,6},{5,7},{6,4},{7,5},{8,10},{9,11},{10,... | collective-permute-start | bytes 393224 | tf_op jit(solution)/shard_map/ppermute | solution.py:38
  157.2 6.2 %collective-permute-start.38 = (f32[128,256]{1,0:T(8,128)S(1)}, f32[128,256]{1,0:T(8,128)S(1)}, u32[]{:S(2)}, u32[]{:S(2)}) collective-permute-start(f32[128,256]{1,0:T(8,128)S(1)} %get-tuple-element.98), channel_id=1, source_target_pairs={{0,1},{1,2},{2,3},{3,0},{4,5},{5,6},{6,7},{7,4},{8,9},{9,10},{10,1... | collective-permute-start | bytes 393224 | tf_op jit(solution)/shard_map/ppermute | solution.py:38
  158.7 5.0 %collective-permute-start.39 = (f32[128,256]{1,0:T(8,128)S(1)}, f32[128,256]{1,0:T(8,128)S(1)}, u32[]{:S(2)}, u32[]{:S(2)}) collective-permute-start(f32[128,256]{1,0:T(8,128)S(1)} %get-tuple-element.99), channel_id=1, source_target_pairs={{0,3},{1,0},{2,1},{3,2},{4,7},{5,4},{6,5},{7,6},{8,11},{9,8},{10,9... | collective-permute-start | bytes 393224 | tf_op jit(solution)/shard_map/ppermute | solution.py:38
  164.0 6.6 %collective-permute-start.40 = (f32[128,256]{1,0:T(8,128)S(1)}, f32[128,256]{1,0:T(8,128)S(1)}, u32[]{:S(2)}, u32[]{:S(2)}) collective-permute-start(f32[128,256]{1,0:T(8,128)S(1)} %shard_map.86), channel_id=1, source_target_pairs={{0,64},{16,80},{32,96},{48,112},{64,0},{80,16},{96,32},{112,48},{1... | collective-permute-start | bytes 393224 | tf_op jit(solution)/shard_map/ppermute | solution.py:43
  165.8 6.2 %collective-permute-start.41 = (f32[128,256]{1,0:T(8,128)S(1)}, f32[128,256]{1,0:T(8,128)S(1)}, u32[]{:S(2)}, u32[]{:S(2)}) collective-permute-start(f32[128,256]{1,0:T(8,128)S(1)} %shard_map.86), channel_id=1, source_target_pairs={{0,32},{16,48},{32,64},{48,80},{64,96},{80,112},{96,0},{112,16},{1... | collective-permute-start | bytes 393224 | tf_op jit(solution)/shard_map/ppermute | solution.py:43
  167.6 5.0 %collective-permute-start.42 = (f32[128,256]{1,0:T(8,128)S(1)}, f32[128,256]{1,0:T(8,128)S(1)}, u32[]{:S(2)}, u32[]{:S(2)}) collective-permute-start(f32[128,256]{1,0:T(8,128)S(1)} %shard_map.86), channel_id=1, source_target_pairs={{0,96},{16,112},{32,0},{48,16},{64,32},{80,48},{96,64},{112,80},{1... | collective-permute-start | bytes 393224 | tf_op jit(solution)/shard_map/ppermute | solution.py:43
  172.6 2.0 collective-permute-start.43
  177.0 10.9 %collective-permute-start.44 = (f32[4,128,256]{2,1,0:T(8,128)S(1)}, f32[4,128,256]{2,1,0:T(8,128)S(1)}, u32[]{:S(2)}, u32[]{:S(2)}) collective-permute-start(f32[4,128,256]{2,1,0:T(8,128)S(1)} %get-tuple-element.104), channel_id=1, source_target_pairs={{0,8},{1,9},{2,10},{3,11},{4,12},{5,13},{6,14},{7,15},{8,0},{9,1},... | collective-permute-start | bytes 1572872 | tf_op jit(solution)/shard_map/ppermute | solution.py:38
  177.8 15.6 %collective-permute-start.45 = (f32[4,128,256]{2,1,0:T(8,128)S(1)}, f32[4,128,256]{2,1,0:T(8,128)S(1)}, u32[]{:S(2)}, u32[]{:S(2)}) collective-permute-start(f32[4,128,256]{2,1,0:T(8,128)S(1)} %get-tuple-element.105), channel_id=1, source_target_pairs={{0,4},{1,5},{2,6},{3,7},{4,8},{5,9},{6,10},{7,11},{8,12},{9,13},{1... | collective-permute-start | bytes 1572872 | tf_op jit(solution)/shard_map/ppermute | solution.py:38
  180.0 13.4 %collective-permute-start.46 = (f32[4,128,256]{2,1,0:T(8,128)S(1)}, f32[4,128,256]{2,1,0:T(8,128)S(1)}, u32[]{:S(2)}, u32[]{:S(2)}) collective-permute-start(f32[4,128,256]{2,1,0:T(8,128)S(1)} %get-tuple-element.106), channel_id=1, source_target_pairs={{0,12},{1,13},{2,14},{3,15},{4,0},{5,1},{6,2},{7,3},{8,4},{9,5},{1... | collective-permute-start | bytes 1572872 | tf_op jit(solution)/shard_map/ppermute | solution.py:38
  193.5 6.6 %collective-permute-start.47 = (f32[128,256]{1,0:T(8,128)S(1)}, f32[128,256]{1,0:T(8,128)S(1)}, u32[]{:S(2)}, u32[]{:S(2)}) collective-permute-start(f32[128,256]{1,0:T(8,128)S(1)} %get-tuple-element.112), channel_id=1, source_target_pairs={{0,2},{1,3},{2,0},{3,1},{4,6},{5,7},{6,4},{7,5},{8,10},{9,11},{10,... | collective-permute-start | bytes 393224 | tf_op jit(solution)/shard_map/ppermute | solution.py:38
  195.6 6.2 %collective-permute-start.48 = (f32[128,256]{1,0:T(8,128)S(1)}, f32[128,256]{1,0:T(8,128)S(1)}, u32[]{:S(2)}, u32[]{:S(2)}) collective-permute-start(f32[128,256]{1,0:T(8,128)S(1)} %get-tuple-element.113), channel_id=1, source_target_pairs={{0,1},{1,2},{2,3},{3,0},{4,5},{5,6},{6,7},{7,4},{8,9},{9,10},{10,1... | collective-permute-start | bytes 393224 | tf_op jit(solution)/shard_map/ppermute | solution.py:38
  197.5 5.0 %collective-permute-start.49 = (f32[128,256]{1,0:T(8,128)S(1)}, f32[128,256]{1,0:T(8,128)S(1)}, u32[]{:S(2)}, u32[]{:S(2)}) collective-permute-start(f32[128,256]{1,0:T(8,128)S(1)} %get-tuple-element.114), channel_id=1, source_target_pairs={{0,3},{1,0},{2,1},{3,2},{4,7},{5,4},{6,5},{7,6},{8,11},{9,8},{10,9... | collective-permute-start | bytes 393224 | tf_op jit(solution)/shard_map/ppermute | solution.py:38
  202.8 6.6 %collective-permute-start.50 = (f32[128,256]{1,0:T(8,128)S(1)}, f32[128,256]{1,0:T(8,128)S(1)}, u32[]{:S(2)}, u32[]{:S(2)}) collective-permute-start(f32[128,256]{1,0:T(8,128)S(1)} %shard_map.90), channel_id=1, source_target_pairs={{0,64},{16,80},{32,96},{48,112},{64,0},{80,16},{96,32},{112,48},{1... | collective-permute-start | bytes 393224 | tf_op jit(solution)/shard_map/ppermute | solution.py:43
  204.5 6.3 %collective-permute-start.51 = (f32[128,256]{1,0:T(8,128)S(1)}, f32[128,256]{1,0:T(8,128)S(1)}, u32[]{:S(2)}, u32[]{:S(2)}) collective-permute-start(f32[128,256]{1,0:T(8,128)S(1)} %shard_map.90), channel_id=1, source_target_pairs={{0,32},{16,48},{32,64},{48,80},{64,96},{80,112},{96,0},{112,16},{1... | collective-permute-start | bytes 393224 | tf_op jit(solution)/shard_map/ppermute | solution.py:43
  206.3 5.0 %collective-permute-start.52 = (f32[128,256]{1,0:T(8,128)S(1)}, f32[128,256]{1,0:T(8,128)S(1)}, u32[]{:S(2)}, u32[]{:S(2)}) collective-permute-start(f32[128,256]{1,0:T(8,128)S(1)} %shard_map.90), channel_id=1, source_target_pairs={{0,96},{16,112},{32,0},{48,16},{64,32},{80,48},{96,64},{112,80},{1... | collective-permute-start | bytes 393224 | tf_op jit(solution)/shard_map/ppermute | solution.py:43
  211.3 2.0 collective-permute-start.53
  215.6 10.9 %collective-permute-start.54 = (f32[4,128,256]{2,1,0:T(8,128)S(1)}, f32[4,128,256]{2,1,0:T(8,128)S(1)}, u32[]{:S(2)}, u32[]{:S(2)}) collective-permute-start(f32[4,128,256]{2,1,0:T(8,128)S(1)} %get-tuple-element.119), channel_id=1, source_target_pairs={{0,8},{1,9},{2,10},{3,11},{4,12},{5,13},{6,14},{7,15},{8,0},{9,1},... | collective-permute-start | bytes 1572872 | tf_op jit(solution)/shard_map/ppermute | solution.py:38
  216.4 15.6 %collective-permute-start.55 = (f32[4,128,256]{2,1,0:T(8,128)S(1)}, f32[4,128,256]{2,1,0:T(8,128)S(1)}, u32[]{:S(2)}, u32[]{:S(2)}) collective-permute-start(f32[4,128,256]{2,1,0:T(8,128)S(1)} %get-tuple-element.120), channel_id=1, source_target_pairs={{0,4},{1,5},{2,6},{3,7},{4,8},{5,9},{6,10},{7,11},{8,12},{9,13},{1... | collective-permute-start | bytes 1572872 | tf_op jit(solution)/shard_map/ppermute | solution.py:38
  218.7 13.4 %collective-permute-start.56 = (f32[4,128,256]{2,1,0:T(8,128)S(1)}, f32[4,128,256]{2,1,0:T(8,128)S(1)}, u32[]{:S(2)}, u32[]{:S(2)}) collective-permute-start(f32[4,128,256]{2,1,0:T(8,128)S(1)} %get-tuple-element.121), channel_id=1, source_target_pairs={{0,12},{1,13},{2,14},{3,15},{4,0},{5,1},{6,2},{7,3},{8,4},{9,5},{1... | collective-permute-start | bytes 1572872 | tf_op jit(solution)/shard_map/ppermute | solution.py:38
  232.1 6.6 %collective-permute-start.57 = (f32[128,256]{1,0:T(8,128)S(1)}, f32[128,256]{1,0:T(8,128)S(1)}, u32[]{:S(2)}, u32[]{:S(2)}) collective-permute-start(f32[128,256]{1,0:T(8,128)S(1)} %get-tuple-element.123), channel_id=1, source_target_pairs={{0,2},{1,3},{2,0},{3,1},{4,6},{5,7},{6,4},{7,5},{8,10},{9,11},{10,... | collective-permute-start | bytes 393224 | tf_op jit(solution)/shard_map/ppermute | solution.py:38
  233.3 6.8 %collective-permute-start.58 = (f32[128,256]{1,0:T(8,128)S(1)}, f32[128,256]{1,0:T(8,128)S(1)}, u32[]{:S(2)}, u32[]{:S(2)}) collective-permute-start(f32[128,256]{1,0:T(8,128)S(1)} %get-tuple-element.124), channel_id=1, source_target_pairs={{0,1},{1,2},{2,3},{3,0},{4,5},{5,6},{6,7},{7,4},{8,9},{9,10},{10,1... | collective-permute-start | bytes 393224 | tf_op jit(solution)/shard_map/ppermute | solution.py:38
  235.7 5.0 %collective-permute-start.59 = (f32[128,256]{1,0:T(8,128)S(1)}, f32[128,256]{1,0:T(8,128)S(1)}, u32[]{:S(2)}, u32[]{:S(2)}) collective-permute-start(f32[128,256]{1,0:T(8,128)S(1)} %get-tuple-element.125), channel_id=1, source_target_pairs={{0,3},{1,0},{2,1},{3,2},{4,7},{5,4},{6,5},{7,6},{8,11},{9,8},{10,9... | collective-permute-start | bytes 393224 | tf_op jit(solution)/shard_map/ppermute | solution.py:38

commit v7 on v6

--- a/solution.py
+++ b/solution.py
@@ -209,6 +209,34 @@
         ],
         compiler_params=pltpu.CompilerParams(vmem_limit_bytes=16 * 1024 * 1024),
     )(far(inverse), far(base))
+
+
+def last_kernel(inverse, base, *refs):
+    gone, done, (out, value, sems) = refs[:4], refs[4 : 3 + LEV], refs[3 + LEV :]
+    copies = [
+        pltpu.make_async_copy(ref, out.at[k], sems.at[k]) for k, ref in enumerate(done, 1)
+    ]
+    for copy in copies:
+        copy.start()
+    update = gone[0][...] + gone[1][...] + gone[2][...] + gone[3][...]
+    value[...] = dot(inverse[0].T, base[...] - update)
+    copies.append(pltpu.make_async_copy(value, out.at[0], sems.at[0]))
+    copies[-1].start()
+    for copy in copies:
+        copy.wait()
+
+
+def last_solve(inverse, base, gone, done):
+    operands = [inverse, base, *gone, *done]
+    return pl.pallas_call(
+        last_kernel,
+        in_specs=[pl.BlockSpec(memory_space=pltpu.VMEM)] * len(operands),
+        out_specs=pl.BlockSpec(memory_space=pl.ANY),
+        out_shape=pltpu.HBM((LEV, W, R), jnp.float32),
+        scratch_shapes=[pltpu.VMEM((W, R), jnp.float32), pltpu.SemaphoreType.DMA((LEV,))],
+        compiler_params=pltpu.CompilerParams(vmem_limit_bytes=16 * 1024 * 1024),
+        cost_estimate=pl.CostEstimate(flops=12 * W * W * R, bytes_accessed=4096, transcendentals=0),
+    )(*[near(value) for value in operands])
 
 
 def load_kernel(blocks, after, out, sems):
@@ -328,9 +356,11 @@
             return done
 
         gone = scatter_plane(back(level, level - 1, vectors, sums[level - 1], ()), beside)
-        (result[level - 1],) = solve(level - 1, (True,), inverse, solved[level - 1], gone)
+        if level > 1:
+            (result[level - 1],) = solve(level - 1, (True,), inverse, solved[level - 1], gone)
+    stacked = last_solve(inverse, solved[0], gone, result[1:])
     forward = jnp.stack(solved)[:, None, None]
-    solution = jnp.stack(result)[:, None, None]
+    solution = stacked[:, None, None]
     return (forward, solution)
 
 

time: 242 us -> 242 us (level)
    pallas_call x24 -> x23, Pallas kernels: 33.7 us -> 33.4 us  [fast_call(): pl.pallas_call(kernel, in_specs=[pl.BlockSpec(memory_space=pltpu.SMEM)] *...]
where the time goes in v7:
time: 242 us
  waiting for transfers between devices  104 us (43%)
  starting transfers between devices  93.6 us (39%)
  Pallas kernels  40.3 us (17%)
  other arithmetic  3.16 us (1%)
    ppermute x36, waiting for transfers between devices, shift_plane(): return lax.ppermute(value, BOTH, pairs)  67.3 us
    ppermute x36, starting transfers between devices, shift_plane(): return lax.ppermute(value, BOTH, pairs)  59.9 us
    pallas_call x23, Pallas kernels, fast_call(): pl.pallas_call(kernel, in_specs=[pl.BlockSpec(memory_space=pltpu.SMEM)] *...  33.4 us
    ppermute x18, starting transfers between devices, shift_z(): return lax.ppermute(value, 'prow', pairs)  33.2 us
    ppermute x18, waiting for transfers between devices, shift_z(): return lax.ppermute(value, 'prow', pairs)  24.9 us
    ppermute x6, waiting for transfers between devices, swap_core(): return lax.ppermute(value, 'prow', pairs)  11.4 us
  transfers between devices with their start and end apart: 60, of which 48 were waited for; matrix products, arithmetic and copies ran while one was open for 1% of the time, Pallas kernels for 9%

profile of v7, /device:TPU:0, one launch (start us, length us, event | category | flops | bytes accessed | tf_op | source)
XLA Modules:
  0.0 241.9 jit_solution(14332032102314217910)
XLA Ops:
  5.2 1.9 collective-permute-start
  8.5 3.2 %collective-permute-done = f32[128,256]{1,0:T(8,128)S(1)} collective-permute-done((f32[128,256]{1,0:T(8,128)S(1)}, f32[128,256]{1,0:T(8,128)S(1)}, u32[]{:S(2)}, u32[]{:S(2)}) %collective-permute-start) | collective-permute-done | bytes 131104 | tf_op jit(solution)/shard_map/ppermute | solution.py:38
  11.7 3.4 %collective-permute-start.3 = (f32[4,128,256]{2,1,0:T(8,128)S(1)}, f32[4,128,256]{2,1,0:T(8,128)S(1)}, u32[]{:S(2)}, u32[]{:S(2)}) collective-permute-start(f32[4,128,256]{2,1,0:T(8,128)S(1)} %fusion.4.after.refs_0_), channel_id=1, source_target_pairs={{0,2},{1,3},{2,0},{3,1},{4,6},{5,7},{6,4},{7,5},{8,10},{9,11},{10,... | collective-permute-start | bytes 1572872 | tf_op jit(solution)/shard_map/ppermute | solution.py:38
  15.7 2.6 %collective-permute-start.5 = (f32[4,128,256]{2,1,0:T(8,128)S(1)}, f32[4,128,256]{2,1,0:T(8,128)S(1)}, u32[]{:S(2)}, u32[]{:S(2)}) collective-permute-start(f32[4,128,256]{2,1,0:T(8,128)S(1)} %fusion.4.after.refs_0_), channel_id=1, source_target_pairs={{0,3},{1,0},{2,1},{3,2},{4,7},{5,4},{6,5},{7,6},{8,11},{9,8},{10,9... | collective-permute-start | bytes 1572872 | tf_op jit(solution)/shard_map/ppermute | solution.py:38
  19.0 4.7 %shard_map.69.refs_4_.refs_2_ = f32[6,32,128,128]{3,2,1,0:T(8,128)S(1)} custom-call(f32[6,32,128,128]{3,2,1,0:T(8,128)} %bitcast.196, f32[4,128,256]{2,1,0:T(8,128)S(1)} %fusion.4.after.refs_0_), custom_call_target="tpu_custom_call" | custom-call | bytes 12582912 | tf_op jit(solution)/shard_map/pallas_call | solution.py:253
  23.8 4.3 %collective-permute-done.4.refs_2_ = f32[4,128,256]{2,1,0:T(8,128)S(1)} collective-permute-done((f32[4,128,256]{2,1,0:T(8,128)S(1)}, f32[4,128,256]{2,1,0:T(8,128)S(1)}, u32[]{:S(2)}, u32[]{:S(2)}) %collective-permute-start.4) | collective-permute-done | bytes 524320 | tf_op jit(solution)/shard_map/ppermute | solution.py:38
  28.5 2.3 shard_map.70
  31.0 1.9 collective-permute-done.6.refs_1_
  32.9 4.0 %collective-permute-start.7 = (f32[128,256]{1,0:T(8,128)S(1)}, f32[128,256]{1,0:T(8,128)S(1)}, u32[]{:S(2)}, u32[]{:S(2)}) collective-permute-start(f32[128,256]{1,0:T(8,128)S(1)} %get-tuple-element.67), channel_id=1, source_target_pairs={{0,64},{16,80},{32,96},{48,112},{64,0},{80,16},{96,32},{112,48},{1... | collective-permute-start | bytes 393224 | tf_op jit(solution)/shard_map/ppermute | solution.py:43
  37.9 2.2 collective-permute-start.9
  41.2 2.5 %collective-permute-done.8.refs_2_ = f32[128,256]{1,0:T(8,128)S(1)} collective-permute-done((f32[128,256]{1,0:T(8,128)S(1)}, f32[128,256]{1,0:T(8,128)S(1)}, u32[]{:S(2)}, u32[]{:S(2)}) %collective-permute-start.8) | collective-permute-done | bytes 131104 | tf_op jit(solution)/shard_map/ppermute | solution.py:43
  44.5 1.9 collective-permute-start.10
  47.0 2.6 %collective-permute-start.12 = (f32[128,256]{1,0:T(8,128)S(1)}, f32[128,256]{1,0:T(8,128)S(1)}, u32[]{:S(2)}, u32[]{:S(2)}) collective-permute-start(f32[128,256]{1,0:T(8,128)S(1)} %shard_map.72.base), channel_id=1, source_target_pairs={{0,12},{1,13},{2,14},{3,15},{4,0},{5,1},{6,2},{7,3},{8,4},{9,5},{1... | collective-permute-start | bytes 393224 | tf_op jit(solution)/shard_map/ppermute | solution.py:38
  52.6 2.1 collective-permute-start.13
  56.2 1.8 collective-permute-start.15
  58.0 2.9 %shard_map.73 = (f32[4,128,256]{2,1,0:T(8,128)S(1)}, f32[4,128,256]{2,1,0:T(8,128)S(1)}) custom-call(s32[32]{0:T(128)S(1)} %get-tuple-element.164.take, s32[32]{0:T(128)S(1)} %get-tuple-element.149.put, s32[32]{0:T(128)S(1)} %get-tuple-element.143.live, f32[4,128,256]{2,1,0:T(8,128)S(1)} %fusion.4.after.refs_0_, ...), custom_call_target="tpu_custom_call" | custom-call | flops 1073741824 | bytes 4096 | tf_op jit(solution)/shard_map/pallas_call | solution.py:66
  60.8 2.7 %collective-permute-done.13.refs_1_ = f32[4,128,256]{2,1,0:T(8,128)S(1)} collective-permute-done((f32[4,128,256]{2,1,0:T(8,128)S(1)}, f32[4,128,256]{2,1,0:T(8,128)S(1)}, u32[]{:S(2)}, u32[]{:S(2)}) %collective-permute-start.13) | collective-permute-done | bytes 524320 | tf_op jit(solution)/shard_map/ppermute | solution.py:38
  63.5 5.5 %collective-permute-done.14.refs_2_ = f32[4,128,256]{2,1,0:T(8,128)S(1)} collective-permute-done((f32[4,128,256]{2,1,0:T(8,128)S(1)}, f32[4,128,256]{2,1,0:T(8,128)S(1)}, u32[]{:S(2)}, u32[]{:S(2)}) %collective-permute-start.14) | collective-permute-done | bytes 524320 | tf_op jit(solution)/shard_map/ppermute | solution.py:38
  69.0 2.3 shard_map.74
  71.5 1.9 collective-permute-done.16.refs_1_
  73.4 2.2 collective-permute-start.17
  78.8 2.5 %collective-permute-done.17.refs_1_ = f32[128,256]{1,0:T(8,128)S(1)} collective-permute-done((f32[128,256]{1,0:T(8,128)S(1)}, f32[128,256]{1,0:T(8,128)S(1)}, u32[]{:S(2)}, u32[]{:S(2)}) %collective-permute-start.17) | collective-permute-done | bytes 131104 | tf_op jit(solution)/shard_map/ppermute | solution.py:43
  81.3 2.0 collective-permute-done.18.refs_2_
  83.7 1.8 collective-permute-start.20
  85.5 2.4 collective-permute-start.21
  92.9 2.3 collective-permute-start.23
  96.7 1.8 collective-permute-start.25
  98.5 2.9 %shard_map.77 = (f32[4,128,256]{2,1,0:T(8,128)S(1)}, f32[4,128,256]{2,1,0:T(8,128)S(1)}) custom-call(s32[32]{0:T(128)S(1)} %get-tuple-element.167.take, s32[32]{0:T(128)S(1)} %get-tuple-element.146.put, s32[32]{0:T(128)S(1)} %get-tuple-element.140.live, f32[4,128,256]{2,1,0:T(8,128)S(1)} %fusion.4.after.refs_0_, ...), custom_call_target="tpu_custom_call" | custom-call | flops 1073741824 | bytes 4096 | tf_op jit(solution)/shard_map/pallas_call | solution.py:66
  101.3 2.9 %shard_map.78 = (f32[4,128,256]{2,1,0:T(8,128)S(1)}, f32[4,128,256]{2,1,0:T(8,128)S(1)}) custom-call(s32[32]{0:T(128)S(1)} %get-tuple-element.166.take, s32[32]{0:T(128)S(1)} %get-tuple-element.147.put, s32[32]{0:T(128)S(1)} %get-tuple-element.141.live, f32[4,128,256]{2,1,0:T(8,128)S(1)} %pad_maximum_fusion.2.refs_0_, ...), custom_call_target="tpu_custom_call" | custom-call | flops 1073741824 | bytes 4096 | tf_op jit(solution)/shard_map/pallas_call | solution.py:66
  104.2 5.3 %collective-permute-done.24.refs_2_ = f32[4,128,256]{2,1,0:T(8,128)S(1)} collective-permute-done((f32[4,128,256]{2,1,0:T(8,128)S(1)}, f32[4,128,256]{2,1,0:T(8,128)S(1)}, u32[]{:S(2)}, u32[]{:S(2)}) %collective-permute-start.24) | collective-permute-done | bytes 524320 | tf_op jit(solution)/shard_map/ppermute | solution.py:38
  109.5 2.3 shard_map.79
  111.9 1.9 collective-permute-done.26.refs_1_
  113.9 2.1 collective-permute-start.27
  119.2 2.6 %collective-permute-done.27.refs_1_ = f32[128,256]{1,0:T(8,128)S(1)} collective-permute-done((f32[128,256]{1,0:T(8,128)S(1)}, f32[128,256]{1,0:T(8,128)S(1)}, u32[]{:S(2)}, u32[]{:S(2)}) %collective-permute-start.27) | collective-permute-done | bytes 131104 | tf_op jit(solution)/shard_map/ppermute | solution.py:43
  121.8 2.0 collective-permute-done.28.refs_2_
  124.5 2.1 collective-permute-start.30
  129.8 2.7 %collective-permute-done.30 = f32[128,256]{1,0:T(8,128)S(1)} collective-permute-done((f32[128,256]{1,0:T(8,128)S(1)}, f32[128,256]{1,0:T(8,128)S(1)}, u32[]{:S(2)}, u32[]{:S(2)}) %collective-permute-start.30) | collective-permute-done | bytes 131104 | tf_op jit(solution)/shard_map/ppermute | solution.py:43
  134.3 1.9 collective-permute-done.33.refs_1_
  136.2 2.4 shard_map.82
  139.3 2.2 collective-permute-start.35
  142.6 6.9 %collective-permute-done.34.refs_3_.refs_1_ = f32[4,128,256]{2,1,0:T(8,128)S(1)} collective-permute-done((f32[4,128,256]{2,1,0:T(8,128)S(1)}, f32[4,128,256]{2,1,0:T(8,128)S(1)}, u32[]{:S(2)}, u32[]{:S(2)}) %collective-permute-start.34) | collective-permute-done | bytes 524320 | tf_op jit(solution)/shard_map/ppermute | solution.py:38
  149.4 2.6 %shard_map.84 = (f32[4,128,256]{2,1,0:T(8,128)S(1)}, f32[4,128,256]{2,1,0:T(8,128)S(1)}, f32[4,128,256]{2,1,0:T(8,128)S(1)}, f32[4,128,256]{2,1,0:T(8,128)S(1)}) custom-call(s32[32]{0:T(128)S(1)} %get-tuple-element.172.take, s32[32]{0:T(128)S(1)} %get-tuple-element.129.put, s32[32]{0:T(128)S(1)} %get-tuple-element.140.live, ...), custom_call_target="tpu_custom_call" | custom-call | flops 1073741824 | bytes 4096 | tf_op jit(solution)/shard_map/pallas_call | solution.py:66
  152.1 2.6 %shard_map.83 = (f32[4,128,256]{2,1,0:T(8,128)S(1)}, f32[4,128,256]{2,1,0:T(8,128)S(1)}, f32[4,128,256]{2,1,0:T(8,128)S(1)}, f32[4,128,256]{2,1,0:T(8,128)S(1)}) custom-call(s32[32]{0:T(128)S(1)} %get-tuple-element.171.take, s32[32]{0:T(128)S(1)} %get-tuple-element.130.put, s32[32]{0:T(128)S(1)} %get-tuple-element.141.live, ...), custom_call_target="tpu_custom_call" | custom-call | flops 1073741824 | bytes 4096 | tf_op jit(solution)/shard_map/pallas_call | solution.py:66
  155.1 2.1 collective-permute-start.37
  158.7 1.8 collective-permute-start.39
  164.0 1.8 collective-permute-start.40
  165.8 1.9 collective-permute-start.41
  172.7 1.9 collective-permute-done.43.refs_1_
  174.6 2.4 shard_map.87
  177.8 2.2 collective-permute-start.45
  181.0 6.9 %collective-permute-done.44.refs_7_.refs_1_ = f32[4,128,256]{2,1,0:T(8,128)S(1)} collective-permute-done((f32[4,128,256]{2,1,0:T(8,128)S(1)}, f32[4,128,256]{2,1,0:T(8,128)S(1)}, u32[]{:S(2)}, u32[]{:S(2)}) %collective-permute-start.44) | collective-permute-done | bytes 524320 | tf_op jit(solution)/shard_map/ppermute | solution.py:38
  187.9 3.1 %shard_map.88 = (f32[4,128,256]{2,1,0:T(8,128)S(1)}, f32[4,128,256]{2,1,0:T(8,128)S(1)}, f32[4,128,256]{2,1,0:T(8,128)S(1)}, f32[4,128,256]{2,1,0:T(8,128)S(1)}) custom-call(s32[32]{0:T(128)S(1)} %get-tuple-element.173.take, s32[32]{0:T(128)S(1)} %get-tuple-element.128.put, s32[32]{0:T(128)S(1)} %get-tuple-element.143.live, ...), custom_call_target="tpu_custom_call" | custom-call | flops 1073741824 | bytes 4096 | tf_op jit(solution)/shard_map/pallas_call | solution.py:66
  190.9 2.4 %collective-permute-done.45.refs_2_ = f32[4,128,256]{2,1,0:T(8,128)S(1)} collective-permute-done((f32[4,128,256]{2,1,0:T(8,128)S(1)}, f32[4,128,256]{2,1,0:T(8,128)S(1)}, u32[]{:S(2)}, u32[]{:S(2)}) %collective-permute-start.45) | collective-permute-done | bytes 524320 | tf_op jit(solution)/shard_map/ppermute | solution.py:38
  193.5 2.1 collective-permute-start.47
  195.6 1.8 collective-permute-start.48
  200.1 1.7 collective-permute-done.48.refs_2_
  202.8 1.8 collective-permute-start.50
  204.5 1.8 collective-permute-start.51
  211.4 1.9 collective-permute-done.53.refs_1_
  213.3 2.4 shard_map.91
  216.5 2.2 collective-permute-start.55
  219.7 6.8 %collective-permute-done.54.refs_1_ = f32[4,128,256]{2,1,0:T(8,128)S(1)} collective-permute-done((f32[4,128,256]{2,1,0:T(8,128)S(1)}, f32[4,128,256]{2,1,0:T(8,128)S(1)}, u32[]{:S(2)}, u32[]{:S(2)}) %collective-permute-start.54) | collective-permute-done | bytes 524320 | tf_op jit(solution)/shard_map/ppermute | solution.py:38
  226.5 5.5 %collective-permute-done.55.refs_2_ = f32[4,128,256]{2,1,0:T(8,128)S(1)} collective-permute-done((f32[4,128,256]{2,1,0:T(8,128)S(1)}, f32[4,128,256]{2,1,0:T(8,128)S(1)}, u32[]{:S(2)}, u32[]{:S(2)}) %collective-permute-start.55) | collective-permute-done | bytes 524320 | tf_op jit(solution)/shard_map/ppermute | solution.py:38
  233.3 2.4 collective-permute-start.58
  (99 shorter events, 67.2 us)
Async XLA Ops:
  1.9 6.6 %collective-permute-start.1 = (f32[128,256]{1,0:T(8,128)S(1)}, f32[128,256]{1,0:T(8,128)S(1)}, u32[]{:S(2)}, u32[]{:S(2)}) collective-permute-start(f32[128,256]{1,0:T(8,128)S(1)} %shard_map.68.base), channel_id=1, source_target_pairs={{0,4},{1,5},{2,6},{3,7},{4,8},{5,9},{6,10},{7,11},{8,12},{9,13},{1... | collective-permute-start | bytes 393224 | tf_op jit(solution)/shard_map/ppermute | solution.py:38
  3.5 5.0 %collective-permute-start.2 = (f32[128,256]{1,0:T(8,128)S(1)}, f32[128,256]{1,0:T(8,128)S(1)}, u32[]{:S(2)}, u32[]{:S(2)}) collective-permute-start(f32[128,256]{1,0:T(8,128)S(1)} %shard_map.68.base), channel_id=1, source_target_pairs={{0,12},{1,13},{2,14},{3,15},{4,0},{5,1},{6,2},{7,3},{8,4},{9,5},{1... | collective-permute-start | bytes 393224 | tf_op jit(solution)/shard_map/ppermute | solution.py:38
  5.2 6.5 %collective-permute-start = (f32[128,256]{1,0:T(8,128)S(1)}, f32[128,256]{1,0:T(8,128)S(1)}, u32[]{:S(2)}, u32[]{:S(2)}) collective-permute-start(f32[128,256]{1,0:T(8,128)S(1)} %shard_map.68.base), channel_id=1, source_target_pairs={{0,8},{1,9},{2,10},{3,11},{4,12},{5,13},{6,14},{7,15},{8,0},{9,1},... | collective-permute-start | bytes 393224 | tf_op jit(solution)/shard_map/ppermute | solution.py:38
  11.7 12.1 %collective-permute-start.3 = (f32[4,128,256]{2,1,0:T(8,128)S(1)}, f32[4,128,256]{2,1,0:T(8,128)S(1)}, u32[]{:S(2)}, u32[]{:S(2)}) collective-permute-start(f32[4,128,256]{2,1,0:T(8,128)S(1)} %fusion.4.after.refs_0_), channel_id=1, source_target_pairs={{0,2},{1,3},{2,0},{3,1},{4,6},{5,7},{6,4},{7,5},{8,10},{9,11},{10,... | collective-permute-start | bytes 1572872 | tf_op jit(solution)/shard_map/ppermute | solution.py:38
  15.0 13.0 %collective-permute-start.4 = (f32[4,128,256]{2,1,0:T(8,128)S(1)}, f32[4,128,256]{2,1,0:T(8,128)S(1)}, u32[]{:S(2)}, u32[]{:S(2)}) collective-permute-start(f32[4,128,256]{2,1,0:T(8,128)S(1)} %fusion.4.after.refs_0_), channel_id=1, source_target_pairs={{0,1},{1,2},{2,3},{3,0},{4,5},{5,6},{6,7},{7,4},{8,9},{9,10},{10,1... | collective-permute-start | bytes 1572872 | tf_op jit(solution)/shard_map/ppermute | solution.py:38
  15.7 12.8 %collective-permute-start.5 = (f32[4,128,256]{2,1,0:T(8,128)S(1)}, f32[4,128,256]{2,1,0:T(8,128)S(1)}, u32[]{:S(2)}, u32[]{:S(2)}) collective-permute-start(f32[4,128,256]{2,1,0:T(8,128)S(1)} %fusion.4.after.refs_0_), channel_id=1, source_target_pairs={{0,3},{1,0},{2,1},{3,2},{4,7},{5,4},{6,5},{7,6},{8,11},{9,8},{10,9... | collective-permute-start | bytes 1572872 | tf_op jit(solution)/shard_map/ppermute | solution.py:38
  23.7 20.5 %copy-start = (f32[4,1,1,128,128]{4,3,2,1,0:T(8,128)S(1)}, f32[4,1,1,128,128]{4,3,2,1,0:T(8,128)}, u32[]{:S(2)}) copy-start(f32[4,1,1,128,128]{4,3,2,1,0:T(8,128)} %param.6) | copy-start | bytes 786436
  23.7 20.5 %copy-start.1 = (f32[4,1,1,128,256]{4,3,2,1,0:T(8,128)S(1)}, f32[4,1,1,128,256]{4,3,2,1,0:T(8,128)}, u32[]{:S(2)}) copy-start(f32[4,1,1,128,256]{4,3,2,1,0:T(8,128)} %param.5) | copy-start | bytes 1572868
  30.9 2.0 collective-permute-start.6
  32.9 8.2 %collective-permute-start.7 = (f32[128,256]{1,0:T(8,128)S(1)}, f32[128,256]{1,0:T(8,128)S(1)}, u32[]{:S(2)}, u32[]{:S(2)}) collective-permute-start(f32[128,256]{1,0:T(8,128)S(1)} %get-tuple-element.67), channel_id=1, source_target_pairs={{0,64},{16,80},{32,96},{48,112},{64,0},{80,16},{96,32},{112,48},{1... | collective-permute-start | bytes 393224 | tf_op jit(solution)/shard_map/ppermute | solution.py:43
  36.9 6.8 %collective-permute-start.8 = (f32[128,256]{1,0:T(8,128)S(1)}, f32[128,256]{1,0:T(8,128)S(1)}, u32[]{:S(2)}, u32[]{:S(2)}) collective-permute-start(f32[128,256]{1,0:T(8,128)S(1)} %get-tuple-element.68), channel_id=1, source_target_pairs={{0,32},{16,48},{32,64},{48,80},{64,96},{80,112},{96,0},{112,16},{1... | collective-permute-start | bytes 393224 | tf_op jit(solution)/shard_map/ppermute | solution.py:43
  37.9 6.3 %collective-permute-start.9 = (f32[128,256]{1,0:T(8,128)S(1)}, f32[128,256]{1,0:T(8,128)S(1)}, u32[]{:S(2)}, u32[]{:S(2)}) collective-permute-start(f32[128,256]{1,0:T(8,128)S(1)} %get-tuple-element.69), channel_id=1, source_target_pairs={{0,96},{16,112},{32,0},{48,16},{64,32},{80,48},{96,64},{112,80},{1... | collective-permute-start | bytes 393224 | tf_op jit(solution)/shard_map/ppermute | solution.py:43
  44.5 6.6 %collective-permute-start.10 = (f32[128,256]{1,0:T(8,128)S(1)}, f32[128,256]{1,0:T(8,128)S(1)}, u32[]{:S(2)}, u32[]{:S(2)}) collective-permute-start(f32[128,256]{1,0:T(8,128)S(1)} %shard_map.72.base), channel_id=1, source_target_pairs={{0,8},{1,9},{2,10},{3,11},{4,12},{5,13},{6,14},{7,15},{8,0},{9,1},... | collective-permute-start | bytes 393224 | tf_op jit(solution)/shard_map/ppermute | solution.py:38
  46.4 6.2 %collective-permute-start.11 = (f32[128,256]{1,0:T(8,128)S(1)}, f32[128,256]{1,0:T(8,128)S(1)}, u32[]{:S(2)}, u32[]{:S(2)}) collective-permute-start(f32[128,256]{1,0:T(8,128)S(1)} %shard_map.72.base), channel_id=1, source_target_pairs={{0,4},{1,5},{2,6},{3,7},{4,8},{5,9},{6,10},{7,11},{8,12},{9,13},{1... | collective-permute-start | bytes 393224 | tf_op jit(solution)/shard_map/ppermute | solution.py:38
  47.0 5.6 %collective-permute-start.12 = (f32[128,256]{1,0:T(8,128)S(1)}, f32[128,256]{1,0:T(8,128)S(1)}, u32[]{:S(2)}, u32[]{:S(2)}) collective-permute-start(f32[128,256]{1,0:T(8,128)S(1)} %shard_map.72.base), channel_id=1, source_target_pairs={{0,12},{1,13},{2,14},{3,15},{4,0},{5,1},{6,2},{7,3},{8,4},{9,5},{1... | collective-permute-start | bytes 393224 | tf_op jit(solution)/shard_map/ppermute | solution.py:38
  52.6 10.9 %collective-permute-start.13 = (f32[4,128,256]{2,1,0:T(8,128)S(1)}, f32[4,128,256]{2,1,0:T(8,128)S(1)}, u32[]{:S(2)}, u32[]{:S(2)}) collective-permute-start(f32[4,128,256]{2,1,0:T(8,128)S(1)} %pad_maximum_fusion.2.refs_0_), channel_id=1, source_target_pairs={{0,2},{1,3},{2,0},{3,1},{4,6},{5,7},{6,4},{7,5},{8,10},{9,11},{10,... | collective-permute-start | bytes 1572872 | tf_op jit(solution)/shard_map/ppermute | solution.py:38
  54.7 14.3 %collective-permute-start.14 = (f32[4,128,256]{2,1,0:T(8,128)S(1)}, f32[4,128,256]{2,1,0:T(8,128)S(1)}, u32[]{:S(2)}, u32[]{:S(2)}) collective-permute-start(f32[4,128,256]{2,1,0:T(8,128)S(1)} %pad_maximum_fusion.2.refs_0_), channel_id=1, source_target_pairs={{0,1},{1,2},{2,3},{3,0},{4,5},{5,6},{6,7},{7,4},{8,9},{9,10},{10,1... | collective-permute-start | bytes 1572872 | tf_op jit(solution)/shard_map/ppermute | solution.py:38
  56.2 12.8 %collective-permute-start.15 = (f32[4,128,256]{2,1,0:T(8,128)S(1)}, f32[4,128,256]{2,1,0:T(8,128)S(1)}, u32[]{:S(2)}, u32[]{:S(2)}) collective-permute-start(f32[4,128,256]{2,1,0:T(8,128)S(1)} %pad_maximum_fusion.2.refs_0_), channel_id=1, source_target_pairs={{0,3},{1,0},{2,1},{3,2},{4,7},{5,4},{6,5},{7,6},{8,11},{9,8},{10,9... | collective-permute-start | bytes 1572872 | tf_op jit(solution)/shard_map/ppermute | solution.py:38
  71.4 2.0 collective-permute-start.16
  73.4 7.9 %collective-permute-start.17 = (f32[128,256]{1,0:T(8,128)S(1)}, f32[128,256]{1,0:T(8,128)S(1)}, u32[]{:S(2)}, u32[]{:S(2)}) collective-permute-start(f32[128,256]{1,0:T(8,128)S(1)} %get-tuple-element.75), channel_id=1, source_target_pairs={{0,64},{16,80},{32,96},{48,112},{64,0},{80,16},{96,32},{112,48},{1... | collective-permute-start | bytes 393224 | tf_op jit(solution)/shard_map/ppermute | solution.py:43
  75.6 7.8 %collective-permute-start.18 = (f32[128,256]{1,0:T(8,128)S(1)}, f32[128,256]{1,0:T(8,128)S(1)}, u32[]{:S(2)}, u32[]{:S(2)}) collective-permute-start(f32[128,256]{1,0:T(8,128)S(1)} %get-tuple-element.76), channel_id=1, source_target_pairs={{0,32},{16,48},{32,64},{48,80},{64,96},{80,112},{96,0},{112,16},{1... | collective-permute-start | bytes 393224 | tf_op jit(solution)/shard_map/ppermute | solution.py:43
  77.1 6.3 %collective-permute-start.19 = (f32[128,256]{1,0:T(8,128)S(1)}, f32[128,256]{1,0:T(8,128)S(1)}, u32[]{:S(2)}, u32[]{:S(2)}) collective-permute-start(f32[128,256]{1,0:T(8,128)S(1)} %get-tuple-element.77), channel_id=1, source_target_pairs={{0,96},{16,112},{32,0},{48,16},{64,32},{80,48},{96,64},{112,80},{1... | collective-permute-start | bytes 393224 | tf_op jit(solution)/shard_map/ppermute | solution.py:43
  83.7 6.6 %collective-permute-start.20 = (f32[128,256]{1,0:T(8,128)S(1)}, f32[128,256]{1,0:T(8,128)S(1)}, u32[]{:S(2)}, u32[]{:S(2)}) collective-permute-start(f32[128,256]{1,0:T(8,128)S(1)} %shard_map.76.base), channel_id=1, source_target_pairs={{0,8},{1,9},{2,10},{3,11},{4,12},{5,13},{6,14},{7,15},{8,0},{9,1},... | collective-permute-start | bytes 393224 | tf_op jit(solution)/shard_map/ppermute | solution.py:38
  85.5 6.2 %collective-permute-start.21 = (f32[128,256]{1,0:T(8,128)S(1)}, f32[128,256]{1,0:T(8,128)S(1)}, u32[]{:S(2)}, u32[]{:S(2)}) collective-permute-start(f32[128,256]{1,0:T(8,128)S(1)} %shard_map.76.base), channel_id=1, source_target_pairs={{0,4},{1,5},{2,6},{3,7},{4,8},{5,9},{6,10},{7,11},{8,12},{9,13},{1... | collective-permute-start | bytes 393224 | tf_op jit(solution)/shard_map/ppermute | solution.py:38
  87.9 5.0 %collective-permute-start.22 = (f32[128,256]{1,0:T(8,128)S(1)}, f32[128,256]{1,0:T(8,128)S(1)}, u32[]{:S(2)}, u32[]{:S(2)}) collective-permute-start(f32[128,256]{1,0:T(8,128)S(1)} %shard_map.76.base), channel_id=1, source_target_pairs={{0,12},{1,13},{2,14},{3,15},{4,0},{5,1},{6,2},{7,3},{8,4},{9,5},{1... | collective-permute-start | bytes 393224 | tf_op jit(solution)/shard_map/ppermute | solution.py:38
  92.9 11.3 %collective-permute-start.23 = (f32[4,128,256]{2,1,0:T(8,128)S(1)}, f32[4,128,256]{2,1,0:T(8,128)S(1)}, u32[]{:S(2)}, u32[]{:S(2)}) collective-permute-start(f32[4,128,256]{2,1,0:T(8,128)S(1)} %pad_maximum_fusion.3.refs_0_), channel_id=1, source_target_pairs={{0,2},{1,3},{2,0},{3,1},{4,6},{5,7},{6,4},{7,5},{8,10},{9,11},{10,... | collective-permute-start | bytes 1572872 | tf_op jit(solution)/shard_map/ppermute | solution.py:38
  95.2 14.3 %collective-permute-start.24 = (f32[4,128,256]{2,1,0:T(8,128)S(1)}, f32[4,128,256]{2,1,0:T(8,128)S(1)}, u32[]{:S(2)}, u32[]{:S(2)}) collective-permute-start(f32[4,128,256]{2,1,0:T(8,128)S(1)} %pad_maximum_fusion.3.refs_0_), channel_id=1, source_target_pairs={{0,1},{1,2},{2,3},{3,0},{4,5},{5,6},{6,7},{7,4},{8,9},{9,10},{10,1... | collective-permute-start | bytes 1572872 | tf_op jit(solution)/shard_map/ppermute | solution.py:38
  96.7 12.8 %collective-permute-start.25 = (f32[4,128,256]{2,1,0:T(8,128)S(1)}, f32[4,128,256]{2,1,0:T(8,128)S(1)}, u32[]{:S(2)}, u32[]{:S(2)}) collective-permute-start(f32[4,128,256]{2,1,0:T(8,128)S(1)} %pad_maximum_fusion.3.refs_0_), channel_id=1, source_target_pairs={{0,3},{1,0},{2,1},{3,2},{4,7},{5,4},{6,5},{7,6},{8,11},{9,8},{10,9... | collective-permute-start | bytes 1572872 | tf_op jit(solution)/shard_map/ppermute | solution.py:38
  111.8 2.0 collective-permute-start.26
  113.9 7.9 %collective-permute-start.27 = (f32[128,256]{1,0:T(8,128)S(1)}, f32[128,256]{1,0:T(8,128)S(1)}, u32[]{:S(2)}, u32[]{:S(2)}) collective-permute-start(f32[128,256]{1,0:T(8,128)S(1)} %get-tuple-element.85), channel_id=1, source_target_pairs={{0,64},{16,80},{32,96},{48,112},{64,0},{80,16},{96,32},{112,48},{1... | collective-permute-start | bytes 393224 | tf_op jit(solution)/shard_map/ppermute | solution.py:43
  115.9 7.9 %collective-permute-start.28 = (f32[128,256]{1,0:T(8,128)S(1)}, f32[128,256]{1,0:T(8,128)S(1)}, u32[]{:S(2)}, u32[]{:S(2)}) collective-permute-start(f32[128,256]{1,0:T(8,128)S(1)} %get-tuple-element.86), channel_id=1, source_target_pairs={{0,32},{16,48},{32,64},{48,80},{64,96},{80,112},{96,0},{112,16},{1... | collective-permute-start | bytes 393224 | tf_op jit(solution)/shard_map/ppermute | solution.py:43
  117.5 6.3 %collective-permute-start.29 = (f32[128,256]{1,0:T(8,128)S(1)}, f32[128,256]{1,0:T(8,128)S(1)}, u32[]{:S(2)}, u32[]{:S(2)}) collective-permute-start(f32[128,256]{1,0:T(8,128)S(1)} %get-tuple-element.87), channel_id=1, source_target_pairs={{0,96},{16,112},{32,0},{48,16},{64,32},{80,48},{96,64},{112,80},{1... | collective-permute-start | bytes 393224 | tf_op jit(solution)/shard_map/ppermute | solution.py:43
  124.5 8.0 %collective-permute-start.30 = (f32[128,256]{1,0:T(8,128)S(1)}, f32[128,256]{1,0:T(8,128)S(1)}, u32[]{:S(2)}, u32[]{:S(2)}) collective-permute-start(f32[128,256]{1,0:T(8,128)S(1)} %get-tuple-element.89.refs_6_), channel_id=1, source_target_pairs={{0,64},{16,80},{32,96},{48,112},{64,0},{80,16},{96,32},{112,48},{1... | collective-permute-start | bytes 393224 | tf_op jit(solution)/shard_map/ppermute | solution.py:43
  126.6 7.6 %collective-permute-start.31 = (f32[128,256]{1,0:T(8,128)S(1)}, f32[128,256]{1,0:T(8,128)S(1)}, u32[]{:S(2)}, u32[]{:S(2)}) collective-permute-start(f32[128,256]{1,0:T(8,128)S(1)} %get-tuple-element.89.refs_6_), channel_id=1, source_target_pairs={{0,32},{16,48},{32,64},{48,80},{64,96},{80,112},{96,0},{112,16},{1... | collective-permute-start | bytes 393224 | tf_op jit(solution)/shard_map/ppermute | solution.py:43
  128.1 6.0 %collective-permute-start.32 = (f32[128,256]{1,0:T(8,128)S(1)}, f32[128,256]{1,0:T(8,128)S(1)}, u32[]{:S(2)}, u32[]{:S(2)}) collective-permute-start(f32[128,256]{1,0:T(8,128)S(1)} %get-tuple-element.89.refs_6_), channel_id=1, source_target_pairs={{0,96},{16,112},{32,0},{48,16},{64,32},{80,48},{96,64},{112,80},{1... | collective-permute-start | bytes 393224 | tf_op jit(solution)/shard_map/ppermute | solution.py:43
  134.2 2.0 collective-permute-start.33
  138.6 10.9 %collective-permute-start.34 = (f32[4,128,256]{2,1,0:T(8,128)S(1)}, f32[4,128,256]{2,1,0:T(8,128)S(1)}, u32[]{:S(2)}, u32[]{:S(2)}) collective-permute-start(f32[4,128,256]{2,1,0:T(8,128)S(1)} %get-tuple-element.91), channel_id=1, source_target_pairs={{0,8},{1,9},{2,10},{3,11},{4,12},{5,13},{6,14},{7,15},{8,0},{9,1},... | collective-permute-start | bytes 1572872 | tf_op jit(solution)/shard_map/ppermute | solution.py:38
  139.3 15.6 %collective-permute-start.35 = (f32[4,128,256]{2,1,0:T(8,128)S(1)}, f32[4,128,256]{2,1,0:T(8,128)S(1)}, u32[]{:S(2)}, u32[]{:S(2)}) collective-permute-start(f32[4,128,256]{2,1,0:T(8,128)S(1)} %get-tuple-element.92), channel_id=1, source_target_pairs={{0,4},{1,5},{2,6},{3,7},{4,8},{5,9},{6,10},{7,11},{8,12},{9,13},{1... | collective-permute-start | bytes 1572872 | tf_op jit(solution)/shard_map/ppermute | solution.py:38
  141.5 13.4 %collective-permute-start.36 = (f32[4,128,256]{2,1,0:T(8,128)S(1)}, f32[4,128,256]{2,1,0:T(8,128)S(1)}, u32[]{:S(2)}, u32[]{:S(2)}) collective-permute-start(f32[4,128,256]{2,1,0:T(8,128)S(1)} %get-tuple-element.93), channel_id=1, source_target_pairs={{0,12},{1,13},{2,14},{3,15},{4,0},{5,1},{6,2},{7,3},{8,4},{9,5},{1... | collective-permute-start | bytes 1572872 | tf_op jit(solution)/shard_map/ppermute | solution.py:38
  155.1 6.6 %collective-permute-start.37 = (f32[128,256]{1,0:T(8,128)S(1)}, f32[128,256]{1,0:T(8,128)S(1)}, u32[]{:S(2)}, u32[]{:S(2)}) collective-permute-start(f32[128,256]{1,0:T(8,128)S(1)} %get-tuple-element.97), channel_id=1, source_target_pairs={{0,2},{1,3},{2,0},{3,1},{4,6},{5,7},{6,4},{7,5},{8,10},{9,11},{10,... | collective-permute-start | bytes 393224 | tf_op jit(solution)/shard_map/ppermute | solution.py:38
  157.2 6.2 %collective-permute-start.38 = (f32[128,256]{1,0:T(8,128)S(1)}, f32[128,256]{1,0:T(8,128)S(1)}, u32[]{:S(2)}, u32[]{:S(2)}) collective-permute-start(f32[128,256]{1,0:T(8,128)S(1)} %get-tuple-element.98), channel_id=1, source_target_pairs={{0,1},{1,2},{2,3},{3,0},{4,5},{5,6},{6,7},{7,4},{8,9},{9,10},{10,1... | collective-permute-start | bytes 393224 | tf_op jit(solution)/shard_map/ppermute | solution.py:38
  158.7 5.0 %collective-permute-start.39 = (f32[128,256]{1,0:T(8,128)S(1)}, f32[128,256]{1,0:T(8,128)S(1)}, u32[]{:S(2)}, u32[]{:S(2)}) collective-permute-start(f32[128,256]{1,0:T(8,128)S(1)} %get-tuple-element.99), channel_id=1, source_target_pairs={{0,3},{1,0},{2,1},{3,2},{4,7},{5,4},{6,5},{7,6},{8,11},{9,8},{10,9... | collective-permute-start | bytes 393224 | tf_op jit(solution)/shard_map/ppermute | solution.py:38
  164.0 6.6 %collective-permute-start.40 = (f32[128,256]{1,0:T(8,128)S(1)}, f32[128,256]{1,0:T(8,128)S(1)}, u32[]{:S(2)}, u32[]{:S(2)}) collective-permute-start(f32[128,256]{1,0:T(8,128)S(1)} %shard_map.86.refs_5_), channel_id=1, source_target_pairs={{0,64},{16,80},{32,96},{48,112},{64,0},{80,16},{96,32},{112,48},{1... | collective-permute-start | bytes 393224 | tf_op jit(solution)/shard_map/ppermute | solution.py:43
  165.8 6.2 %collective-permute-start.41 = (f32[128,256]{1,0:T(8,128)S(1)}, f32[128,256]{1,0:T(8,128)S(1)}, u32[]{:S(2)}, u32[]{:S(2)}) collective-permute-start(f32[128,256]{1,0:T(8,128)S(1)} %shard_map.86.refs_5_), channel_id=1, source_target_pairs={{0,32},{16,48},{32,64},{48,80},{64,96},{80,112},{96,0},{112,16},{1... | collective-permute-start | bytes 393224 | tf_op jit(solution)/shard_map/ppermute | solution.py:43
  167.6 5.0 %collective-permute-start.42 = (f32[128,256]{1,0:T(8,128)S(1)}, f32[128,256]{1,0:T(8,128)S(1)}, u32[]{:S(2)}, u32[]{:S(2)}) collective-permute-start(f32[128,256]{1,0:T(8,128)S(1)} %shard_map.86.refs_5_), channel_id=1, source_target_pairs={{0,96},{16,112},{32,0},{48,16},{64,32},{80,48},{96,64},{112,80},{1... | collective-permute-start | bytes 393224 | tf_op jit(solution)/shard_map/ppermute | solution.py:43
  172.6 2.0 collective-permute-start.43
  177.0 10.9 %collective-permute-start.44 = (f32[4,128,256]{2,1,0:T(8,128)S(1)}, f32[4,128,256]{2,1,0:T(8,128)S(1)}, u32[]{:S(2)}, u32[]{:S(2)}) collective-permute-start(f32[4,128,256]{2,1,0:T(8,128)S(1)} %get-tuple-element.104), channel_id=1, source_target_pairs={{0,8},{1,9},{2,10},{3,11},{4,12},{5,13},{6,14},{7,15},{8,0},{9,1},... | collective-permute-start | bytes 1572872 | tf_op jit(solution)/shard_map/ppermute | solution.py:38
  177.8 15.6 %collective-permute-start.45 = (f32[4,128,256]{2,1,0:T(8,128)S(1)}, f32[4,128,256]{2,1,0:T(8,128)S(1)}, u32[]{:S(2)}, u32[]{:S(2)}) collective-permute-start(f32[4,128,256]{2,1,0:T(8,128)S(1)} %get-tuple-element.105), channel_id=1, source_target_pairs={{0,4},{1,5},{2,6},{3,7},{4,8},{5,9},{6,10},{7,11},{8,12},{9,13},{1... | collective-permute-start | bytes 1572872 | tf_op jit(solution)/shard_map/ppermute | solution.py:38
  180.0 13.4 %collective-permute-start.46 = (f32[4,128,256]{2,1,0:T(8,128)S(1)}, f32[4,128,256]{2,1,0:T(8,128)S(1)}, u32[]{:S(2)}, u32[]{:S(2)}) collective-permute-start(f32[4,128,256]{2,1,0:T(8,128)S(1)} %get-tuple-element.106), channel_id=1, source_target_pairs={{0,12},{1,13},{2,14},{3,15},{4,0},{5,1},{6,2},{7,3},{8,4},{9,5},{1... | collective-permute-start | bytes 1572872 | tf_op jit(solution)/shard_map/ppermute | solution.py:38
  193.5 6.6 %collective-permute-start.47 = (f32[128,256]{1,0:T(8,128)S(1)}, f32[128,256]{1,0:T(8,128)S(1)}, u32[]{:S(2)}, u32[]{:S(2)}) collective-permute-start(f32[128,256]{1,0:T(8,128)S(1)} %get-tuple-element.112), channel_id=1, source_target_pairs={{0,2},{1,3},{2,0},{3,1},{4,6},{5,7},{6,4},{7,5},{8,10},{9,11},{10,... | collective-permute-start | bytes 393224 | tf_op jit(solution)/shard_map/ppermute | solution.py:38
  195.6 6.2 %collective-permute-start.48 = (f32[128,256]{1,0:T(8,128)S(1)}, f32[128,256]{1,0:T(8,128)S(1)}, u32[]{:S(2)}, u32[]{:S(2)}) collective-permute-start(f32[128,256]{1,0:T(8,128)S(1)} %get-tuple-element.113), channel_id=1, source_target_pairs={{0,1},{1,2},{2,3},{3,0},{4,5},{5,6},{6,7},{7,4},{8,9},{9,10},{10,1... | collective-permute-start | bytes 393224 | tf_op jit(solution)/shard_map/ppermute | solution.py:38
  197.5 5.0 %collective-permute-start.49 = (f32[128,256]{1,0:T(8,128)S(1)}, f32[128,256]{1,0:T(8,128)S(1)}, u32[]{:S(2)}, u32[]{:S(2)}) collective-permute-start(f32[128,256]{1,0:T(8,128)S(1)} %get-tuple-element.114), channel_id=1, source_target_pairs={{0,3},{1,0},{2,1},{3,2},{4,7},{5,4},{6,5},{7,6},{8,11},{9,8},{10,9... | collective-permute-start | bytes 393224 | tf_op jit(solution)/shard_map/ppermute | solution.py:38
  202.8 6.6 %collective-permute-start.50 = (f32[128,256]{1,0:T(8,128)S(1)}, f32[128,256]{1,0:T(8,128)S(1)}, u32[]{:S(2)}, u32[]{:S(2)}) collective-permute-start(f32[128,256]{1,0:T(8,128)S(1)} %shard_map.90.refs_4_), channel_id=1, source_target_pairs={{0,64},{16,80},{32,96},{48,112},{64,0},{80,16},{96,32},{112,48},{1... | collective-permute-start | bytes 393224 | tf_op jit(solution)/shard_map/ppermute | solution.py:43
  204.5 6.2 %collective-permute-start.51 = (f32[128,256]{1,0:T(8,128)S(1)}, f32[128,256]{1,0:T(8,128)S(1)}, u32[]{:S(2)}, u32[]{:S(2)}) collective-permute-start(f32[128,256]{1,0:T(8,128)S(1)} %shard_map.90.refs_4_), channel_id=1, source_target_pairs={{0,32},{16,48},{32,64},{48,80},{64,96},{80,112},{96,0},{112,16},{1... | collective-permute-start | bytes 393224 | tf_op jit(solution)/shard_map/ppermute | solution.py:43
  206.3 5.0 %collective-permute-start.52 = (f32[128,256]{1,0:T(8,128)S(1)}, f32[128,256]{1,0:T(8,128)S(1)}, u32[]{:S(2)}, u32[]{:S(2)}) collective-permute-start(f32[128,256]{1,0:T(8,128)S(1)} %shard_map.90.refs_4_), channel_id=1, source_target_pairs={{0,96},{16,112},{32,0},{48,16},{64,32},{80,48},{96,64},{112,80},{1... | collective-permute-start | bytes 393224 | tf_op jit(solution)/shard_map/ppermute | solution.py:43
  211.3 2.0 collective-permute-start.53
  215.7 10.9 %collective-permute-start.54 = (f32[4,128,256]{2,1,0:T(8,128)S(1)}, f32[4,128,256]{2,1,0:T(8,128)S(1)}, u32[]{:S(2)}, u32[]{:S(2)}) collective-permute-start(f32[4,128,256]{2,1,0:T(8,128)S(1)} %get-tuple-element.119), channel_id=1, source_target_pairs={{0,8},{1,9},{2,10},{3,11},{4,12},{5,13},{6,14},{7,15},{8,0},{9,1},... | collective-permute-start | bytes 1572872 | tf_op jit(solution)/shard_map/ppermute | solution.py:38
  216.5 15.6 %collective-permute-start.55 = (f32[4,128,256]{2,1,0:T(8,128)S(1)}, f32[4,128,256]{2,1,0:T(8,128)S(1)}, u32[]{:S(2)}, u32[]{:S(2)}) collective-permute-start(f32[4,128,256]{2,1,0:T(8,128)S(1)} %get-tuple-element.120), channel_id=1, source_target_pairs={{0,4},{1,5},{2,6},{3,7},{4,8},{5,9},{6,10},{7,11},{8,12},{9,13},{1... | collective-permute-start | bytes 1572872 | tf_op jit(solution)/shard_map/ppermute | solution.py:38
  218.7 13.4 %collective-permute-start.56 = (f32[4,128,256]{2,1,0:T(8,128)S(1)}, f32[4,128,256]{2,1,0:T(8,128)S(1)}, u32[]{:S(2)}, u32[]{:S(2)}) collective-permute-start(f32[4,128,256]{2,1,0:T(8,128)S(1)} %get-tuple-element.121), channel_id=1, source_target_pairs={{0,12},{1,13},{2,14},{3,15},{4,0},{5,1},{6,2},{7,3},{8,4},{9,5},{1... | collective-permute-start | bytes 1572872 | tf_op jit(solution)/shard_map/ppermute | solution.py:38
  232.2 6.6 %collective-permute-start.57 = (f32[128,256]{1,0:T(8,128)S(1)}, f32[128,256]{1,0:T(8,128)S(1)}, u32[]{:S(2)}, u32[]{:S(2)}) collective-permute-start(f32[128,256]{1,0:T(8,128)S(1)} %get-tuple-element.123), channel_id=1, source_target_pairs={{0,2},{1,3},{2,0},{3,1},{4,6},{5,7},{6,4},{7,5},{8,10},{9,11},{10,... | collective-permute-start | bytes 393224 | tf_op jit(solution)/shard_map/ppermute | solution.py:38
  233.3 6.8 %collective-permute-start.58 = (f32[128,256]{1,0:T(8,128)S(1)}, f32[128,256]{1,0:T(8,128)S(1)}, u32[]{:S(2)}, u32[]{:S(2)}) collective-permute-start(f32[128,256]{1,0:T(8,128)S(1)} %get-tuple-element.124), channel_id=1, source_target_pairs={{0,1},{1,2},{2,3},{3,0},{4,5},{5,6},{6,7},{7,4},{8,9},{9,10},{10,1... | collective-permute-start | bytes 393224 | tf_op jit(solution)/shard_map/ppermute | solution.py:38
  235.7 5.0 %collective-permute-start.59 = (f32[128,256]{1,0:T(8,128)S(1)}, f32[128,256]{1,0:T(8,128)S(1)}, u32[]{:S(2)}, u32[]{:S(2)}) collective-permute-start(f32[128,256]{1,0:T(8,128)S(1)} %get-tuple-element.125), channel_id=1, source_target_pairs={{0,3},{1,0},{2,1},{3,2},{4,7},{5,4},{6,5},{7,6},{8,11},{9,8},{10,9... | collective-permute-start | bytes 393224 | tf_op jit(solution)/shard_map/ppermute | solution.py:38

commit v8 on v6

--- a/solution.py
+++ b/solution.py
@@ -75,7 +75,7 @@
     )(*scalars, *[near(value) for value in operands])
 
 
-def pair_kernel(index, unroll, n_in, n_out, flip, has_init, waits, take, put, live, *refs):
+def pair_kernel(index, unroll, n_in, n_out, flip, has_init, waits, take, put, *refs):
     vectors, refs = refs[:n_in], refs[n_in:]
     blocks, refs = refs[0], refs[1:]
     init, refs = (refs[:n_out], refs[n_out:]) if has_init else ((), refs)
@@ -104,7 +104,7 @@
     def _(start):
         for j in range(unroll):
             slot = start + j
-            block = jnp.where(live[slot] > 0, blocks[index, slot], 0.0)
+            block = blocks[index, slot]
             if flip:
                 block = block.T
             high, low = split(block)
@@ -211,20 +211,28 @@
     )(far(inverse), far(base))
 
 
-def load_kernel(blocks, after, out, sems):
+def load_kernel(live, blocks, after, out, sems):
     copies = [
         pltpu.make_async_copy(blocks.at[k], out.at[k], sems.at[k]) for k in range(blocks.shape[0])
     ]
     for copy in copies:
         copy.start()
-    for copy in copies:
+    for k, copy in enumerate(copies):
         copy.wait()
 
-
-def load(blocks, after):
+        @pl.loop(0, blocks.shape[1])
+        def _(slot, k=k):
+            out[k, slot] = jnp.where(live[k, slot] > 0, out[k, slot], 0.0)
+
+
+def load(live, blocks, after):
     return pl.pallas_call(
         load_kernel,
-        in_specs=[pl.BlockSpec(memory_space=pl.ANY), pl.BlockSpec(memory_space=pltpu.VMEM)],
+        in_specs=[
+            pl.BlockSpec(memory_space=pltpu.SMEM),
+            pl.BlockSpec(memory_space=pl.ANY),
+            pl.BlockSpec(memory_space=pltpu.VMEM),
+        ],
         out_specs=pl.BlockSpec(memory_space=pltpu.VMEM),
         out_shape=pltpu.VMEM(blocks.shape, jnp.float32),
         scratch_shapes=[pltpu.SemaphoreType.DMA((blocks.shape[0],))],
@@ -232,7 +240,7 @@
         cost_estimate=pl.CostEstimate(
             flops=0, bytes_accessed=blocks.size * 4, transcendentals=0
         ),
-    )(far(blocks), near(after))
+    )(live, far(blocks), near(after))
 
 
 def gather_plane(value):
@@ -288,13 +296,13 @@
 
     def forth(high, low, vectors, init):
         index = pair_index(high, low)
-        scalars = (take_plane[index], put_z[index], live[index])
+        scalars = (take_plane[index], put_z[index])
         unroll = WHOLE if high == low + 1 else SHORT
         return pair_product(index, unroll, False, scalars, vectors, panels, init, (), 2, 8)
 
     def back(high, low, vectors, init, after):
         index = pair_index(high, low)
-        scalars = (take_z[index], put_plane[index], live[index])
+        scalars = (take_z[index], put_plane[index])
         unroll = WHOLE if high == low + 1 else HALF if high == LEV - 1 else SHORT
         return pair_product(index, unroll, True, scalars, vectors, panels, init, after, 4, 16)
 
@@ -313,7 +321,7 @@
             (solved[level],) = solve(level, (False,), inverse, right, gone)
         vectors = gather_plane(solved[level])
         if level == 0:
-            panels = load(blocks[0, 0], vectors[0])
+            panels = load(live, blocks[0, 0], vectors[0])
         for high in range(level + 1, LEV):
             sums[high] = forth(high, level, vectors, sums[high])
     sums = [None] * LEV

time: 242 us -> 242 us (level)
  transfers between devices with their start and end apart: 60 -> 60, of which waited for: 48 -> 50; matrix products, arithmetic and copies ran while one was open for 1% -> 1% of each run, Pallas kernels for 9% -> 9%
where the time goes in v8:
time: 242 us
  waiting for transfers between devices  102 us (42%)
  starting transfers between devices  93.5 us (39%)
  Pallas kernels  41 us (17%)
  other arithmetic  4 us (2%)
    ppermute x36, waiting for transfers between devices, shift_plane(): return lax.ppermute(value, BOTH, pairs)  66.2 us
    ppermute x36, starting transfers between devices, shift_plane(): return lax.ppermute(value, BOTH, pairs)  59.6 us
    pallas_call x24, Pallas kernels, fast_call(): pl.pallas_call(kernel, in_specs=[pl.BlockSpec(memory_space=pltpu.SMEM)] *...  34 us
    ppermute x18, starting transfers between devices, shift_z(): return lax.ppermute(value, 'prow', pairs)  33.4 us
    ppermute x18, waiting for transfers between devices, shift_z(): return lax.ppermute(value, 'prow', pairs)  24.8 us
    ppermute x6, waiting for transfers between devices, swap_core(): return lax.ppermute(value, 'prow', pairs)  11.4 us
    pallas_call x1, Pallas kernels, load(): pl.pallas_call(load_kernel, in_specs=[pl.BlockSpec(memory_space=pltpu.SME...  5.78 us
  transfers between devices with their start and end apart: 60, of which 50 were waited for; matrix products, arithmetic and copies ran while one was open for 1% of the time, Pallas kernels for 9%

profile of v8, /device:TPU:0, one launch (start us, length us, event | category | flops | bytes accessed | tf_op | source)
XLA Modules:
  0.0 242.0 jit_solution(16345711328347174764)
XLA Ops:
  1.9 2.9 %collective-permute-start.2 = (f32[128,256]{1,0:T(8,128)S(1)}, f32[128,256]{1,0:T(8,128)S(1)}, u32[]{:S(2)}, u32[]{:S(2)}) collective-permute-start(f32[128,256]{1,0:T(8,128)S(1)} %shard_map.68.base), channel_id=1, source_target_pairs={{0,12},{1,13},{2,14},{3,15},{4,0},{5,1},{6,2},{7,3},{8,4},{9,5},{1... | collective-permute-start | bytes 393224 | tf_op jit(solution)/shard_map/ppermute | solution.py:38
  8.7 2.6 %collective-permute-done = f32[128,256]{1,0:T(8,128)S(1)} collective-permute-done((f32[128,256]{1,0:T(8,128)S(1)}, f32[128,256]{1,0:T(8,128)S(1)}, u32[]{:S(2)}, u32[]{:S(2)}) %collective-permute-start) | collective-permute-done | bytes 131104 | tf_op jit(solution)/shard_map/ppermute | solution.py:38
  12.7 3.3 %collective-permute-start.3 = (f32[4,128,256]{2,1,0:T(8,128)S(1)}, f32[4,128,256]{2,1,0:T(8,128)S(1)}, u32[]{:S(2)}, u32[]{:S(2)}) collective-permute-start(f32[4,128,256]{2,1,0:T(8,128)S(1)} %fusion.4.after.refs_0_), channel_id=1, source_target_pairs={{0,2},{1,3},{2,0},{3,1},{4,6},{5,7},{6,4},{7,5},{8,10},{9,11},{10,... | collective-permute-start | bytes 1572872 | tf_op jit(solution)/shard_map/ppermute | solution.py:38
  16.6 2.6 %collective-permute-start.5 = (f32[4,128,256]{2,1,0:T(8,128)S(1)}, f32[4,128,256]{2,1,0:T(8,128)S(1)}, u32[]{:S(2)}, u32[]{:S(2)}) collective-permute-start(f32[4,128,256]{2,1,0:T(8,128)S(1)} %fusion.4.after.refs_0_), channel_id=1, source_target_pairs={{0,3},{1,0},{2,1},{3,2},{4,7},{5,4},{6,5},{7,6},{8,11},{9,8},{10,9... | collective-permute-start | bytes 1572872 | tf_op jit(solution)/shard_map/ppermute | solution.py:38
  20.6 5.8 %shard_map.69.refs_4_.refs_2_ = f32[6,32,128,128]{3,2,1,0:T(8,128)S(1)} custom-call(s32[6,32]{1,0:T(8,128)S(1)} %convert_bitcast_fusion.live, f32[6,32,128,128]{3,2,1,0:T(8,128)} %bitcast.192, f32[4,128,256]{2,1,0:T(8,128)S(1)} %fusion.4.after.refs_0_), custom_call_target="tpu_custom_call" | custom-call | bytes 12582912 | tf_op jit(solution)/shard_map/pallas_call | solution.py:229
  26.4 2.6 %collective-permute-done.4.refs_2_ = f32[4,128,256]{2,1,0:T(8,128)S(1)} collective-permute-done((f32[4,128,256]{2,1,0:T(8,128)S(1)}, f32[4,128,256]{2,1,0:T(8,128)S(1)}, u32[]{:S(2)}, u32[]{:S(2)}) %collective-permute-start.4) | collective-permute-done | bytes 524320 | tf_op jit(solution)/shard_map/ppermute | solution.py:38
  29.5 2.4 shard_map.70
  31.9 1.9 collective-permute-done.6.refs_1_
  33.9 4.0 %collective-permute-start.7 = (f32[128,256]{1,0:T(8,128)S(1)}, f32[128,256]{1,0:T(8,128)S(1)}, u32[]{:S(2)}, u32[]{:S(2)}) collective-permute-start(f32[128,256]{1,0:T(8,128)S(1)} %get-tuple-element.67), channel_id=1, source_target_pairs={{0,64},{16,80},{32,96},{48,112},{64,0},{80,16},{96,32},{112,48},{1... | collective-permute-start | bytes 393224 | tf_op jit(solution)/shard_map/ppermute | solution.py:43
  38.9 2.2 collective-permute-start.9
  42.2 2.5 %collective-permute-done.8.refs_2_ = f32[128,256]{1,0:T(8,128)S(1)} collective-permute-done((f32[128,256]{1,0:T(8,128)S(1)}, f32[128,256]{1,0:T(8,128)S(1)}, u32[]{:S(2)}, u32[]{:S(2)}) %collective-permute-start.8) | collective-permute-done | bytes 131104 | tf_op jit(solution)/shard_map/ppermute | solution.py:43
  47.0 2.6 %collective-permute-start.12 = (f32[128,256]{1,0:T(8,128)S(1)}, f32[128,256]{1,0:T(8,128)S(1)}, u32[]{:S(2)}, u32[]{:S(2)}) collective-permute-start(f32[128,256]{1,0:T(8,128)S(1)} %shard_map.72.base), channel_id=1, source_target_pairs={{0,12},{1,13},{2,14},{3,15},{4,0},{5,1},{6,2},{7,3},{8,4},{9,5},{1... | collective-permute-start | bytes 393224 | tf_op jit(solution)/shard_map/ppermute | solution.py:38
  49.6 2.5 %collective-permute-done.10 = f32[128,256]{1,0:T(8,128)S(1)} collective-permute-done((f32[128,256]{1,0:T(8,128)S(1)}, f32[128,256]{1,0:T(8,128)S(1)}, u32[]{:S(2)}, u32[]{:S(2)}) %collective-permute-start.10) | collective-permute-done | bytes 131104 | tf_op jit(solution)/shard_map/ppermute | solution.py:38
  53.5 2.1 collective-permute-start.13
  57.1 1.8 collective-permute-start.15
  58.8 2.9 %shard_map.73 = (f32[4,128,256]{2,1,0:T(8,128)S(1)}, f32[4,128,256]{2,1,0:T(8,128)S(1)}) custom-call(s32[32]{0:T(128)S(1)} %get-tuple-element.158.take, s32[32]{0:T(128)S(1)} %get-tuple-element.143.put, f32[4,128,256]{2,1,0:T(8,128)S(1)} %fusion.4.after.refs_0_, f32[4,128,256]{2,1,0:T(8,128)S(1)} %collective-permute-done.3.refs_1_, ...), custom_call_target="tpu_custom_call" | custom-call | flops 1073741824 | bytes 4096 | tf_op jit(solution)/shard_map/pallas_call | solution.py:66
  61.7 2.6 %collective-permute-done.13.refs_1_ = f32[4,128,256]{2,1,0:T(8,128)S(1)} collective-permute-done((f32[4,128,256]{2,1,0:T(8,128)S(1)}, f32[4,128,256]{2,1,0:T(8,128)S(1)}, u32[]{:S(2)}, u32[]{:S(2)}) %collective-permute-start.13) | collective-permute-done | bytes 524320 | tf_op jit(solution)/shard_map/ppermute | solution.py:38
  64.4 5.5 %collective-permute-done.14.refs_2_ = f32[4,128,256]{2,1,0:T(8,128)S(1)} collective-permute-done((f32[4,128,256]{2,1,0:T(8,128)S(1)}, f32[4,128,256]{2,1,0:T(8,128)S(1)}, u32[]{:S(2)}, u32[]{:S(2)}) %collective-permute-start.14) | collective-permute-done | bytes 524320 | tf_op jit(solution)/shard_map/ppermute | solution.py:38
  69.9 2.4 shard_map.74
  72.4 1.9 collective-permute-done.16.refs_1_
  74.3 2.2 collective-permute-start.17
  79.7 2.5 %collective-permute-done.17.refs_1_ = f32[128,256]{1,0:T(8,128)S(1)} collective-permute-done((f32[128,256]{1,0:T(8,128)S(1)}, f32[128,256]{1,0:T(8,128)S(1)}, u32[]{:S(2)}, u32[]{:S(2)}) %collective-permute-start.17) | collective-permute-done | bytes 131104 | tf_op jit(solution)/shard_map/ppermute | solution.py:43
  82.3 2.0 collective-permute-done.18.refs_2_
  85.5 2.4 collective-permute-start.21
  88.8 2.5 %collective-permute-done.20 = f32[128,256]{1,0:T(8,128)S(1)} collective-permute-done((f32[128,256]{1,0:T(8,128)S(1)}, f32[128,256]{1,0:T(8,128)S(1)}, u32[]{:S(2)}, u32[]{:S(2)}) %collective-permute-start.20) | collective-permute-done | bytes 131104 | tf_op jit(solution)/shard_map/ppermute | solution.py:38
  92.9 2.1 collective-permute-start.23
  96.5 1.8 collective-permute-start.25
  98.3 2.9 %shard_map.77 = (f32[4,128,256]{2,1,0:T(8,128)S(1)}, f32[4,128,256]{2,1,0:T(8,128)S(1)}) custom-call(s32[32]{0:T(128)S(1)} %get-tuple-element.161.take, s32[32]{0:T(128)S(1)} %get-tuple-element.140.put, f32[4,128,256]{2,1,0:T(8,128)S(1)} %fusion.4.after.refs_0_, f32[4,128,256]{2,1,0:T(8,128)S(1)} %collective-permute-done.3.refs_1_, ...), custom_call_target="tpu_custom_call" | custom-call | flops 1073741824 | bytes 4096 | tf_op jit(solution)/shard_map/pallas_call | solution.py:66
  101.2 2.9 %shard_map.78 = (f32[4,128,256]{2,1,0:T(8,128)S(1)}, f32[4,128,256]{2,1,0:T(8,128)S(1)}) custom-call(s32[32]{0:T(128)S(1)} %get-tuple-element.160.take, s32[32]{0:T(128)S(1)} %get-tuple-element.141.put, f32[4,128,256]{2,1,0:T(8,128)S(1)} %pad_maximum_fusion.2.refs_0_, f32[4,128,256]{2,1,0:T(8,128)S(1)} %collective-permute-done.13.refs_1_, ...), custom_call_target="tpu_custom_call" | custom-call | flops 1073741824 | bytes 4096 | tf_op jit(solution)/shard_map/pallas_call | solution.py:66
  104.1 5.2 %collective-permute-done.24.refs_2_ = f32[4,128,256]{2,1,0:T(8,128)S(1)} collective-permute-done((f32[4,128,256]{2,1,0:T(8,128)S(1)}, f32[4,128,256]{2,1,0:T(8,128)S(1)}, u32[]{:S(2)}, u32[]{:S(2)}) %collective-permute-start.24) | collective-permute-done | bytes 524320 | tf_op jit(solution)/shard_map/ppermute | solution.py:38
  109.3 2.4 shard_map.79
  111.8 1.9 collective-permute-done.26.refs_1_
  113.8 2.1 collective-permute-start.27
  119.1 2.6 %collective-permute-done.27.refs_1_ = f32[128,256]{1,0:T(8,128)S(1)} collective-permute-done((f32[128,256]{1,0:T(8,128)S(1)}, f32[128,256]{1,0:T(8,128)S(1)}, u32[]{:S(2)}, u32[]{:S(2)}) %collective-permute-start.27) | collective-permute-done | bytes 131104 | tf_op jit(solution)/shard_map/ppermute | solution.py:43
  121.7 2.0 collective-permute-done.28.refs_2_
  124.4 2.1 collective-permute-start.30
  129.7 2.7 %collective-permute-done.30 = f32[128,256]{1,0:T(8,128)S(1)} collective-permute-done((f32[128,256]{1,0:T(8,128)S(1)}, f32[128,256]{1,0:T(8,128)S(1)}, u32[]{:S(2)}, u32[]{:S(2)}) %collective-permute-start.30) | collective-permute-done | bytes 131104 | tf_op jit(solution)/shard_map/ppermute | solution.py:43
  134.2 1.9 collective-permute-done.33.refs_1_
  136.1 2.4 shard_map.82
  141.5 1.8 collective-permute-start.36
  143.3 6.0 %collective-permute-done.34.refs_3_.refs_1_ = f32[4,128,256]{2,1,0:T(8,128)S(1)} collective-permute-done((f32[4,128,256]{2,1,0:T(8,128)S(1)}, f32[4,128,256]{2,1,0:T(8,128)S(1)}, u32[]{:S(2)}, u32[]{:S(2)}) %collective-permute-start.34) | collective-permute-done | bytes 524320 | tf_op jit(solution)/shard_map/ppermute | solution.py:38
  149.3 2.6 %shard_map.84 = (f32[4,128,256]{2,1,0:T(8,128)S(1)}, f32[4,128,256]{2,1,0:T(8,128)S(1)}, f32[4,128,256]{2,1,0:T(8,128)S(1)}, f32[4,128,256]{2,1,0:T(8,128)S(1)}) custom-call(s32[32]{0:T(128)S(1)} %get-tuple-element.165.take, s32[32]{0:T(128)S(1)} %get-tuple-element.130.put, f32[4,128,256]{2,1,0:T(8,128)S(1)} %pad_maximum_fusion.4.refs_0_, ...), custom_call_target="tpu_custom_call" | custom-call | flops 1073741824 | bytes 4096 | tf_op jit(solution)/shard_map/pallas_call | solution.py:66
  152.0 2.6 %shard_map.83 = (f32[4,128,256]{2,1,0:T(8,128)S(1)}, f32[4,128,256]{2,1,0:T(8,128)S(1)}, f32[4,128,256]{2,1,0:T(8,128)S(1)}, f32[4,128,256]{2,1,0:T(8,128)S(1)}) custom-call(s32[32]{0:T(128)S(1)} %get-tuple-element.164.take, s32[32]{0:T(128)S(1)} %get-tuple-element.131.put, f32[4,128,256]{2,1,0:T(8,128)S(1)} %pad_maximum_fusion.4.refs_0_, ...), custom_call_target="tpu_custom_call" | custom-call | flops 1073741824 | bytes 4096 | tf_op jit(solution)/shard_map/pallas_call | solution.py:66
  155.0 2.1 collective-permute-start.37
  158.6 1.8 collective-permute-start.39
  161.6 1.7 collective-permute-done.38.refs_2_
  163.9 2.0 collective-permute-start.40
  165.9 1.9 collective-permute-start.41
  172.9 1.9 collective-permute-done.43.refs_1_
  174.8 2.4 shard_map.87
  180.2 1.8 collective-permute-start.46
  182.0 6.0 %collective-permute-done.44.refs_7_.refs_1_ = f32[4,128,256]{2,1,0:T(8,128)S(1)} collective-permute-done((f32[4,128,256]{2,1,0:T(8,128)S(1)}, f32[4,128,256]{2,1,0:T(8,128)S(1)}, u32[]{:S(2)}, u32[]{:S(2)}) %collective-permute-start.44) | collective-permute-done | bytes 524320 | tf_op jit(solution)/shard_map/ppermute | solution.py:38
  188.1 3.0 %shard_map.88 = (f32[4,128,256]{2,1,0:T(8,128)S(1)}, f32[4,128,256]{2,1,0:T(8,128)S(1)}, f32[4,128,256]{2,1,0:T(8,128)S(1)}, f32[4,128,256]{2,1,0:T(8,128)S(1)}) custom-call(s32[32]{0:T(128)S(1)} %get-tuple-element.166.take, s32[32]{0:T(128)S(1)} %get-tuple-element.129.put, f32[4,128,256]{2,1,0:T(8,128)S(1)} %pad_maximum_fusion.5.refs_0_, ...), custom_call_target="tpu_custom_call" | custom-call | flops 1073741824 | bytes 4096 | tf_op jit(solution)/shard_map/pallas_call | solution.py:66
  191.1 2.5 %collective-permute-done.45.refs_2_ = f32[4,128,256]{2,1,0:T(8,128)S(1)} collective-permute-done((f32[4,128,256]{2,1,0:T(8,128)S(1)}, f32[4,128,256]{2,1,0:T(8,128)S(1)}, u32[]{:S(2)}, u32[]{:S(2)}) %collective-permute-start.45) | collective-permute-done | bytes 524320 | tf_op jit(solution)/shard_map/ppermute | solution.py:38
  193.7 2.1 collective-permute-start.47
  195.8 1.9 collective-permute-start.48
  202.9 1.7 collective-permute-start.50
  204.6 1.8 collective-permute-start.51
  211.5 1.9 collective-permute-done.53.refs_1_
  213.4 2.4 shard_map.91
  218.9 1.9 collective-permute-start.56
  220.7 6.0 %collective-permute-done.54.refs_1_ = f32[4,128,256]{2,1,0:T(8,128)S(1)} collective-permute-done((f32[4,128,256]{2,1,0:T(8,128)S(1)}, f32[4,128,256]{2,1,0:T(8,128)S(1)}, u32[]{:S(2)}, u32[]{:S(2)}) %collective-permute-start.54) | collective-permute-done | bytes 524320 | tf_op jit(solution)/shard_map/ppermute | solution.py:38
  226.7 5.5 %collective-permute-done.55.refs_2_ = f32[4,128,256]{2,1,0:T(8,128)S(1)} collective-permute-done((f32[4,128,256]{2,1,0:T(8,128)S(1)}, f32[4,128,256]{2,1,0:T(8,128)S(1)}, u32[]{:S(2)}, u32[]{:S(2)}) %collective-permute-start.55) | collective-permute-done | bytes 524320 | tf_op jit(solution)/shard_map/ppermute | solution.py:38
  233.5 2.4 collective-permute-start.58
  (99 shorter events, 69.6 us)
Async XLA Ops:
  1.9 6.8 %collective-permute-start.2 = (f32[128,256]{1,0:T(8,128)S(1)}, f32[128,256]{1,0:T(8,128)S(1)}, u32[]{:S(2)}, u32[]{:S(2)}) collective-permute-start(f32[128,256]{1,0:T(8,128)S(1)} %shard_map.68.base), channel_id=1, source_target_pairs={{0,12},{1,13},{2,14},{3,15},{4,0},{5,1},{6,2},{7,3},{8,4},{9,5},{1... | collective-permute-start | bytes 393224 | tf_op jit(solution)/shard_map/ppermute | solution.py:38
  4.8 6.6 %collective-permute-start = (f32[128,256]{1,0:T(8,128)S(1)}, f32[128,256]{1,0:T(8,128)S(1)}, u32[]{:S(2)}, u32[]{:S(2)}) collective-permute-start(f32[128,256]{1,0:T(8,128)S(1)} %shard_map.68.base), channel_id=1, source_target_pairs={{0,8},{1,9},{2,10},{3,11},{4,12},{5,13},{6,14},{7,15},{8,0},{9,1},... | collective-permute-start | bytes 393224 | tf_op jit(solution)/shard_map/ppermute | solution.py:38
  5.6 7.1 %collective-permute-start.1 = (f32[128,256]{1,0:T(8,128)S(1)}, f32[128,256]{1,0:T(8,128)S(1)}, u32[]{:S(2)}, u32[]{:S(2)}) collective-permute-start(f32[128,256]{1,0:T(8,128)S(1)} %shard_map.68.base), channel_id=1, source_target_pairs={{0,4},{1,5},{2,6},{3,7},{4,8},{5,9},{6,10},{7,11},{8,12},{9,13},{1... | collective-permute-start | bytes 393224 | tf_op jit(solution)/shard_map/ppermute | solution.py:38
  12.7 13.8 %collective-permute-start.3 = (f32[4,128,256]{2,1,0:T(8,128)S(1)}, f32[4,128,256]{2,1,0:T(8,128)S(1)}, u32[]{:S(2)}, u32[]{:S(2)}) collective-permute-start(f32[4,128,256]{2,1,0:T(8,128)S(1)} %fusion.4.after.refs_0_), channel_id=1, source_target_pairs={{0,2},{1,3},{2,0},{3,1},{4,6},{5,7},{6,4},{7,5},{8,10},{9,11},{10,... | collective-permute-start | bytes 1572872 | tf_op jit(solution)/shard_map/ppermute | solution.py:38
  16.0 13.1 %collective-permute-start.4 = (f32[4,128,256]{2,1,0:T(8,128)S(1)}, f32[4,128,256]{2,1,0:T(8,128)S(1)}, u32[]{:S(2)}, u32[]{:S(2)}) collective-permute-start(f32[4,128,256]{2,1,0:T(8,128)S(1)} %fusion.4.after.refs_0_), channel_id=1, source_target_pairs={{0,1},{1,2},{2,3},{3,0},{4,5},{5,6},{6,7},{7,4},{8,9},{9,10},{10,1... | collective-permute-start | bytes 1572872 | tf_op jit(solution)/shard_map/ppermute | solution.py:38
  16.6 12.8 %collective-permute-start.5 = (f32[4,128,256]{2,1,0:T(8,128)S(1)}, f32[4,128,256]{2,1,0:T(8,128)S(1)}, u32[]{:S(2)}, u32[]{:S(2)}) collective-permute-start(f32[4,128,256]{2,1,0:T(8,128)S(1)} %fusion.4.after.refs_0_), channel_id=1, source_target_pairs={{0,3},{1,0},{2,1},{3,2},{4,7},{5,4},{6,5},{7,6},{8,11},{9,8},{10,9... | collective-permute-start | bytes 1572872 | tf_op jit(solution)/shard_map/ppermute | solution.py:38
  26.4 18.8 %copy-start = (f32[4,1,1,128,128]{4,3,2,1,0:T(8,128)S(1)}, f32[4,1,1,128,128]{4,3,2,1,0:T(8,128)}, u32[]{:S(2)}) copy-start(f32[4,1,1,128,128]{4,3,2,1,0:T(8,128)} %param.6) | copy-start | bytes 786436
  26.4 18.8 %copy-start.1 = (f32[4,1,1,128,256]{4,3,2,1,0:T(8,128)S(1)}, f32[4,1,1,128,256]{4,3,2,1,0:T(8,128)}, u32[]{:S(2)}) copy-start(f32[4,1,1,128,256]{4,3,2,1,0:T(8,128)} %param.5) | copy-start | bytes 1572868
  31.8 2.0 collective-permute-start.6
  33.9 8.2 %collective-permute-start.7 = (f32[128,256]{1,0:T(8,128)S(1)}, f32[128,256]{1,0:T(8,128)S(1)}, u32[]{:S(2)}, u32[]{:S(2)}) collective-permute-start(f32[128,256]{1,0:T(8,128)S(1)} %get-tuple-element.67), channel_id=1, source_target_pairs={{0,64},{16,80},{32,96},{48,112},{64,0},{80,16},{96,32},{112,48},{1... | collective-permute-start | bytes 393224 | tf_op jit(solution)/shard_map/ppermute | solution.py:43
  37.9 6.8 %collective-permute-start.8 = (f32[128,256]{1,0:T(8,128)S(1)}, f32[128,256]{1,0:T(8,128)S(1)}, u32[]{:S(2)}, u32[]{:S(2)}) collective-permute-start(f32[128,256]{1,0:T(8,128)S(1)} %get-tuple-element.68), channel_id=1, source_target_pairs={{0,32},{16,48},{32,64},{48,80},{64,96},{80,112},{96,0},{112,16},{1... | collective-permute-start | bytes 393224 | tf_op jit(solution)/shard_map/ppermute | solution.py:43
  38.9 6.3 %collective-permute-start.9 = (f32[128,256]{1,0:T(8,128)S(1)}, f32[128,256]{1,0:T(8,128)S(1)}, u32[]{:S(2)}, u32[]{:S(2)}) collective-permute-start(f32[128,256]{1,0:T(8,128)S(1)} %get-tuple-element.69), channel_id=1, source_target_pairs={{0,96},{16,112},{32,0},{48,16},{64,32},{80,48},{96,64},{112,80},{1... | collective-permute-start | bytes 393224 | tf_op jit(solution)/shard_map/ppermute | solution.py:43
  45.5 6.6 %collective-permute-start.10 = (f32[128,256]{1,0:T(8,128)S(1)}, f32[128,256]{1,0:T(8,128)S(1)}, u32[]{:S(2)}, u32[]{:S(2)}) collective-permute-start(f32[128,256]{1,0:T(8,128)S(1)} %shard_map.72.base), channel_id=1, source_target_pairs={{0,8},{1,9},{2,10},{3,11},{4,12},{5,13},{6,14},{7,15},{8,0},{9,1},... | collective-permute-start | bytes 393224 | tf_op jit(solution)/shard_map/ppermute | solution.py:38
  46.4 7.1 %collective-permute-start.11 = (f32[128,256]{1,0:T(8,128)S(1)}, f32[128,256]{1,0:T(8,128)S(1)}, u32[]{:S(2)}, u32[]{:S(2)}) collective-permute-start(f32[128,256]{1,0:T(8,128)S(1)} %shard_map.72.base), channel_id=1, source_target_pairs={{0,4},{1,5},{2,6},{3,7},{4,8},{5,9},{6,10},{7,11},{8,12},{9,13},{1... | collective-permute-start | bytes 393224 | tf_op jit(solution)/shard_map/ppermute | solution.py:38
  47.0 6.5 %collective-permute-start.12 = (f32[128,256]{1,0:T(8,128)S(1)}, f32[128,256]{1,0:T(8,128)S(1)}, u32[]{:S(2)}, u32[]{:S(2)}) collective-permute-start(f32[128,256]{1,0:T(8,128)S(1)} %shard_map.72.base), channel_id=1, source_target_pairs={{0,12},{1,13},{2,14},{3,15},{4,0},{5,1},{6,2},{7,3},{8,4},{9,5},{1... | collective-permute-start | bytes 393224 | tf_op jit(solution)/shard_map/ppermute | solution.py:38
  53.5 10.9 %collective-permute-start.13 = (f32[4,128,256]{2,1,0:T(8,128)S(1)}, f32[4,128,256]{2,1,0:T(8,128)S(1)}, u32[]{:S(2)}, u32[]{:S(2)}) collective-permute-start(f32[4,128,256]{2,1,0:T(8,128)S(1)} %pad_maximum_fusion.2.refs_0_), channel_id=1, source_target_pairs={{0,2},{1,3},{2,0},{3,1},{4,6},{5,7},{6,4},{7,5},{8,10},{9,11},{10,... | collective-permute-start | bytes 1572872 | tf_op jit(solution)/shard_map/ppermute | solution.py:38
  55.6 14.3 %collective-permute-start.14 = (f32[4,128,256]{2,1,0:T(8,128)S(1)}, f32[4,128,256]{2,1,0:T(8,128)S(1)}, u32[]{:S(2)}, u32[]{:S(2)}) collective-permute-start(f32[4,128,256]{2,1,0:T(8,128)S(1)} %pad_maximum_fusion.2.refs_0_), channel_id=1, source_target_pairs={{0,1},{1,2},{2,3},{3,0},{4,5},{5,6},{6,7},{7,4},{8,9},{9,10},{10,1... | collective-permute-start | bytes 1572872 | tf_op jit(solution)/shard_map/ppermute | solution.py:38
  57.1 12.8 %collective-permute-start.15 = (f32[4,128,256]{2,1,0:T(8,128)S(1)}, f32[4,128,256]{2,1,0:T(8,128)S(1)}, u32[]{:S(2)}, u32[]{:S(2)}) collective-permute-start(f32[4,128,256]{2,1,0:T(8,128)S(1)} %pad_maximum_fusion.2.refs_0_), channel_id=1, source_target_pairs={{0,3},{1,0},{2,1},{3,2},{4,7},{5,4},{6,5},{7,6},{8,11},{9,8},{10,9... | collective-permute-start | bytes 1572872 | tf_op jit(solution)/shard_map/ppermute | solution.py:38
  72.3 2.0 collective-permute-start.16
  74.3 7.9 %collective-permute-start.17 = (f32[128,256]{1,0:T(8,128)S(1)}, f32[128,256]{1,0:T(8,128)S(1)}, u32[]{:S(2)}, u32[]{:S(2)}) collective-permute-start(f32[128,256]{1,0:T(8,128)S(1)} %get-tuple-element.75), channel_id=1, source_target_pairs={{0,64},{16,80},{32,96},{48,112},{64,0},{80,16},{96,32},{112,48},{1... | collective-permute-start | bytes 393224 | tf_op jit(solution)/shard_map/ppermute | solution.py:43
  76.5 7.8 %collective-permute-start.18 = (f32[128,256]{1,0:T(8,128)S(1)}, f32[128,256]{1,0:T(8,128)S(1)}, u32[]{:S(2)}, u32[]{:S(2)}) collective-permute-start(f32[128,256]{1,0:T(8,128)S(1)} %get-tuple-element.76), channel_id=1, source_target_pairs={{0,32},{16,48},{32,64},{48,80},{64,96},{80,112},{96,0},{112,16},{1... | collective-permute-start | bytes 393224 | tf_op jit(solution)/shard_map/ppermute | solution.py:43
  78.0 6.3 %collective-permute-start.19 = (f32[128,256]{1,0:T(8,128)S(1)}, f32[128,256]{1,0:T(8,128)S(1)}, u32[]{:S(2)}, u32[]{:S(2)}) collective-permute-start(f32[128,256]{1,0:T(8,128)S(1)} %get-tuple-element.77), channel_id=1, source_target_pairs={{0,96},{16,112},{32,0},{48,16},{64,32},{80,48},{96,64},{112,80},{1... | collective-permute-start | bytes 393224 | tf_op jit(solution)/shard_map/ppermute | solution.py:43
  84.7 6.6 %collective-permute-start.20 = (f32[128,256]{1,0:T(8,128)S(1)}, f32[128,256]{1,0:T(8,128)S(1)}, u32[]{:S(2)}, u32[]{:S(2)}) collective-permute-start(f32[128,256]{1,0:T(8,128)S(1)} %shard_map.76.base), channel_id=1, source_target_pairs={{0,8},{1,9},{2,10},{3,11},{4,12},{5,13},{6,14},{7,15},{8,0},{9,1},... | collective-permute-start | bytes 393224 | tf_op jit(solution)/shard_map/ppermute | solution.py:38
  85.5 7.1 %collective-permute-start.21 = (f32[128,256]{1,0:T(8,128)S(1)}, f32[128,256]{1,0:T(8,128)S(1)}, u32[]{:S(2)}, u32[]{:S(2)}) collective-permute-start(f32[128,256]{1,0:T(8,128)S(1)} %shard_map.76.base), channel_id=1, source_target_pairs={{0,4},{1,5},{2,6},{3,7},{4,8},{5,9},{6,10},{7,11},{8,12},{9,13},{1... | collective-permute-start | bytes 393224 | tf_op jit(solution)/shard_map/ppermute | solution.py:38
  87.9 5.0 %collective-permute-start.22 = (f32[128,256]{1,0:T(8,128)S(1)}, f32[128,256]{1,0:T(8,128)S(1)}, u32[]{:S(2)}, u32[]{:S(2)}) collective-permute-start(f32[128,256]{1,0:T(8,128)S(1)} %shard_map.76.base), channel_id=1, source_target_pairs={{0,12},{1,13},{2,14},{3,15},{4,0},{5,1},{6,2},{7,3},{8,4},{9,5},{1... | collective-permute-start | bytes 393224 | tf_op jit(solution)/shard_map/ppermute | solution.py:38
  92.9 11.1 %collective-permute-start.23 = (f32[4,128,256]{2,1,0:T(8,128)S(1)}, f32[4,128,256]{2,1,0:T(8,128)S(1)}, u32[]{:S(2)}, u32[]{:S(2)}) collective-permute-start(f32[4,128,256]{2,1,0:T(8,128)S(1)} %pad_maximum_fusion.3.refs_0_), channel_id=1, source_target_pairs={{0,2},{1,3},{2,0},{3,1},{4,6},{5,7},{6,4},{7,5},{8,10},{9,11},{10,... | collective-permute-start | bytes 1572872 | tf_op jit(solution)/shard_map/ppermute | solution.py:38
  95.0 14.3 %collective-permute-start.24 = (f32[4,128,256]{2,1,0:T(8,128)S(1)}, f32[4,128,256]{2,1,0:T(8,128)S(1)}, u32[]{:S(2)}, u32[]{:S(2)}) collective-permute-start(f32[4,128,256]{2,1,0:T(8,128)S(1)} %pad_maximum_fusion.3.refs_0_), channel_id=1, source_target_pairs={{0,1},{1,2},{2,3},{3,0},{4,5},{5,6},{6,7},{7,4},{8,9},{9,10},{10,1... | collective-permute-start | bytes 1572872 | tf_op jit(solution)/shard_map/ppermute | solution.py:38
  96.5 12.8 %collective-permute-start.25 = (f32[4,128,256]{2,1,0:T(8,128)S(1)}, f32[4,128,256]{2,1,0:T(8,128)S(1)}, u32[]{:S(2)}, u32[]{:S(2)}) collective-permute-start(f32[4,128,256]{2,1,0:T(8,128)S(1)} %pad_maximum_fusion.3.refs_0_), channel_id=1, source_target_pairs={{0,3},{1,0},{2,1},{3,2},{4,7},{5,4},{6,5},{7,6},{8,11},{9,8},{10,9... | collective-permute-start | bytes 1572872 | tf_op jit(solution)/shard_map/ppermute | solution.py:38
  111.7 2.0 collective-permute-start.26
  113.8 7.9 %collective-permute-start.27 = (f32[128,256]{1,0:T(8,128)S(1)}, f32[128,256]{1,0:T(8,128)S(1)}, u32[]{:S(2)}, u32[]{:S(2)}) collective-permute-start(f32[128,256]{1,0:T(8,128)S(1)} %get-tuple-element.85), channel_id=1, source_target_pairs={{0,64},{16,80},{32,96},{48,112},{64,0},{80,16},{96,32},{112,48},{1... | collective-permute-start | bytes 393224 | tf_op jit(solution)/shard_map/ppermute | solution.py:43
  115.8 7.9 %collective-permute-start.28 = (f32[128,256]{1,0:T(8,128)S(1)}, f32[128,256]{1,0:T(8,128)S(1)}, u32[]{:S(2)}, u32[]{:S(2)}) collective-permute-start(f32[128,256]{1,0:T(8,128)S(1)} %get-tuple-element.86), channel_id=1, source_target_pairs={{0,32},{16,48},{32,64},{48,80},{64,96},{80,112},{96,0},{112,16},{1... | collective-permute-start | bytes 393224 | tf_op jit(solution)/shard_map/ppermute | solution.py:43
  117.4 6.3 %collective-permute-start.29 = (f32[128,256]{1,0:T(8,128)S(1)}, f32[128,256]{1,0:T(8,128)S(1)}, u32[]{:S(2)}, u32[]{:S(2)}) collective-permute-start(f32[128,256]{1,0:T(8,128)S(1)} %get-tuple-element.87), channel_id=1, source_target_pairs={{0,96},{16,112},{32,0},{48,16},{64,32},{80,48},{96,64},{112,80},{1... | collective-permute-start | bytes 393224 | tf_op jit(solution)/shard_map/ppermute | solution.py:43
  124.4 8.0 %collective-permute-start.30 = (f32[128,256]{1,0:T(8,128)S(1)}, f32[128,256]{1,0:T(8,128)S(1)}, u32[]{:S(2)}, u32[]{:S(2)}) collective-permute-start(f32[128,256]{1,0:T(8,128)S(1)} %get-tuple-element.89), channel_id=1, source_target_pairs={{0,64},{16,80},{32,96},{48,112},{64,0},{80,16},{96,32},{112,48},{1... | collective-permute-start | bytes 393224 | tf_op jit(solution)/shard_map/ppermute | solution.py:43
  126.4 7.6 %collective-permute-start.31 = (f32[128,256]{1,0:T(8,128)S(1)}, f32[128,256]{1,0:T(8,128)S(1)}, u32[]{:S(2)}, u32[]{:S(2)}) collective-permute-start(f32[128,256]{1,0:T(8,128)S(1)} %get-tuple-element.89), channel_id=1, source_target_pairs={{0,32},{16,48},{32,64},{48,80},{64,96},{80,112},{96,0},{112,16},{1... | collective-permute-start | bytes 393224 | tf_op jit(solution)/shard_map/ppermute | solution.py:43
  128.0 6.0 %collective-permute-start.32 = (f32[128,256]{1,0:T(8,128)S(1)}, f32[128,256]{1,0:T(8,128)S(1)}, u32[]{:S(2)}, u32[]{:S(2)}) collective-permute-start(f32[128,256]{1,0:T(8,128)S(1)} %get-tuple-element.89), channel_id=1, source_target_pairs={{0,96},{16,112},{32,0},{48,16},{64,32},{80,48},{96,64},{112,80},{1... | collective-permute-start | bytes 393224 | tf_op jit(solution)/shard_map/ppermute | solution.py:43
  134.1 2.0 collective-permute-start.33
  138.5 10.9 %collective-permute-start.34 = (f32[4,128,256]{2,1,0:T(8,128)S(1)}, f32[4,128,256]{2,1,0:T(8,128)S(1)}, u32[]{:S(2)}, u32[]{:S(2)}) collective-permute-start(f32[4,128,256]{2,1,0:T(8,128)S(1)} %get-tuple-element.91), channel_id=1, source_target_pairs={{0,8},{1,9},{2,10},{3,11},{4,12},{5,13},{6,14},{7,15},{8,0},{9,1},... | collective-permute-start | bytes 1572872 | tf_op jit(solution)/shard_map/ppermute | solution.py:38
  140.1 14.8 %collective-permute-start.35 = (f32[4,128,256]{2,1,0:T(8,128)S(1)}, f32[4,128,256]{2,1,0:T(8,128)S(1)}, u32[]{:S(2)}, u32[]{:S(2)}) collective-permute-start(f32[4,128,256]{2,1,0:T(8,128)S(1)} %get-tuple-element.92), channel_id=1, source_target_pairs={{0,4},{1,5},{2,6},{3,7},{4,8},{5,9},{6,10},{7,11},{8,12},{9,13},{1... | collective-permute-start | bytes 1572872 | tf_op jit(solution)/shard_map/ppermute | solution.py:38
  141.5 13.4 %collective-permute-start.36 = (f32[4,128,256]{2,1,0:T(8,128)S(1)}, f32[4,128,256]{2,1,0:T(8,128)S(1)}, u32[]{:S(2)}, u32[]{:S(2)}) collective-permute-start(f32[4,128,256]{2,1,0:T(8,128)S(1)} %get-tuple-element.93), channel_id=1, source_target_pairs={{0,12},{1,13},{2,14},{3,15},{4,0},{5,1},{6,2},{7,3},{8,4},{9,5},{1... | collective-permute-start | bytes 1572872 | tf_op jit(solution)/shard_map/ppermute | solution.py:38
  155.0 6.6 %collective-permute-start.37 = (f32[128,256]{1,0:T(8,128)S(1)}, f32[128,256]{1,0:T(8,128)S(1)}, u32[]{:S(2)}, u32[]{:S(2)}) collective-permute-start(f32[128,256]{1,0:T(8,128)S(1)} %get-tuple-element.97), channel_id=1, source_target_pairs={{0,2},{1,3},{2,0},{3,1},{4,6},{5,7},{6,4},{7,5},{8,10},{9,11},{10,... | collective-permute-start | bytes 393224 | tf_op jit(solution)/shard_map/ppermute | solution.py:38
  157.1 6.2 %collective-permute-start.38 = (f32[128,256]{1,0:T(8,128)S(1)}, f32[128,256]{1,0:T(8,128)S(1)}, u32[]{:S(2)}, u32[]{:S(2)}) collective-permute-start(f32[128,256]{1,0:T(8,128)S(1)} %get-tuple-element.98), channel_id=1, source_target_pairs={{0,1},{1,2},{2,3},{3,0},{4,5},{5,6},{6,7},{7,4},{8,9},{9,10},{10,1... | collective-permute-start | bytes 393224 | tf_op jit(solution)/shard_map/ppermute | solution.py:38
  158.6 5.0 %collective-permute-start.39 = (f32[128,256]{1,0:T(8,128)S(1)}, f32[128,256]{1,0:T(8,128)S(1)}, u32[]{:S(2)}, u32[]{:S(2)}) collective-permute-start(f32[128,256]{1,0:T(8,128)S(1)} %get-tuple-element.99), channel_id=1, source_target_pairs={{0,3},{1,0},{2,1},{3,2},{4,7},{5,4},{6,5},{7,6},{8,11},{9,8},{10,9... | collective-permute-start | bytes 393224 | tf_op jit(solution)/shard_map/ppermute | solution.py:38
  163.9 6.8 %collective-permute-start.40 = (f32[128,256]{1,0:T(8,128)S(1)}, f32[128,256]{1,0:T(8,128)S(1)}, u32[]{:S(2)}, u32[]{:S(2)}) collective-permute-start(f32[128,256]{1,0:T(8,128)S(1)} %shard_map.86), channel_id=1, source_target_pairs={{0,64},{16,80},{32,96},{48,112},{64,0},{80,16},{96,32},{112,48},{1... | collective-permute-start | bytes 393224 | tf_op jit(solution)/shard_map/ppermute | solution.py:43
  165.9 6.2 %collective-permute-start.41 = (f32[128,256]{1,0:T(8,128)S(1)}, f32[128,256]{1,0:T(8,128)S(1)}, u32[]{:S(2)}, u32[]{:S(2)}) collective-permute-start(f32[128,256]{1,0:T(8,128)S(1)} %shard_map.86), channel_id=1, source_target_pairs={{0,32},{16,48},{32,64},{48,80},{64,96},{80,112},{96,0},{112,16},{1... | collective-permute-start | bytes 393224 | tf_op jit(solution)/shard_map/ppermute | solution.py:43
  167.8 5.0 %collective-permute-start.42 = (f32[128,256]{1,0:T(8,128)S(1)}, f32[128,256]{1,0:T(8,128)S(1)}, u32[]{:S(2)}, u32[]{:S(2)}) collective-permute-start(f32[128,256]{1,0:T(8,128)S(1)} %shard_map.86), channel_id=1, source_target_pairs={{0,96},{16,112},{32,0},{48,16},{64,32},{80,48},{96,64},{112,80},{1... | collective-permute-start | bytes 393224 | tf_op jit(solution)/shard_map/ppermute | solution.py:43
  172.8 2.0 collective-permute-start.43
  177.2 10.9 %collective-permute-start.44 = (f32[4,128,256]{2,1,0:T(8,128)S(1)}, f32[4,128,256]{2,1,0:T(8,128)S(1)}, u32[]{:S(2)}, u32[]{:S(2)}) collective-permute-start(f32[4,128,256]{2,1,0:T(8,128)S(1)} %get-tuple-element.104), channel_id=1, source_target_pairs={{0,8},{1,9},{2,10},{3,11},{4,12},{5,13},{6,14},{7,15},{8,0},{9,1},... | collective-permute-start | bytes 1572872 | tf_op jit(solution)/shard_map/ppermute | solution.py:38
  178.8 14.8 %collective-permute-start.45 = (f32[4,128,256]{2,1,0:T(8,128)S(1)}, f32[4,128,256]{2,1,0:T(8,128)S(1)}, u32[]{:S(2)}, u32[]{:S(2)}) collective-permute-start(f32[4,128,256]{2,1,0:T(8,128)S(1)} %get-tuple-element.105), channel_id=1, source_target_pairs={{0,4},{1,5},{2,6},{3,7},{4,8},{5,9},{6,10},{7,11},{8,12},{9,13},{1... | collective-permute-start | bytes 1572872 | tf_op jit(solution)/shard_map/ppermute | solution.py:38
  180.2 13.4 %collective-permute-start.46 = (f32[4,128,256]{2,1,0:T(8,128)S(1)}, f32[4,128,256]{2,1,0:T(8,128)S(1)}, u32[]{:S(2)}, u32[]{:S(2)}) collective-permute-start(f32[4,128,256]{2,1,0:T(8,128)S(1)} %get-tuple-element.106), channel_id=1, source_target_pairs={{0,12},{1,13},{2,14},{3,15},{4,0},{5,1},{6,2},{7,3},{8,4},{9,5},{1... | collective-permute-start | bytes 1572872 | tf_op jit(solution)/shard_map/ppermute | solution.py:38
  193.7 6.6 %collective-permute-start.47 = (f32[128,256]{1,0:T(8,128)S(1)}, f32[128,256]{1,0:T(8,128)S(1)}, u32[]{:S(2)}, u32[]{:S(2)}) collective-permute-start(f32[128,256]{1,0:T(8,128)S(1)} %get-tuple-element.112), channel_id=1, source_target_pairs={{0,2},{1,3},{2,0},{3,1},{4,6},{5,7},{6,4},{7,5},{8,10},{9,11},{10,... | collective-permute-start | bytes 393224 | tf_op jit(solution)/shard_map/ppermute | solution.py:38
  195.8 6.2 %collective-permute-start.48 = (f32[128,256]{1,0:T(8,128)S(1)}, f32[128,256]{1,0:T(8,128)S(1)}, u32[]{:S(2)}, u32[]{:S(2)}) collective-permute-start(f32[128,256]{1,0:T(8,128)S(1)} %get-tuple-element.113), channel_id=1, source_target_pairs={{0,1},{1,2},{2,3},{3,0},{4,5},{5,6},{6,7},{7,4},{8,9},{9,10},{10,1... | collective-permute-start | bytes 393224 | tf_op jit(solution)/shard_map/ppermute | solution.py:38
  197.6 5.0 %collective-permute-start.49 = (f32[128,256]{1,0:T(8,128)S(1)}, f32[128,256]{1,0:T(8,128)S(1)}, u32[]{:S(2)}, u32[]{:S(2)}) collective-permute-start(f32[128,256]{1,0:T(8,128)S(1)} %get-tuple-element.114), channel_id=1, source_target_pairs={{0,3},{1,0},{2,1},{3,2},{4,7},{5,4},{6,5},{7,6},{8,11},{9,8},{10,9... | collective-permute-start | bytes 393224 | tf_op jit(solution)/shard_map/ppermute | solution.py:38
  202.9 6.6 %collective-permute-start.50 = (f32[128,256]{1,0:T(8,128)S(1)}, f32[128,256]{1,0:T(8,128)S(1)}, u32[]{:S(2)}, u32[]{:S(2)}) collective-permute-start(f32[128,256]{1,0:T(8,128)S(1)} %shard_map.90), channel_id=1, source_target_pairs={{0,64},{16,80},{32,96},{48,112},{64,0},{80,16},{96,32},{112,48},{1... | collective-permute-start | bytes 393224 | tf_op jit(solution)/shard_map/ppermute | solution.py:43
  204.6 6.2 %collective-permute-start.51 = (f32[128,256]{1,0:T(8,128)S(1)}, f32[128,256]{1,0:T(8,128)S(1)}, u32[]{:S(2)}, u32[]{:S(2)}) collective-permute-start(f32[128,256]{1,0:T(8,128)S(1)} %shard_map.90), channel_id=1, source_target_pairs={{0,32},{16,48},{32,64},{48,80},{64,96},{80,112},{96,0},{112,16},{1... | collective-permute-start | bytes 393224 | tf_op jit(solution)/shard_map/ppermute | solution.py:43
  206.4 5.0 %collective-permute-start.52 = (f32[128,256]{1,0:T(8,128)S(1)}, f32[128,256]{1,0:T(8,128)S(1)}, u32[]{:S(2)}, u32[]{:S(2)}) collective-permute-start(f32[128,256]{1,0:T(8,128)S(1)} %shard_map.90), channel_id=1, source_target_pairs={{0,96},{16,112},{32,0},{48,16},{64,32},{80,48},{96,64},{112,80},{1... | collective-permute-start | bytes 393224 | tf_op jit(solution)/shard_map/ppermute | solution.py:43
  211.4 2.0 collective-permute-start.53
  215.9 10.9 %collective-permute-start.54 = (f32[4,128,256]{2,1,0:T(8,128)S(1)}, f32[4,128,256]{2,1,0:T(8,128)S(1)}, u32[]{:S(2)}, u32[]{:S(2)}) collective-permute-start(f32[4,128,256]{2,1,0:T(8,128)S(1)} %get-tuple-element.119), channel_id=1, source_target_pairs={{0,8},{1,9},{2,10},{3,11},{4,12},{5,13},{6,14},{7,15},{8,0},{9,1},... | collective-permute-start | bytes 1572872 | tf_op jit(solution)/shard_map/ppermute | solution.py:38
  217.5 14.8 %collective-permute-start.55 = (f32[4,128,256]{2,1,0:T(8,128)S(1)}, f32[4,128,256]{2,1,0:T(8,128)S(1)}, u32[]{:S(2)}, u32[]{:S(2)}) collective-permute-start(f32[4,128,256]{2,1,0:T(8,128)S(1)} %get-tuple-element.120), channel_id=1, source_target_pairs={{0,4},{1,5},{2,6},{3,7},{4,8},{5,9},{6,10},{7,11},{8,12},{9,13},{1... | collective-permute-start | bytes 1572872 | tf_op jit(solution)/shard_map/ppermute | solution.py:38
  218.9 13.4 %collective-permute-start.56 = (f32[4,128,256]{2,1,0:T(8,128)S(1)}, f32[4,128,256]{2,1,0:T(8,128)S(1)}, u32[]{:S(2)}, u32[]{:S(2)}) collective-permute-start(f32[4,128,256]{2,1,0:T(8,128)S(1)} %get-tuple-element.121), channel_id=1, source_target_pairs={{0,12},{1,13},{2,14},{3,15},{4,0},{5,1},{6,2},{7,3},{8,4},{9,5},{1... | collective-permute-start | bytes 1572872 | tf_op jit(solution)/shard_map/ppermute | solution.py:38
  232.3 6.6 %collective-permute-start.57 = (f32[128,256]{1,0:T(8,128)S(1)}, f32[128,256]{1,0:T(8,128)S(1)}, u32[]{:S(2)}, u32[]{:S(2)}) collective-permute-start(f32[128,256]{1,0:T(8,128)S(1)} %get-tuple-element.123), channel_id=1, source_target_pairs={{0,2},{1,3},{2,0},{3,1},{4,6},{5,7},{6,4},{7,5},{8,10},{9,11},{10,... | collective-permute-start | bytes 393224 | tf_op jit(solution)/shard_map/ppermute | solution.py:38
  233.5 6.8 %collective-permute-start.58 = (f32[128,256]{1,0:T(8,128)S(1)}, f32[128,256]{1,0:T(8,128)S(1)}, u32[]{:S(2)}, u32[]{:S(2)}) collective-permute-start(f32[128,256]{1,0:T(8,128)S(1)} %get-tuple-element.124), channel_id=1, source_target_pairs={{0,1},{1,2},{2,3},{3,0},{4,5},{5,6},{6,7},{7,4},{8,9},{9,10},{10,1... | collective-permute-start | bytes 393224 | tf_op jit(solution)/shard_map/ppermute | solution.py:38
  235.9 5.0 %collective-permute-start.59 = (f32[128,256]{1,0:T(8,128)S(1)}, f32[128,256]{1,0:T(8,128)S(1)}, u32[]{:S(2)}, u32[]{:S(2)}) collective-permute-start(f32[128,256]{1,0:T(8,128)S(1)} %get-tuple-element.125), channel_id=1, source_target_pairs={{0,3},{1,0},{2,1},{3,2},{4,7},{5,4},{6,5},{7,6},{8,11},{9,8},{10,9... | collective-permute-start | bytes 393224 | tf_op jit(solution)/shard_map/ppermute | solution.py:38
